TPU v7x, 32 devices: a whole 2x2x4 slice. The times are simulated.
32 devices in a mesh: grp: 2 (over x), ap: 16 (over z, y, core).
Axes of the slice: x: 2, y: 2, z: 4, core: 2. Of those that a mesh axis runs over, the one named last changes fastest.
Arguments:
- raw_echo: bfloat16 [2, 4096, 1024], P(None, 'ap', 'grp'), parts along dimension 2, may hold values from -6 to 6
- range_filter: float32 [2, 4096], replicated, may hold values from -4.2 to 4.2
- range_offsets: int32 [1024], P(('grp', 'ap')), parts along dimension 0, may hold values from 0 to 4095
- interp_weight: bfloat16 [2, 2, 2, 256, 128], replicated, may hold values from -0.25 to 0.25
- phase_rate: float32 [2], replicated, may hold values from 2 to 12
Outputs:
- focused: float32 [2, 1024, 32768], P(None, None, ('grp', 'ap')), parts along dimension 2
There are 2 independent parts, one for each index of `grp`. A program takes and returns all parts, laid end to end along the dimension named above; an argument that names none is the same for every part. Nothing has to cross between parts.
All inputs are finite; a program needn't handle non-finite values.
Results may differ from a plain program's by a relative error of at most 0.012.
Values may be sent and summed in bfloat16 or wider, within the bound.
No kernel may reach another device: no remote copies, remote signals or barrier semaphores. Data moves between devices by JAX's collectives and lax.ppermute only.
A program may use at most 128 MiB of HBM per device.

v0:
```python
import functools
import math

import jax
import jax.numpy as jnp
import ml_dtypes
import numpy as np
from jax import lax
from jax.experimental import pallas as pl
from jax.experimental.pallas import tpu as pltpu
from jax.sharding import PartitionSpec as P

A0 = 256
QUAD = 4
LANES = 128
FIRST = 16
TILE = 16


def as_real(matrix):
    top = np.concatenate([matrix.real, -matrix.imag], 1)
    low = np.concatenate([matrix.imag, matrix.real], 1)
    return np.concatenate([top, low], 0).astype(ml_dtypes.bfloat16)


def root(length, turns):
    return np.exp(-2j * np.pi / length * (turns % length))


def dft_tables(total):
    second = total // FIRST
    one = np.arange(FIRST)
    low = np.arange(TILE)
    k_one = one[:, None, None, None]
    l_row = low[None, :, None, None]
    n_one = one[None, None, :, None]
    l_col = low[None, None, None, :]
    same = l_row == l_col
    forward_one = root(FIRST, k_one * n_one) * root(total, l_row * k_one) * same
    forward_one = forward_one.reshape(FIRST * TILE, FIRST * TILE)
    two = np.arange(second)
    forward_two = root(second, two[:, None] * two[None, :])
    inverse_two = forward_two.conj()
    kept = np.arange(FIRST // QUAD)[:, None, None, None]
    inverse_one = (root(FIRST, kept * n_one) * root(total, l_col * n_one)).conj() * same
    inverse_one = inverse_one.reshape(FIRST // QUAD * TILE, FIRST * TILE)
    return [as_real(t) for t in (forward_one, forward_two, inverse_two, inverse_one)]


def steer_table(angle_count, pulse_count):
    angle_index = np.arange(angle_count)[:, None]
    pulse_index = np.arange(pulse_count)[None, :]
    value = root(angle_count, (angle_index + angle_count // 2) * pulse_index)
    value = value / math.sqrt(pulse_count)
    return np.stack([value.real, value.imag]).astype(ml_dtypes.bfloat16)


def unit(angle):
    return jnp.cos(angle), jnp.sin(angle)


def times(left, right):
    return (
        left[0] * right[0] - left[1] * right[1],
        left[0] * right[1] + left[1] * right[0],
    )


def spectrum_gain(range_filter, offsets, quarter, total):
    second = total // FIRST
    shift = offsets - quarter * (total // QUAD)
    k_one = jnp.arange(FIRST, dtype=jnp.int32)[:, None]
    k_two = jnp.arange(second, dtype=jnp.int32)[:, None]
    scale = -2.0 * math.pi / total
    part_one = unit(scale * (k_one * shift % total).astype(jnp.float32))
    part_two = unit(scale * (FIRST * k_two * shift % total).astype(jnp.float32))
    by_k = range_filter.reshape(2, second, FIRST).transpose(0, 2, 1) / total
    ramp = times(
        (part_one[0][:, None], part_one[1][:, None]),
        (part_two[0][None], part_two[1][None]),
    )
    return jnp.stack(times((by_k[0][:, :, None], by_k[1][:, :, None]), ramp))


def level_one_rows(weight, pulse_count):
    steer = jnp.asarray(steer_table(A0, pulse_count)).reshape(2, -1, weight.shape[3], pulse_count)
    dot = functools.partial(
        jnp.einsum, "cpj,bjq->bpcq", preferred_element_type=jnp.float32
    )
    real = dot(weight[:, 0], steer[0]) - dot(weight[:, 1], steer[1])
    imag = dot(weight[:, 0], steer[1]) + dot(weight[:, 1], steer[0])
    angles = real.shape[0] * real.shape[1]
    sign = jnp.array([1.0, -1.0], jnp.float32)[:, None]
    rows = []
    for factor in (1.0, sign):
        real_f = (real * factor).reshape(angles, 2 * pulse_count)
        imag_f = (imag * factor).reshape(angles, 2 * pulse_count)
        rows += [(real_f, -imag_f), (imag_f, real_f)]
    zero = jnp.zeros((angles, LANES - 2 * pulse_count), jnp.float32)
    first = [jnp.concatenate([a, zero, b, zero], 1) for a, b in rows]
    other = [jnp.concatenate([zero, a, zero, b], 1) for a, b in rows]
    return jnp.stack([jnp.stack(first), jnp.stack(other)]).astype(jnp.bfloat16)


def level_two_rows(weight):
    return jnp.concatenate(
        [
            jnp.concatenate([weight[:, 0], -weight[:, 1]], 2),
            jnp.concatenate([weight[:, 1], weight[:, 0]], 2),
        ],
        1,
    )


def phase_table(rate, angles, start, width, total):
    angle_pos = (jnp.arange(angles, dtype=jnp.float32) + 0.5) / angles - 0.5
    slope = (rate * angle_pos)[None, :, None]
    blocks = width // LANES
    block_start = (start + LANES * jnp.arange(blocks, dtype=jnp.int32)).astype(jnp.float32)
    coarse = unit(slope * (1.0 + block_start / total)[:, None, None])
    fine = unit(slope * (jnp.arange(LANES, dtype=jnp.float32) / total)[None, None, :])
    return jnp.stack(times(coarse, fine)).astype(jnp.bfloat16)


def kernel(
    count,
    total,
    place_ref,
    fone_ref,
    ftwo_ref,
    itwo_ref,
    ione_ref,
    gain_ref,
    rows_one_ref,
    rows_two_ref,
    phase_one_ref,
    phase_two_ref,
    *rest,
):
    pieces = rest[:count]
    out_ref, samples, partial_ref, folded, compressed, image, sem = rest[count:]
    groups = count // QUAD
    span = total // count
    second = total // FIRST
    chunks = second // TILE
    f32 = jnp.float32

    def dot(left, right):
        return jnp.dot(left, right, preferred_element_type=f32)

    @pl.when(pl.program_id(0) == 0)
    def _():
        group = place_ref[0]
        member = place_ref[1]
        copies = []
        for rel in range(QUAD):
            for step in range(groups):
                source = QUAD * lax.rem(group - step + groups, groups) + (member ^ rel)
                first_row = pl.multiple_of(source * span, span)
                copies.append(
                    pltpu.make_async_copy(
                        pieces[rel * groups + step],
                        samples.at[:, pl.ds(first_row, span), :],
                        sem,
                    )
                )
        for copy in copies:
            copy.start()
        for copy in copies:
            copy.wait()

        def chunk_of(part, chunk):
            picked = [
                samples[part, n_one * second + chunk * TILE : n_one * second + (chunk + 1) * TILE, :]
                for n_one in range(FIRST)
            ]
            return jnp.concatenate(picked, 0)

        half = FIRST * TILE
        for pair in range(chunks // 2):
            right = jnp.concatenate(
                [
                    jnp.concatenate([chunk_of(0, c), chunk_of(1, c)], 0)
                    for c in (2 * pair, 2 * pair + 1)
                ],
                1,
            )
            result = dot(fone_ref[...], right)
            for side in range(2):
                chunk = 2 * pair + side
                lanes = slice(side * LANES, (side + 1) * LANES)
                for k_one in range(FIRST):
                    real = result[k_one * TILE : (k_one + 1) * TILE, lanes]
                    imag = result[half + k_one * TILE : half + (k_one + 1) * TILE, lanes]
                    turn = -2.0 * math.pi * (TILE * chunk * k_one % total) / total
                    cosine, sine = math.cos(turn), math.sin(turn)
                    at = slice(chunk * TILE, (chunk + 1) * TILE)
                    partial_ref[k_one, 0, at, :] = (cosine * real - sine * imag).astype(jnp.bfloat16)
                    partial_ref[k_one, 1, at, :] = (cosine * imag + sine * real).astype(jnp.bfloat16)

        for pair in range(FIRST // 2):
            right = jnp.concatenate(
                [partial_ref[k].reshape(2 * second, LANES) for k in (2 * pair, 2 * pair + 1)], 1
            )
            result = dot(ftwo_ref[...], right)
            scaled = []
            for side in range(2):
                k_one = 2 * pair + side
                lanes = slice(side * LANES, (side + 1) * LANES)
                real, imag = result[:second, lanes], result[second:, lanes]
                gain_real, gain_imag = gain_ref[0, k_one], gain_ref[1, k_one]
                scaled.append(
                    jnp.concatenate(
                        [
                            (real * gain_real - imag * gain_imag).astype(jnp.bfloat16),
                            (real * gain_imag + imag * gain_real).astype(jnp.bfloat16),
                        ],
                        0,
                    )
                )
            result = dot(itwo_ref[...], jnp.concatenate(scaled, 1))
            for side in range(2):
                k_one = 2 * pair + side
                lanes = slice(side * LANES, (side + 1) * LANES)
                for chunk in range(chunks):
                    real = result[chunk * TILE : (chunk + 1) * TILE, lanes]
                    imag = result[second + chunk * TILE : second + (chunk + 1) * TILE, lanes]
                    turn = 2.0 * math.pi * (TILE * chunk * k_one % total) / total
                    cosine, sine = math.cos(turn), math.sin(turn)
                    at = slice(k_one * TILE, (k_one + 1) * TILE)
                    folded[chunk, 0, at, :] = (cosine * real - sine * imag).astype(jnp.bfloat16)
                    folded[chunk, 1, at, :] = (cosine * imag + sine * real).astype(jnp.bfloat16)

        kept = FIRST // QUAD
        for pair in range(chunks // 2):
            right = jnp.concatenate(
                [folded[c].reshape(2 * half, LANES) for c in (2 * pair, 2 * pair + 1)], 1
            )
            result = dot(ione_ref[...], right).astype(jnp.bfloat16)
            for side in range(2):
                chunk = 2 * pair + side
                lanes = slice(side * LANES, (side + 1) * LANES)
                for part in range(2):
                    for n_one in range(kept):
                        row = (part * kept + n_one) * TILE
                        compressed[
                            n_one * second + chunk * TILE : n_one * second + (chunk + 1) * TILE,
                            part * LANES : (part + 1) * LANES,
                        ] = result[row : row + TILE, lanes]

    width = out_ref.shape[2]
    blocks = width // LANES
    start = pl.multiple_of(pl.program_id(0) * width, width)
    columns = compressed[pl.ds(start, width), :]

    def phases(ref, rows):
        return [
            jnp.concatenate([ref[part, b, rows, :] for b in range(blocks)], 1).astype(f32)
            for part in range(2)
        ]

    block_angles = image.shape[3]
    for block in range(image.shape[1]):
        rows = slice(block * block_angles, (block + 1) * block_angles)
        cosine, sine = phases(phase_one_ref, rows)
        for pick in range(2):
            terms = [
                lax.dot_general(
                    rows_one_ref[pick, kind, rows, :],
                    columns,
                    (((1,), (1,)), ((), ())),
                    preferred_element_type=f32,
                )
                for kind in range(4)
            ]
            image[pick, block, 0] = (cosine * terms[0] + sine * terms[3]).astype(jnp.bfloat16)
            image[pick, block, 1] = (cosine * terms[1] - sine * terms[2]).astype(jnp.bfloat16)

    wide = rows_two_ref.shape[1] // 2
    for block in range(image.shape[1]):
        rows = slice(block * wide, (block + 1) * wide)
        cosine, sine = phases(phase_two_ref, rows)
        lower = dot(rows_two_ref[0], image[0, block].reshape(2 * block_angles, width))
        upper = dot(rows_two_ref[1], image[1, block].reshape(2 * block_angles, width))
        lower_real, lower_imag = lower[:wide], lower[wide:]
        upper_real, upper_imag = upper[:wide], upper[wide:]
        out_ref[0, rows, :] = cosine * (lower_real + upper_real) + sine * (lower_imag - upper_imag)
        out_ref[1, rows, :] = cosine * (lower_imag + upper_imag) + sine * (upper_real - lower_real)


def body(raw_echo, range_filter, range_offsets, interp_weight, phase_rate):
    count = lax.axis_size("ap")
    index = lax.axis_index("ap")
    total = range_filter.shape[1]
    pulse_count = range_offsets.shape[0]
    groups = count // QUAD
    group, member = index // QUAD, index % QUAD

    def move(value, target):
        return lax.ppermute(value, "ap", [(i, target(i)) for i in range(count)])

    def block_for(step):
        return lax.dynamic_slice_in_dim(
            raw_echo, (group + step) % groups * LANES, LANES, axis=2
        )

    own = [block_for(0)]
    for step in range(1, groups):
        own.append(move(block_for(step), lambda i, s=step: (i + QUAD * s) % count))
    across = [move(piece, lambda i: i ^ 2) for piece in own]
    beside = [move(piece, lambda i: i ^ 1) for piece in own]
    diagonal = [move(piece, lambda i: i ^ 1) for piece in across]
    pieces = own + beside + across + diagonal

    offset_near = jnp.stack([range_offsets, move(range_offsets, lambda i: i ^ 1)])
    offset_far = move(offset_near, lambda i: i ^ 2)
    offsets = jnp.concatenate([offset_near, offset_far])[
        jnp.arange(QUAD, dtype=jnp.int32) ^ member
    ].reshape(1, QUAD * pulse_count)

    gain = spectrum_gain(range_filter, offsets, member, total)
    rows_one = level_one_rows(interp_weight[0], pulse_count)
    rows_two = level_two_rows(interp_weight[1])
    width = total // QUAD
    start = member * width
    phase_one = phase_table(phase_rate[0], 2 * A0, start, width, total)
    phase_two = phase_table(phase_rate[1], 4 * A0, start, width, total)
    place = jnp.stack([group, member]).astype(jnp.int32)
    tables = [jnp.asarray(t) for t in dft_tables(total)]

    step_width = 256
    second = total // FIRST
    chunks = second // TILE

    def whole(array):
        return pl.BlockSpec(array.shape, lambda i, n=array.ndim: (0,) * n)

    def by_range(array):
        shape = array.shape[:1] + (step_width // LANES,) + array.shape[2:]
        return pl.BlockSpec(shape, lambda i: (0, i, 0, 0))

    bf16 = jnp.bfloat16
    return pl.pallas_call(
        functools.partial(kernel, count, total),
        grid=(width // step_width,),
        out_shape=jax.ShapeDtypeStruct((2, 4 * A0, width), jnp.float32),
        in_specs=[pl.BlockSpec(memory_space=pltpu.SMEM)]
        + [whole(a) for a in tables + [gain, rows_one, rows_two]]
        + [by_range(phase_one), by_range(phase_two)]
        + [pl.BlockSpec(memory_space=pl.ANY)] * len(pieces),
        out_specs=pl.BlockSpec((2, 4 * A0, step_width), lambda i: (0, 0, i)),
        scratch_shapes=[
            pltpu.VMEM((2, total, LANES), bf16),
            pltpu.VMEM((FIRST, 2, second, LANES), bf16),
            pltpu.VMEM((chunks, 2, FIRST * TILE, LANES), bf16),
            pltpu.VMEM((width, 2 * LANES), bf16),
            pltpu.VMEM((2, 4, 2, LANES, step_width), bf16),
            pltpu.SemaphoreType.DMA,
        ],
        compiler_params=pltpu.CompilerParams(vmem_limit_bytes=48 * 1024 * 1024),
    )(place, *tables, gain, rows_one, rows_two, phase_one, phase_two, *pieces)


def solution(mesh):
    placed = (P(None, "ap", "grp"), P(), P(("grp", "ap")), P(), P())
    return jax.shard_map(
        body, mesh=mesh, in_specs=placed, out_specs=P(None, None, ("grp", "ap")), check_vma=False
    )
```

profile of v0, /device:TPU:0, one launch (start us, length us, event | category | flops | bytes accessed | tf_op | source)
XLA Modules:
  0.0 75.1 jit_solution(1161202433165666373)
XLA Ops:
  0.0 1.9 %constant_dynamic-slice_fusion = (bf16[2,256,128]{2,1,0:T(8,128)(2,1)}, bf16[2,256,128]{2,1,0:T(8,128)(2,1)}, bf16[2,256,128]{2,1,0:T(8,128)(2,1)S(1)}, bf16[2,256,128]{2,1,0:T(8,128)(2,1)}) fusion(bf16[2,256,512]{2,1,0:T(8,128)(2,1)} %param.11, s32[]{:T(128)S(6)} %select_n.87, s32[]{:T(128)S(6)} %select_n.83, s32[]{:T(128)S(6)} %select_n.81, s32[]{:T(128)S(6)} %select_n.85), kind=kLoop, calls=%fused_computation.108 | loop fusion | bytes 1048592 | tf_op jit(solution)/shard_map/dynamic_slice | solution.py:303
  1.9 3.0 %collective-permute-start.9 = (bf16[2,256,128]{2,1,0:T(8,128)(2,1)S(1)}, bf16[2,256,128]{2,1,0:T(8,128)(2,1)S(1)}, u32[]{:S(2)}, u32[]{:S(2)}) collective-permute-start(bf16[2,256,128]{2,1,0:T(8,128)(2,1)S(1)} %get-tuple-element.11.rest_0_), channel_id=1, source_target_pairs={{0,2},{1,3},{2,0},{3,1},{4,6},{5,7},{6,4},{7,5},{8,10},{9,11},{10,... | collective-permute-start | bytes 393224 | tf_op jit(solution)/shard_map/ppermute | solution.py:300
  4.8 0.5 collective-permute-start
  5.3 3.6 %collective-permute-start.4 = (bf16[2,256,128]{2,1,0:T(8,128)(2,1)}, bf16[2,256,128]{2,1,0:T(8,128)(2,1)S(1)}, u32[]{:S(2)}, u32[]{:S(2)}) collective-permute-start(bf16[2,256,128]{2,1,0:T(8,128)(2,1)} %get-tuple-element.9), channel_id=1, source_target_pairs={{0,12},{1,13},{2,14},{3,15},{4,0},{5,1},{6,2},{7,3},{8,4},{9,5},{1... | collective-permute-start | bytes 393224 | tf_op jit(solution)/shard_map/ppermute | solution.py:300
  9.0 1.1 %fusion.37 = (bf16[1,2,2,256,128]{4,3,2,1,0:T(8,128)(2,1)S(1)}, bf16[1,2,2,256,128]{4,3,2,1,0:T(8,128)(2,1)S(1)}) fusion(bf16[2,2,2,256,128]{4,3,2,1,0:T(8,128)(2,1)} %param.14), kind=kLoop, calls=%fused_computation.117 | loop fusion | bytes 1048576 | tf_op jit(solution)/shard_map/slice | solution.py:323
  10.2 0.6 fusion.38
  10.8 0.7 add_multiply_fusion.1
  11.5 0.7 add_multiply_fusion
  12.2 0.7 multiply_cosine_fusion.3
  12.9 0.8 %multiply_cosine_fusion.2 = (f32[8,1024]{1,0:T(8,128)}, f32[8,1024]{1,0:T(8,128)}) fusion(f32[8]{0:T(128)S(1)} %multiply_add_fusion.2, f32[1024]{0:T(1024)S(1)} %add_multiply_fusion), kind=kLoop, calls=%fused_computation.85 | loop fusion | flops 8192 | bytes 69664 | tf_op jit(solution)/shard_map/cos | solution.py:59
  13.7 1.0 %multiply_cosine_fusion.1 = (f32[512,128]{1,0:T(8,128)S(1)}, f32[512,128]{1,0:T(8,128)S(1)}) fusion(f32[128]{0:T(128)S(1)} %iota_multiply_fusion.1, f32[512]{0:T(512)S(1)} %add_multiply_fusion.1), kind=kLoop, calls=%fused_computation.37 | loop fusion | flops 65536 | bytes 526848 | tf_op jit(solution)/shard_map/cos | solution.py:59
  14.7 1.9 %multiply_cosine_fusion = (f32[1024,128]{1,0:T(8,128)S(1)}, f32[1024,128]{1,0:T(8,128)S(1)}) fusion(f32[128]{0:T(128)S(1)} %iota_multiply_fusion.1, f32[1024]{0:T(1024)S(1)} %add_multiply_fusion), kind=kLoop, calls=%fused_computation.18 | loop fusion | flops 131072 | bytes 1053184 | tf_op jit(solution)/shard_map/cos | solution.py:59
  16.6 0.6 pad_clamp_fusion
  17.2 0.1 div.45
  17.4 0.7 slice_bitcast_fusion.5
  18.1 0.2 fusion.19
  18.2 0.2 fusion.20
  18.4 0.2 convolution_add_fusion
  18.6 0.8 %convert_bitcast_fusion.1 = (bf16[2,256,2,32]{1,3,2,0:T(8,128)(2,1)S(1)}, bf16[2,256,2,32]{1,3,2,0:T(8,128)(2,1)S(1)}, bf16[2,256,2,32]{1,3,2,0:T(8,128)(2,1)S(1...) fusion(f32[2]{0:T(128)} %constant.123.clone, ...), kind=kOutput, calls=%fused_computation.81 | convolution fusion | flops 8749056 | bytes 802824 | tf_op jit(solution)/shard_map/cpj,bjq->bpcq/dot_general | solution.py:90
  19.4 0.1 copy.24
  19.5 0.1 copy.26
  19.6 0.1 copy.31
  19.7 0.1 copy.33
  19.9 0.1 copy.28
  20.0 0.1 copy.29
  20.1 0.1 copy.25
  20.2 0.1 copy.27
  20.3 0.1 copy.35
  20.4 0.1 copy.36
  20.5 0.1 copy.32
  20.6 0.6 copy.55
  21.2 1.0 %copy.34 = bf16[512,64]{1,0:T(8,128)(2,1)S(1)} copy(bf16[512,64]{0,1:T(8,128)(2,1)} %bitcast.113) | data formatting | bytes 131072 | tf_op jit(solution)/shard_map/convert.44
  22.2 0.5 fusion.14
  22.8 0.5 fusion.12
  23.3 0.1 maximum_bitcast_fusion
  23.5 0.1 maximum_bitcast_fusion.1
  23.6 1.5 %pad_maximum_fusion.2.rows_one_ref = bf16[2,4,512,256]{3,2,1,0:T(8,128)(2,1)} fusion(bf16[1,4,512,256]{3,2,1,0:T(8,128)(2,1)S(1)} %maximum_bitcast_fusion.1, bf16[1,4,512,256]{3,2,1,0:T(8,128)(2,1)S(1)} %maximum_bitcast_fusion), kind=kLoop, calls=%fused_computation.5 | loop fusion | flops 1048576 | bytes 4194304 | tf_op jit(solution)/shard_map/stack | solution.py:102
  25.1 1.2 %subtract_convert_fusion.1 = (bf16[1,8,512,128]{3,2,1,0:T(8,128)(2,1)S(1)}, bf16[1,8,512,128]{3,2,1,0:T(8,128)(2,1)S(1)}) fusion(f32[512,128]{1,0:T(8,128)S(1)} %get-tuple-element.46, f32[8,512]{1,0:T(8,128)S(1)} %copy-done.10, f32[512,128]{1,0:T(8,128)S(1)} %get-tuple-element.45, f32[8,512]{1,0:T(8,128)S(1)} %get-tuple-element.43), kind=kLoop, calls=%fused_computation.8 | loop fusion | flops 4194304 | bytes 2654208 | tf_op jit(solution)/shard_map/convert.2
  26.4 1.6 %pad_maximum_fusion.3.phase_one_ref = bf16[2,8,512,128]{3,2,1,0:T(8,128)(2,1)} fusion(bf16[1,8,512,128]{3,2,1,0:T(8,128)(2,1)S(1)} %get-tuple-element.8, bf16[1,8,512,128]{3,2,1,0:T(8,128)(2,1)S(1)} %get-tuple-element.7), kind=kLoop, calls=%fused_computation.6 | loop fusion | flops 1048576 | bytes 4194304 | tf_op jit(solution)/shard_map/stack | solution.py:122
  28.0 2.5 %subtract_convert_fusion = (bf16[1,8,1024,128]{3,2,1,0:T(8,128)(2,1)S(1)}, bf16[1,8,1024,128]{3,2,1,0:T(8,128)(2,1)S(1)}) fusion(f32[1024,128]{1,0:T(8,128)S(1)} %get-tuple-element.42, f32[8,1024]{1,0:T(8,128)S(1)} %copy-done.7, f32[1024,128]{1,0:T(8,128)S(1)} %get-tuple-element.41, f32[8,1024]{1,0:T(8,128)S(1)} %copy-done.6), kind=kLoop, calls=%fused_computation.4 | loop fusion | flops 8388608 | bytes 5308416 | tf_op jit(solution)/shard_map/convert
  30.5 2.3 %pad_maximum_fusion.1.phase_two_ref = bf16[2,8,1024,128]{3,2,1,0:T(8,128)(2,1)} fusion(bf16[1,8,1024,128]{3,2,1,0:T(8,128)(2,1)S(1)} %get-tuple-element.6, bf16[1,8,1024,128]{3,2,1,0:T(8,128)(2,1)S(1)} %get-tuple-element.5), kind=kLoop, calls=%fused_computation.2 | loop fusion | flops 2097152 | bytes 8388608 | tf_op jit(solution)/shard_map/stack | solution.py:122
  32.9 0.6 pad_add_fusion.1
  33.5 0.5 collective-permute-start.1
  34.0 0.1 pad_add_fusion.2.place_ref
  34.1 0.1 copy.22
  34.2 2.9 %collective-permute-done.1 = s32[2,32]{1,0:T(2,128)S(1)} collective-permute-done((s32[2,32]{1,0:T(2,128)S(1)}, s32[2,32]{1,0:T(2,128)S(1)}, u32[]{:S(2)}, u32[]{:S(2)}) %collective-permute-start.1) | collective-permute-done | bytes 288 | tf_op jit(solution)/shard_map/ppermute | solution.py:300
  37.0 1.0 %collective-permute-start.3 = (bf16[2,256,128]{2,1,0:T(8,128)(2,1)S(1)}, bf16[2,256,128]{2,1,0:T(8,128)(2,1)S(1)}, u32[]{:S(2)}, u32[]{:S(2)}) collective-permute-start(bf16[2,256,128]{2,1,0:T(8,128)(2,1)S(1)} %copy-done.5), channel_id=1, source_target_pairs={{0,8},{1,9},{2,10},{3,11},{4,12},{5,13},{6,14},{7,15},{8,0},{9,1},... | collective-permute-start | bytes 393224 | tf_op jit(solution)/shard_map/ppermute | solution.py:300
  38.0 0.6 pad_add_fusion
  38.6 0.7 gather_fusion
  39.3 0.1 sub.77
  39.4 0.6 fusion.26
  40.0 0.1 fusion.34
  40.1 0.6 collective-permute-start.12
  40.7 4.1 %collective-permute-done.3.rest_2_ = bf16[2,256,128]{2,1,0:T(8,128)(2,1)S(1)} collective-permute-done((bf16[2,256,128]{2,1,0:T(8,128)(2,1)S(1)}, bf16[2,256,128]{2,1,0:T(8,128)(2,1)S(1)}, u32[]{:S(2)}, u32[]{:S(2)}) %collective-permute-start.3) | collective-permute-done | bytes 131104 | tf_op jit(solution)/shard_map/ppermute | solution.py:300
  44.7 0.5 collective-permute-start.10
  45.2 1.6 %collective-permute-start.11 = (bf16[2,256,128]{2,1,0:T(8,128)(2,1)S(1)}, bf16[2,256,128]{2,1,0:T(8,128)(2,1)S(1)}, u32[]{:S(2)}, u32[]{:S(2)}) collective-permute-start(bf16[2,256,128]{2,1,0:T(8,128)(2,1)S(1)} %collective-permute-done.3.rest_2_), channel_id=1, source_target_pairs={{0,2},{1,3},{2,0},{3,1},{4,6},{5,7},{6,4},{7,5},{8,10},{9,11},{10,... | collective-permute-start | bytes 393224 | tf_op jit(solution)/shard_map/ppermute | solution.py:300
  46.8 1.4 %multiply_subtract_fusion = (f32[1,16,256,128]{3,2,1,0:T(8,128)S(1)}, f32[1,16,256,128]{3,2,1,0:T(8,128)S(1)}) fusion(f32[16,256]{1,0:T(8,128)S(1)} %copy.22, f32[256,128]{1,0:T(8,128)S(1)} %get-tuple-element.48, f32[16,128]{1,0:T(8,128)S(1)} %get-tuple-element.56, f32[256,128]{1,0:T(8,128)S(1)} %get-tuple-element.47, f32[16,128]{1,0:T(8,128)S(1)} %get-tuple-element.55, ...), kind=kLoop, calls=%fused_computation.10 | loop fusion | flops 6291456 | bytes 4505600 | tf_op jit(solution)/shard_map/sub | solution.py:64
  48.2 0.2 collective-permute-start.7
  48.4 0.3 collective-permute-start.13
  48.8 2.2 %collective-permute-done.10.rest_9_ = bf16[2,256,128]{2,1,0:T(8,128)(2,1)S(1)} collective-permute-done((bf16[2,256,128]{2,1,0:T(8,128)(2,1)S(1)}, bf16[2,256,128]{2,1,0:T(8,128)(2,1)S(1)}, u32[]{:S(2)}, u32[]{:S(2)}) %collective-permute-start.10) | collective-permute-done | bytes 131104 | tf_op jit(solution)/shard_map/ppermute | solution.py:300
  51.0 0.5 collective-permute-start.14
  51.6 0.9 %collective-permute-done.11.rest_10_ = bf16[2,256,128]{2,1,0:T(8,128)(2,1)S(1)} collective-permute-done((bf16[2,256,128]{2,1,0:T(8,128)(2,1)S(1)}, bf16[2,256,128]{2,1,0:T(8,128)(2,1)S(1)}, u32[]{:S(2)}, u32[]{:S(2)}) %collective-permute-start.11) | collective-permute-done | bytes 131104 | tf_op jit(solution)/shard_map/ppermute | solution.py:300
  52.5 2.5 %pad_maximum_fusion.gain_ref = f32[2,16,256,128]{3,2,1,0:T(8,128)} fusion(f32[1,16,256,128]{3,2,1,0:T(8,128)S(1)} %get-tuple-element.24, f32[1,16,256,128]{3,2,1,0:T(8,128)S(1)} %get-tuple-element.23), kind=kLoop, calls=%fused_computation.1 | loop fusion | flops 1048576 | bytes 8388608 | tf_op jit(solution)/shard_map/stack | solution.py:82
  55.1 19.8 %shard_map.109 = f32[2,1024,1024]{2,1,0:T(8,128)} custom-call(s32[2]{0:T(128)S(1)} %pad_add_fusion.2.place_ref, bf16[512,512]{1,0:T(8,128)(2,1)S(1)} %copy-done.2, bf16[512,512]{1,0:T(8,128)(2,1)S(1)} %copy-done.1, bf16[512,512]{1,0:T(8,128)(2,1)S(1)} %copy-done, bf16[128,512]{1,0:T(8,128)(2,1)S(1)} %copy-done.3, ...), custom_call_target="tpu_custom_call" | custom-call | tf_op jit(solution)/shard_map/pallas_call | solution.py:343
  (64 shorter events, 0.4 us)
Async XLA Ops:
  0.0 10.2 %copy-start.12 = (f32[2]{0:T(128)S(1)}, f32[2]{0:T(128)}, u32[]{:S(2)}) copy-start(f32[2]{0:T(128)} %param.15) | copy-start | bytes 28
  1.9 43.4 %collective-permute-start.9 = (bf16[2,256,128]{2,1,0:T(8,128)(2,1)S(1)}, bf16[2,256,128]{2,1,0:T(8,128)(2,1)S(1)}, u32[]{:S(2)}, u32[]{:S(2)}) collective-permute-start(bf16[2,256,128]{2,1,0:T(8,128)(2,1)S(1)} %get-tuple-element.11.rest_0_), channel_id=1, source_target_pairs={{0,2},{1,3},{2,0},{3,1},{4,6},{5,7},{6,4},{7,5},{8,10},{9,11},{10,... | collective-permute-start | bytes 393224 | tf_op jit(solution)/shard_map/ppermute | solution.py:300
  4.8 40.4 %collective-permute-start.5 = (bf16[2,256,128]{2,1,0:T(8,128)(2,1)S(1)}, bf16[2,256,128]{2,1,0:T(8,128)(2,1)S(1)}, u32[]{:S(2)}, u32[]{:S(2)}) collective-permute-start(bf16[2,256,128]{2,1,0:T(8,128)(2,1)S(1)} %get-tuple-element.11.rest_0_), channel_id=1, source_target_pairs={{0,1},{1,0},{2,3},{3,2},{4,5},{5,4},{6,7},{7,6},{8,9},{9,8},{10,11... | collective-permute-start | bytes 393224 | tf_op jit(solution)/shard_map/ppermute | solution.py:300
  4.8 28.0 %collective-permute-start = (s32[32]{0:T(128)}, s32[32]{0:T(128)}, u32[]{:S(2)}, u32[]{:S(2)}) collective-permute-start(s32[32]{0:T(128)} %param.13), channel_id=1, source_target_pairs={{0,1},{1,0},{2,3},{3,2},{4,5},{5,4},{6,7},{7,6},{8,9},{9,8},{10,11... | collective-permute-start | bytes 392 | tf_op jit(solution)/shard_map/ppermute | solution.py:300
  5.3 34.7 %collective-permute-start.4 = (bf16[2,256,128]{2,1,0:T(8,128)(2,1)}, bf16[2,256,128]{2,1,0:T(8,128)(2,1)S(1)}, u32[]{:S(2)}, u32[]{:S(2)}) collective-permute-start(bf16[2,256,128]{2,1,0:T(8,128)(2,1)} %get-tuple-element.9), channel_id=1, source_target_pairs={{0,12},{1,13},{2,14},{3,15},{4,0},{5,1},{6,2},{7,3},{8,4},{9,5},{1... | collective-permute-start | bytes 393224 | tf_op jit(solution)/shard_map/ppermute | solution.py:300
  8.9 31.7 %collective-permute-start.2 = (bf16[2,256,128]{2,1,0:T(8,128)(2,1)}, bf16[2,256,128]{2,1,0:T(8,128)(2,1)S(1)}, u32[]{:S(2)}, u32[]{:S(2)}) collective-permute-start(bf16[2,256,128]{2,1,0:T(8,128)(2,1)} %get-tuple-element.10), channel_id=1, source_target_pairs={{0,4},{1,5},{2,6},{3,7},{4,8},{5,9},{6,10},{7,11},{8,12},{9,13},{1... | collective-permute-start | bytes 393224 | tf_op jit(solution)/shard_map/ppermute | solution.py:300
  9.0 8.3 %copy-start.11 = (f32[2,4096]{1,0:T(2,128)S(1)}, f32[2,4096]{1,0:T(2,128)}, u32[]{:S(2)}) copy-start(f32[2,4096]{1,0:T(2,128)} %param.12) | copy-start | bytes 98308
  10.0 8.0 %copy-start.8 = (bf16[2,128,32,1]{1,2,3,0:T(8,128)(2,1)S(1)}, bf16[2,128,32,1]{1,2,3,0:T(8,128)(2,1)}, u32[]{:S(2)}) copy-start(bf16[2,128,32,1]{1,2,3,0:T(8,128)(2,1)} %constant.133) | copy-start | bytes 49156
  10.1 8.1 %copy-start.9 = (bf16[2,128,32,1]{1,2,3,0:T(8,128)(2,1)S(1)}, bf16[2,128,32,1]{1,2,3,0:T(8,128)(2,1)}, u32[]{:S(2)}) copy-start(bf16[2,128,32,1]{1,2,3,0:T(8,128)(2,1)} %constant.132) | copy-start | bytes 49156
  23.6 1.5 %copy-start.10 = (f32[8,512]{1,0:T(8,128)S(1)}, f32[8,512]{1,0:T(8,128)}, u32[]{:S(2)}) copy-start(f32[8,512]{1,0:T(8,128)} %get-tuple-element.44) | copy-start | bytes 49156
  26.4 1.6 %copy-start.6 = (f32[8,1024]{1,0:T(8,128)S(1)}, f32[8,1024]{1,0:T(8,128)}, u32[]{:S(2)}) copy-start(f32[8,1024]{1,0:T(8,128)} %get-tuple-element.39) | copy-start | bytes 98308
  26.4 1.6 %copy-start.7 = (f32[8,1024]{1,0:T(8,128)S(1)}, f32[8,1024]{1,0:T(8,128)}, u32[]{:S(2)}) copy-start(f32[8,1024]{1,0:T(8,128)} %get-tuple-element.40) | copy-start | bytes 98308
  30.4 2.4 %copy-start.13 = (s32[32]{0:T(128)S(1)}, s32[32]{0:T(128)}, u32[]{:S(2)}) copy-start(s32[32]{0:T(128)} %param.13) | copy-start | bytes 388
  30.5 3.6 %copy-start.4 = (f32[16,256]{0,1:T(8,128)S(1)}, f32[16,256]{0,1:T(8,128)}, u32[]{:S(2)}) copy-start(f32[16,256]{0,1:T(8,128)} %get-tuple-element.31) | copy-start | bytes 49156
  30.5 6.6 %copy-start.5 = (bf16[2,256,128]{2,1,0:T(8,128)(2,1)S(1)}, bf16[2,256,128]{2,1,0:T(8,128)(2,1)}, u32[]{:S(2)}) copy-start(bf16[2,256,128]{2,1,0:T(8,128)(2,1)} %get-tuple-element.12) | copy-start | bytes 393220
  33.5 3.6 %collective-permute-start.1 = (s32[2,32]{1,0:T(2,128)S(1)}, s32[2,32]{1,0:T(2,128)S(1)}, u32[]{:S(2)}, u32[]{:S(2)}) collective-permute-start(s32[2,32]{1,0:T(2,128)S(1)} %pad_add_fusion.1), channel_id=1, source_target_pairs={{0,2},{1,3},{2,0},{3,1},{4,6},{5,7},{6,4},{7,5},{8,10},{9,11},{10,... | collective-permute-start | bytes 776 | tf_op jit(solution)/shard_map/ppermute | solution.py:300
  37.0 7.7 %collective-permute-start.3 = (bf16[2,256,128]{2,1,0:T(8,128)(2,1)S(1)}, bf16[2,256,128]{2,1,0:T(8,128)(2,1)S(1)}, u32[]{:S(2)}, u32[]{:S(2)}) collective-permute-start(bf16[2,256,128]{2,1,0:T(8,128)(2,1)S(1)} %copy-done.5), channel_id=1, source_target_pairs={{0,8},{1,9},{2,10},{3,11},{4,12},{5,13},{6,14},{7,15},{8,0},{9,1},... | collective-permute-start | bytes 393224 | tf_op jit(solution)/shard_map/ppermute | solution.py:300
  40.1 8.1 %collective-permute-start.12 = (bf16[2,256,128]{2,1,0:T(8,128)(2,1)S(1)}, bf16[2,256,128]{2,1,0:T(8,128)(2,1)S(1)}, u32[]{:S(2)}, u32[]{:S(2)}) collective-permute-start(bf16[2,256,128]{2,1,0:T(8,128)(2,1)S(1)} %collective-permute-done.4.rest_3_), channel_id=1, source_target_pairs={{0,2},{1,3},{2,0},{3,1},{4,6},{5,7},{6,4},{7,5},{8,10},{9,11},{10,... | collective-permute-start | bytes 393224 | tf_op jit(solution)/shard_map/ppermute | solution.py:300
  40.7 7.8 %collective-permute-start.8 = (bf16[2,256,128]{2,1,0:T(8,128)(2,1)S(1)}, bf16[2,256,128]{2,1,0:T(8,128)(2,1)S(1)}, u32[]{:S(2)}, u32[]{:S(2)}) collective-permute-start(bf16[2,256,128]{2,1,0:T(8,128)(2,1)S(1)} %collective-permute-done.4.rest_3_), channel_id=1, source_target_pairs={{0,1},{1,0},{2,3},{3,2},{4,5},{5,4},{6,7},{7,6},{8,9},{9,8},{10,11... | collective-permute-start | bytes 393224 | tf_op jit(solution)/shard_map/ppermute | solution.py:300
  44.7 6.3 %collective-permute-start.10 = (bf16[2,256,128]{2,1,0:T(8,128)(2,1)S(1)}, bf16[2,256,128]{2,1,0:T(8,128)(2,1)S(1)}, u32[]{:S(2)}, u32[]{:S(2)}) collective-permute-start(bf16[2,256,128]{2,1,0:T(8,128)(2,1)S(1)} %collective-permute-done.2.rest_1_), channel_id=1, source_target_pairs={{0,2},{1,3},{2,0},{3,1},{4,6},{5,7},{6,4},{7,5},{8,10},{9,11},{10,... | collective-permute-start | bytes 393224 | tf_op jit(solution)/shard_map/ppermute | solution.py:300
  45.2 5.8 %collective-permute-start.6 = (bf16[2,256,128]{2,1,0:T(8,128)(2,1)S(1)}, bf16[2,256,128]{2,1,0:T(8,128)(2,1)S(1)}, u32[]{:S(2)}, u32[]{:S(2)}) collective-permute-start(bf16[2,256,128]{2,1,0:T(8,128)(2,1)S(1)} %collective-permute-done.2.rest_1_), channel_id=1, source_target_pairs={{0,1},{1,0},{2,3},{3,2},{4,5},{5,4},{6,7},{7,6},{8,9},{9,8},{10,11... | collective-permute-start | bytes 393224 | tf_op jit(solution)/shard_map/ppermute | solution.py:300
  45.2 7.3 %collective-permute-start.11 = (bf16[2,256,128]{2,1,0:T(8,128)(2,1)S(1)}, bf16[2,256,128]{2,1,0:T(8,128)(2,1)S(1)}, u32[]{:S(2)}, u32[]{:S(2)}) collective-permute-start(bf16[2,256,128]{2,1,0:T(8,128)(2,1)S(1)} %collective-permute-done.3.rest_2_), channel_id=1, source_target_pairs={{0,2},{1,3},{2,0},{3,1},{4,6},{5,7},{6,4},{7,5},{8,10},{9,11},{10,... | collective-permute-start | bytes 393224 | tf_op jit(solution)/shard_map/ppermute | solution.py:300
  48.2 6.8 %collective-permute-start.7 = (bf16[2,256,128]{2,1,0:T(8,128)(2,1)S(1)}, bf16[2,256,128]{2,1,0:T(8,128)(2,1)S(1)}, u32[]{:S(2)}, u32[]{:S(2)}) collective-permute-start(bf16[2,256,128]{2,1,0:T(8,128)(2,1)S(1)} %collective-permute-done.3.rest_2_), channel_id=1, source_target_pairs={{0,1},{1,0},{2,3},{3,2},{4,5},{5,4},{6,7},{7,6},{8,9},{9,8},{10,11... | collective-permute-start | bytes 393224 | tf_op jit(solution)/shard_map/ppermute | solution.py:300
  48.4 6.6 %collective-permute-start.13 = (bf16[2,256,128]{2,1,0:T(8,128)(2,1)S(1)}, bf16[2,256,128]{2,1,0:T(8,128)(2,1)S(1)}, u32[]{:S(2)}, u32[]{:S(2)}) collective-permute-start(bf16[2,256,128]{2,1,0:T(8,128)(2,1)S(1)} %collective-permute-done.9.rest_8_), channel_id=1, source_target_pairs={{0,1},{1,0},{2,3},{3,2},{4,5},{5,4},{6,7},{7,6},{8,9},{9,8},{10,11... | collective-permute-start | bytes 393224 | tf_op jit(solution)/shard_map/ppermute | solution.py:300
  51.0 4.0 %collective-permute-start.16 = (bf16[2,256,128]{2,1,0:T(8,128)(2,1)S(1)}, bf16[2,256,128]{2,1,0:T(8,128)(2,1)S(1)}, u32[]{:S(2)}, u32[]{:S(2)}) collective-permute-start(bf16[2,256,128]{2,1,0:T(8,128)(2,1)S(1)} %collective-permute-done.12.rest_11_), channel_id=1, source_target_pairs={{0,1},{1,0},{2,3},{3,2},{4,5},{5,4},{6,7},{7,6},{8,9},{9,8},{10,11... | collective-permute-start | bytes 393224 | tf_op jit(solution)/shard_map/ppermute | solution.py:300
  51.0 4.0 %collective-permute-start.14 = (bf16[2,256,128]{2,1,0:T(8,128)(2,1)S(1)}, bf16[2,256,128]{2,1,0:T(8,128)(2,1)S(1)}, u32[]{:S(2)}, u32[]{:S(2)}) collective-permute-start(bf16[2,256,128]{2,1,0:T(8,128)(2,1)S(1)} %collective-permute-done.10.rest_9_), channel_id=1, source_target_pairs={{0,1},{1,0},{2,3},{3,2},{4,5},{5,4},{6,7},{7,6},{8,9},{9,8},{10,11... | collective-permute-start | bytes 393224 | tf_op jit(solution)/shard_map/ppermute | solution.py:300
  52.5 2.5 %collective-permute-start.15 = (bf16[2,256,128]{2,1,0:T(8,128)(2,1)S(1)}, bf16[2,256,128]{2,1,0:T(8,128)(2,1)S(1)}, u32[]{:S(2)}, u32[]{:S(2)}) collective-permute-start(bf16[2,256,128]{2,1,0:T(8,128)(2,1)S(1)} %collective-permute-done.11.rest_10_), channel_id=1, source_target_pairs={{0,1},{1,0},{2,3},{3,2},{4,5},{5,4},{6,7},{7,6},{8,9},{9,8},{10,11... | collective-permute-start | bytes 393224 | tf_op jit(solution)/shard_map/ppermute | solution.py:300
  52.5 2.5 %copy-start = (bf16[512,512]{1,0:T(8,128)(2,1)S(1)}, bf16[512,512]{1,0:T(8,128)(2,1)}, u32[]{:S(2)}) copy-start(bf16[512,512]{1,0:T(8,128)(2,1)} %constant.126.clone.itwo_ref) | copy-start | bytes 1572868
  52.5 2.5 %copy-start.1 = (bf16[512,512]{1,0:T(8,128)(2,1)S(1)}, bf16[512,512]{1,0:T(8,128)(2,1)}, u32[]{:S(2)}) copy-start(bf16[512,512]{1,0:T(8,128)(2,1)} %constant.125.clone.ftwo_ref) | copy-start | bytes 1572868
  52.5 2.6 %copy-start.2 = (bf16[512,512]{1,0:T(8,128)(2,1)S(1)}, bf16[512,512]{1,0:T(8,128)(2,1)}, u32[]{:S(2)}) copy-start(bf16[512,512]{1,0:T(8,128)(2,1)} %constant.124.clone.fone_ref) | copy-start | bytes 1572868
  52.5 2.6 %copy-start.3 = (bf16[128,512]{1,0:T(8,128)(2,1)S(1)}, bf16[128,512]{1,0:T(8,128)(2,1)}, u32[]{:S(2)}) copy-start(bf16[128,512]{1,0:T(8,128)(2,1)} %constant.127.clone.ione_ref) | copy-start | bytes 393220
where the time goes:
time: 75.4 us; the launch traced here: 75.1 us
  other arithmetic  22.7 us (30%)
  Pallas kernels  19.8 us (26%)
  starting transfers between devices  12.3 us (16%)
  waiting for transfers between devices  10.2 us (14%)
  local copies, waits for them, and re-layouts  8.04 us (11%)
  matrix products  1.35 us (2%)
    pallas_call x1, Pallas kernels, body(): pl.pallas_call(functools.partial(kernel, count, total), grid=(width // st...  19.8 us
    ppermute x17, starting transfers between devices, move(): return lax.ppermute(value, 'ap', [(i, target(i)) for i in range(count)])  12.3 us
    ppermute x17, waiting for transfers between devices, move(): return lax.ppermute(value, 'ap', [(i, target(i)) for i in range(count)])  10.2 us
    cos x6, other arithmetic, unit(): return (jnp.cos(angle), jnp.sin(angle))  5.08 us
    another operation x2, other arithmetic, phase_table(): return jnp.stack(times(coarse, fine)).astype(jnp.bfloat16)  3.93 us
    another operation x2, other arithmetic  3.68 us
    another operation x5, other arithmetic, level_one_rows(): return jnp.stack([jnp.stack(first), jnp.stack(other)]).astype(jnp.bfloat16)  2.85 us
    another operation x1, other arithmetic, spectrum_gain(): return jnp.stack(times((by_k[0][:, :, None], by_k[1][:, :, None]), ramp))  2.48 us
  transfers between devices with their start and end apart: 17, of which 4 were waited for; matrix products, arithmetic and copies ran while one was open for 40% of the time, Pallas kernels for 0%

commit v1 on v0

v1 whole, which is shorter than its diff:
```python
import functools
import math

import jax
import jax.numpy as jnp
import ml_dtypes
import numpy as np
from jax import lax
from jax.experimental import pallas as pl
from jax.experimental.pallas import tpu as pltpu
from jax.sharding import PartitionSpec as P

A0 = 256
QUAD = 4
LANES = 128
FIRST = 16
TILE = 16


def as_real(matrix):
    top = np.concatenate([matrix.real, -matrix.imag], 1)
    low = np.concatenate([matrix.imag, matrix.real], 1)
    return np.concatenate([top, low], 0).astype(ml_dtypes.bfloat16)


def root(length, turns):
    return np.exp(-2j * np.pi / length * (turns % length))


def dft_tables(total):
    second = total // FIRST
    one = np.arange(FIRST)
    low = np.arange(TILE)
    k_one = one[:, None, None, None]
    l_row = low[None, :, None, None]
    n_one = one[None, None, :, None]
    l_col = low[None, None, None, :]
    same = l_row == l_col
    forward_one = root(FIRST, k_one * n_one) * root(total, l_row * k_one) * same
    forward_one = forward_one.reshape(FIRST * TILE, FIRST * TILE)
    two = np.arange(second)
    forward_two = root(second, two[:, None] * two[None, :])
    inverse_two = forward_two.conj()
    kept = np.arange(FIRST // QUAD)[:, None, None, None]
    inverse_one = (root(FIRST, kept * n_one) * root(total, l_col * n_one)).conj() * same
    inverse_one = inverse_one.reshape(FIRST // QUAD * TILE, FIRST * TILE)
    return [as_real(t) for t in (forward_one, forward_two, inverse_two, inverse_one)]


def steer_table(angle_count, pulse_count):
    angle_index = np.arange(angle_count)[:, None]
    pulse_index = np.arange(pulse_count)[None, :]
    value = root(angle_count, (angle_index + angle_count // 2) * pulse_index)
    value = (value / math.sqrt(pulse_count)).astype(np.complex64)
    return value.real.astype(ml_dtypes.bfloat16), value.imag.astype(ml_dtypes.bfloat16)


def steer_blocks(pulse_count, child_angles):
    real, imag = steer_table(A0, pulse_count)
    real, imag = real[:child_angles], imag[:child_angles]
    table = np.zeros((2, 2, child_angles, 2, 2, 2, 2, 2, pulse_count), ml_dtypes.bfloat16)
    for pair in range(2):
        for child in range(2):
            spot = (pair, child)
            table[child, 0, :, pair, 0, 0, *spot] = real
            table[child, 0, :, pair, 0, 1, *spot] = -imag
            table[child, 1, :, pair, 0, 0, *spot] = -imag
            table[child, 1, :, pair, 0, 1, *spot] = -real
            table[child, 0, :, pair, 1, 0, *spot] = imag
            table[child, 0, :, pair, 1, 1, *spot] = real
            table[child, 1, :, pair, 1, 0, *spot] = real
            table[child, 1, :, pair, 1, 1, *spot] = -imag
    return table.reshape(4 * child_angles, 32 * pulse_count)


def small_unit(angle):
    square = angle * angle
    cosine = 1.0 + square * (-1 / 2 + square * (1 / 24 + square * (-1 / 720 + square / 40320)))
    sine = angle * (1.0 + square * (-1 / 6 + square * (1 / 120 + square * (-1 / 5040))))
    return cosine, sine


def unit(angle):
    quarter = jnp.floor(angle * (2.0 / math.pi) + 0.5)
    rest = angle - quarter * 1.5703125
    rest = rest - quarter * (math.pi / 2 - 1.5703125)
    cosine, sine = small_unit(rest)
    turn = quarter.astype(jnp.int32)
    odd = (turn & 1) == 1
    first = jnp.where(odd, sine, cosine)
    second = jnp.where(odd, cosine, sine)
    first = jnp.where(((turn + 1) & 2) == 2, -first, first)
    second = jnp.where((turn & 2) == 2, -second, second)
    return first, second


def times(left, right):
    return (
        left[0] * right[0] - left[1] * right[1],
        left[0] * right[1] + left[1] * right[0],
    )


def cut_kernel(place_ref, raw_ref, *outs):
    for step, out in enumerate(outs):
        first = pl.multiple_of((place_ref[0] ^ step) * LANES, LANES)
        out[...] = raw_ref[:, :, pl.ds(first, LANES)]


def phase_kernel(total, place_ref, rate_ref, one_ref, two_ref):
    start = (place_ref[1] * (total // QUAD)).astype(jnp.float32)
    size = (LANES, LANES)
    for level, ref in ((0, one_ref), (1, two_ref)):
        blocks, angles = ref.shape[1], ref.shape[2]
        rate = rate_ref[level]
        lane = lax.broadcasted_iota(jnp.int32, size, 1).astype(jnp.float32)
        factor = 1.0 + (lane + start) / total

        @pl.loop(0, angles // LANES)
        def _(part):
            row = lax.broadcasted_iota(jnp.int32, size, 0) + part * LANES
            slope = rate * ((row.astype(jnp.float32) + 0.5) / angles - 0.5)
            value = unit(slope * factor)
            step = unit(slope * (LANES / total))
            at = pl.ds(pl.multiple_of(part * LANES, LANES), LANES)
            for block in range(blocks):
                ref[0, block, at, :] = value[0].astype(jnp.bfloat16)
                ref[1, block, at, :] = value[1].astype(jnp.bfloat16)
                if block + 1 < blocks:
                    value = times(value, step)


def weight_kernel(pulse_count, weight_ref, steer_ref, one_ref, two_ref):
    joined = jnp.concatenate([weight_ref[0, c, part] for c in range(2) for part in range(2)], 1)
    parents = joined.shape[0]
    width = one_ref.shape[3]
    lane = lax.broadcasted_iota(jnp.int32, (parents, width), 1)
    odd_pulse = lane % 2 == 1
    odd_child = lane // pulse_count % 2 == 1
    for pair in range(2):
        for part in range(2):
            at = (pair * 2 + part) * width
            value = jnp.dot(
                joined, steer_ref[:, at : at + width], preferred_element_type=jnp.float32
            )
            for block in range(one_ref.shape[2] // parents):
                rows = slice(block * parents, (block + 1) * parents)
                turned = jnp.where(odd_pulse, -value, value) if block % 2 else value
                one_ref[pair, part, rows, :] = turned.astype(jnp.bfloat16)
                one_ref[pair, 2 + part, rows, :] = jnp.where(odd_child, -turned, turned).astype(
                    jnp.bfloat16
                )
    for child in range(2):
        real, imag = weight_ref[1, child, 0], weight_ref[1, child, 1]
        two_ref[child] = jnp.concatenate(
            [jnp.concatenate([real, -imag], 1), jnp.concatenate([imag, real], 1)], 0
        )


def gain_kernel(total, place_ref, offset_ref, filter_ref, out_ref):
    second = total // FIRST
    offsets = jnp.concatenate(
        [
            offset_ref[pl.ds(place_ref[1] ^ member, 1), :]
            for member in range(QUAD)
        ],
        1,
    )
    shift = offsets - place_ref[1] * (total // QUAD)
    scale = -2.0 * math.pi / total

    def ramp(rows, stride):
        k_index = stride * lax.broadcasted_iota(jnp.int32, (rows, LANES), 0)
        return unit(scale * ((k_index * shift) & (total - 1)).astype(jnp.float32))

    low, high = ramp(FIRST, 1), ramp(second, FIRST)
    for k_one in range(FIRST):
        row = (low[0][k_one : k_one + 1] * (1.0 / total), low[1][k_one : k_one + 1] * (1.0 / total))
        column = (filter_ref[0, :, k_one : k_one + 1], filter_ref[1, :, k_one : k_one + 1])
        value = times(times(high, row), column)
        out_ref[0, k_one] = value[0]
        out_ref[1, k_one] = value[1]


def kernel(
    count,
    total,
    place_ref,
    fone_ref,
    ftwo_ref,
    itwo_ref,
    ione_ref,
    gain_ref,
    rows_one_ref,
    rows_two_ref,
    phase_one_ref,
    phase_two_ref,
    *rest,
):
    pieces = rest[:count]
    out_ref, samples, partial_ref, folded, compressed, image, ready, sems = rest[count:]
    groups = count // QUAD
    span = total // count
    second = total // FIRST
    chunks = second // TILE
    f32 = jnp.float32

    def dot(left, right):
        return jnp.dot(left, right, preferred_element_type=f32)

    index = place_ref[0] * QUAD + place_ref[1]
    for number, piece in enumerate(pieces):
        source = index ^ number
        first_row = pl.multiple_of(source * span, span)
        samples[:, pl.ds(first_row, span), :] = piece[...]

    def chunk_of(part, chunk):
        picked = [
            samples[part, n_one * second + chunk * TILE : n_one * second + (chunk + 1) * TILE, :]
            for n_one in range(FIRST)
        ]
        return jnp.concatenate(picked, 0)

    half = FIRST * TILE
    for pair in range(chunks // 2):
        right = jnp.concatenate(
            [
                jnp.concatenate([chunk_of(0, c), chunk_of(1, c)], 0)
                for c in (2 * pair, 2 * pair + 1)
            ],
            1,
        )
        result = dot(fone_ref[...], right)
        for side in range(2):
            chunk = 2 * pair + side
            lanes = slice(side * LANES, (side + 1) * LANES)
            for k_one in range(FIRST):
                real = result[k_one * TILE : (k_one + 1) * TILE, lanes]
                imag = result[half + k_one * TILE : half + (k_one + 1) * TILE, lanes]
                turn = -2.0 * math.pi * (TILE * chunk * k_one % total) / total
                cosine, sine = math.cos(turn), math.sin(turn)
                at = slice(chunk * TILE, (chunk + 1) * TILE)
                partial_ref[k_one, 0, at, :] = (cosine * real - sine * imag).astype(jnp.bfloat16)
                partial_ref[k_one, 1, at, :] = (cosine * imag + sine * real).astype(jnp.bfloat16)

    for pair in range(FIRST // 2):
        right = jnp.concatenate(
            [partial_ref[k].reshape(2 * second, LANES) for k in (2 * pair, 2 * pair + 1)], 1
        )
        result = dot(ftwo_ref[...], right)
        scaled = []
        for side in range(2):
            k_one = 2 * pair + side
            lanes = slice(side * LANES, (side + 1) * LANES)
            real, imag = result[:second, lanes], result[second:, lanes]
            gain_real, gain_imag = gain_ref[0, k_one], gain_ref[1, k_one]
            scaled.append(
                jnp.concatenate(
                    [
                        (real * gain_real - imag * gain_imag).astype(jnp.bfloat16),
                        (real * gain_imag + imag * gain_real).astype(jnp.bfloat16),
                    ],
                    0,
                )
            )
        result = dot(itwo_ref[...], jnp.concatenate(scaled, 1))
        for side in range(2):
            k_one = 2 * pair + side
            lanes = slice(side * LANES, (side + 1) * LANES)
            for chunk in range(chunks):
                real = result[chunk * TILE : (chunk + 1) * TILE, lanes]
                imag = result[second + chunk * TILE : second + (chunk + 1) * TILE, lanes]
                turn = 2.0 * math.pi * (TILE * chunk * k_one % total) / total
                cosine, sine = math.cos(turn), math.sin(turn)
                at = slice(k_one * TILE, (k_one + 1) * TILE)
                folded[chunk, 0, at, :] = (cosine * real - sine * imag).astype(jnp.bfloat16)
                folded[chunk, 1, at, :] = (cosine * imag + sine * real).astype(jnp.bfloat16)

    kept = FIRST // QUAD
    for pair in range(chunks // 2):
        right = jnp.concatenate(
            [folded[c].reshape(2 * half, LANES) for c in (2 * pair, 2 * pair + 1)], 1
        )
        result = dot(ione_ref[...], right).astype(jnp.bfloat16)
        for side in range(2):
            chunk = 2 * pair + side
            lanes = slice(side * LANES, (side + 1) * LANES)
            for part in range(2):
                for n_one in range(kept):
                    row = (part * kept + n_one) * TILE
                    compressed[
                        n_one * second + chunk * TILE : n_one * second + (chunk + 1) * TILE,
                        part * LANES : (part + 1) * LANES,
                    ] = result[row : row + TILE, lanes]

    width = image.shape[4]
    blocks = width // LANES
    block_angles = image.shape[3]
    steps = compressed.shape[0] // width

    def out_copy(step):
        at = pl.ds(step * width, width)
        return pltpu.make_async_copy(
            ready.at[step % 2], out_ref.at[:, :, at], sems.at[step % 2]
        )

    for step in range(steps):
        slot = step % 2
        columns = compressed[step * width : (step + 1) * width, :]

        def phases(ref, rows):
            return [
                jnp.concatenate(
                    [ref[part, step * blocks + b, rows, :] for b in range(blocks)], 1
                ).astype(f32)
                for part in range(2)
            ]

        for block in range(image.shape[1]):
            rows = slice(block * block_angles, (block + 1) * block_angles)
            cosine, sine = phases(phase_one_ref, rows)
            for pick in range(2):
                terms = [
                    lax.dot_general(
                        rows_one_ref[pick, kind, rows, :],
                        columns,
                        (((1,), (1,)), ((), ())),
                        preferred_element_type=f32,
                    )
                    for kind in range(4)
                ]
                image[pick, block, 0] = (cosine * terms[0] + sine * terms[3]).astype(jnp.bfloat16)
                image[pick, block, 1] = (cosine * terms[1] - sine * terms[2]).astype(jnp.bfloat16)

        if step >= 2:
            out_copy(step - 2).wait()
        wide = rows_two_ref.shape[1] // 2
        for block in range(image.shape[1]):
            rows = slice(block * wide, (block + 1) * wide)
            cosine, sine = phases(phase_two_ref, rows)
            lower = dot(rows_two_ref[0], image[0, block].reshape(2 * block_angles, width))
            upper = dot(rows_two_ref[1], image[1, block].reshape(2 * block_angles, width))
            lower_real, lower_imag = lower[:wide], lower[wide:]
            upper_real, upper_imag = upper[:wide], upper[wide:]
            ready[slot, 0, rows, :] = cosine * (lower_real + upper_real) + sine * (
                lower_imag - upper_imag
            )
            ready[slot, 1, rows, :] = cosine * (lower_imag + upper_imag) + sine * (
                upper_real - lower_real
            )
        out_copy(step).start()
    for step in range(max(steps - 2, 0), steps):
        out_copy(step).wait()


def body(raw_echo, range_filter, range_offsets, interp_weight, phase_rate):
    count = lax.axis_size("ap")
    index = lax.axis_index("ap")
    total = range_filter.shape[1]
    pulse_count = range_offsets.shape[0]
    groups = count // QUAD
    width = total // QUAD
    step_width = 256
    second = total // FIRST
    chunks = second // TILE
    f32, bf16 = jnp.float32, jnp.bfloat16
    smem = pl.BlockSpec(memory_space=pltpu.SMEM)
    vmem = pl.BlockSpec(memory_space=pltpu.VMEM)
    far = pl.BlockSpec(memory_space=pl.ANY)
    place = jnp.stack([index // QUAD, index % QUAD]).astype(jnp.int32)

    def move(value, bits):
        return lax.ppermute(value, "ap", [(i, i ^ bits) for i in range(count)])

    def shape(dims, kind=bf16):
        return jax.ShapeDtypeStruct(dims, kind)

    small = pltpu.CompilerParams(vmem_limit_bytes=2 * 1024 * 1024)

    def cost(flops, moved):
        return pl.CostEstimate(flops=flops, bytes_accessed=moved, transcendentals=0)

    cut = pl.pallas_call(
        cut_kernel,
        out_shape=[shape((2, total // count, LANES))] * groups,
        in_specs=[smem, vmem],
        out_specs=[vmem] * groups,
        compiler_params=small,
    )(place, raw_echo)
    own = [cut[0]] + [move(cut[step], QUAD * step) for step in range(1, groups)]
    across = [move(piece, 2) for piece in own]
    beside = [move(piece, 1) for piece in own]
    diagonal = [move(piece, 1) for piece in across]
    pieces = [part for four in zip(own, beside, across, diagonal) for part in four]

    offset_near = jnp.stack([range_offsets, move(range_offsets, 1)])
    offsets = jnp.concatenate([offset_near, move(offset_near, 2)])

    phase_one, phase_two = pl.pallas_call(
        functools.partial(phase_kernel, total),
        out_shape=[
            shape((2, width // LANES, 2 * A0, LANES)),
            shape((2, width // LANES, 4 * A0, LANES)),
        ],
        in_specs=[smem, smem],
        out_specs=[vmem, vmem],
        cost_estimate=cost(2**30, 2**23),
        compiler_params=small,
    )(place, phase_rate)
    child_angles = interp_weight.shape[4]
    rows_one, rows_two = pl.pallas_call(
        functools.partial(weight_kernel, pulse_count),
        out_shape=[
            shape((2, 4, 2 * A0, 2 * LANES)),
            shape((2, 2 * interp_weight.shape[3], 2 * child_angles)),
        ],
        in_specs=[vmem, vmem],
        out_specs=[vmem, vmem],
        cost_estimate=cost(2**29, 2**22),
        compiler_params=small,
    )(interp_weight, jnp.asarray(steer_blocks(pulse_count, child_angles)))
    gain = pl.pallas_call(
        functools.partial(gain_kernel, total),
        out_shape=shape((2, FIRST, second, LANES), f32),
        in_specs=[smem, vmem, vmem],
        out_specs=vmem,
        cost_estimate=cost(2**28, 2**22),
        compiler_params=small,
    )(place, offsets, range_filter.reshape(2, second, FIRST))

    tables = [jnp.asarray(t) for t in dft_tables(total)]
    return pl.pallas_call(
        functools.partial(kernel, count, total),
        out_shape=shape((2, 4 * A0, width), f32),
        in_specs=[smem] + [vmem] * (9 + count),
        out_specs=far,
        scratch_shapes=[
            pltpu.VMEM((2, total, LANES), bf16),
            pltpu.VMEM((FIRST, 2, second, LANES), bf16),
            pltpu.VMEM((chunks, 2, FIRST * TILE, LANES), bf16),
            pltpu.VMEM((width, 2 * LANES), bf16),
            pltpu.VMEM((2, 4, 2, child_angles, step_width), bf16),
            pltpu.VMEM((2, 2, 4 * A0, step_width), f32),
            pltpu.SemaphoreType.DMA((2,)),
        ],
        compiler_params=pltpu.CompilerParams(vmem_limit_bytes=24 * 1024 * 1024),
    )(place, *tables, gain, rows_one, rows_two, phase_one, phase_two, *pieces)


def solution(mesh):
    placed = (P(None, "ap", "grp"), P(), P(("grp", "ap")), P(), P())
    return jax.shard_map(
        body, mesh=mesh, in_specs=placed, out_specs=P(None, None, ("grp", "ap")), check_vma=False
    )
```

time: 75.4 us -> 49.2 us (0.65)
  other arithmetic: 22.7 us -> 0.75 us
  waiting for transfers between devices: 10.2 us -> 6.77 us
  Pallas kernels: 19.8 us -> 23.2 us
  local copies, waits for them, and re-layouts: 8.04 us -> 4.87 us
  matrix products: 1.35 us -> 0 us
    another operation x12 -> x2, other arithmetic: 13.6 us -> 0.74 us  [the longest x1 0.66 us: body(): offset_near = jnp.stack([range_offsets, move(range_offsets, 1)])]
    cos x6 -> x0, other arithmetic: 5.08 us -> none  [unit(): return (jnp.cos(angle), jnp.sin(angle))]
    ppermute x17, waiting for transfers between devices: 10.2 us -> 6.77 us  [move(): return lax.ppermute(value, 'ap', [(i, i ^ bits) for i in range(count)])]
    pallas_call x1 -> x5, Pallas kernels: 19.8 us -> 23.2 us  [the longest x1 15.7 us: body(): pl.pallas_call(functools.partial(kernel, count, total), out_shape=shape((...]
    unnamed x34 -> x18, local copies, waits for them, and re-layouts: 0.76 us -> 3.98 us
    another operation x12 -> x0, local copies, waits for them, and re-layouts: 1.97 us -> none
    dynamic_slice x1 -> x0, local copies, waits for them, and re-layouts: 1.86 us -> none  [block_for(): lax.dynamic_slice_in_dim(raw_echo, (group + step) % groups * LANES, LANES...]
    slice x2 -> x0, local copies, waits for them, and re-layouts: 1.67 us -> none  [the longest x1 1.08 us: body(): rows_two = level_two_rows(interp_weight[1])]
  transfers between devices with their start and end apart: 17 -> 17, of which waited for: 4 -> 1; matrix products, arithmetic and copies ran while one was open for 40% -> 3% of each run, Pallas kernels for 0% -> 15%
where the time goes in v1:
time: 49.2 us; the launch traced here: 48.8 us
  Pallas kernels  23.2 us (47%)
  starting transfers between devices  12.9 us (26%)
  waiting for transfers between devices  6.77 us (14%)
  local copies, waits for them, and re-layouts  4.87 us (10%)
  other arithmetic  0.75 us (2%)
    pallas_call x1, Pallas kernels, body(): pl.pallas_call(functools.partial(kernel, count, total), out_shape=shape((...  15.7 us
    ppermute x17, starting transfers between devices, move(): return lax.ppermute(value, 'ap', [(i, i ^ bits) for i in range(count)])  12.9 us
    ppermute x17, waiting for transfers between devices, move(): return lax.ppermute(value, 'ap', [(i, i ^ bits) for i in range(count)])  6.77 us
    pallas_call x1, Pallas kernels, body(): pl.pallas_call(functools.partial(phase_kernel, total), out_shape=[shape((...  4.37 us
    unnamed x18, local copies, waits for them, and re-layouts  3.98 us
    pallas_call x1, Pallas kernels, body(): pl.pallas_call(functools.partial(gain_kernel, total), out_shape=shape((2,...  1.93 us
  transfers between devices with their start and end apart: 17, of which 1 were waited for; matrix products, arithmetic and copies ran while one was open for 3% of the time, Pallas kernels for 15%

profile of v1, /device:TPU:0, one launch (start us, length us, event | category | flops | bytes accessed | tf_op | source)
XLA Modules:
  0.0 48.8 jit_solution(7168915855378339803)
XLA Ops:
  0.0 0.0 copy-start.8
  0.0 0.5 collective-permute-start
  0.5 0.1 pad_add_fusion.2.place_ref
  0.5 0.0 copy-start.3
  0.5 1.0 %copy-done.3 = bf16[2,256,512]{2,1,0:T(8,128)(2,1)S(1)} copy-done((bf16[2,256,512]{2,1,0:T(8,128)(2,1)S(1)}, bf16[2,256,512]{2,1,0:T(8,128)(2,1)}, u32[]{:S(2)}) %copy-start.3) | copy-done | bytes 524312
  1.6 0.6 %shard_map.103 = (bf16[2,256,128]{2,1,0:T(8,128)(2,1)S(1)}, bf16[2,256,128]{2,1,0:T(8,128)(2,1)S(1)}, bf16[2,256,128]{2,1,0:T(8,128)(2,1)S(1)}, bf16[2,256,128]{2,1,0:T(8,128)(2,1)S(1)}) custom-call(s32[2]{0:T(128)S(1)} %pad_add_fusion.2.place_ref, bf16[2,256,512]{2,1,0:T(8,128)(2,1)S(1)} %copy-done.3), custom_call_target="tpu_custom_call" | custom-call | tf_op jit(solution)/shard_map/pallas_call | solution.py:383
  2.2 2.6 %collective-permute-start.5 = (bf16[2,256,128]{2,1,0:T(8,128)(2,1)S(1)}, bf16[2,256,128]{2,1,0:T(8,128)(2,1)S(1)}, u32[]{:S(2)}, u32[]{:S(2)}) collective-permute-start(bf16[2,256,128]{2,1,0:T(8,128)(2,1)S(1)} %get-tuple-element.18), channel_id=1, source_target_pairs={{0,4},{1,5},{2,6},{3,7},{4,0},{5,1},{6,2},{7,3},{8,12},{9,13},{10,... | collective-permute-start | bytes 393224 | tf_op jit(solution)/shard_map/ppermute | solution.py:373
  4.9 0.0 collective-permute-done
  4.9 0.7 %pad_add_fusion.1 = s32[2,32]{1,0:T(2,128)S(1)} fusion(s32[1,32]{1,0:T(1,128)S(1)} %bitcast.6, s32[1,32]{1,0:T(1,128)} %bitcast.4), kind=kLoop, calls=%fused_computation.1 | loop fusion | flops 64 | bytes 512 | tf_op jit(solution)/shard_map/stack | solution.py:396
  5.5 1.5 %collective-permute-start.1 = (s32[2,32]{1,0:T(2,128)S(1)}, s32[2,32]{1,0:T(2,128)S(1)}, u32[]{:S(2)}, u32[]{:S(2)}) collective-permute-start(s32[2,32]{1,0:T(2,128)S(1)} %pad_add_fusion.1), channel_id=1, source_target_pairs={{0,2},{1,3},{2,0},{3,1},{4,6},{5,7},{6,4},{7,5},{8,10},{9,11},{10,... | collective-permute-start | bytes 776 | tf_op jit(solution)/shard_map/ppermute | solution.py:373
  7.0 2.6 %collective-permute-start.9 = (bf16[2,256,128]{2,1,0:T(8,128)(2,1)S(1)}, bf16[2,256,128]{2,1,0:T(8,128)(2,1)S(1)}, u32[]{:S(2)}, u32[]{:S(2)}) collective-permute-start(bf16[2,256,128]{2,1,0:T(8,128)(2,1)S(1)} %get-tuple-element.19), channel_id=1, source_target_pairs={{0,8},{1,9},{2,10},{3,11},{4,12},{5,13},{6,14},{7,15},{8,0},{9,1},... | collective-permute-start | bytes 393224 | tf_op jit(solution)/shard_map/ppermute | solution.py:373
  9.6 0.2 collective-permute-start.13
  9.9 0.3 collective-permute-start.3
  10.1 0.0 collective-permute-done.1
  10.1 0.0 collective-permute-start.2
  10.2 0.9 %reshape.3.filter_ref = f32[2,256,16]{2,1,0:T(8,128)S(1)} reshape(f32[2,4096]{1,0:T(2,128)} %param.11) | data formatting | bytes 65536 | tf_op jit(solution)/shard_map/reshape | solution.py:429
  11.0 0.0 collective-permute-done.5.rest_4_
  11.1 1.8 %collective-permute-start.7 = (bf16[2,256,128]{2,1,0:T(8,128)(2,1)S(1)}, bf16[2,256,128]{2,1,0:T(8,128)(2,1)S(1)}, u32[]{:S(2)}, u32[]{:S(2)}) collective-permute-start(bf16[2,256,128]{2,1,0:T(8,128)(2,1)S(1)} %collective-permute-done.5.rest_4_), channel_id=1, source_target_pairs={{0,2},{1,3},{2,0},{3,1},{4,6},{5,7},{6,4},{7,5},{8,10},{9,11},{10,... | collective-permute-start | bytes 393224 | tf_op jit(solution)/shard_map/ppermute | solution.py:373
  12.9 6.7 %collective-permute-done.9.rest_8_ = bf16[2,256,128]{2,1,0:T(8,128)(2,1)S(1)} collective-permute-done((bf16[2,256,128]{2,1,0:T(8,128)(2,1)S(1)}, bf16[2,256,128]{2,1,0:T(8,128)(2,1)S(1)}, u32[]{:S(2)}, u32[]{:S(2)}) %collective-permute-start.9) | collective-permute-done | bytes 131104 | tf_op jit(solution)/shard_map/ppermute | solution.py:373
  19.6 0.0 collective-permute-start.6
  19.6 0.0 collective-permute-done.13.rest_12_
  19.6 0.8 %collective-permute-start.11 = (bf16[2,256,128]{2,1,0:T(8,128)(2,1)S(1)}, bf16[2,256,128]{2,1,0:T(8,128)(2,1)S(1)}, u32[]{:S(2)}, u32[]{:S(2)}) collective-permute-start(bf16[2,256,128]{2,1,0:T(8,128)(2,1)S(1)} %collective-permute-done.9.rest_8_), channel_id=1, source_target_pairs={{0,2},{1,3},{2,0},{3,1},{4,6},{5,7},{6,4},{7,5},{8,10},{9,11},{10,... | collective-permute-start | bytes 393224 | tf_op jit(solution)/shard_map/ppermute | solution.py:373
  20.4 0.0 collective-permute-done.3.rest_2_
  20.4 0.2 collective-permute-start.10
  20.7 0.0 collective-permute-done.2.rest_1_
  20.7 1.2 %collective-permute-start.15 = (bf16[2,256,128]{2,1,0:T(8,128)(2,1)S(1)}, bf16[2,256,128]{2,1,0:T(8,128)(2,1)S(1)}, u32[]{:S(2)}, u32[]{:S(2)}) collective-permute-start(bf16[2,256,128]{2,1,0:T(8,128)(2,1)S(1)} %collective-permute-done.13.rest_12_), channel_id=1, source_target_pairs={{0,2},{1,3},{2,0},{3,1},{4,6},{5,7},{6,4},{7,5},{8,10},{9,11},{10,... | collective-permute-start | bytes 393224 | tf_op jit(solution)/shard_map/ppermute | solution.py:373
  21.9 0.0 copy-start.5
  21.9 1.0 %copy-done.5 = bf16[2,2,2,256,128]{4,3,2,1,0:T(8,128)(2,1)S(1)} copy-done((bf16[2,2,2,256,128]{4,3,2,1,0:T(8,128)(2,1)S(1)}, bf16[2,2,2,256,128]{4,3,2,1,0:T(8,128)(2,1)}, u32[]{:S(2)}) %copy-start.5) | copy-done | bytes 524312
  22.9 0.0 copy-start.7
  22.9 1.2 %copy-done.7 = bf16[512,1024]{1,0:T(8,128)(2,1)S(1)} copy-done((bf16[512,1024]{1,0:T(8,128)(2,1)S(1)}, bf16[512,1024]{1,0:T(8,128)(2,1)}, u32[]{:S(2)}) %copy-start.7) | copy-done | bytes 1048600
  24.1 0.5 %shard_map.101 = (bf16[2,4,512,256]{3,2,1,0:T(8,128)(2,1)S(1)}, bf16[2,512,256]{2,1,0:T(8,128)(2,1)S(1)}) custom-call(bf16[2,2,2,256,128]{4,3,2,1,0:T(8,128)(2,1)S(1)} %copy-done.5, bf16[512,1024]{1,0:T(8,128)(2,1)S(1)} %copy-done.7), custom_call_target="tpu_custom_call" | custom-call | flops 536870912 | bytes 4194304 | tf_op jit(solution)/shard_map/pallas_call | solution.py:411
  24.7 0.0 copy-start.6
  24.7 0.6 %copy-done.6 = f32[2]{0:T(128)S(1)} copy-done((f32[2]{0:T(128)S(1)}, f32[2]{0:T(128)}, u32[]{:S(2)}) %copy-start.6) | copy-done | bytes 32
  25.3 0.0 copy-start
  25.3 0.0 copy-start.1
  25.3 0.0 copy-start.2
  25.3 0.0 copy-start.4
  25.4 4.4 %shard_map.102 = (bf16[2,8,512,128]{3,2,1,0:T(8,128)(2,1)S(1)}, bf16[2,8,1024,128]{3,2,1,0:T(8,128)(2,1)S(1)}) custom-call(s32[2]{0:T(128)S(1)} %pad_add_fusion.2.place_ref, f32[2]{0:T(128)S(1)} %copy-done.6), custom_call_target="tpu_custom_call" | custom-call | flops 1073741824 | bytes 8388608 | tf_op jit(solution)/shard_map/pallas_call | solution.py:399
  29.7 0.0 collective-permute-done.7.rest_6_
  29.7 0.1 collective-permute-start.14
  29.8 0.0 collective-permute-done.6.rest_5_
  29.8 0.5 %collective-permute-start.4 = (bf16[2,256,128]{2,1,0:T(8,128)(2,1)S(1)}, bf16[2,256,128]{2,1,0:T(8,128)(2,1)S(1)}, u32[]{:S(2)}, u32[]{:S(2)}) collective-permute-start(bf16[2,256,128]{2,1,0:T(8,128)(2,1)S(1)} %collective-permute-done.3.rest_2_), channel_id=1, source_target_pairs={{0,1},{1,0},{2,3},{3,2},{4,5},{5,4},{6,7},{7,6},{8,9},{9,8},{10,11... | collective-permute-start | bytes 393224 | tf_op jit(solution)/shard_map/ppermute | solution.py:373
  30.3 0.0 collective-permute-done.11.rest_10_
  30.3 0.1 collective-permute-start.8
  30.4 0.0 collective-permute-done.10.rest_9_
  30.4 0.4 collective-permute-start.12
  30.8 0.0 collective-permute-done.15.rest_14_
  30.8 0.1 collective-permute-start.16
  30.9 0.0 copy-done.8
  30.9 1.9 %shard_map.100.gain_ref = f32[2,16,256,128]{3,2,1,0:T(8,128)S(1)} custom-call(s32[2]{0:T(128)S(1)} %pad_add_fusion.2.place_ref, s32[4,32]{1,0:T(4,128)S(1)} %pad_add_fusion.offset_ref, f32[2,256,16]{2,1,0:T(8,128)S(1)} %reshape.3.filter_ref), custom_call_target="tpu_custom_call" | custom-call | flops 268435456 | bytes 4194304 | tf_op jit(solution)/shard_map/pallas_call | solution.py:422
  32.9 0.0 collective-permute-done.14.rest_13_
  32.9 0.0 collective-permute-done.4.rest_3_
  32.9 0.0 collective-permute-done.8.rest_7_
  32.9 0.0 collective-permute-done.12.rest_11_
  32.9 0.0 collective-permute-done.16.rest_15_
  32.9 0.0 copy-done
  32.9 0.0 copy-done.1
  32.9 0.0 copy-done.2
  33.0 0.0 copy-done.4
  33.0 15.7 %shard_map.104 = f32[2,1024,1024]{2,1,0:T(8,128)} custom-call(s32[2]{0:T(128)S(1)} %pad_add_fusion.2.place_ref, bf16[512,512]{1,0:T(8,128)(2,1)S(1)} %copy-done.2, bf16[512,512]{1,0:T(8,128)(2,1)S(1)} %copy-done.1, bf16[512,512]{1,0:T(8,128)(2,1)S(1)} %copy-done, bf16[128,512]{1,0:T(8,128)(2,1)S(1)} %copy-done.4, ...), custom_call_target="tpu_custom_call" | custom-call | tf_op jit(solution)/shard_map/pallas_call | solution.py:432
  (1 shorter events, 0.0 us)
Async XLA Ops:
  0.0 30.9 %copy-start.8 = (s32[32]{0:T(128)S(1)}, s32[32]{0:T(128)}, u32[]{:S(2)}) copy-start(s32[32]{0:T(128)} %param.12) | copy-start | bytes 388
  0.0 4.9 %collective-permute-start = (s32[32]{0:T(128)}, s32[32]{0:T(128)S(1)}, u32[]{:S(2)}, u32[]{:S(2)}) collective-permute-start(s32[32]{0:T(128)} %param.12), channel_id=1, source_target_pairs={{0,1},{1,0},{2,3},{3,2},{4,5},{5,4},{6,7},{7,6},{8,9},{9,8},{10,11... | collective-permute-start | bytes 392 | tf_op jit(solution)/shard_map/ppermute | solution.py:373
  0.5 1.0 %copy-start.3 = (bf16[2,256,512]{2,1,0:T(8,128)(2,1)S(1)}, bf16[2,256,512]{2,1,0:T(8,128)(2,1)}, u32[]{:S(2)}) copy-start(bf16[2,256,512]{2,1,0:T(8,128)(2,1)} %raw_ref.1) | copy-start | bytes 1572868
  2.2 8.8 %collective-permute-start.5 = (bf16[2,256,128]{2,1,0:T(8,128)(2,1)S(1)}, bf16[2,256,128]{2,1,0:T(8,128)(2,1)S(1)}, u32[]{:S(2)}, u32[]{:S(2)}) collective-permute-start(bf16[2,256,128]{2,1,0:T(8,128)(2,1)S(1)} %get-tuple-element.18), channel_id=1, source_target_pairs={{0,4},{1,5},{2,6},{3,7},{4,0},{5,1},{6,2},{7,3},{8,12},{9,13},{10,... | collective-permute-start | bytes 393224 | tf_op jit(solution)/shard_map/ppermute | solution.py:373
  5.5 4.6 %collective-permute-start.1 = (s32[2,32]{1,0:T(2,128)S(1)}, s32[2,32]{1,0:T(2,128)S(1)}, u32[]{:S(2)}, u32[]{:S(2)}) collective-permute-start(s32[2,32]{1,0:T(2,128)S(1)} %pad_add_fusion.1), channel_id=1, source_target_pairs={{0,2},{1,3},{2,0},{3,1},{4,6},{5,7},{6,4},{7,5},{8,10},{9,11},{10,... | collective-permute-start | bytes 776 | tf_op jit(solution)/shard_map/ppermute | solution.py:373
  7.0 12.5 %collective-permute-start.9 = (bf16[2,256,128]{2,1,0:T(8,128)(2,1)S(1)}, bf16[2,256,128]{2,1,0:T(8,128)(2,1)S(1)}, u32[]{:S(2)}, u32[]{:S(2)}) collective-permute-start(bf16[2,256,128]{2,1,0:T(8,128)(2,1)S(1)} %get-tuple-element.19), channel_id=1, source_target_pairs={{0,8},{1,9},{2,10},{3,11},{4,12},{5,13},{6,14},{7,15},{8,0},{9,1},... | collective-permute-start | bytes 393224 | tf_op jit(solution)/shard_map/ppermute | solution.py:373
  9.6 10.0 %collective-permute-start.13 = (bf16[2,256,128]{2,1,0:T(8,128)(2,1)S(1)}, bf16[2,256,128]{2,1,0:T(8,128)(2,1)S(1)}, u32[]{:S(2)}, u32[]{:S(2)}) collective-permute-start(bf16[2,256,128]{2,1,0:T(8,128)(2,1)S(1)} %get-tuple-element.20), channel_id=1, source_target_pairs={{0,12},{1,13},{2,14},{3,15},{4,8},{5,9},{6,10},{7,11},{8,4},{9,5},... | collective-permute-start | bytes 393224 | tf_op jit(solution)/shard_map/ppermute | solution.py:373
  9.9 10.6 %collective-permute-start.3 = (bf16[2,256,128]{2,1,0:T(8,128)(2,1)S(1)}, bf16[2,256,128]{2,1,0:T(8,128)(2,1)S(1)}, u32[]{:S(2)}, u32[]{:S(2)}) collective-permute-start(bf16[2,256,128]{2,1,0:T(8,128)(2,1)S(1)} %get-tuple-element.17.rest_0_), channel_id=1, source_target_pairs={{0,2},{1,3},{2,0},{3,1},{4,6},{5,7},{6,4},{7,5},{8,10},{9,11},{10,... | collective-permute-start | bytes 393224 | tf_op jit(solution)/shard_map/ppermute | solution.py:373
  10.1 10.5 %collective-permute-start.2 = (bf16[2,256,128]{2,1,0:T(8,128)(2,1)S(1)}, bf16[2,256,128]{2,1,0:T(8,128)(2,1)S(1)}, u32[]{:S(2)}, u32[]{:S(2)}) collective-permute-start(bf16[2,256,128]{2,1,0:T(8,128)(2,1)S(1)} %get-tuple-element.17.rest_0_), channel_id=1, source_target_pairs={{0,1},{1,0},{2,3},{3,2},{4,5},{5,4},{6,7},{7,6},{8,9},{9,8},{10,11... | collective-permute-start | bytes 393224 | tf_op jit(solution)/shard_map/ppermute | solution.py:373
  11.1 18.7 %collective-permute-start.7 = (bf16[2,256,128]{2,1,0:T(8,128)(2,1)S(1)}, bf16[2,256,128]{2,1,0:T(8,128)(2,1)S(1)}, u32[]{:S(2)}, u32[]{:S(2)}) collective-permute-start(bf16[2,256,128]{2,1,0:T(8,128)(2,1)S(1)} %collective-permute-done.5.rest_4_), channel_id=1, source_target_pairs={{0,2},{1,3},{2,0},{3,1},{4,6},{5,7},{6,4},{7,5},{8,10},{9,11},{10,... | collective-permute-start | bytes 393224 | tf_op jit(solution)/shard_map/ppermute | solution.py:373
  19.6 10.2 %collective-permute-start.6 = (bf16[2,256,128]{2,1,0:T(8,128)(2,1)S(1)}, bf16[2,256,128]{2,1,0:T(8,128)(2,1)S(1)}, u32[]{:S(2)}, u32[]{:S(2)}) collective-permute-start(bf16[2,256,128]{2,1,0:T(8,128)(2,1)S(1)} %collective-permute-done.5.rest_4_), channel_id=1, source_target_pairs={{0,1},{1,0},{2,3},{3,2},{4,5},{5,4},{6,7},{7,6},{8,9},{9,8},{10,11... | collective-permute-start | bytes 393224 | tf_op jit(solution)/shard_map/ppermute | solution.py:373
  19.6 10.7 %collective-permute-start.11 = (bf16[2,256,128]{2,1,0:T(8,128)(2,1)S(1)}, bf16[2,256,128]{2,1,0:T(8,128)(2,1)S(1)}, u32[]{:S(2)}, u32[]{:S(2)}) collective-permute-start(bf16[2,256,128]{2,1,0:T(8,128)(2,1)S(1)} %collective-permute-done.9.rest_8_), channel_id=1, source_target_pairs={{0,2},{1,3},{2,0},{3,1},{4,6},{5,7},{6,4},{7,5},{8,10},{9,11},{10,... | collective-permute-start | bytes 393224 | tf_op jit(solution)/shard_map/ppermute | solution.py:373
  20.4 10.0 %collective-permute-start.10 = (bf16[2,256,128]{2,1,0:T(8,128)(2,1)S(1)}, bf16[2,256,128]{2,1,0:T(8,128)(2,1)S(1)}, u32[]{:S(2)}, u32[]{:S(2)}) collective-permute-start(bf16[2,256,128]{2,1,0:T(8,128)(2,1)S(1)} %collective-permute-done.9.rest_8_), channel_id=1, source_target_pairs={{0,1},{1,0},{2,3},{3,2},{4,5},{5,4},{6,7},{7,6},{8,9},{9,8},{10,11... | collective-permute-start | bytes 393224 | tf_op jit(solution)/shard_map/ppermute | solution.py:373
  20.7 10.2 %collective-permute-start.15 = (bf16[2,256,128]{2,1,0:T(8,128)(2,1)S(1)}, bf16[2,256,128]{2,1,0:T(8,128)(2,1)S(1)}, u32[]{:S(2)}, u32[]{:S(2)}) collective-permute-start(bf16[2,256,128]{2,1,0:T(8,128)(2,1)S(1)} %collective-permute-done.13.rest_12_), channel_id=1, source_target_pairs={{0,2},{1,3},{2,0},{3,1},{4,6},{5,7},{6,4},{7,5},{8,10},{9,11},{10,... | collective-permute-start | bytes 393224 | tf_op jit(solution)/shard_map/ppermute | solution.py:373
  21.9 1.0 %copy-start.5 = (bf16[2,2,2,256,128]{4,3,2,1,0:T(8,128)(2,1)S(1)}, bf16[2,2,2,256,128]{4,3,2,1,0:T(8,128)(2,1)}, u32[]{:S(2)}) copy-start(bf16[2,2,2,256,128]{4,3,2,1,0:T(8,128)(2,1)} %weight_ref.1) | copy-start | bytes 1572868
  22.9 1.2 %copy-start.7 = (bf16[512,1024]{1,0:T(8,128)(2,1)S(1)}, bf16[512,1024]{1,0:T(8,128)(2,1)}, u32[]{:S(2)}) copy-start(bf16[512,1024]{1,0:T(8,128)(2,1)} %constant.40.clone.steer_ref) | copy-start | bytes 3145732
  24.7 0.7 %copy-start.6 = (f32[2]{0:T(128)S(1)}, f32[2]{0:T(128)}, u32[]{:S(2)}) copy-start(f32[2]{0:T(128)} %rate_ref.1) | copy-start | bytes 28
  25.3 7.6 %copy-start = (bf16[512,512]{1,0:T(8,128)(2,1)S(1)}, bf16[512,512]{1,0:T(8,128)(2,1)}, u32[]{:S(2)}) copy-start(bf16[512,512]{1,0:T(8,128)(2,1)} %constant.43.clone.itwo_ref) | copy-start | bytes 1572868
  25.3 7.6 %copy-start.1 = (bf16[512,512]{1,0:T(8,128)(2,1)S(1)}, bf16[512,512]{1,0:T(8,128)(2,1)}, u32[]{:S(2)}) copy-start(bf16[512,512]{1,0:T(8,128)(2,1)} %constant.42.clone.ftwo_ref) | copy-start | bytes 1572868
  25.3 7.6 %copy-start.2 = (bf16[512,512]{1,0:T(8,128)(2,1)S(1)}, bf16[512,512]{1,0:T(8,128)(2,1)}, u32[]{:S(2)}) copy-start(bf16[512,512]{1,0:T(8,128)(2,1)} %constant.41.clone.fone_ref) | copy-start | bytes 1572868
  25.3 7.6 %copy-start.4 = (bf16[128,512]{1,0:T(8,128)(2,1)S(1)}, bf16[128,512]{1,0:T(8,128)(2,1)}, u32[]{:S(2)}) copy-start(bf16[128,512]{1,0:T(8,128)(2,1)} %constant.44.clone.ione_ref) | copy-start | bytes 393220
  29.7 3.1 %collective-permute-start.14 = (bf16[2,256,128]{2,1,0:T(8,128)(2,1)S(1)}, bf16[2,256,128]{2,1,0:T(8,128)(2,1)S(1)}, u32[]{:S(2)}, u32[]{:S(2)}) collective-permute-start(bf16[2,256,128]{2,1,0:T(8,128)(2,1)S(1)} %collective-permute-done.13.rest_12_), channel_id=1, source_target_pairs={{0,1},{1,0},{2,3},{3,2},{4,5},{5,4},{6,7},{7,6},{8,9},{9,8},{10,11... | collective-permute-start | bytes 393224 | tf_op jit(solution)/shard_map/ppermute | solution.py:373
  29.8 3.1 %collective-permute-start.4 = (bf16[2,256,128]{2,1,0:T(8,128)(2,1)S(1)}, bf16[2,256,128]{2,1,0:T(8,128)(2,1)S(1)}, u32[]{:S(2)}, u32[]{:S(2)}) collective-permute-start(bf16[2,256,128]{2,1,0:T(8,128)(2,1)S(1)} %collective-permute-done.3.rest_2_), channel_id=1, source_target_pairs={{0,1},{1,0},{2,3},{3,2},{4,5},{5,4},{6,7},{7,6},{8,9},{9,8},{10,11... | collective-permute-start | bytes 393224 | tf_op jit(solution)/shard_map/ppermute | solution.py:373
  30.3 2.6 %collective-permute-start.8 = (bf16[2,256,128]{2,1,0:T(8,128)(2,1)S(1)}, bf16[2,256,128]{2,1,0:T(8,128)(2,1)S(1)}, u32[]{:S(2)}, u32[]{:S(2)}) collective-permute-start(bf16[2,256,128]{2,1,0:T(8,128)(2,1)S(1)} %collective-permute-done.7.rest_6_), channel_id=1, source_target_pairs={{0,1},{1,0},{2,3},{3,2},{4,5},{5,4},{6,7},{7,6},{8,9},{9,8},{10,11... | collective-permute-start | bytes 393224 | tf_op jit(solution)/shard_map/ppermute | solution.py:373
  30.4 2.5 %collective-permute-start.12 = (bf16[2,256,128]{2,1,0:T(8,128)(2,1)S(1)}, bf16[2,256,128]{2,1,0:T(8,128)(2,1)S(1)}, u32[]{:S(2)}, u32[]{:S(2)}) collective-permute-start(bf16[2,256,128]{2,1,0:T(8,128)(2,1)S(1)} %collective-permute-done.11.rest_10_), channel_id=1, source_target_pairs={{0,1},{1,0},{2,3},{3,2},{4,5},{5,4},{6,7},{7,6},{8,9},{9,8},{10,11... | collective-permute-start | bytes 393224 | tf_op jit(solution)/shard_map/ppermute | solution.py:373
  30.8 2.1 %collective-permute-start.16 = (bf16[2,256,128]{2,1,0:T(8,128)(2,1)S(1)}, bf16[2,256,128]{2,1,0:T(8,128)(2,1)S(1)}, u32[]{:S(2)}, u32[]{:S(2)}) collective-permute-start(bf16[2,256,128]{2,1,0:T(8,128)(2,1)S(1)} %collective-permute-done.15.rest_14_), channel_id=1, source_target_pairs={{0,1},{1,0},{2,3},{3,2},{4,5},{5,4},{6,7},{7,6},{8,9},{9,8},{10,11... | collective-permute-start | bytes 393224 | tf_op jit(solution)/shard_map/ppermute | solution.py:373

commit v2 on v1

v2 whole, which is shorter than its diff:
```python
import functools
import math

import jax
import jax.numpy as jnp
import ml_dtypes
import numpy as np
from jax import lax
from jax.experimental import pallas as pl
from jax.experimental.pallas import tpu as pltpu
from jax.sharding import PartitionSpec as P

A0 = 256
QUAD = 4
LANES = 128
FIRST = 16
TILE = 16


def as_real(matrix):
    top = np.concatenate([matrix.real, -matrix.imag], 1)
    low = np.concatenate([matrix.imag, matrix.real], 1)
    return np.concatenate([top, low], 0).astype(ml_dtypes.bfloat16)


def by_tile(matrix):
    shaped = matrix.reshape(2, -1, TILE, matrix.shape[1])
    return shaped.transpose(1, 0, 2, 3).reshape(matrix.shape)


def root(length, turns):
    return np.exp(-2j * np.pi / length * (turns % length))


def dft_tables(total):
    second = total // FIRST
    one = np.arange(FIRST)
    low = np.arange(TILE)
    k_one = one[:, None, None, None]
    l_row = low[None, :, None, None]
    n_one = one[None, None, :, None]
    l_col = low[None, None, None, :]
    same = l_row == l_col
    forward_one = root(FIRST, k_one * n_one) * root(total, l_row * k_one) * same
    forward_one = forward_one.reshape(FIRST * TILE, FIRST * TILE)
    two = np.arange(second)
    forward_two = root(second, two[:, None] * two[None, :])
    inverse_two = forward_two.conj()
    kept = np.arange(FIRST // QUAD)[:, None, None, None]
    inverse_one = (root(FIRST, kept * n_one) * root(total, l_col * n_one)).conj() * same
    inverse_one = inverse_one.reshape(FIRST // QUAD * TILE, FIRST * TILE)
    one, two, three, four = (
        as_real(t) for t in (forward_one, forward_two, inverse_two, inverse_one)
    )
    return [by_tile(one), by_tile(two), by_tile(by_tile(three).T).T, four]


def turn_table(total):
    chunks = total // FIRST // TILE
    value = root(total, TILE * np.arange(chunks)[:, None] * np.arange(FIRST)[None, :]).conj()
    return np.stack([value.real, value.imag]).astype(np.float32)


def steer_table(angle_count, pulse_count):
    angle_index = np.arange(angle_count)[:, None]
    pulse_index = np.arange(pulse_count)[None, :]
    value = root(angle_count, (angle_index + angle_count // 2) * pulse_index)
    value = (value / math.sqrt(pulse_count)).astype(np.complex64)
    return value.real.astype(ml_dtypes.bfloat16), value.imag.astype(ml_dtypes.bfloat16)


def steer_blocks(pulse_count, child_angles):
    real, imag = steer_table(A0, pulse_count)
    real, imag = real[:child_angles], imag[:child_angles]
    table = np.zeros((2, 2, child_angles, 2, 2, 2, 2, 2, pulse_count), ml_dtypes.bfloat16)
    for pair in range(2):
        for child in range(2):
            spot = (pair, child)
            table[child, 0, :, pair, 0, 0, *spot] = real
            table[child, 0, :, pair, 0, 1, *spot] = -imag
            table[child, 1, :, pair, 0, 0, *spot] = -imag
            table[child, 1, :, pair, 0, 1, *spot] = -real
            table[child, 0, :, pair, 1, 0, *spot] = imag
            table[child, 0, :, pair, 1, 1, *spot] = real
            table[child, 1, :, pair, 1, 0, *spot] = real
            table[child, 1, :, pair, 1, 1, *spot] = -imag
    return table.reshape(4 * child_angles, 32 * pulse_count)


def small_unit(angle):
    square = angle * angle
    cosine = 1.0 + square * (-1 / 2 + square * (1 / 24 + square * (-1 / 720 + square / 40320)))
    sine = angle * (1.0 + square * (-1 / 6 + square * (1 / 120 + square * (-1 / 5040))))
    return cosine, sine


def unit(angle):
    quarter = jnp.floor(angle * (2.0 / math.pi) + 0.5)
    rest = angle - quarter * 1.5703125
    rest = rest - quarter * (math.pi / 2 - 1.5703125)
    cosine, sine = small_unit(rest)
    turn = quarter.astype(jnp.int32)
    odd = (turn & 1) == 1
    first = jnp.where(odd, sine, cosine)
    second = jnp.where(odd, cosine, sine)
    first = jnp.where(((turn + 1) & 2) == 2, -first, first)
    second = jnp.where((turn & 2) == 2, -second, second)
    return first, second


def times(left, right):
    return (
        left[0] * right[0] - left[1] * right[1],
        left[0] * right[1] + left[1] * right[0],
    )


def cut_kernel(place_ref, raw_ref, *outs):
    for step, out in enumerate(outs):
        first = pl.multiple_of((place_ref[0] ^ step) * LANES, LANES)
        out[...] = raw_ref[:, :, pl.ds(first, LANES)]


def phase_kernel(total, place_ref, rate_ref, one_ref, two_ref, done_ref):
    done_ref[0] = 1
    start = (place_ref[1] * (total // QUAD)).astype(jnp.float32)
    size = (LANES, LANES)
    for level, ref in ((0, one_ref), (1, two_ref)):
        blocks, angles = ref.shape[1], ref.shape[2]
        rate = rate_ref[level]
        lane = lax.broadcasted_iota(jnp.int32, size, 1).astype(jnp.float32)
        factor = 1.0 + (lane + start) / total

        @pl.loop(0, angles // LANES)
        def _(part):
            row = lax.broadcasted_iota(jnp.int32, size, 0) + part * LANES
            slope = rate * ((row.astype(jnp.float32) + 0.5) / angles - 0.5)
            value = unit(slope * factor)
            step = unit(slope * (LANES / total))
            at = pl.ds(pl.multiple_of(part * LANES, LANES), LANES)
            for block in range(blocks):
                ref[0, block, at, :] = value[0].astype(jnp.bfloat16)
                ref[1, block, at, :] = value[1].astype(jnp.bfloat16)
                if block + 1 < blocks:
                    value = times(value, step)


def weight_kernel(pulse_count, weight_ref, steer_ref, one_ref, two_ref, done_ref):
    done_ref[0] = 1
    joined = jnp.concatenate([weight_ref[0, c, part] for c in range(2) for part in range(2)], 1)
    parents = joined.shape[0]
    width = one_ref.shape[2]
    lane = lax.broadcasted_iota(jnp.int32, (parents, width), 1)
    odd_pulse = lane % 2 == 1
    odd_child = lane // pulse_count % 2 == 1
    children = one_ref.shape[1] // 8
    for pair in range(2):
        for part in range(2):
            at = (pair * 2 + part) * width
            value = jnp.dot(
                joined, steer_ref[:, at : at + width], preferred_element_type=jnp.float32
            )
            for turn in range(2):
                turned = jnp.where(odd_pulse, -value, value) if turn else value
                kinds = (turned, jnp.where(odd_child, -turned, turned))
                for kind, rows in enumerate(kinds):
                    rows = rows.astype(jnp.bfloat16)
                    for first in range(0, parents, TILE):
                        block, tile = divmod(first, children)
                        row = (tile // TILE * 8 + pair * 4 + kind * 2 + part) * TILE
                        one_ref[turn * (parents // children) + block, row : row + TILE, :] = rows[
                            first : first + TILE
                        ]
    for child in range(2):
        for tile in range(parents // TILE):
            at = slice(tile * TILE, (tile + 1) * TILE)
            real, imag = weight_ref[1, child, 0, at], weight_ref[1, child, 1, at]
            row = 2 * tile * TILE
            two_ref[child, row : row + TILE] = jnp.concatenate([real, -imag], 1)
            two_ref[child, row + TILE : row + 2 * TILE] = jnp.concatenate([imag, real], 1)


def gain_kernel(total, place_ref, offset_ref, filter_ref, out_ref, done_ref):
    done_ref[0] = 1
    second = total // FIRST
    offsets = jnp.concatenate(
        [
            offset_ref[pl.ds(place_ref[1] ^ member, 1), :]
            for member in range(QUAD)
        ],
        1,
    )
    shift = offsets - place_ref[1] * (total // QUAD)
    scale = -2.0 * math.pi / total

    def ramp(rows, stride):
        k_index = stride * lax.broadcasted_iota(jnp.int32, (rows, LANES), 0)
        return unit(scale * ((k_index * shift) & (total - 1)).astype(jnp.float32))

    low, high = ramp(FIRST, 1), ramp(second, FIRST)
    for k_one in range(FIRST):
        row = (low[0][k_one : k_one + 1] * (1.0 / total), low[1][k_one : k_one + 1] * (1.0 / total))
        column = (filter_ref[0, :, k_one : k_one + 1], filter_ref[1, :, k_one : k_one + 1])
        value = times(times(high, row), column)
        out_ref[0, k_one] = value[0]
        out_ref[1, k_one] = value[1]


LOADED = 9


def kernel(count, total, place_ref, turn_ref, *rest):
    sources, rest = rest[:LOADED], rest[LOADED:]
    pieces, out_ref, rest = rest[:count], rest[count], rest[count + 1 :]
    held, rest = rest[:LOADED], rest[LOADED:]
    samples, partial_ref, folded, compressed, image, ready, load_sems, sems = rest
    fone_ref, gain_ref, ftwo_ref, itwo_ref, ione_ref = held[:5]
    rows_one_ref, phase_one_ref, rows_two_ref, phase_two_ref = held[5:]
    loads = [
        pltpu.make_async_copy(source, target, load_sems.at[number])
        for number, (source, target) in enumerate(zip(sources, held))
    ]
    for load in loads:
        load.start()

    span = total // count
    second = total // FIRST
    chunks = second // TILE
    kept = FIRST // QUAD
    half = FIRST * TILE
    f32, bf16 = jnp.float32, jnp.bfloat16

    def dot(left, right):
        return jnp.dot(left, right, preferred_element_type=f32)

    def turned(real, imag, chunk, k_one, sign):
        cosine, sine = turn_ref[0, chunk, k_one], turn_ref[1, chunk, k_one] * sign
        return (
            (cosine * real - sine * imag).astype(bf16),
            (cosine * imag + sine * real).astype(bf16),
        )

    index = place_ref[0] * QUAD + place_ref[1]
    tiles = span // TILE
    per_row = chunks // tiles
    for number, piece in enumerate(pieces):
        source = index ^ number
        first_tile = pl.multiple_of(source % per_row * tiles, tiles)
        samples[:, source // per_row, pl.ds(first_tile, tiles)] = piece[...].reshape(
            2, tiles, TILE, LANES
        )

    loads[0].wait()

    @pl.loop(0, chunks // 2, unroll=True)
    def _(pair):
        right = jnp.concatenate(
            [samples[:, :, 2 * pair + side].reshape(2 * half, LANES) for side in range(2)], 1
        )
        result = dot(fone_ref[...], right)
        for side in range(2):
            chunk = 2 * pair + side
            lanes = slice(side * LANES, (side + 1) * LANES)
            for k_one in range(FIRST):
                row = 2 * k_one * TILE
                real = result[row : row + TILE, lanes]
                imag = result[row + TILE : row + 2 * TILE, lanes]
                real, imag = turned(real, imag, chunk, k_one, -1.0)
                partial_ref[k_one, 0, chunk] = real
                partial_ref[k_one, 1, chunk] = imag

    for load in loads[1:4]:
        load.wait()

    @pl.loop(0, FIRST // 2, unroll=True)
    def _(pair):
        right = jnp.concatenate(
            [partial_ref[2 * pair + side].reshape(2 * second, LANES) for side in range(2)], 1
        )
        result = dot(ftwo_ref[...], right)
        scaled = []
        for side in range(2):
            k_one = 2 * pair + side
            lanes = slice(side * LANES, (side + 1) * LANES)
            parts = []
            for chunk in range(chunks):
                row = 2 * chunk * TILE
                at = slice(chunk * TILE, (chunk + 1) * TILE)
                real = result[row : row + TILE, lanes]
                imag = result[row + TILE : row + 2 * TILE, lanes]
                gain_real, gain_imag = gain_ref[0, k_one, at], gain_ref[1, k_one, at]
                parts.append((real * gain_real - imag * gain_imag).astype(bf16))
                parts.append((real * gain_imag + imag * gain_real).astype(bf16))
            scaled.append(jnp.concatenate(parts, 0))
        result = dot(itwo_ref[...], jnp.concatenate(scaled, 1))
        for side in range(2):
            k_one = 2 * pair + side
            lanes = slice(side * LANES, (side + 1) * LANES)
            for chunk in range(chunks):
                row = 2 * chunk * TILE
                real = result[row : row + TILE, lanes]
                imag = result[row + TILE : row + 2 * TILE, lanes]
                real, imag = turned(real, imag, chunk, k_one, 1.0)
                folded[chunk, 0, k_one] = real
                folded[chunk, 1, k_one] = imag

    for load in loads[4:]:
        load.wait()

    @pl.loop(0, chunks // 2, unroll=True)
    def _(pair):
        right = jnp.concatenate(
            [folded[2 * pair + side].reshape(2 * half, LANES) for side in range(2)], 1
        )
        result = dot(ione_ref[...], right).astype(bf16)
        for side in range(2):
            lanes = slice(side * LANES, (side + 1) * LANES)
            for part in range(2):
                for n_one in range(kept):
                    row = (part * kept + n_one) * TILE
                    compressed[n_one, 2 * pair + side, :, part * LANES : (part + 1) * LANES] = (
                        result[row : row + TILE, lanes]
                    )

    width = image.shape[4]
    blocks = width // LANES
    block_angles = image.shape[3]
    angle_blocks = image.shape[1]
    wide = rows_two_ref.shape[1] // 2
    steps = total // QUAD // width
    per_step = second // width

    def out_copy(step, slot):
        at = pl.ds(pl.multiple_of(step * width, width), width)
        return pltpu.make_async_copy(ready.at[slot], out_ref.at[:, :, at], sems.at[slot])

    @pl.loop(0, steps)
    def _(step):
        slot = step % 2
        tiles_wide = width // TILE
        first_tile = pl.multiple_of(step % per_step * tiles_wide, tiles_wide)
        columns = compressed[step // per_step, pl.ds(first_tile, tiles_wide)].reshape(
            width, 2 * LANES
        )

        def phases(ref, rows):
            return [
                jnp.concatenate(
                    [ref[part, step * blocks + b, rows, :] for b in range(blocks)], 1
                ).astype(f32)
                for part in range(2)
            ]

        for block in range(angle_blocks):
            result = lax.dot_general(
                rows_one_ref[block],
                columns,
                (((1,), (1,)), ((), ())),
                preferred_element_type=f32,
            )
            for tile in range(block_angles // TILE):
                at = slice(tile * TILE, (tile + 1) * TILE)
                cosine, sine = phases(
                    phase_one_ref, pl.ds(block * block_angles + tile * TILE, TILE)
                )
                for pick in range(2):
                    terms = [
                        result[row : row + TILE]
                        for row in [((tile * 2 + pick) * 4 + kind) * TILE for kind in range(4)]
                    ]
                    image[pick, block, 0, at] = (cosine * terms[0] + sine * terms[3]).astype(bf16)
                    image[pick, block, 1, at] = (cosine * terms[1] - sine * terms[2]).astype(bf16)

        @pl.when(step >= 2)
        def _():
            out_copy(step - 2, slot).wait()

        for block in range(angle_blocks):
            lower = dot(rows_two_ref[0], image[0, block].reshape(2 * block_angles, width))
            upper = dot(rows_two_ref[1], image[1, block].reshape(2 * block_angles, width))
            for tile in range(wide // TILE):
                rows = pl.ds(block * wide + tile * TILE, TILE)
                cosine, sine = phases(phase_two_ref, rows)
                real = slice(2 * tile * TILE, (2 * tile + 1) * TILE)
                imag = slice((2 * tile + 1) * TILE, (2 * tile + 2) * TILE)
                ready[slot, 0, rows, :] = cosine * (lower[real] + upper[real]) + sine * (
                    lower[imag] - upper[imag]
                )
                ready[slot, 1, rows, :] = cosine * (lower[imag] + upper[imag]) + sine * (
                    upper[real] - lower[real]
                )
        out_copy(step, slot).start()

    for step in range(max(steps - 2, 0), steps):
        out_copy(step, step % 2).wait()


def hold_kernel(*refs):
    pass


def hold(value, *flags):
    far = pl.BlockSpec(memory_space=pl.ANY)
    return pl.pallas_call(
        hold_kernel,
        out_shape=jax.ShapeDtypeStruct(value.shape, value.dtype),
        in_specs=[far] + [pl.BlockSpec(memory_space=pltpu.SMEM)] * len(flags),
        out_specs=far,
        input_output_aliases={0: 0},
        compiler_params=pltpu.CompilerParams(vmem_limit_bytes=1024 * 1024),
    )(value, *flags)


def focus(place, turns, tables, gain, rows_one, rows_two, phase_one, phase_two, pieces):
    count = len(pieces)
    total = phase_one.shape[1] * phase_one.shape[3] * QUAD
    second = total // FIRST
    chunks = second // TILE
    step_width = 256
    bf16, f32 = jnp.bfloat16, jnp.float32
    smem = pl.BlockSpec(memory_space=pltpu.SMEM)
    vmem = pl.BlockSpec(memory_space=pltpu.VMEM)
    parents, children = rows_two.shape[1] // 2, rows_two.shape[2] // 2
    angle_blocks = rows_one.shape[0]
    fone, ftwo, itwo, ione = tables
    sources = [fone, gain, ftwo, itwo, ione, rows_one, phase_one, rows_two, phase_two]
    far = pl.BlockSpec(memory_space=pl.ANY)
    return pl.pallas_call(
        functools.partial(kernel, count, total),
        out_shape=jax.ShapeDtypeStruct((2, angle_blocks * parents, total // QUAD), f32),
        in_specs=[smem, smem] + [far] * len(sources) + [vmem] * count,
        out_specs=far,
        scratch_shapes=[pltpu.VMEM(source.shape, source.dtype) for source in sources]
        + [
            pltpu.VMEM((2, FIRST, chunks, TILE, LANES), bf16),
            pltpu.VMEM((FIRST, 2, chunks, TILE, LANES), bf16),
            pltpu.VMEM((chunks, 2, FIRST, TILE, LANES), bf16),
            pltpu.VMEM((FIRST // QUAD, chunks, TILE, 2 * LANES), bf16),
            pltpu.VMEM((2, angle_blocks, 2, children, step_width), bf16),
            pltpu.VMEM((2, 2, angle_blocks * parents, step_width), f32),
            pltpu.SemaphoreType.DMA((LOADED,)),
            pltpu.SemaphoreType.DMA((2,)),
        ],
        compiler_params=pltpu.CompilerParams(vmem_limit_bytes=50 * 1024 * 1024),
    )(place, turns, *sources, *pieces)


def body(raw_echo, range_filter, range_offsets, interp_weight, phase_rate):
    count = lax.axis_size("ap")
    index = lax.axis_index("ap")
    total = range_filter.shape[1]
    pulse_count = range_offsets.shape[0]
    groups = count // QUAD
    width = total // QUAD
    second = total // FIRST
    f32, bf16 = jnp.float32, jnp.bfloat16
    smem = pl.BlockSpec(memory_space=pltpu.SMEM)
    vmem = pl.BlockSpec(memory_space=pltpu.VMEM)
    place = jnp.stack([index // QUAD, index % QUAD]).astype(jnp.int32)

    def move(value, bits):
        return lax.ppermute(value, "ap", [(i, i ^ bits) for i in range(count)])

    def shape(dims, kind=bf16):
        return jax.ShapeDtypeStruct(dims, kind)

    flag = shape((1,), jnp.int32)
    small = pltpu.CompilerParams(vmem_limit_bytes=2 * 1024 * 1024)

    def cost(flops, moved):
        return pl.CostEstimate(flops=flops, bytes_accessed=moved, transcendentals=0)

    cut = pl.pallas_call(
        cut_kernel,
        out_shape=[shape((2, total // count, LANES))] * groups,
        in_specs=[smem, vmem],
        out_specs=[vmem] * groups,
        compiler_params=small,
    )(place, raw_echo)
    offset_near = jnp.stack([range_offsets, move(range_offsets, 1)])
    offsets = jnp.concatenate([offset_near, move(offset_near, 2)])

    phase_one, phase_two, phase_done = pl.pallas_call(
        functools.partial(phase_kernel, total),
        out_shape=[
            shape((2, width // LANES, 2 * A0, LANES)),
            shape((2, width // LANES, 4 * A0, LANES)),
            flag,
        ],
        in_specs=[smem, smem],
        out_specs=[vmem, vmem, smem],
        cost_estimate=cost(2**30, 2**23),
        compiler_params=small,
    )(place, phase_rate)
    child_angles = interp_weight.shape[4]
    rows_one, rows_two, weight_done = pl.pallas_call(
        functools.partial(weight_kernel, pulse_count),
        out_shape=[
            shape((2 * A0 // child_angles, 8 * child_angles, 2 * LANES)),
            shape((2, 2 * interp_weight.shape[3], 2 * child_angles)),
            flag,
        ],
        in_specs=[vmem, vmem],
        out_specs=[vmem, vmem, smem],
        cost_estimate=cost(2**29, 2**22),
        compiler_params=small,
    )(interp_weight, jnp.asarray(steer_blocks(pulse_count, child_angles)))
    gain, gain_done = pl.pallas_call(
        functools.partial(gain_kernel, total),
        out_shape=[shape((2, FIRST, second, LANES), f32), flag],
        in_specs=[smem, vmem, vmem],
        out_specs=[vmem, smem],
        cost_estimate=cost(2**28, 2**22),
        compiler_params=small,
    )(place, offsets, range_filter.reshape(2, second, FIRST))

    tables = [jnp.asarray(t) for t in dft_tables(total)]
    turns = jnp.asarray(turn_table(total))

    own = [cut[0]] + [move(cut[step], QUAD * step) for step in range(1, groups)]
    own[1] = hold(own[1], phase_done, weight_done)
    if groups > 2:
        own[2] = hold(own[2], gain_done)
    across = [move(piece, 2) for piece in own]
    beside = [move(piece, 1) for piece in own]
    diagonal = [move(piece, 1) for piece in across]
    pieces = [part for four in zip(own, beside, across, diagonal) for part in four]
    return focus(place, turns, tables, gain, rows_one, rows_two, phase_one, phase_two, pieces)


def solution(mesh):
    placed = (P(None, "ap", "grp"), P(), P(("grp", "ap")), P(), P())
    return jax.shard_map(
        body, mesh=mesh, in_specs=placed, out_specs=P(None, None, ("grp", "ap")), check_vma=False
    )
```

time: 49.2 us -> 54.3 us (1.10)
  local copies, waits for them, and re-layouts: 4.87 us -> 10.7 us
  waiting for transfers between devices: 6.77 us -> 5.65 us
  starting transfers between devices: 12.9 us -> 13.7 us
    unnamed x18 -> x32, local copies, waits for them, and re-layouts: 3.98 us -> 10.6 us
    ppermute x17, waiting for transfers between devices: 6.77 us -> 5.65 us  [move(): return lax.ppermute(value, 'ap', [(i, i ^ bits) for i in range(count)])]
    ppermute x17, starting transfers between devices: 12.9 us -> 13.7 us  [move(): return lax.ppermute(value, 'ap', [(i, i ^ bits) for i in range(count)])]
    reshape x1, local copies, waits for them, and re-layouts: 0.89 us -> 0.13 us  [body(): range_filter.reshape(2, second, FIRST)]
    pallas_call x2 -> x4, Pallas kernels: 17.6 us -> 17.4 us  [the longest x1 13.5 us: focus(): pl.pallas_call(functools.partial(kernel, count, total), out_shape=jax.Sha...]
  transfers between devices with their start and end apart: 17 -> 17, of which waited for: 1 -> 4; matrix products, arithmetic and copies ran while one was open for 3% -> 1% of each run, Pallas kernels for 15% -> 16%
where the time goes in v2:
time: 54.3 us; the launch traced here: 54.1 us
  Pallas kernels  23 us (42%)
  starting transfers between devices  13.7 us (25%)
  local copies, waits for them, and re-layouts  10.7 us (20%)
  waiting for transfers between devices  5.65 us (10%)
  other arithmetic  0.75 us (1%)
    ppermute x17, starting transfers between devices, move(): return lax.ppermute(value, 'ap', [(i, i ^ bits) for i in range(count)])  13.7 us
    pallas_call x1, Pallas kernels, focus(): pl.pallas_call(functools.partial(kernel, count, total), out_shape=jax.Sha...  13.5 us
    unnamed x32, local copies, waits for them, and re-layouts  10.6 us
    ppermute x17, waiting for transfers between devices, move(): return lax.ppermute(value, 'ap', [(i, i ^ bits) for i in range(count)])  5.65 us
    pallas_call x1, Pallas kernels, body(): pl.pallas_call(functools.partial(phase_kernel, total), out_shape=[shape((...  4.41 us
    pallas_call x2, Pallas kernels, hold(): pl.pallas_call(hold_kernel, out_shape=jax.ShapeDtypeStruct(value.shape, v...  1.95 us
    pallas_call x1, Pallas kernels, body(): pl.pallas_call(functools.partial(gain_kernel, total), out_shape=[shape((2...  1.94 us
  transfers between devices with their start and end apart: 17, of which 4 were waited for; matrix products, arithmetic and copies ran while one was open for 1% of the time, Pallas kernels for 16%

profile of v2, /device:TPU:0, one launch (start us, length us, event | category | flops | bytes accessed | tf_op | source)
XLA Modules:
  0.0 54.1 jit_solution(16840857549234498674)
XLA Ops:
  0.0 0.0 copy-start.4
  0.0 0.1 pad_add_fusion.2.place_ref
  0.1 1.1 %copy-done.8 = bf16[2,256,512]{2,1,0:T(8,128)(2,1)S(1)} copy-done((bf16[2,256,512]{2,1,0:T(8,128)(2,1)S(1)}, bf16[2,256,512]{2,1,0:T(8,128)(2,1)}, u32[]{:S(2)}) %copy-start.8) | copy-done | bytes 524312
  1.2 0.6 %shard_map.112 = (bf16[2,256,128]{2,1,0:T(8,128)(2,1)S(1)}, bf16[2,256,128]{2,1,0:T(8,128)(2,1)S(1)}, bf16[2,256,128]{2,1,0:T(8,128)(2,1)S(1)}, bf16[2,256,128]{2,1,0:T(8,128)(2,1)S(1)}) custom-call(s32[2]{0:T(128)S(1)} %pad_add_fusion.2.place_ref, bf16[2,256,512]{2,1,0:T(8,128)(2,1)S(1)} %copy-done.8), custom_call_target="tpu_custom_call" | custom-call | tf_op jit(solution)/shard_map/pallas_call | solution.py:473
  1.9 3.1 %collective-permute-start.3 = (bf16[2,256,128]{2,1,0:T(8,128)(2,1)S(1)}, bf16[2,256,128]{2,1,0:T(8,128)(2,1)S(1)}, u32[]{:S(2)}, u32[]{:S(2)}) collective-permute-start(bf16[2,256,128]{2,1,0:T(8,128)(2,1)S(1)} %get-tuple-element.22.rest_9_), channel_id=1, source_target_pairs={{0,2},{1,3},{2,0},{3,1},{4,6},{5,7},{6,4},{7,5},{8,10},{9,11},{10,... | collective-permute-start | bytes 393224 | tf_op jit(solution)/shard_map/ppermute | solution.py:462
  4.9 0.0 collective-permute-start.2
  4.9 0.5 collective-permute-start
  5.4 1.6 %collective-permute-start.5 = (bf16[2,256,128]{2,1,0:T(8,128)(2,1)S(1)}, bf16[2,256,128]{2,1,0:T(8,128)(2,1)S(1)}, u32[]{:S(2)}, u32[]{:S(2)}) collective-permute-start(bf16[2,256,128]{2,1,0:T(8,128)(2,1)S(1)} %get-tuple-element.23), channel_id=1, source_target_pairs={{0,4},{1,5},{2,6},{3,7},{4,0},{5,1},{6,2},{7,3},{8,12},{9,13},{10,... | collective-permute-start | bytes 393224 | tf_op jit(solution)/shard_map/ppermute | solution.py:462
  7.0 2.6 %collective-permute-start.9 = (bf16[2,256,128]{2,1,0:T(8,128)(2,1)S(1)}, bf16[2,256,128]{2,1,0:T(8,128)(2,1)S(1)}, u32[]{:S(2)}, u32[]{:S(2)}) collective-permute-start(bf16[2,256,128]{2,1,0:T(8,128)(2,1)S(1)} %get-tuple-element.26), channel_id=1, source_target_pairs={{0,8},{1,9},{2,10},{3,11},{4,12},{5,13},{6,14},{7,15},{8,0},{9,1},... | collective-permute-start | bytes 393224 | tf_op jit(solution)/shard_map/ppermute | solution.py:462
  9.6 0.7 %copy-done.12 = f32[2]{0:T(128)S(1)} copy-done((f32[2]{0:T(128)S(1)}, f32[2]{0:T(128)}, u32[]{:S(2)}) %copy-start.12) | copy-done | bytes 32
  10.3 4.4 %shard_map.111 = (bf16[2,8,512,128]{3,2,1,0:T(8,128)(2,1)S(1)}, bf16[2,8,1024,128]{3,2,1,0:T(8,128)(2,1)S(1)}, s32[1]{0:T(128)}) custom-call(s32[2]{0:T(128)S(1)} %pad_add_fusion.2.place_ref, f32[2]{0:T(128)S(1)} %copy-done.12), custom_call_target="tpu_custom_call" | custom-call | flops 1073741824 | bytes 8388608 | tf_op jit(solution)/shard_map/pallas_call | solution.py:483
  14.7 0.0 copy-start
  14.7 2.0 %copy-done = bf16[2,8,1024,128]{3,2,1,0:T(8,128)(2,1)} copy-done((bf16[2,8,1024,128]{3,2,1,0:T(8,128)(2,1)}, bf16[2,8,1024,128]{3,2,1,0:T(8,128)(2,1)S(1)}, u32[]{:S(2)}) %copy-start) | copy-done | bytes 4194328
  16.6 1.4 %copy-done.2 = bf16[2,8,512,128]{3,2,1,0:T(8,128)(2,1)} copy-done((bf16[2,8,512,128]{3,2,1,0:T(8,128)(2,1)}, bf16[2,8,512,128]{3,2,1,0:T(8,128)(2,1)S(1)}, u32[]{:S(2)}) %copy-start.2) | copy-done | bytes 2097176
  18.0 0.0 collective-permute-done
  18.0 0.7 %pad_add_fusion.1 = s32[2,32]{1,0:T(2,128)S(1)} fusion(s32[1,32]{1,0:T(1,128)S(1)} %bitcast.6, s32[1,32]{1,0:T(1,128)} %bitcast.4), kind=kLoop, calls=%fused_computation.1 | loop fusion | flops 64 | bytes 512 | tf_op jit(solution)/shard_map/stack | solution.py:480
  18.7 0.5 collective-permute-start.1
  19.2 0.0 copy-done.11
  19.2 1.2 %copy-done.13 = bf16[512,1024]{1,0:T(8,128)(2,1)S(1)} copy-done((bf16[512,1024]{1,0:T(8,128)(2,1)S(1)}, bf16[512,1024]{1,0:T(8,128)(2,1)}, u32[]{:S(2)}) %copy-start.13) | copy-done | bytes 1048600
  20.4 0.6 %shard_map.110 = (bf16[4,1024,256]{2,1,0:T(8,128)(2,1)S(1)}, bf16[2,512,256]{2,1,0:T(8,128)(2,1)S(1)}, s32[1]{0:T(128)}) custom-call(bf16[2,2,2,256,128]{4,3,2,1,0:T(8,128)(2,1)S(1)} %copy-done.11, bf16[512,1024]{1,0:T(8,128)(2,1)S(1)} %copy-done.13), custom_call_target="tpu_custom_call" | custom-call | flops 536870912 | bytes 4194304 | tf_op jit(solution)/shard_map/pallas_call | solution.py:496
  21.0 0.0 copy-start.3
  21.0 1.4 %copy-done.3 = bf16[4,1024,256]{2,1,0:T(8,128)(2,1)} copy-done((bf16[4,1024,256]{2,1,0:T(8,128)(2,1)}, bf16[4,1024,256]{2,1,0:T(8,128)(2,1)S(1)}, u32[]{:S(2)}) %copy-start.3) | copy-done | bytes 2097176
  22.4 0.8 %copy-done.7 = bf16[2,512,256]{2,1,0:T(8,128)(2,1)} copy-done((bf16[2,512,256]{2,1,0:T(8,128)(2,1)}, bf16[2,512,256]{2,1,0:T(8,128)(2,1)S(1)}, u32[]{:S(2)}) %copy-start.7) | copy-done | bytes 524312
  23.2 0.0 copy-done.14
  23.2 0.1 reshape.3.filter_ref
  23.4 0.0 collective-permute-done.1
  23.4 0.1 collective-permute-start.13
  23.5 0.0 copy-done.15
  23.5 1.9 %shard_map.109 = (f32[2,16,256,128]{3,2,1,0:T(8,128)S(1)}, s32[1]{0:T(128)}) custom-call(s32[2]{0:T(128)S(1)} %pad_add_fusion.2.place_ref, s32[4,32]{1,0:T(4,128)S(1)} %pad_add_fusion.offset_ref, f32[2,256,16]{2,1,0:T(8,128)S(1)} %reshape.3.filter_ref), custom_call_target="tpu_custom_call" | custom-call | flops 268435456 | bytes 4194304 | tf_op jit(solution)/shard_map/pallas_call | solution.py:508
  25.4 0.0 copy-start.1
  25.4 2.0 %copy-done.1 = f32[2,16,256,128]{3,2,1,0:T(8,128)} copy-done((f32[2,16,256,128]{3,2,1,0:T(8,128)}, f32[2,16,256,128]{3,2,1,0:T(8,128)S(1)}, u32[]{:S(2)}) %copy-start.1) | copy-done | bytes 4194328
  27.5 0.0 collective-permute-done.9.refs_0_
  27.5 0.6 %shard_map.114.rest_17_ = bf16[2,256,128]{2,1,0:T(8,128)(2,1)S(1)} custom-call(bf16[2,256,128]{2,1,0:T(8,128)(2,1)S(1)} %collective-permute-done.9.refs_0_, s32[1]{0:T(128)} %get-tuple-element.27.refs_1_), custom_call_target="tpu_custom_call", output_to_operand_aliasing={{}: (0, {})} | custom-call | tf_op jit(solution)/shard_map/pallas_call | solution.py:404
  28.1 1.8 %collective-permute-start.11 = (bf16[2,256,128]{2,1,0:T(8,128)(2,1)S(1)}, bf16[2,256,128]{2,1,0:T(8,128)(2,1)S(1)}, u32[]{:S(2)}, u32[]{:S(2)}) collective-permute-start(bf16[2,256,128]{2,1,0:T(8,128)(2,1)S(1)} %shard_map.114.rest_17_), channel_id=1, source_target_pairs={{0,2},{1,3},{2,0},{3,1},{4,6},{5,7},{6,4},{7,5},{8,10},{9,11},{10,... | collective-permute-start | bytes 393224 | tf_op jit(solution)/shard_map/ppermute | solution.py:462
  29.9 0.4 collective-permute-done.13.rest_21_
  30.3 1.5 %collective-permute-start.15 = (bf16[2,256,128]{2,1,0:T(8,128)(2,1)S(1)}, bf16[2,256,128]{2,1,0:T(8,128)(2,1)S(1)}, u32[]{:S(2)}, u32[]{:S(2)}) collective-permute-start(bf16[2,256,128]{2,1,0:T(8,128)(2,1)S(1)} %collective-permute-done.13.rest_21_), channel_id=1, source_target_pairs={{0,2},{1,3},{2,0},{3,1},{4,6},{5,7},{6,4},{7,5},{8,10},{9,11},{10,... | collective-permute-start | bytes 393224 | tf_op jit(solution)/shard_map/ppermute | solution.py:462
  31.8 0.0 collective-permute-done.5.refs_0_
  31.8 0.0 collective-permute-start.14
  31.8 0.0 collective-permute-done.3.rest_11_
  31.8 0.5 collective-permute-start.4
  32.3 1.3 %shard_map.113.rest_13_ = bf16[2,256,128]{2,1,0:T(8,128)(2,1)S(1)} custom-call(bf16[2,256,128]{2,1,0:T(8,128)(2,1)S(1)} %collective-permute-done.5.refs_0_, s32[1]{0:T(128)} %get-tuple-element.24.refs_1_, s32[1]{0:T(128)} %get-tuple-element.25.refs_2_), custom_call_target="tpu_custom_call", output_to_operand_aliasing={{}: (0, {})} | custom-call | tf_op jit(solution)/shard_map/pallas_call | solution.py:404
  33.6 0.0 collective-permute-done.2.rest_10_
  33.6 0.6 %collective-permute-start.7 = (bf16[2,256,128]{2,1,0:T(8,128)(2,1)S(1)}, bf16[2,256,128]{2,1,0:T(8,128)(2,1)S(1)}, u32[]{:S(2)}, u32[]{:S(2)}) collective-permute-start(bf16[2,256,128]{2,1,0:T(8,128)(2,1)S(1)} %shard_map.113.rest_13_), channel_id=1, source_target_pairs={{0,2},{1,3},{2,0},{3,1},{4,6},{5,7},{6,4},{7,5},{8,10},{9,11},{10,... | collective-permute-start | bytes 393224 | tf_op jit(solution)/shard_map/ppermute | solution.py:462
  34.2 1.4 %collective-permute-done.15.rest_23_ = bf16[2,256,128]{2,1,0:T(8,128)(2,1)S(1)} collective-permute-done((bf16[2,256,128]{2,1,0:T(8,128)(2,1)S(1)}, bf16[2,256,128]{2,1,0:T(8,128)(2,1)S(1)}, u32[]{:S(2)}, u32[]{:S(2)}) %collective-permute-start.15) | collective-permute-done | bytes 131104 | tf_op jit(solution)/shard_map/ppermute | solution.py:462
  35.6 0.0 collective-permute-start.10
  35.6 0.0 collective-permute-done.14.rest_22_
  35.6 0.5 collective-permute-start.6
  36.1 0.0 collective-permute-done.4.rest_12_
  36.1 0.1 collective-permute-start.16
  36.1 0.0 collective-permute-done.11.rest_19_
  36.1 0.4 collective-permute-start.12
  36.6 2.6 %collective-permute-done.7.rest_15_ = bf16[2,256,128]{2,1,0:T(8,128)(2,1)S(1)} collective-permute-done((bf16[2,256,128]{2,1,0:T(8,128)(2,1)S(1)}, bf16[2,256,128]{2,1,0:T(8,128)(2,1)S(1)}, u32[]{:S(2)}, u32[]{:S(2)}) %collective-permute-start.7) | collective-permute-done | bytes 131104 | tf_op jit(solution)/shard_map/ppermute | solution.py:462
  39.2 0.0 collective-permute-start.8
  39.2 0.0 collective-permute-done.10.rest_18_
  39.2 0.0 collective-permute-done.6.rest_14_
  39.2 0.0 collective-permute-done.16.rest_24_
  39.2 0.0 collective-permute-done.12.rest_20_
  39.2 1.3 %collective-permute-done.8.rest_16_ = bf16[2,256,128]{2,1,0:T(8,128)(2,1)S(1)} collective-permute-done((bf16[2,256,128]{2,1,0:T(8,128)(2,1)S(1)}, bf16[2,256,128]{2,1,0:T(8,128)(2,1)S(1)}, u32[]{:S(2)}, u32[]{:S(2)}) %collective-permute-start.8) | collective-permute-done | bytes 131104 | tf_op jit(solution)/shard_map/ppermute | solution.py:462
  40.5 0.0 copy-done.4
  40.5 0.0 copy-done.5
  40.5 0.0 copy-done.6
  40.5 0.0 copy-done.9
  40.5 0.0 copy-done.10
  40.5 13.5 %shard_map.115 = f32[2,1024,1024]{2,1,0:T(8,128)} custom-call(s32[2]{0:T(128)S(1)} %pad_add_fusion.2.place_ref, f32[2,16,16]{2,1,0:T(8,128)S(1)} %copy-done.10, bf16[512,512]{1,0:T(8,128)(2,1)S(1)} %copy-done.6, f32[2,16,256,128]{3,2,1,0:T(8,128)} %copy-done.1, bf16[512,512]{1,0:T(8,128)(2,1)S(1)} %copy-done.5, bf16[512,512]{1,0:T(8,128)(2,1)S(1)} %copy-done.4, ...), custom_call_target="tpu_custom_call" | custom-call | tf_op jit(solution)/shard_map/pallas_call | solution.py:428
  (13 shorter events, 0.0 us)
Async XLA Ops:
  0.0 40.5 %copy-start.4 = (bf16[512,512]{1,0:T(8,128)(2,1)S(1)}, bf16[512,512]{1,0:T(8,128)(2,1)}, u32[]{:S(2)}) copy-start(bf16[512,512]{1,0:T(8,128)(2,1)} %constant.45.clone.rest_3_) | copy-start | bytes 1572868
  0.0 40.5 %copy-start.5 = (bf16[512,512]{1,0:T(8,128)(2,1)S(1)}, bf16[512,512]{1,0:T(8,128)(2,1)}, u32[]{:S(2)}) copy-start(bf16[512,512]{1,0:T(8,128)(2,1)} %constant.44.clone.rest_2_) | copy-start | bytes 1572868
  0.0 40.5 %copy-start.6 = (bf16[512,512]{1,0:T(8,128)(2,1)S(1)}, bf16[512,512]{1,0:T(8,128)(2,1)}, u32[]{:S(2)}) copy-start(bf16[512,512]{1,0:T(8,128)(2,1)} %constant.43.clone.rest_0_) | copy-start | bytes 1572868
  0.1 1.1 %copy-start.8 = (bf16[2,256,512]{2,1,0:T(8,128)(2,1)S(1)}, bf16[2,256,512]{2,1,0:T(8,128)(2,1)}, u32[]{:S(2)}) copy-start(bf16[2,256,512]{2,1,0:T(8,128)(2,1)} %raw_ref.1) | copy-start | bytes 1572868
  1.2 18.0 %copy-start.11 = (bf16[2,2,2,256,128]{4,3,2,1,0:T(8,128)(2,1)S(1)}, bf16[2,2,2,256,128]{4,3,2,1,0:T(8,128)(2,1)}, u32[]{:S(2)}) copy-start(bf16[2,2,2,256,128]{4,3,2,1,0:T(8,128)(2,1)} %weight_ref.1) | copy-start | bytes 1572868
  1.2 39.3 %copy-start.9 = (bf16[128,512]{1,0:T(8,128)(2,1)S(1)}, bf16[128,512]{1,0:T(8,128)(2,1)}, u32[]{:S(2)}) copy-start(bf16[128,512]{1,0:T(8,128)(2,1)} %constant.46.clone.rest_4_) | copy-start | bytes 393220
  1.2 39.3 %copy-start.10 = (f32[2,16,16]{2,1,0:T(8,128)S(1)}, f32[2,16,16]{2,1,0:T(8,128)}, u32[]{:S(2)}) copy-start(f32[2,16,16]{2,1,0:T(8,128)} %constant.47.clone.turn_ref) | copy-start | bytes 6148
  1.9 29.9 %collective-permute-start.3 = (bf16[2,256,128]{2,1,0:T(8,128)(2,1)S(1)}, bf16[2,256,128]{2,1,0:T(8,128)(2,1)S(1)}, u32[]{:S(2)}, u32[]{:S(2)}) collective-permute-start(bf16[2,256,128]{2,1,0:T(8,128)(2,1)S(1)} %get-tuple-element.22.rest_9_), channel_id=1, source_target_pairs={{0,2},{1,3},{2,0},{3,1},{4,6},{5,7},{6,4},{7,5},{8,10},{9,11},{10,... | collective-permute-start | bytes 393224 | tf_op jit(solution)/shard_map/ppermute | solution.py:462
  4.9 28.7 %collective-permute-start.2 = (bf16[2,256,128]{2,1,0:T(8,128)(2,1)S(1)}, bf16[2,256,128]{2,1,0:T(8,128)(2,1)S(1)}, u32[]{:S(2)}, u32[]{:S(2)}) collective-permute-start(bf16[2,256,128]{2,1,0:T(8,128)(2,1)S(1)} %get-tuple-element.22.rest_9_), channel_id=1, source_target_pairs={{0,1},{1,0},{2,3},{3,2},{4,5},{5,4},{6,7},{7,6},{8,9},{9,8},{10,11... | collective-permute-start | bytes 393224 | tf_op jit(solution)/shard_map/ppermute | solution.py:462
  4.9 13.1 %collective-permute-start = (s32[32]{0:T(128)}, s32[32]{0:T(128)S(1)}, u32[]{:S(2)}, u32[]{:S(2)}) collective-permute-start(s32[32]{0:T(128)} %param.13), channel_id=1, source_target_pairs={{0,1},{1,0},{2,3},{3,2},{4,5},{5,4},{6,7},{7,6},{8,9},{9,8},{10,11... | collective-permute-start | bytes 392 | tf_op jit(solution)/shard_map/ppermute | solution.py:462
  5.4 26.3 %collective-permute-start.5 = (bf16[2,256,128]{2,1,0:T(8,128)(2,1)S(1)}, bf16[2,256,128]{2,1,0:T(8,128)(2,1)S(1)}, u32[]{:S(2)}, u32[]{:S(2)}) collective-permute-start(bf16[2,256,128]{2,1,0:T(8,128)(2,1)S(1)} %get-tuple-element.23), channel_id=1, source_target_pairs={{0,4},{1,5},{2,6},{3,7},{4,0},{5,1},{6,2},{7,3},{8,12},{9,13},{10,... | collective-permute-start | bytes 393224 | tf_op jit(solution)/shard_map/ppermute | solution.py:462
  7.0 20.4 %collective-permute-start.9 = (bf16[2,256,128]{2,1,0:T(8,128)(2,1)S(1)}, bf16[2,256,128]{2,1,0:T(8,128)(2,1)S(1)}, u32[]{:S(2)}, u32[]{:S(2)}) collective-permute-start(bf16[2,256,128]{2,1,0:T(8,128)(2,1)S(1)} %get-tuple-element.26), channel_id=1, source_target_pairs={{0,8},{1,9},{2,10},{3,11},{4,12},{5,13},{6,14},{7,15},{8,0},{9,1},... | collective-permute-start | bytes 393224 | tf_op jit(solution)/shard_map/ppermute | solution.py:462
  9.6 0.7 %copy-start.12 = (f32[2]{0:T(128)S(1)}, f32[2]{0:T(128)}, u32[]{:S(2)}) copy-start(f32[2]{0:T(128)} %rate_ref.1) | copy-start | bytes 28
  10.3 13.0 %copy-start.14 = (f32[2,4096]{1,0:T(2,128)S(1)}, f32[2,4096]{1,0:T(2,128)}, u32[]{:S(2)}) copy-start(f32[2,4096]{1,0:T(2,128)} %param.12) | copy-start | bytes 98308
  10.3 13.2 %copy-start.15 = (s32[32]{0:T(128)S(1)}, s32[32]{0:T(128)}, u32[]{:S(2)}) copy-start(s32[32]{0:T(128)} %param.13) | copy-start | bytes 388
  14.7 2.0 %copy-start = (bf16[2,8,1024,128]{3,2,1,0:T(8,128)(2,1)}, bf16[2,8,1024,128]{3,2,1,0:T(8,128)(2,1)S(1)}, u32[]{:S(2)}) copy-start(bf16[2,8,1024,128]{3,2,1,0:T(8,128)(2,1)S(1)} %get-tuple-element.21.rest_8_) | copy-start | bytes 12582916
  16.6 1.4 %copy-start.2 = (bf16[2,8,512,128]{3,2,1,0:T(8,128)(2,1)}, bf16[2,8,512,128]{3,2,1,0:T(8,128)(2,1)S(1)}, u32[]{:S(2)}) copy-start(bf16[2,8,512,128]{3,2,1,0:T(8,128)(2,1)S(1)} %get-tuple-element.19.rest_6_) | copy-start | bytes 6291460
  18.7 4.7 %collective-permute-start.1 = (s32[2,32]{1,0:T(2,128)S(1)}, s32[2,32]{1,0:T(2,128)S(1)}, u32[]{:S(2)}, u32[]{:S(2)}) collective-permute-start(s32[2,32]{1,0:T(2,128)S(1)} %pad_add_fusion.1), channel_id=1, source_target_pairs={{0,2},{1,3},{2,0},{3,1},{4,6},{5,7},{6,4},{7,5},{8,10},{9,11},{10,... | collective-permute-start | bytes 776 | tf_op jit(solution)/shard_map/ppermute | solution.py:462
  19.2 1.2 %copy-start.13 = (bf16[512,1024]{1,0:T(8,128)(2,1)S(1)}, bf16[512,1024]{1,0:T(8,128)(2,1)}, u32[]{:S(2)}) copy-start(bf16[512,1024]{1,0:T(8,128)(2,1)} %constant.42.clone.steer_ref) | copy-start | bytes 3145732
  21.0 1.4 %copy-start.3 = (bf16[4,1024,256]{2,1,0:T(8,128)(2,1)}, bf16[4,1024,256]{2,1,0:T(8,128)(2,1)S(1)}, u32[]{:S(2)}) copy-start(bf16[4,1024,256]{2,1,0:T(8,128)(2,1)S(1)} %get-tuple-element.18.rest_5_) | copy-start | bytes 6291460
  22.4 0.8 %copy-start.7 = (bf16[2,512,256]{2,1,0:T(8,128)(2,1)}, bf16[2,512,256]{2,1,0:T(8,128)(2,1)S(1)}, u32[]{:S(2)}) copy-start(bf16[2,512,256]{2,1,0:T(8,128)(2,1)S(1)} %get-tuple-element.20.rest_7_) | copy-start | bytes 1572868
  23.4 6.9 %collective-permute-start.13 = (bf16[2,256,128]{2,1,0:T(8,128)(2,1)S(1)}, bf16[2,256,128]{2,1,0:T(8,128)(2,1)S(1)}, u32[]{:S(2)}, u32[]{:S(2)}) collective-permute-start(bf16[2,256,128]{2,1,0:T(8,128)(2,1)S(1)} %get-tuple-element.28), channel_id=1, source_target_pairs={{0,12},{1,13},{2,14},{3,15},{4,8},{5,9},{6,10},{7,11},{8,4},{9,5},... | collective-permute-start | bytes 393224 | tf_op jit(solution)/shard_map/ppermute | solution.py:462
  25.4 2.0 %copy-start.1 = (f32[2,16,256,128]{3,2,1,0:T(8,128)}, f32[2,16,256,128]{3,2,1,0:T(8,128)S(1)}, u32[]{:S(2)}) copy-start(f32[2,16,256,128]{3,2,1,0:T(8,128)S(1)} %get-tuple-element.17.rest_1_) | copy-start | bytes 12582916
  28.1 8.0 %collective-permute-start.11 = (bf16[2,256,128]{2,1,0:T(8,128)(2,1)S(1)}, bf16[2,256,128]{2,1,0:T(8,128)(2,1)S(1)}, u32[]{:S(2)}, u32[]{:S(2)}) collective-permute-start(bf16[2,256,128]{2,1,0:T(8,128)(2,1)S(1)} %shard_map.114.rest_17_), channel_id=1, source_target_pairs={{0,2},{1,3},{2,0},{3,1},{4,6},{5,7},{6,4},{7,5},{8,10},{9,11},{10,... | collective-permute-start | bytes 393224 | tf_op jit(solution)/shard_map/ppermute | solution.py:462
  30.3 5.3 %collective-permute-start.15 = (bf16[2,256,128]{2,1,0:T(8,128)(2,1)S(1)}, bf16[2,256,128]{2,1,0:T(8,128)(2,1)S(1)}, u32[]{:S(2)}, u32[]{:S(2)}) collective-permute-start(bf16[2,256,128]{2,1,0:T(8,128)(2,1)S(1)} %collective-permute-done.13.rest_21_), channel_id=1, source_target_pairs={{0,2},{1,3},{2,0},{3,1},{4,6},{5,7},{6,4},{7,5},{8,10},{9,11},{10,... | collective-permute-start | bytes 393224 | tf_op jit(solution)/shard_map/ppermute | solution.py:462
  31.8 3.8 %collective-permute-start.14 = (bf16[2,256,128]{2,1,0:T(8,128)(2,1)S(1)}, bf16[2,256,128]{2,1,0:T(8,128)(2,1)S(1)}, u32[]{:S(2)}, u32[]{:S(2)}) collective-permute-start(bf16[2,256,128]{2,1,0:T(8,128)(2,1)S(1)} %collective-permute-done.13.rest_21_), channel_id=1, source_target_pairs={{0,1},{1,0},{2,3},{3,2},{4,5},{5,4},{6,7},{7,6},{8,9},{9,8},{10,11... | collective-permute-start | bytes 393224 | tf_op jit(solution)/shard_map/ppermute | solution.py:462
  31.8 4.3 %collective-permute-start.4 = (bf16[2,256,128]{2,1,0:T(8,128)(2,1)S(1)}, bf16[2,256,128]{2,1,0:T(8,128)(2,1)S(1)}, u32[]{:S(2)}, u32[]{:S(2)}) collective-permute-start(bf16[2,256,128]{2,1,0:T(8,128)(2,1)S(1)} %collective-permute-done.3.rest_11_), channel_id=1, source_target_pairs={{0,1},{1,0},{2,3},{3,2},{4,5},{5,4},{6,7},{7,6},{8,9},{9,8},{10,11... | collective-permute-start | bytes 393224 | tf_op jit(solution)/shard_map/ppermute | solution.py:462
  33.6 5.5 %collective-permute-start.7 = (bf16[2,256,128]{2,1,0:T(8,128)(2,1)S(1)}, bf16[2,256,128]{2,1,0:T(8,128)(2,1)S(1)}, u32[]{:S(2)}, u32[]{:S(2)}) collective-permute-start(bf16[2,256,128]{2,1,0:T(8,128)(2,1)S(1)} %shard_map.113.rest_13_), channel_id=1, source_target_pairs={{0,2},{1,3},{2,0},{3,1},{4,6},{5,7},{6,4},{7,5},{8,10},{9,11},{10,... | collective-permute-start | bytes 393224 | tf_op jit(solution)/shard_map/ppermute | solution.py:462
  35.6 3.6 %collective-permute-start.10 = (bf16[2,256,128]{2,1,0:T(8,128)(2,1)S(1)}, bf16[2,256,128]{2,1,0:T(8,128)(2,1)S(1)}, u32[]{:S(2)}, u32[]{:S(2)}) collective-permute-start(bf16[2,256,128]{2,1,0:T(8,128)(2,1)S(1)} %shard_map.114.rest_17_), channel_id=1, source_target_pairs={{0,1},{1,0},{2,3},{3,2},{4,5},{5,4},{6,7},{7,6},{8,9},{9,8},{10,11... | collective-permute-start | bytes 393224 | tf_op jit(solution)/shard_map/ppermute | solution.py:462
  35.6 3.6 %collective-permute-start.6 = (bf16[2,256,128]{2,1,0:T(8,128)(2,1)S(1)}, bf16[2,256,128]{2,1,0:T(8,128)(2,1)S(1)}, u32[]{:S(2)}, u32[]{:S(2)}) collective-permute-start(bf16[2,256,128]{2,1,0:T(8,128)(2,1)S(1)} %shard_map.113.rest_13_), channel_id=1, source_target_pairs={{0,1},{1,0},{2,3},{3,2},{4,5},{5,4},{6,7},{7,6},{8,9},{9,8},{10,11... | collective-permute-start | bytes 393224 | tf_op jit(solution)/shard_map/ppermute | solution.py:462
  36.1 3.1 %collective-permute-start.16 = (bf16[2,256,128]{2,1,0:T(8,128)(2,1)S(1)}, bf16[2,256,128]{2,1,0:T(8,128)(2,1)S(1)}, u32[]{:S(2)}, u32[]{:S(2)}) collective-permute-start(bf16[2,256,128]{2,1,0:T(8,128)(2,1)S(1)} %collective-permute-done.15.rest_23_), channel_id=1, source_target_pairs={{0,1},{1,0},{2,3},{3,2},{4,5},{5,4},{6,7},{7,6},{8,9},{9,8},{10,11... | collective-permute-start | bytes 393224 | tf_op jit(solution)/shard_map/ppermute | solution.py:462
  36.1 3.0 %collective-permute-start.12 = (bf16[2,256,128]{2,1,0:T(8,128)(2,1)S(1)}, bf16[2,256,128]{2,1,0:T(8,128)(2,1)S(1)}, u32[]{:S(2)}, u32[]{:S(2)}) collective-permute-start(bf16[2,256,128]{2,1,0:T(8,128)(2,1)S(1)} %collective-permute-done.11.rest_19_), channel_id=1, source_target_pairs={{0,1},{1,0},{2,3},{3,2},{4,5},{5,4},{6,7},{7,6},{8,9},{9,8},{10,11... | collective-permute-start | bytes 393224 | tf_op jit(solution)/shard_map/ppermute | solution.py:462
  39.2 1.3 %collective-permute-start.8 = (bf16[2,256,128]{2,1,0:T(8,128)(2,1)S(1)}, bf16[2,256,128]{2,1,0:T(8,128)(2,1)S(1)}, u32[]{:S(2)}, u32[]{:S(2)}) collective-permute-start(bf16[2,256,128]{2,1,0:T(8,128)(2,1)S(1)} %collective-permute-done.7.rest_15_), channel_id=1, source_target_pairs={{0,1},{1,0},{2,3},{3,2},{4,5},{5,4},{6,7},{7,6},{8,9},{9,8},{10,11... | collective-permute-start | bytes 393224 | tf_op jit(solution)/shard_map/ppermute | solution.py:462

commit v3 on v2

--- a/solution.py
+++ b/solution.py
@@ -121,32 +121,27 @@
         out[...] = raw_ref[:, :, pl.ds(first, LANES)]
 
 
-def phase_kernel(total, place_ref, rate_ref, one_ref, two_ref, done_ref):
-    done_ref[0] = 1
-    start = (place_ref[1] * (total // QUAD)).astype(jnp.float32)
+def phase_rows(ref, rate, start, total):
     size = (LANES, LANES)
-    for level, ref in ((0, one_ref), (1, two_ref)):
-        blocks, angles = ref.shape[1], ref.shape[2]
-        rate = rate_ref[level]
-        lane = lax.broadcasted_iota(jnp.int32, size, 1).astype(jnp.float32)
-        factor = 1.0 + (lane + start) / total
-
-        @pl.loop(0, angles // LANES)
-        def _(part):
-            row = lax.broadcasted_iota(jnp.int32, size, 0) + part * LANES
-            slope = rate * ((row.astype(jnp.float32) + 0.5) / angles - 0.5)
-            value = unit(slope * factor)
-            step = unit(slope * (LANES / total))
-            at = pl.ds(pl.multiple_of(part * LANES, LANES), LANES)
-            for block in range(blocks):
-                ref[0, block, at, :] = value[0].astype(jnp.bfloat16)
-                ref[1, block, at, :] = value[1].astype(jnp.bfloat16)
-                if block + 1 < blocks:
-                    value = times(value, step)
-
-
-def weight_kernel(pulse_count, weight_ref, steer_ref, one_ref, two_ref, done_ref):
-    done_ref[0] = 1
+    blocks, angles = ref.shape[1], ref.shape[2]
+    lane = lax.broadcasted_iota(jnp.int32, size, 1).astype(jnp.float32)
+    factor = 1.0 + (lane + start) / total
+
+    @pl.loop(0, angles // LANES)
+    def _(part):
+        row = lax.broadcasted_iota(jnp.int32, size, 0) + part * LANES
+        slope = rate * ((row.astype(jnp.float32) + 0.5) / angles - 0.5)
+        value = unit(slope * factor)
+        step = small_unit(slope * (LANES / total))
+        at = pl.ds(pl.multiple_of(part * LANES, LANES), LANES)
+        for block in range(blocks):
+            ref[0, block, at, :] = value[0].astype(jnp.bfloat16)
+            ref[1, block, at, :] = value[1].astype(jnp.bfloat16)
+            if block + 1 < blocks:
+                value = times(value, step)
+
+
+def weight_rows(pulse_count, weight_ref, steer_ref, one_ref, two_ref):
     joined = jnp.concatenate([weight_ref[0, c, part] for c in range(2) for part in range(2)], 1)
     parents = joined.shape[0]
     width = one_ref.shape[2]
@@ -180,6 +175,34 @@
             two_ref[child, row + TILE : row + 2 * TILE] = jnp.concatenate([imag, real], 1)
 
 
+def table_kernel(pulse_count, total, place_ref, rate_ref, near_ref, *refs):
+    sources, targets, done_ref = refs[:2], refs[2:6], refs[6]
+    inputs, held, sems = refs[7:9], refs[9:13], refs[13]
+    loads = [
+        pltpu.make_async_copy(source, ref, sems.at[spot])
+        for spot, (source, ref) in enumerate(zip(sources, inputs))
+    ]
+    stores = [
+        pltpu.make_async_copy(ref, target, sems.at[spot + 2])
+        for spot, (ref, target) in enumerate(zip(held, targets))
+    ]
+    for load in loads:
+        load.start()
+    start = (place_ref[1] * (total // QUAD)).astype(jnp.float32)
+    phase_rows(held[3], rate_ref[1], start, total)
+    stores[3].start()
+    phase_rows(held[2], rate_ref[0], start, total)
+    stores[2].start()
+    for load in loads:
+        load.wait()
+    weight_rows(pulse_count, *inputs, *held[:2])
+    stores[0].start()
+    stores[1].start()
+    done_ref[0] = 1
+    for store in stores:
+        store.wait()
+
+
 def gain_kernel(total, place_ref, offset_ref, filter_ref, out_ref, done_ref):
     done_ref[0] = 1
     second = total // FIRST
@@ -202,23 +225,24 @@
         row = (low[0][k_one : k_one + 1] * (1.0 / total), low[1][k_one : k_one + 1] * (1.0 / total))
         column = (filter_ref[0, :, k_one : k_one + 1], filter_ref[1, :, k_one : k_one + 1])
         value = times(times(high, row), column)
-        out_ref[0, k_one] = value[0]
-        out_ref[1, k_one] = value[1]
-
-
-LOADED = 9
+        out_ref[0, k_one] = value[0].astype(jnp.bfloat16)
+        out_ref[1, k_one] = value[1].astype(jnp.bfloat16)
+
+
+def packs_of(packs):
+    single = (len(packs) - 2) // 2
+    return zip((0, 1, *[2] * single, *[3] * single), packs)
 
 
 def kernel(count, total, place_ref, turn_ref, *rest):
-    sources, rest = rest[:LOADED], rest[LOADED:]
-    pieces, out_ref, rest = rest[:count], rest[count], rest[count + 1 :]
-    held, rest = rest[:LOADED], rest[LOADED:]
+    fone_ref, ftwo_ref, itwo_ref, ione_ref = rest[:4]
+    sources, packs, out_ref, rest = rest[4:9], rest[9:-14], rest[-14], rest[-13:]
+    held, rest = rest[:5], rest[5:]
+    gain_ref, rows_one_ref, rows_two_ref, phase_one_ref, phase_two_ref = held
     samples, partial_ref, folded, compressed, image, ready, load_sems, sems = rest
-    fone_ref, gain_ref, ftwo_ref, itwo_ref, ione_ref = held[:5]
-    rows_one_ref, phase_one_ref, rows_two_ref, phase_two_ref = held[5:]
     loads = [
-        pltpu.make_async_copy(source, target, load_sems.at[number])
-        for number, (source, target) in enumerate(zip(sources, held))
+        pltpu.make_async_copy(source, ref, load_sems.at[spot])
+        for spot, (source, ref) in enumerate(zip(sources, held))
     ]
     for load in loads:
         load.start()
@@ -243,14 +267,15 @@
     index = place_ref[0] * QUAD + place_ref[1]
     tiles = span // TILE
     per_row = chunks // tiles
-    for number, piece in enumerate(pieces):
-        source = index ^ number
-        first_tile = pl.multiple_of(source % per_row * tiles, tiles)
-        samples[:, source // per_row, pl.ds(first_tile, tiles)] = piece[...].reshape(
-            2, tiles, TILE, LANES
-        )
-
-    loads[0].wait()
+    number = [0] * QUAD
+    for rel, pack in packs_of(packs):
+        for spot in range(math.prod(pack.shape[:-3])):
+            source = index ^ (QUAD * number[rel] + rel)
+            number[rel] += 1
+            first_tile = pl.multiple_of(source % per_row * tiles, tiles)
+            samples[:, source // per_row, pl.ds(first_tile, tiles)] = (pack[spot] if len(pack.shape) == 4 else pack[...]).reshape(
+                2, tiles, TILE, LANES
+            )
 
     @pl.loop(0, chunks // 2, unroll=True)
     def _(pair):
@@ -269,8 +294,7 @@
                 partial_ref[k_one, 0, chunk] = real
                 partial_ref[k_one, 1, chunk] = imag
 
-    for load in loads[1:4]:
-        load.wait()
+    loads[0].wait()
 
     @pl.loop(0, FIRST // 2, unroll=True)
     def _(pair):
@@ -288,7 +312,8 @@
                 at = slice(chunk * TILE, (chunk + 1) * TILE)
                 real = result[row : row + TILE, lanes]
                 imag = result[row + TILE : row + 2 * TILE, lanes]
-                gain_real, gain_imag = gain_ref[0, k_one, at], gain_ref[1, k_one, at]
+                gain_real = gain_ref[0, k_one, at].astype(f32)
+                gain_imag = gain_ref[1, k_one, at].astype(f32)
                 parts.append((real * gain_real - imag * gain_imag).astype(bf16))
                 parts.append((real * gain_imag + imag * gain_real).astype(bf16))
             scaled.append(jnp.concatenate(parts, 0))
@@ -304,7 +329,7 @@
                 folded[chunk, 0, k_one] = real
                 folded[chunk, 1, k_one] = imag
 
-    for load in loads[4:]:
+    for load in loads[1:]:
         load.wait()
 
     @pl.loop(0, chunks // 2, unroll=True)
@@ -407,12 +432,31 @@
         in_specs=[far] + [pl.BlockSpec(memory_space=pltpu.SMEM)] * len(flags),
         out_specs=far,
         input_output_aliases={0: 0},
+        cost_estimate=pl.CostEstimate(flops=1, bytes_accessed=1, transcendentals=0),
         compiler_params=pltpu.CompilerParams(vmem_limit_bytes=1024 * 1024),
     )(value, *flags)
 
 
-def focus(place, turns, tables, gain, rows_one, rows_two, phase_one, phase_two, pieces):
-    count = len(pieces)
+def pack_kernel(*refs):
+    for spot in range(refs[-1].shape[0]):
+        refs[-1][spot] = refs[spot][...]
+
+
+def pack(pieces, *flags):
+    vmem = pl.BlockSpec(memory_space=pltpu.VMEM)
+    return pl.pallas_call(
+        pack_kernel,
+        out_shape=jax.ShapeDtypeStruct((len(pieces), *pieces[0].shape), pieces[0].dtype),
+        in_specs=[vmem] * len(pieces) + [pl.BlockSpec(memory_space=pltpu.SMEM)] * len(flags),
+        out_specs=vmem,
+        cost_estimate=pl.CostEstimate(flops=1, bytes_accessed=1, transcendentals=0),
+        compiler_params=pltpu.CompilerParams(vmem_limit_bytes=1024 * 1024),
+    )(*pieces, *flags)
+
+
+def focus(place, turns, tables, made, packs):
+    _, rows_one, rows_two, phase_one, _ = made
+    count = QUAD * packs[0].shape[0]
     total = phase_one.shape[1] * phase_one.shape[3] * QUAD
     second = total // FIRST
     chunks = second // TILE
@@ -420,17 +464,15 @@
     bf16, f32 = jnp.bfloat16, jnp.float32
     smem = pl.BlockSpec(memory_space=pltpu.SMEM)
     vmem = pl.BlockSpec(memory_space=pltpu.VMEM)
+    far = pl.BlockSpec(memory_space=pltpu.HBM)
     parents, children = rows_two.shape[1] // 2, rows_two.shape[2] // 2
     angle_blocks = rows_one.shape[0]
-    fone, ftwo, itwo, ione = tables
-    sources = [fone, gain, ftwo, itwo, ione, rows_one, phase_one, rows_two, phase_two]
-    far = pl.BlockSpec(memory_space=pl.ANY)
     return pl.pallas_call(
         functools.partial(kernel, count, total),
         out_shape=jax.ShapeDtypeStruct((2, angle_blocks * parents, total // QUAD), f32),
-        in_specs=[smem, smem] + [far] * len(sources) + [vmem] * count,
+        in_specs=[smem, smem] + [vmem] * 4 + [far] * len(made) + [vmem] * len(packs),
         out_specs=far,
-        scratch_shapes=[pltpu.VMEM(source.shape, source.dtype) for source in sources]
+        scratch_shapes=[pltpu.VMEM(array.shape, bf16) for array in made]
         + [
             pltpu.VMEM((2, FIRST, chunks, TILE, LANES), bf16),
             pltpu.VMEM((FIRST, 2, chunks, TILE, LANES), bf16),
@@ -438,11 +480,11 @@
             pltpu.VMEM((FIRST // QUAD, chunks, TILE, 2 * LANES), bf16),
             pltpu.VMEM((2, angle_blocks, 2, children, step_width), bf16),
             pltpu.VMEM((2, 2, angle_blocks * parents, step_width), f32),
-            pltpu.SemaphoreType.DMA((LOADED,)),
+            pltpu.SemaphoreType.DMA((5,)),
             pltpu.SemaphoreType.DMA((2,)),
         ],
         compiler_params=pltpu.CompilerParams(vmem_limit_bytes=50 * 1024 * 1024),
-    )(place, turns, *sources, *pieces)
+    )(place, turns, *tables, *made, *packs)
 
 
 def body(raw_echo, range_filter, range_offsets, interp_weight, phase_rate):
@@ -480,52 +522,46 @@
     offset_near = jnp.stack([range_offsets, move(range_offsets, 1)])
     offsets = jnp.concatenate([offset_near, move(offset_near, 2)])
 
-    phase_one, phase_two, phase_done = pl.pallas_call(
-        functools.partial(phase_kernel, total),
-        out_shape=[
-            shape((2, width // LANES, 2 * A0, LANES)),
-            shape((2, width // LANES, 4 * A0, LANES)),
-            flag,
-        ],
-        in_specs=[smem, smem],
-        out_specs=[vmem, vmem, smem],
+    far = pl.BlockSpec(memory_space=pltpu.HBM)
+    child_angles = interp_weight.shape[4]
+    steer = jnp.asarray(steer_blocks(pulse_count, child_angles))
+    made_shapes = [
+        (2 * A0 // child_angles, 8 * child_angles, 2 * LANES),
+        (2, 2 * interp_weight.shape[3], 2 * child_angles),
+        (2, width // LANES, 2 * A0, LANES),
+        (2, width // LANES, 4 * A0, LANES),
+    ]
+    *made, made_flag = pl.pallas_call(
+        functools.partial(table_kernel, pulse_count, total),
+        out_shape=[shape(dims) for dims in made_shapes] + [flag],
+        in_specs=[smem, smem, vmem, far, far],
+        out_specs=[far] * 4 + [smem],
+        scratch_shapes=[
+            pltpu.VMEM(dims, bf16) for dims in [interp_weight.shape, steer.shape, *made_shapes]
+        ]
+        + [pltpu.SemaphoreType.DMA((6,))],
         cost_estimate=cost(2**30, 2**23),
-        compiler_params=small,
-    )(place, phase_rate)
-    child_angles = interp_weight.shape[4]
-    rows_one, rows_two, weight_done = pl.pallas_call(
-        functools.partial(weight_kernel, pulse_count),
-        out_shape=[
-            shape((2 * A0 // child_angles, 8 * child_angles, 2 * LANES)),
-            shape((2, 2 * interp_weight.shape[3], 2 * child_angles)),
-            flag,
-        ],
-        in_specs=[vmem, vmem],
-        out_specs=[vmem, vmem, smem],
-        cost_estimate=cost(2**29, 2**22),
-        compiler_params=small,
-    )(interp_weight, jnp.asarray(steer_blocks(pulse_count, child_angles)))
-    gain, gain_done = pl.pallas_call(
+        compiler_params=pltpu.CompilerParams(vmem_limit_bytes=52 * 1024 * 1024),
+    )(place, phase_rate, offset_near, interp_weight, steer)
+
+    own = [cut[0]] + [move(cut[step], QUAD * step) for step in range(1, groups)]
+    own[1] = hold(own[1], made_flag, offsets)
+    gain, gain_flag = pl.pallas_call(
         functools.partial(gain_kernel, total),
-        out_shape=[shape((2, FIRST, second, LANES), f32), flag],
+        out_shape=[shape((2, FIRST, second, LANES)), flag],
         in_specs=[smem, vmem, vmem],
         out_specs=[vmem, smem],
         cost_estimate=cost(2**28, 2**22),
         compiler_params=small,
     )(place, offsets, range_filter.reshape(2, second, FIRST))
-
+    if groups > 2:
+        own[2] = hold(own[2], gain_flag)
+    across = [move(piece, 2) for piece in own]
+    mine = pack(own)
+    beside = move(mine, 1)
+    packs = [mine, beside, *across, *[move(piece, 1) for piece in across]]
     tables = [jnp.asarray(t) for t in dft_tables(total)]
-    turns = jnp.asarray(turn_table(total))
-
-    own = [cut[0]] + [move(cut[step], QUAD * step) for step in range(1, groups)]
-    own[1] = hold(own[1], phase_done, weight_done)
-    if groups > 2:
-        own[2] = hold(own[2], gain_done)
-    across = [move(piece, 2) for piece in own]
-    beside = [move(piece, 1) for piece in own]
-    diagonal = [move(piece, 1) for piece in across]
-    pieces = [part for four in zip(own, beside, across, diagonal) for part in four]
-    return focus(place, turns, tables, gain, rows_one, rows_two, phase_one, phase_two, pieces)
+    return focus(place, jnp.asarray(turn_table(total)), tables, [gain, *made], packs)
 
 
 def solution(mesh):

time: 54.3 us -> 54.7 us (level)
  waiting for transfers between devices: 5.65 us -> 11.6 us
  local copies, waits for them, and re-layouts: 10.7 us -> 5.83 us
  starting transfers between devices: 13.7 us -> 11.6 us
  Pallas kernels: 23 us -> 24.4 us
    ppermute x17 -> x14, waiting for transfers between devices: 5.65 us -> 11.6 us  [move(): return lax.ppermute(value, 'ap', [(i, i ^ bits) for i in range(count)])]
    unnamed x32 -> x22, local copies, waits for them, and re-layouts: 10.6 us -> 4.93 us
    ppermute x17 -> x14, starting transfers between devices: 13.7 us -> 11.6 us  [move(): return lax.ppermute(value, 'ap', [(i, i ^ bits) for i in range(count)])]
    pallas_call x2, Pallas kernels: 4.99 us -> 6.74 us  [the longest x1 6.7 us: body(): pl.pallas_call(functools.partial(table_kernel, pulse_count, total), out_s...]
    reshape x1, local copies, waits for them, and re-layouts: 0.13 us -> 0.9 us  [body(): range_filter.reshape(2, second, FIRST)]
  transfers between devices with their start and end apart: 17 -> 14, of which waited for: 4 -> 5; matrix products, arithmetic and copies ran while one was open for 1% -> 3% of each run, Pallas kernels for 16% -> 21%
where the time goes in v3:
time: 54.7 us; the launch traced here: 54.3 us
  Pallas kernels  24.4 us (45%)
  starting transfers between devices  11.6 us (21%)
  waiting for transfers between devices  11.6 us (21%)
  local copies, waits for them, and re-layouts  5.83 us (11%)
  other arithmetic  0.75 us (1%)
    pallas_call x1, Pallas kernels, focus(): pl.pallas_call(functools.partial(kernel, count, total), out_shape=jax.Sha...  13.2 us
    ppermute x14, starting transfers between devices, move(): return lax.ppermute(value, 'ap', [(i, i ^ bits) for i in range(count)])  11.6 us
    ppermute x14, waiting for transfers between devices, move(): return lax.ppermute(value, 'ap', [(i, i ^ bits) for i in range(count)])  11.6 us
    pallas_call x1, Pallas kernels, body(): pl.pallas_call(functools.partial(table_kernel, pulse_count, total), out_s...  6.7 us
    unnamed x22, local copies, waits for them, and re-layouts  4.93 us
    pallas_call x1, Pallas kernels, body(): pl.pallas_call(functools.partial(gain_kernel, total), out_shape=[shape((2...  2.02 us
    pallas_call x2, Pallas kernels, hold(): pl.pallas_call(hold_kernel, out_shape=jax.ShapeDtypeStruct(value.shape, v...  1.83 us
  transfers between devices with their start and end apart: 14, of which 5 were waited for; matrix products, arithmetic and copies ran while one was open for 3% of the time, Pallas kernels for 21%

profile of v3, /device:TPU:0, one launch (start us, length us, event | category | flops | bytes accessed | tf_op | source)
XLA Modules:
  0.0 54.3 jit_solution(5569321249049289117)
XLA Ops:
  0.0 0.5 collective-permute-start
  0.5 0.1 pad_add_fusion.2.place_ref
  0.5 0.0 copy-start.4
  0.5 1.0 %copy-done.4 = bf16[2,256,512]{2,1,0:T(8,128)(2,1)S(1)} copy-done((bf16[2,256,512]{2,1,0:T(8,128)(2,1)S(1)}, bf16[2,256,512]{2,1,0:T(8,128)(2,1)}, u32[]{:S(2)}) %copy-start.4) | copy-done | bytes 524312
  1.6 0.6 %shard_map.111 = (bf16[2,256,128]{2,1,0:T(8,128)(2,1)S(1)}, bf16[2,256,128]{2,1,0:T(8,128)(2,1)S(1)}, bf16[2,256,128]{2,1,0:T(8,128)(2,1)S(1)}, bf16[2,256,128]{2,1,0:T(8,128)(2,1)S(1)}) custom-call(s32[2]{0:T(128)S(1)} %pad_add_fusion.2.place_ref, bf16[2,256,512]{2,1,0:T(8,128)(2,1)S(1)} %copy-done.4), custom_call_target="tpu_custom_call" | custom-call | tf_op jit(solution)/shard_map/pallas_call | solution.py:515
  2.2 2.6 %collective-permute-start.2 = (bf16[2,256,128]{2,1,0:T(8,128)(2,1)S(1)}, bf16[2,256,128]{2,1,0:T(8,128)(2,1)S(1)}, u32[]{:S(2)}, u32[]{:S(2)}) collective-permute-start(bf16[2,256,128]{2,1,0:T(8,128)(2,1)S(1)} %get-tuple-element.22), channel_id=1, source_target_pairs={{0,4},{1,5},{2,6},{3,7},{4,0},{5,1},{6,2},{7,3},{8,12},{9,13},{10,... | collective-permute-start | bytes 393224 | tf_op jit(solution)/shard_map/ppermute | solution.py:504
  4.9 2.6 %collective-permute-start.3 = (bf16[2,256,128]{2,1,0:T(8,128)(2,1)S(1)}, bf16[2,256,128]{2,1,0:T(8,128)(2,1)S(1)}, u32[]{:S(2)}, u32[]{:S(2)}) collective-permute-start(bf16[2,256,128]{2,1,0:T(8,128)(2,1)S(1)} %get-tuple-element.24), channel_id=1, source_target_pairs={{0,8},{1,9},{2,10},{3,11},{4,12},{5,13},{6,14},{7,15},{8,0},{9,1},... | collective-permute-start | bytes 393224 | tf_op jit(solution)/shard_map/ppermute | solution.py:504
  7.4 0.0 copy-start.10
  7.4 0.0 collective-permute-start.4
  7.5 0.9 %reshape.3.filter_ref = f32[2,256,16]{2,1,0:T(8,128)S(1)} reshape(f32[2,4096]{1,0:T(2,128)} %param.12) | data formatting | bytes 65536 | tf_op jit(solution)/shard_map/reshape | solution.py:556
  8.4 0.0 collective-permute-done
  8.4 0.7 %pad_add_fusion.1.near_ref = s32[2,32]{1,0:T(2,128)S(1)} fusion(s32[1,32]{1,0:T(1,128)S(1)} %bitcast.6, s32[1,32]{1,0:T(1,128)} %bitcast.4), kind=kLoop, calls=%fused_computation.1 | loop fusion | flops 64 | bytes 512 | tf_op jit(solution)/shard_map/stack | solution.py:522
  9.0 1.7 %collective-permute-start.1 = (s32[2,32]{1,0:T(2,128)S(1)}, s32[2,32]{1,0:T(2,128)S(1)}, u32[]{:S(2)}, u32[]{:S(2)}) collective-permute-start(s32[2,32]{1,0:T(2,128)S(1)} %pad_add_fusion.1.near_ref), channel_id=1, source_target_pairs={{0,2},{1,3},{2,0},{3,1},{4,6},{5,7},{6,4},{7,5},{8,10},{9,11},{10,... | collective-permute-start | bytes 776 | tf_op jit(solution)/shard_map/ppermute | solution.py:504
  10.8 0.0 copy-start.7
  10.8 1.0 %copy-done.7 = bf16[2,2,2,256,128]{4,3,2,1,0:T(8,128)(2,1)S(1)} copy-done((bf16[2,2,2,256,128]{4,3,2,1,0:T(8,128)(2,1)S(1)}, bf16[2,2,2,256,128]{4,3,2,1,0:T(8,128)(2,1)}, u32[]{:S(2)}) %copy-start.7) | copy-done | bytes 524312
  11.8 0.0 copy-start.8
  11.8 0.7 %copy-done.8 = f32[2]{0:T(128)S(1)} copy-done((f32[2]{0:T(128)S(1)}, f32[2]{0:T(128)}, u32[]{:S(2)}) %copy-start.8) | copy-done | bytes 32
  12.5 6.7 %shard_map.110 = (bf16[4,1024,256]{2,1,0:T(8,128)(2,1)}, bf16[2,512,256]{2,1,0:T(8,128)(2,1)S(1)}, bf16[2,8,512,128]{3,2,1,0:T(8,128)(2,1)}, bf16[2,8,1024,128]{3,2,1,0:T(8,128)(2,1)}, s32[1]{0:T(128)}) custom-call(s32[2]{0:T(128)S(1)} %pad_add_fusion.2.place_ref, f32[2]{0:T(128)S(1)} %copy-done.8, s32[2,32]{1,0:T(2,128)S(1)} %pad_add_fusion.1.near_ref, ...), custom_call_target="tpu_custom_call" | custom-call | flops 1073741824 | bytes 8388608 | tf_op jit(solution)/shard_map/pallas_call | solution.py:534
  19.2 0.0 copy-start.1
  19.2 0.0 copy-start.2
  19.2 0.0 copy-start.3
  19.2 0.0 copy-start.5
  19.2 0.0 copy-start.6
  19.2 0.0 collective-permute-done.1
  19.2 0.0 copy-done.10
  19.3 2.0 %shard_map.109 = (bf16[2,16,256,128]{3,2,1,0:T(8,128)(2,1)S(1)}, s32[1]{0:T(128)}) custom-call(s32[2]{0:T(128)S(1)} %pad_add_fusion.2.place_ref, s32[4,32]{1,0:T(4,128)S(1)} %pad_add_fusion.offset_ref.refs_2_, f32[2,256,16]{2,1,0:T(8,128)S(1)} %reshape.3.filter_ref), custom_call_target="tpu_custom_call" | custom-call | flops 268435456 | bytes 4194304 | tf_op jit(solution)/shard_map/pallas_call | solution.py:549
  21.3 0.0 copy-start
  21.3 1.3 %copy-done = bf16[2,16,256,128]{3,2,1,0:T(8,128)(2,1)} copy-done((bf16[2,16,256,128]{3,2,1,0:T(8,128)(2,1)}, bf16[2,16,256,128]{3,2,1,0:T(8,128)(2,1)S(1)}, u32[]{:S(2)}) %copy-start) | copy-done | bytes 2097176
  22.7 0.0 collective-permute-done.3.refs_0_
  22.7 0.6 %shard_map.113.refs_2_ = bf16[2,256,128]{2,1,0:T(8,128)(2,1)S(1)} custom-call(bf16[2,256,128]{2,1,0:T(8,128)(2,1)S(1)} %collective-permute-done.3.refs_0_, s32[1]{0:T(128)} %get-tuple-element.25.refs_1_), custom_call_target="tpu_custom_call", output_to_operand_aliasing={{}: (0, {})} | custom-call | flops 1 | bytes 1 | tf_op jit(solution)/shard_map/pallas_call | solution.py:429
  23.3 0.0 collective-permute-done.2.refs_0_
  23.3 1.2 %shard_map.112.refs_1_ = bf16[2,256,128]{2,1,0:T(8,128)(2,1)S(1)} custom-call(bf16[2,256,128]{2,1,0:T(8,128)(2,1)S(1)} %collective-permute-done.2.refs_0_, s32[1]{0:T(128)} %get-tuple-element.23.refs_1_, s32[4,32]{1,0:T(4,128)S(1)} %pad_add_fusion.offset_ref.refs_2_), custom_call_target="tpu_custom_call", output_to_operand_aliasing={{}: (0, {})} | custom-call | flops 1 | bytes 1 | tf_op jit(solution)/shard_map/pallas_call | solution.py:429
  24.5 0.0 collective-permute-done.4.refs_3_
  24.6 0.1 collective-permute-start.5
  24.7 0.4 collective-permute-start.6
  25.0 1.7 %collective-permute-start.9 = (bf16[2,256,128]{2,1,0:T(8,128)(2,1)S(1)}, bf16[2,256,128]{2,1,0:T(8,128)(2,1)S(1)}, u32[]{:S(2)}, u32[]{:S(2)}) collective-permute-start(bf16[2,256,128]{2,1,0:T(8,128)(2,1)S(1)} %collective-permute-done.4.refs_3_), channel_id=1, source_target_pairs={{0,2},{1,3},{2,0},{3,1},{4,6},{5,7},{6,4},{7,5},{8,10},{9,11},{10,... | collective-permute-start | bytes 393224 | tf_op jit(solution)/shard_map/ppermute | solution.py:504
  26.7 0.3 collective-permute-start.8
  27.0 1.7 %collective-permute-start.7 = (bf16[2,256,128]{2,1,0:T(8,128)(2,1)S(1)}, bf16[2,256,128]{2,1,0:T(8,128)(2,1)S(1)}, u32[]{:S(2)}, u32[]{:S(2)}) collective-permute-start(bf16[2,256,128]{2,1,0:T(8,128)(2,1)S(1)} %shard_map.112.refs_1_), channel_id=1, source_target_pairs={{0,2},{1,3},{2,0},{3,1},{4,6},{5,7},{6,4},{7,5},{8,10},{9,11},{10,... | collective-permute-start | bytes 393224 | tf_op jit(solution)/shard_map/ppermute | solution.py:504
  28.8 2.2 %collective-permute-done.6.rest_11_ = bf16[2,256,128]{2,1,0:T(8,128)(2,1)S(1)} collective-permute-done((bf16[2,256,128]{2,1,0:T(8,128)(2,1)S(1)}, bf16[2,256,128]{2,1,0:T(8,128)(2,1)S(1)}, u32[]{:S(2)}, u32[]{:S(2)}) %collective-permute-start.6) | collective-permute-done | bytes 131104 | tf_op jit(solution)/shard_map/ppermute | solution.py:504
  31.0 0.0 collective-permute-start.10
  31.0 2.8 %collective-permute-done.9.rest_14_ = bf16[2,256,128]{2,1,0:T(8,128)(2,1)S(1)} collective-permute-done((bf16[2,256,128]{2,1,0:T(8,128)(2,1)S(1)}, bf16[2,256,128]{2,1,0:T(8,128)(2,1)S(1)}, u32[]{:S(2)}, u32[]{:S(2)}) %collective-permute-start.9) | collective-permute-done | bytes 131104 | tf_op jit(solution)/shard_map/ppermute | solution.py:504
  33.8 0.0 collective-permute-start.13
  33.8 2.8 %collective-permute-done.8.rest_13_ = bf16[2,256,128]{2,1,0:T(8,128)(2,1)S(1)} collective-permute-done((bf16[2,256,128]{2,1,0:T(8,128)(2,1)S(1)}, bf16[2,256,128]{2,1,0:T(8,128)(2,1)S(1)}, u32[]{:S(2)}, u32[]{:S(2)}) %collective-permute-start.8) | collective-permute-done | bytes 131104 | tf_op jit(solution)/shard_map/ppermute | solution.py:504
  36.6 0.0 collective-permute-start.12
  36.6 2.4 %collective-permute-done.7.rest_12_ = bf16[2,256,128]{2,1,0:T(8,128)(2,1)S(1)} collective-permute-done((bf16[2,256,128]{2,1,0:T(8,128)(2,1)S(1)}, bf16[2,256,128]{2,1,0:T(8,128)(2,1)S(1)}, u32[]{:S(2)}, u32[]{:S(2)}) %collective-permute-start.7) | collective-permute-done | bytes 131104 | tf_op jit(solution)/shard_map/ppermute | solution.py:504
  39.0 0.0 collective-permute-start.11
  39.0 0.0 collective-permute-done.10.rest_15_
  39.0 0.0 collective-permute-done.13.rest_18_
  39.0 0.0 collective-permute-done.12.rest_17_
  39.0 1.3 %collective-permute-done.11.rest_16_ = bf16[2,256,128]{2,1,0:T(8,128)(2,1)S(1)} collective-permute-done((bf16[2,256,128]{2,1,0:T(8,128)(2,1)S(1)}, bf16[2,256,128]{2,1,0:T(8,128)(2,1)S(1)}, u32[]{:S(2)}, u32[]{:S(2)}) %collective-permute-start.11) | collective-permute-done | bytes 131104 | tf_op jit(solution)/shard_map/ppermute | solution.py:504
  40.3 0.0 collective-permute-done.5.rest_10_
  40.3 0.0 copy-start.9
  40.3 0.8 %copy-done.9 = bf16[4,2,256,128]{3,2,1,0:T(8,128)(2,1)} copy-done((bf16[4,2,256,128]{3,2,1,0:T(8,128)(2,1)}, bf16[4,2,256,128]{3,2,1,0:T(8,128)(2,1)S(1)}, u32[]{:S(2)}) %copy-start.9) | copy-done | bytes 524312
  41.2 0.0 copy-done.1
  41.2 0.0 copy-done.2
  41.2 0.0 copy-done.3
  41.2 0.0 copy-done.5
  41.2 0.0 copy-done.6
  41.2 13.2 %shard_map.115 = f32[2,1024,1024]{2,1,0:T(8,128)} custom-call(s32[2]{0:T(128)S(1)} %pad_add_fusion.2.place_ref, f32[2,16,16]{2,1,0:T(8,128)S(1)} %copy-done.6, bf16[512,512]{1,0:T(8,128)(2,1)S(1)} %copy-done.3, bf16[512,512]{1,0:T(8,128)(2,1)S(1)} %copy-done.2, bf16[512,512]{1,0:T(8,128)(2,1)S(1)} %copy-done.1, bf16[128,512]{1,0:T(8,128)(2,1)S(1)} %copy-done.5, ...), custom_call_target="tpu_custom_call" | custom-call | tf_op jit(solution)/shard_map/pallas_call | solution.py:470
  (2 shorter events, 0.0 us)
Async XLA Ops:
  0.0 8.4 %collective-permute-start = (s32[32]{0:T(128)}, s32[32]{0:T(128)S(1)}, u32[]{:S(2)}, u32[]{:S(2)}) collective-permute-start(s32[32]{0:T(128)} %param.13), channel_id=1, source_target_pairs={{0,1},{1,0},{2,3},{3,2},{4,5},{5,4},{6,7},{7,6},{8,9},{9,8},{10,11... | collective-permute-start | bytes 392 | tf_op jit(solution)/shard_map/ppermute | solution.py:504
  0.5 1.0 %copy-start.4 = (bf16[2,256,512]{2,1,0:T(8,128)(2,1)S(1)}, bf16[2,256,512]{2,1,0:T(8,128)(2,1)}, u32[]{:S(2)}) copy-start(bf16[2,256,512]{2,1,0:T(8,128)(2,1)} %raw_ref.1) | copy-start | bytes 1572868
  2.2 21.1 %collective-permute-start.2 = (bf16[2,256,128]{2,1,0:T(8,128)(2,1)S(1)}, bf16[2,256,128]{2,1,0:T(8,128)(2,1)S(1)}, u32[]{:S(2)}, u32[]{:S(2)}) collective-permute-start(bf16[2,256,128]{2,1,0:T(8,128)(2,1)S(1)} %get-tuple-element.22), channel_id=1, source_target_pairs={{0,4},{1,5},{2,6},{3,7},{4,0},{5,1},{6,2},{7,3},{8,12},{9,13},{10,... | collective-permute-start | bytes 393224 | tf_op jit(solution)/shard_map/ppermute | solution.py:504
  4.9 17.8 %collective-permute-start.3 = (bf16[2,256,128]{2,1,0:T(8,128)(2,1)S(1)}, bf16[2,256,128]{2,1,0:T(8,128)(2,1)S(1)}, u32[]{:S(2)}, u32[]{:S(2)}) collective-permute-start(bf16[2,256,128]{2,1,0:T(8,128)(2,1)S(1)} %get-tuple-element.24), channel_id=1, source_target_pairs={{0,8},{1,9},{2,10},{3,11},{4,12},{5,13},{6,14},{7,15},{8,0},{9,1},... | collective-permute-start | bytes 393224 | tf_op jit(solution)/shard_map/ppermute | solution.py:504
  7.4 11.8 %copy-start.10 = (s32[32]{0:T(128)S(1)}, s32[32]{0:T(128)}, u32[]{:S(2)}) copy-start(s32[32]{0:T(128)} %param.13) | copy-start | bytes 388
  7.4 17.1 %collective-permute-start.4 = (bf16[2,256,128]{2,1,0:T(8,128)(2,1)S(1)}, bf16[2,256,128]{2,1,0:T(8,128)(2,1)S(1)}, u32[]{:S(2)}, u32[]{:S(2)}) collective-permute-start(bf16[2,256,128]{2,1,0:T(8,128)(2,1)S(1)} %get-tuple-element.26), channel_id=1, source_target_pairs={{0,12},{1,13},{2,14},{3,15},{4,8},{5,9},{6,10},{7,11},{8,4},{9,5},... | collective-permute-start | bytes 393224 | tf_op jit(solution)/shard_map/ppermute | solution.py:504
  9.0 10.2 %collective-permute-start.1 = (s32[2,32]{1,0:T(2,128)S(1)}, s32[2,32]{1,0:T(2,128)S(1)}, u32[]{:S(2)}, u32[]{:S(2)}) collective-permute-start(s32[2,32]{1,0:T(2,128)S(1)} %pad_add_fusion.1.near_ref), channel_id=1, source_target_pairs={{0,2},{1,3},{2,0},{3,1},{4,6},{5,7},{6,4},{7,5},{8,10},{9,11},{10,... | collective-permute-start | bytes 776 | tf_op jit(solution)/shard_map/ppermute | solution.py:504
  10.8 1.0 %copy-start.7 = (bf16[2,2,2,256,128]{4,3,2,1,0:T(8,128)(2,1)S(1)}, bf16[2,2,2,256,128]{4,3,2,1,0:T(8,128)(2,1)}, u32[]{:S(2)}) copy-start(bf16[2,2,2,256,128]{4,3,2,1,0:T(8,128)(2,1)} %refs_0_.1) | copy-start | bytes 1572868
  11.8 0.7 %copy-start.8 = (f32[2]{0:T(128)S(1)}, f32[2]{0:T(128)}, u32[]{:S(2)}) copy-start(f32[2]{0:T(128)} %rate_ref.1) | copy-start | bytes 28
  19.2 22.0 %copy-start.1 = (bf16[512,512]{1,0:T(8,128)(2,1)S(1)}, bf16[512,512]{1,0:T(8,128)(2,1)}, u32[]{:S(2)}) copy-start(bf16[512,512]{1,0:T(8,128)(2,1)} %constant.45.clone.rest_2_) | copy-start | bytes 1572868
  19.2 22.0 %copy-start.2 = (bf16[512,512]{1,0:T(8,128)(2,1)S(1)}, bf16[512,512]{1,0:T(8,128)(2,1)}, u32[]{:S(2)}) copy-start(bf16[512,512]{1,0:T(8,128)(2,1)} %constant.44.clone.rest_1_) | copy-start | bytes 1572868
  19.2 22.0 %copy-start.3 = (bf16[512,512]{1,0:T(8,128)(2,1)S(1)}, bf16[512,512]{1,0:T(8,128)(2,1)}, u32[]{:S(2)}) copy-start(bf16[512,512]{1,0:T(8,128)(2,1)} %constant.43.clone.rest_0_) | copy-start | bytes 1572868
  19.2 22.0 %copy-start.5 = (bf16[128,512]{1,0:T(8,128)(2,1)S(1)}, bf16[128,512]{1,0:T(8,128)(2,1)}, u32[]{:S(2)}) copy-start(bf16[128,512]{1,0:T(8,128)(2,1)} %constant.46.clone.rest_3_) | copy-start | bytes 393220
  19.2 21.9 %copy-start.6 = (f32[2,16,16]{2,1,0:T(8,128)S(1)}, f32[2,16,16]{2,1,0:T(8,128)}, u32[]{:S(2)}) copy-start(f32[2,16,16]{2,1,0:T(8,128)} %constant.47.clone.turn_ref) | copy-start | bytes 6148
  21.3 1.4 %copy-start = (bf16[2,16,256,128]{3,2,1,0:T(8,128)(2,1)}, bf16[2,16,256,128]{3,2,1,0:T(8,128)(2,1)S(1)}, u32[]{:S(2)}) copy-start(bf16[2,16,256,128]{3,2,1,0:T(8,128)(2,1)S(1)} %get-tuple-element.16.rest_4_) | copy-start | bytes 6291460
  24.6 15.8 %collective-permute-start.5 = (bf16[4,2,256,128]{3,2,1,0:T(8,128)(2,1)S(1)}, bf16[4,2,256,128]{3,2,1,0:T(8,128)(2,1)S(1)}, u32[]{:S(2)}, u32[]{:S(2)}) collective-permute-start(bf16[4,2,256,128]{3,2,1,0:T(8,128)(2,1)S(1)} %shard_map.114.rest_9_), channel_id=1, source_target_pairs={{0,1},{1,0},{2,3},{3,2},{4,5},{5,4},{6,7},{7,6},{8,9},{9,8},{10,11... | collective-permute-start | bytes 1572872 | tf_op jit(solution)/shard_map/ppermute | solution.py:504
  24.7 6.4 %collective-permute-start.6 = (bf16[2,256,128]{2,1,0:T(8,128)(2,1)S(1)}, bf16[2,256,128]{2,1,0:T(8,128)(2,1)S(1)}, u32[]{:S(2)}, u32[]{:S(2)}) collective-permute-start(bf16[2,256,128]{2,1,0:T(8,128)(2,1)S(1)} %get-tuple-element.21.refs_0_), channel_id=1, source_target_pairs={{0,2},{1,3},{2,0},{3,1},{4,6},{5,7},{6,4},{7,5},{8,10},{9,11},{10,... | collective-permute-start | bytes 393224 | tf_op jit(solution)/shard_map/ppermute | solution.py:504
  25.0 8.8 %collective-permute-start.9 = (bf16[2,256,128]{2,1,0:T(8,128)(2,1)S(1)}, bf16[2,256,128]{2,1,0:T(8,128)(2,1)S(1)}, u32[]{:S(2)}, u32[]{:S(2)}) collective-permute-start(bf16[2,256,128]{2,1,0:T(8,128)(2,1)S(1)} %collective-permute-done.4.refs_3_), channel_id=1, source_target_pairs={{0,2},{1,3},{2,0},{3,1},{4,6},{5,7},{6,4},{7,5},{8,10},{9,11},{10,... | collective-permute-start | bytes 393224 | tf_op jit(solution)/shard_map/ppermute | solution.py:504
  26.7 9.9 %collective-permute-start.8 = (bf16[2,256,128]{2,1,0:T(8,128)(2,1)S(1)}, bf16[2,256,128]{2,1,0:T(8,128)(2,1)S(1)}, u32[]{:S(2)}, u32[]{:S(2)}) collective-permute-start(bf16[2,256,128]{2,1,0:T(8,128)(2,1)S(1)} %shard_map.113.refs_2_), channel_id=1, source_target_pairs={{0,2},{1,3},{2,0},{3,1},{4,6},{5,7},{6,4},{7,5},{8,10},{9,11},{10,... | collective-permute-start | bytes 393224 | tf_op jit(solution)/shard_map/ppermute | solution.py:504
  27.0 11.9 %collective-permute-start.7 = (bf16[2,256,128]{2,1,0:T(8,128)(2,1)S(1)}, bf16[2,256,128]{2,1,0:T(8,128)(2,1)S(1)}, u32[]{:S(2)}, u32[]{:S(2)}) collective-permute-start(bf16[2,256,128]{2,1,0:T(8,128)(2,1)S(1)} %shard_map.112.refs_1_), channel_id=1, source_target_pairs={{0,2},{1,3},{2,0},{3,1},{4,6},{5,7},{6,4},{7,5},{8,10},{9,11},{10,... | collective-permute-start | bytes 393224 | tf_op jit(solution)/shard_map/ppermute | solution.py:504
  31.0 8.0 %collective-permute-start.10 = (bf16[2,256,128]{2,1,0:T(8,128)(2,1)S(1)}, bf16[2,256,128]{2,1,0:T(8,128)(2,1)S(1)}, u32[]{:S(2)}, u32[]{:S(2)}) collective-permute-start(bf16[2,256,128]{2,1,0:T(8,128)(2,1)S(1)} %collective-permute-done.6.rest_11_), channel_id=1, source_target_pairs={{0,1},{1,0},{2,3},{3,2},{4,5},{5,4},{6,7},{7,6},{8,9},{9,8},{10,11... | collective-permute-start | bytes 393224 | tf_op jit(solution)/shard_map/ppermute | solution.py:504
  33.8 5.2 %collective-permute-start.13 = (bf16[2,256,128]{2,1,0:T(8,128)(2,1)S(1)}, bf16[2,256,128]{2,1,0:T(8,128)(2,1)S(1)}, u32[]{:S(2)}, u32[]{:S(2)}) collective-permute-start(bf16[2,256,128]{2,1,0:T(8,128)(2,1)S(1)} %collective-permute-done.9.rest_14_), channel_id=1, source_target_pairs={{0,1},{1,0},{2,3},{3,2},{4,5},{5,4},{6,7},{7,6},{8,9},{9,8},{10,11... | collective-permute-start | bytes 393224 | tf_op jit(solution)/shard_map/ppermute | solution.py:504
  36.6 2.4 %collective-permute-start.12 = (bf16[2,256,128]{2,1,0:T(8,128)(2,1)S(1)}, bf16[2,256,128]{2,1,0:T(8,128)(2,1)S(1)}, u32[]{:S(2)}, u32[]{:S(2)}) collective-permute-start(bf16[2,256,128]{2,1,0:T(8,128)(2,1)S(1)} %collective-permute-done.8.rest_13_), channel_id=1, source_target_pairs={{0,1},{1,0},{2,3},{3,2},{4,5},{5,4},{6,7},{7,6},{8,9},{9,8},{10,11... | collective-permute-start | bytes 393224 | tf_op jit(solution)/shard_map/ppermute | solution.py:504
  39.0 1.3 %collective-permute-start.11 = (bf16[2,256,128]{2,1,0:T(8,128)(2,1)S(1)}, bf16[2,256,128]{2,1,0:T(8,128)(2,1)S(1)}, u32[]{:S(2)}, u32[]{:S(2)}) collective-permute-start(bf16[2,256,128]{2,1,0:T(8,128)(2,1)S(1)} %collective-permute-done.7.rest_12_), channel_id=1, source_target_pairs={{0,1},{1,0},{2,3},{3,2},{4,5},{5,4},{6,7},{7,6},{8,9},{9,8},{10,11... | collective-permute-start | bytes 393224 | tf_op jit(solution)/shard_map/ppermute | solution.py:504
  40.3 0.8 %copy-start.9 = (bf16[4,2,256,128]{3,2,1,0:T(8,128)(2,1)}, bf16[4,2,256,128]{3,2,1,0:T(8,128)(2,1)S(1)}, u32[]{:S(2)}) copy-start(bf16[4,2,256,128]{3,2,1,0:T(8,128)(2,1)S(1)} %collective-permute-done.5.rest_10_) | copy-start | bytes 1572868

commit v4 on v3

--- a/solution.py
+++ b/solution.py
@@ -203,8 +203,7 @@
         store.wait()
 
 
-def gain_kernel(total, place_ref, offset_ref, filter_ref, out_ref, done_ref):
-    done_ref[0] = 1
+def gain_kernel(total, place_ref, offset_ref, filter_ref, out_ref):
     second = total // FIRST
     offsets = jnp.concatenate(
         [
@@ -229,16 +228,11 @@
         out_ref[1, k_one] = value[1].astype(jnp.bfloat16)
 
 
-def packs_of(packs):
-    single = (len(packs) - 2) // 2
-    return zip((0, 1, *[2] * single, *[3] * single), packs)
-
-
 def kernel(count, total, place_ref, turn_ref, *rest):
-    fone_ref, ftwo_ref, itwo_ref, ione_ref = rest[:4]
-    sources, packs, out_ref, rest = rest[4:9], rest[9:-14], rest[-14], rest[-13:]
-    held, rest = rest[:5], rest[5:]
-    gain_ref, rows_one_ref, rows_two_ref, phase_one_ref, phase_two_ref = held
+    fone_ref, ftwo_ref, itwo_ref, ione_ref, gain_ref = rest[:5]
+    sources, pieces, out_ref, rest = rest[5:9], rest[9:-13], rest[-13], rest[-12:]
+    held, rest = rest[:4], rest[4:]
+    rows_one_ref, rows_two_ref, phase_one_ref, phase_two_ref = held
     samples, partial_ref, folded, compressed, image, ready, load_sems, sems = rest
     loads = [
         pltpu.make_async_copy(source, ref, load_sems.at[spot])
@@ -267,15 +261,12 @@
     index = place_ref[0] * QUAD + place_ref[1]
     tiles = span // TILE
     per_row = chunks // tiles
-    number = [0] * QUAD
-    for rel, pack in packs_of(packs):
-        for spot in range(math.prod(pack.shape[:-3])):
-            source = index ^ (QUAD * number[rel] + rel)
-            number[rel] += 1
-            first_tile = pl.multiple_of(source % per_row * tiles, tiles)
-            samples[:, source // per_row, pl.ds(first_tile, tiles)] = (pack[spot] if len(pack.shape) == 4 else pack[...]).reshape(
-                2, tiles, TILE, LANES
-            )
+    for number, piece in enumerate(pieces):
+        source = index ^ number
+        first_tile = pl.multiple_of(source % per_row * tiles, tiles)
+        samples[:, source // per_row, pl.ds(first_tile, tiles)] = piece[...].reshape(
+            2, tiles, TILE, LANES
+        )
 
     @pl.loop(0, chunks // 2, unroll=True)
     def _(pair):
@@ -293,8 +284,6 @@
                 real, imag = turned(real, imag, chunk, k_one, -1.0)
                 partial_ref[k_one, 0, chunk] = real
                 partial_ref[k_one, 1, chunk] = imag
-
-    loads[0].wait()
 
     @pl.loop(0, FIRST // 2, unroll=True)
     def _(pair):
@@ -329,7 +318,7 @@
                 folded[chunk, 0, k_one] = real
                 folded[chunk, 1, k_one] = imag
 
-    for load in loads[1:]:
+    for load in loads:
         load.wait()
 
     @pl.loop(0, chunks // 2, unroll=True)
@@ -424,39 +413,23 @@
     pass
 
 
-def hold(value, *flags):
+def hold(value, flag, after=None):
     far = pl.BlockSpec(memory_space=pl.ANY)
+    others = [] if after is None else [after]
     return pl.pallas_call(
         hold_kernel,
         out_shape=jax.ShapeDtypeStruct(value.shape, value.dtype),
-        in_specs=[far] + [pl.BlockSpec(memory_space=pltpu.SMEM)] * len(flags),
+        in_specs=[far, pl.BlockSpec(memory_space=pltpu.SMEM)] + [far] * len(others),
         out_specs=far,
         input_output_aliases={0: 0},
         cost_estimate=pl.CostEstimate(flops=1, bytes_accessed=1, transcendentals=0),
         compiler_params=pltpu.CompilerParams(vmem_limit_bytes=1024 * 1024),
-    )(value, *flags)
-
-
-def pack_kernel(*refs):
-    for spot in range(refs[-1].shape[0]):
-        refs[-1][spot] = refs[spot][...]
-
-
-def pack(pieces, *flags):
-    vmem = pl.BlockSpec(memory_space=pltpu.VMEM)
-    return pl.pallas_call(
-        pack_kernel,
-        out_shape=jax.ShapeDtypeStruct((len(pieces), *pieces[0].shape), pieces[0].dtype),
-        in_specs=[vmem] * len(pieces) + [pl.BlockSpec(memory_space=pltpu.SMEM)] * len(flags),
-        out_specs=vmem,
-        cost_estimate=pl.CostEstimate(flops=1, bytes_accessed=1, transcendentals=0),
-        compiler_params=pltpu.CompilerParams(vmem_limit_bytes=1024 * 1024),
-    )(*pieces, *flags)
-
-
-def focus(place, turns, tables, made, packs):
-    _, rows_one, rows_two, phase_one, _ = made
-    count = QUAD * packs[0].shape[0]
+    )(value, flag, *others)
+
+
+def focus(place, turns, tables, gain, made, pieces):
+    rows_one, rows_two, phase_one, _ = made
+    count = len(pieces)
     total = phase_one.shape[1] * phase_one.shape[3] * QUAD
     second = total // FIRST
     chunks = second // TILE
@@ -470,7 +443,7 @@
     return pl.pallas_call(
         functools.partial(kernel, count, total),
         out_shape=jax.ShapeDtypeStruct((2, angle_blocks * parents, total // QUAD), f32),
-        in_specs=[smem, smem] + [vmem] * 4 + [far] * len(made) + [vmem] * len(packs),
+        in_specs=[smem, smem] + [vmem] * 5 + [far] * len(made) + [vmem] * len(pieces),
         out_specs=far,
         scratch_shapes=[pltpu.VMEM(array.shape, bf16) for array in made]
         + [
@@ -480,11 +453,11 @@
             pltpu.VMEM((FIRST // QUAD, chunks, TILE, 2 * LANES), bf16),
             pltpu.VMEM((2, angle_blocks, 2, children, step_width), bf16),
             pltpu.VMEM((2, 2, angle_blocks * parents, step_width), f32),
-            pltpu.SemaphoreType.DMA((5,)),
+            pltpu.SemaphoreType.DMA((4,)),
             pltpu.SemaphoreType.DMA((2,)),
         ],
-        compiler_params=pltpu.CompilerParams(vmem_limit_bytes=50 * 1024 * 1024),
-    )(place, turns, *tables, *made, *packs)
+        compiler_params=pltpu.CompilerParams(vmem_limit_bytes=46 * 1024 * 1024),
+    )(place, turns, *tables, gain, *made, *pieces)
 
 
 def body(raw_echo, range_filter, range_offsets, interp_weight, phase_rate):
@@ -545,23 +518,25 @@
     )(place, phase_rate, offset_near, interp_weight, steer)
 
     own = [cut[0]] + [move(cut[step], QUAD * step) for step in range(1, groups)]
-    own[1] = hold(own[1], made_flag, offsets)
-    gain, gain_flag = pl.pallas_call(
+    across = [move(own[0], 2), move(own[1], 2)]
+    if groups > 2:
+        own[2] = hold(own[2], made_flag, after=across[1])
+    else:
+        made[0] = hold(made[0], made_flag)
+    across += [move(piece, 2) for piece in own[2:]]
+    beside = [move(piece, 1) for piece in own]
+    diagonal = [move(piece, 1) for piece in across]
+    gain = pl.pallas_call(
         functools.partial(gain_kernel, total),
-        out_shape=[shape((2, FIRST, second, LANES)), flag],
+        out_shape=shape((2, FIRST, second, LANES)),
         in_specs=[smem, vmem, vmem],
-        out_specs=[vmem, smem],
+        out_specs=vmem,
         cost_estimate=cost(2**28, 2**22),
         compiler_params=small,
     )(place, offsets, range_filter.reshape(2, second, FIRST))
-    if groups > 2:
-        own[2] = hold(own[2], gain_flag)
-    across = [move(piece, 2) for piece in own]
-    mine = pack(own)
-    beside = move(mine, 1)
-    packs = [mine, beside, *across, *[move(piece, 1) for piece in across]]
+    pieces = [part for four in zip(own, beside, across, diagonal) for part in four]
     tables = [jnp.asarray(t) for t in dft_tables(total)]
-    return focus(place, jnp.asarray(turn_table(total)), tables, [gain, *made], packs)
+    return focus(place, jnp.asarray(turn_table(total)), tables, gain, made, pieces)
 
 
 def solution(mesh):

time: 54.7 us -> 49.8 us (0.910)
  waiting for transfers between devices: 11.6 us -> 3.55 us
  starting transfers between devices: 11.6 us -> 13.8 us
  Pallas kernels: 24.4 us -> 25.5 us
  local copies, waits for them, and re-layouts: 5.83 us -> 4.88 us
  other arithmetic: 0.75 us -> 1.43 us
    ppermute x14 -> x17, waiting for transfers between devices: 11.6 us -> 3.55 us  [move(): return lax.ppermute(value, 'ap', [(i, i ^ bits) for i in range(count)])]
    pallas_call x1, Pallas kernels: 13.2 us -> 15.5 us  [focus(): pl.pallas_call(functools.partial(kernel, count, total), out_shape=jax.Sha...]
    ppermute x14 -> x17, starting transfers between devices: 11.6 us -> 13.8 us  [move(): return lax.ppermute(value, 'ap', [(i, i ^ bits) for i in range(count)])]
    pallas_call x2 -> x1, Pallas kernels: 1.83 us -> 0.64 us  [hold(): pl.pallas_call(hold_kernel, out_shape=jax.ShapeDtypeStruct(value.shape, v...]
    unnamed x22 -> x26, local copies, waits for them, and re-layouts: 4.93 us -> 3.99 us
    concatenate x1, other arithmetic: 0.01 us -> 0.69 us  [body(): offsets = jnp.concatenate([offset_near, move(offset_near, 2)])]
    pallas_call x2 -> x1, Pallas kernels: 2.06 us -> 2.01 us  [body(): pl.pallas_call(functools.partial(gain_kernel, total), out_shape=shape((2,...]
  transfers between devices with their start and end apart: 14 -> 17, of which waited for: 5 -> 3; matrix products, arithmetic and copies ran while one was open for 3% -> 5% of each run, Pallas kernels for 21% -> 19%
where the time goes in v4:
time: 49.8 us; the launch traced here: 49.4 us
  Pallas kernels  25.5 us (51%)
  starting transfers between devices  13.8 us (28%)
  local copies, waits for them, and re-layouts  4.88 us (10%)
  waiting for transfers between devices  3.55 us (7%)
  other arithmetic  1.43 us (3%)
    pallas_call x1, Pallas kernels, focus(): pl.pallas_call(functools.partial(kernel, count, total), out_shape=jax.Sha...  15.5 us
    ppermute x17, starting transfers between devices, move(): return lax.ppermute(value, 'ap', [(i, i ^ bits) for i in range(count)])  13.8 us
    pallas_call x1, Pallas kernels, body(): pl.pallas_call(functools.partial(table_kernel, pulse_count, total), out_s...  6.7 us
    unnamed x26, local copies, waits for them, and re-layouts  3.99 us
    ppermute x17, waiting for transfers between devices, move(): return lax.ppermute(value, 'ap', [(i, i ^ bits) for i in range(count)])  3.55 us
    pallas_call x1, Pallas kernels, body(): pl.pallas_call(functools.partial(gain_kernel, total), out_shape=shape((2,...  2.01 us
  transfers between devices with their start and end apart: 17, of which 3 were waited for; matrix products, arithmetic and copies ran while one was open for 5% of the time, Pallas kernels for 19%

profile of v4, /device:TPU:0, one launch (start us, length us, event | category | flops | bytes accessed | tf_op | source)
XLA Modules:
  0.0 49.4 jit_solution(13342689476177930906)
XLA Ops:
  0.0 0.1 pad_add_fusion.2.place_ref
  0.1 0.0 copy-start.3
  0.1 1.0 %copy-done.3 = bf16[2,256,512]{2,1,0:T(8,128)(2,1)S(1)} copy-done((bf16[2,256,512]{2,1,0:T(8,128)(2,1)S(1)}, bf16[2,256,512]{2,1,0:T(8,128)(2,1)}, u32[]{:S(2)}) %copy-start.3) | copy-done | bytes 524312
  1.1 0.0 copy-start.6
  1.1 0.6 %shard_map.111 = (bf16[2,256,128]{2,1,0:T(8,128)(2,1)S(1)}, bf16[2,256,128]{2,1,0:T(8,128)(2,1)S(1)}, bf16[2,256,128]{2,1,0:T(8,128)(2,1)S(1)}, bf16[2,256,128]{2,1,0:T(8,128)(2,1)S(1)}) custom-call(s32[2]{0:T(128)S(1)} %pad_add_fusion.2.place_ref, bf16[2,256,512]{2,1,0:T(8,128)(2,1)S(1)} %copy-done.3), custom_call_target="tpu_custom_call" | custom-call | tf_op jit(solution)/shard_map/pallas_call | solution.py:488
  1.8 3.1 %collective-permute-start.5 = (bf16[2,256,128]{2,1,0:T(8,128)(2,1)S(1)}, bf16[2,256,128]{2,1,0:T(8,128)(2,1)S(1)}, u32[]{:S(2)}, u32[]{:S(2)}) collective-permute-start(bf16[2,256,128]{2,1,0:T(8,128)(2,1)S(1)} %get-tuple-element.19), channel_id=1, source_target_pairs={{0,4},{1,5},{2,6},{3,7},{4,0},{5,1},{6,2},{7,3},{8,12},{9,13},{10,... | collective-permute-start | bytes 393224 | tf_op jit(solution)/shard_map/ppermute | solution.py:477
  4.9 1.5 %collective-permute-start.3 = (bf16[2,256,128]{2,1,0:T(8,128)(2,1)S(1)}, bf16[2,256,128]{2,1,0:T(8,128)(2,1)S(1)}, u32[]{:S(2)}, u32[]{:S(2)}) collective-permute-start(bf16[2,256,128]{2,1,0:T(8,128)(2,1)S(1)} %get-tuple-element.18.rest_9_), channel_id=1, source_target_pairs={{0,2},{1,3},{2,0},{3,1},{4,6},{5,7},{6,4},{7,5},{8,10},{9,11},{10,... | collective-permute-start | bytes 393224 | tf_op jit(solution)/shard_map/ppermute | solution.py:477
  6.4 0.0 collective-permute-start.2
  6.4 0.5 %collective-permute-start = (s32[32]{0:T(128)}, s32[32]{0:T(128)S(1)}, u32[]{:S(2)}, u32[]{:S(2)}) collective-permute-start(s32[32]{0:T(128)} %param.13), channel_id=1, source_target_pairs={{0,1},{1,0},{2,3},{3,2},{4,5},{5,4},{6,7},{7,6},{8,9},{9,8},{10,11... | collective-permute-start | bytes 392 | tf_op jit(solution)/shard_map/ppermute | solution.py:477
  6.9 2.6 %collective-permute-start.9 = (bf16[2,256,128]{2,1,0:T(8,128)(2,1)S(1)}, bf16[2,256,128]{2,1,0:T(8,128)(2,1)S(1)}, u32[]{:S(2)}, u32[]{:S(2)}) collective-permute-start(bf16[2,256,128]{2,1,0:T(8,128)(2,1)S(1)} %get-tuple-element.20), channel_id=1, source_target_pairs={{0,8},{1,9},{2,10},{3,11},{4,12},{5,13},{6,14},{7,15},{8,0},{9,1},... | collective-permute-start | bytes 393224 | tf_op jit(solution)/shard_map/ppermute | solution.py:477
  9.5 0.0 collective-permute-done
  9.5 0.8 %collective-permute-start.13 = (bf16[2,256,128]{2,1,0:T(8,128)(2,1)S(1)}, bf16[2,256,128]{2,1,0:T(8,128)(2,1)S(1)}, u32[]{:S(2)}, u32[]{:S(2)}) collective-permute-start(bf16[2,256,128]{2,1,0:T(8,128)(2,1)S(1)} %get-tuple-element.22), channel_id=1, source_target_pairs={{0,12},{1,13},{2,14},{3,15},{4,8},{5,9},{6,10},{7,11},{8,4},{9,5},... | collective-permute-start | bytes 393224 | tf_op jit(solution)/shard_map/ppermute | solution.py:477
  10.3 0.0 collective-permute-done.5.rest_13_
  10.3 0.5 %collective-permute-start.7 = (bf16[2,256,128]{2,1,0:T(8,128)(2,1)S(1)}, bf16[2,256,128]{2,1,0:T(8,128)(2,1)S(1)}, u32[]{:S(2)}, u32[]{:S(2)}) collective-permute-start(bf16[2,256,128]{2,1,0:T(8,128)(2,1)S(1)} %collective-permute-done.5.rest_13_), channel_id=1, source_target_pairs={{0,2},{1,3},{2,0},{3,1},{4,6},{5,7},{6,4},{7,5},{8,10},{9,11},{10,... | collective-permute-start | bytes 393224 | tf_op jit(solution)/shard_map/ppermute | solution.py:477
  10.8 0.0 copy-done.11
  10.8 0.7 %pad_add_fusion.1.near_ref = s32[2,32]{1,0:T(2,128)S(1)} fusion(s32[1,32]{1,0:T(1,128)S(1)} %bitcast.6, s32[1,32]{1,0:T(1,128)} %bitcast.4), kind=kLoop, calls=%fused_computation.1 | loop fusion | flops 64 | bytes 512 | tf_op jit(solution)/shard_map/stack | solution.py:495
  11.5 0.0 copy-done.6
  11.5 0.0 copy-start.9
  11.5 1.0 %copy-done.9 = bf16[2,2,2,256,128]{4,3,2,1,0:T(8,128)(2,1)S(1)} copy-done((bf16[2,2,2,256,128]{4,3,2,1,0:T(8,128)(2,1)S(1)}, bf16[2,2,2,256,128]{4,3,2,1,0:T(8,128)(2,1)}, u32[]{:S(2)}) %copy-start.9) | copy-done | bytes 524312
  12.5 0.7 %copy-done.10 = f32[2]{0:T(128)S(1)} copy-done((f32[2]{0:T(128)S(1)}, f32[2]{0:T(128)}, u32[]{:S(2)}) %copy-start.10) | copy-done | bytes 32
  13.2 6.7 %shard_map.110 = (bf16[4,1024,256]{2,1,0:T(8,128)(2,1)}, bf16[2,512,256]{2,1,0:T(8,128)(2,1)S(1)}, bf16[2,8,512,128]{3,2,1,0:T(8,128)(2,1)}, bf16[2,8,1024,128]{3,2,1,0:T(8,128)(2,1)}, s32[1]{0:T(128)}) custom-call(s32[2]{0:T(128)S(1)} %pad_add_fusion.2.place_ref, f32[2]{0:T(128)S(1)} %copy-done.10, s32[2,32]{1,0:T(2,128)S(1)} %pad_add_fusion.1.near_ref, ...), custom_call_target="tpu_custom_call" | custom-call | flops 1073741824 | bytes 8388608 | tf_op jit(solution)/shard_map/pallas_call | solution.py:507
  19.9 0.0 copy-start
  19.9 0.0 copy-start.1
  19.9 0.0 copy-start.2
  19.9 0.0 copy-start.4
  20.0 0.0 copy-start.5
  20.0 0.0 collective-permute-done.9.refs_0_
  20.0 1.6 %collective-permute-start.1 = (s32[2,32]{1,0:T(2,128)S(1)}, s32[2,32]{1,0:T(2,128)S(1)}, u32[]{:S(2)}, u32[]{:S(2)}) collective-permute-start(s32[2,32]{1,0:T(2,128)S(1)} %pad_add_fusion.1.near_ref), channel_id=1, source_target_pairs={{0,2},{1,3},{2,0},{3,1},{4,6},{5,7},{6,4},{7,5},{8,10},{9,11},{10,... | collective-permute-start | bytes 776 | tf_op jit(solution)/shard_map/ppermute | solution.py:477
  21.6 0.0 collective-permute-done.13.rest_21_
  21.6 0.0 collective-permute-start.6
  21.6 0.0 collective-permute-done.7.refs_2_.rest_15_
  21.6 0.6 %collective-permute-start.15 = (bf16[2,256,128]{2,1,0:T(8,128)(2,1)S(1)}, bf16[2,256,128]{2,1,0:T(8,128)(2,1)}, u32[]{:S(2)}, u32[]{:S(2)}) collective-permute-start(bf16[2,256,128]{2,1,0:T(8,128)(2,1)S(1)} %collective-permute-done.13.rest_21_), channel_id=1, source_target_pairs={{0,2},{1,3},{2,0},{3,1},{4,6},{5,7},{6,4},{7,5},{8,10},{9,11},{10,... | collective-permute-start | bytes 393224 | tf_op jit(solution)/shard_map/ppermute | solution.py:477
  22.2 0.6 %shard_map.112.rest_17_ = bf16[2,256,128]{2,1,0:T(8,128)(2,1)S(1)} custom-call(bf16[2,256,128]{2,1,0:T(8,128)(2,1)S(1)} %collective-permute-done.9.refs_0_, s32[1]{0:T(128)} %get-tuple-element.21.refs_1_, bf16[2,256,128]{2,1,0:T(8,128)(2,1)S(1)} %collective-permute-done.7.refs_2_.rest_15_), custom_call_target="tpu_custom_call", output_to_operand_aliasing={{}: (0, {})} | custom-call | flops 1 | bytes 1 | tf_op jit(solution)/shard_map/pallas_call | solution.py:419
  22.8 0.8 %collective-permute-done.1 = s32[2,32]{1,0:T(2,128)S(1)} collective-permute-done((s32[2,32]{1,0:T(2,128)S(1)}, s32[2,32]{1,0:T(2,128)S(1)}, u32[]{:S(2)}, u32[]{:S(2)}) %collective-permute-start.1) | collective-permute-done | bytes 288 | tf_op jit(solution)/shard_map/ppermute | solution.py:477
  23.6 0.0 collective-permute-start.14
  23.6 0.0 collective-permute-done.3.rest_11_
  23.6 0.6 %copy-done.12 = s32[2,32]{1,0:T(2,128)} copy-done((s32[2,32]{1,0:T(2,128)}, s32[2,32]{1,0:T(2,128)S(1)}, u32[]{:S(2)}) %copy-start.12) | copy-done | bytes 280
  24.2 1.5 %collective-permute-start.11 = (bf16[2,256,128]{2,1,0:T(8,128)(2,1)S(1)}, bf16[2,256,128]{2,1,0:T(8,128)(2,1)}, u32[]{:S(2)}, u32[]{:S(2)}) collective-permute-start(bf16[2,256,128]{2,1,0:T(8,128)(2,1)S(1)} %shard_map.112.rest_17_), channel_id=1, source_target_pairs={{0,2},{1,3},{2,0},{3,1},{4,6},{5,7},{6,4},{7,5},{8,10},{9,11},{10,... | collective-permute-start | bytes 393224 | tf_op jit(solution)/shard_map/ppermute | solution.py:477
  25.7 0.9 %reshape.3.filter_ref = f32[2,256,16]{2,1,0:T(8,128)S(1)} reshape(f32[2,4096]{1,0:T(2,128)} %param.12) | data formatting | bytes 65536 | tf_op jit(solution)/shard_map/reshape | solution.py:536
  26.6 0.0 collective-permute-done.2.rest_10_
  26.6 0.1 collective-permute-start.4
  26.7 0.0 collective-permute-done.6.rest_14_
  26.7 0.5 collective-permute-start.10
  27.2 0.9 %collective-permute-done.15.rest_23_ = bf16[2,256,128]{2,1,0:T(8,128)(2,1)} collective-permute-done((bf16[2,256,128]{2,1,0:T(8,128)(2,1)S(1)}, bf16[2,256,128]{2,1,0:T(8,128)(2,1)}, u32[]{:S(2)}, u32[]{:S(2)}) %collective-permute-start.15) | collective-permute-done | bytes 131104 | tf_op jit(solution)/shard_map/ppermute | solution.py:477
  28.1 0.0 collective-permute-start.8
  28.1 0.0 collective-permute-done.14.rest_22_
  28.1 0.5 %collective-permute-start.16 = (bf16[2,256,128]{2,1,0:T(8,128)(2,1)}, bf16[2,256,128]{2,1,0:T(8,128)(2,1)S(1)}, u32[]{:S(2)}, u32[]{:S(2)}) collective-permute-start(bf16[2,256,128]{2,1,0:T(8,128)(2,1)} %collective-permute-done.15.rest_23_), channel_id=1, source_target_pairs={{0,1},{1,0},{2,3},{3,2},{4,5},{5,4},{6,7},{7,6},{8,9},{9,8},{10,11... | collective-permute-start | bytes 393224 | tf_op jit(solution)/shard_map/ppermute | solution.py:477
  28.6 1.8 %collective-permute-done.11.rest_19_ = bf16[2,256,128]{2,1,0:T(8,128)(2,1)} collective-permute-done((bf16[2,256,128]{2,1,0:T(8,128)(2,1)S(1)}, bf16[2,256,128]{2,1,0:T(8,128)(2,1)}, u32[]{:S(2)}, u32[]{:S(2)}) %collective-permute-start.11) | collective-permute-done | bytes 131104 | tf_op jit(solution)/shard_map/ppermute | solution.py:477
  30.4 0.0 collective-permute-start.12
  30.4 0.7 %pad_add_fusion.offset_ref = s32[4,32]{1,0:T(4,128)S(1)} fusion(s32[2,32]{1,0:T(2,128)} %copy-done.12, s32[1,32]{1,0:T(1,128)} %bitcast.7, s32[1,32]{1,0:T(1,128)} %bitcast.5), kind=kLoop, calls=%fused_computation | loop fusion | flops 256 | bytes 1024 | tf_op jit(solution)/shard_map/concatenate | solution.py:496
  31.1 0.7 %copy-done.7 = s32[2]{0:T(128)S(1)} copy-done((s32[2]{0:T(128)S(1)}, s32[2]{0:T(128)}, u32[]{:S(2)}) %copy-start.7) | copy-done | bytes 32
  31.8 2.0 %shard_map.109.rest_4_ = bf16[2,16,256,128]{3,2,1,0:T(8,128)(2,1)S(1)} custom-call(s32[2]{0:T(128)S(1)} %copy-done.7, s32[4,32]{1,0:T(4,128)S(1)} %pad_add_fusion.offset_ref, f32[2,256,16]{2,1,0:T(8,128)S(1)} %reshape.3.filter_ref), custom_call_target="tpu_custom_call" | custom-call | flops 268435456 | bytes 4194304 | tf_op jit(solution)/shard_map/pallas_call | solution.py:529
  33.8 0.0 collective-permute-done.4.rest_12_
  33.8 0.0 collective-permute-done.8.rest_16_
  33.8 0.0 collective-permute-done.16.rest_24_
  33.8 0.0 collective-permute-done.10.rest_18_
  33.8 0.0 collective-permute-done.12.rest_20_
  33.8 0.0 copy-done
  33.8 0.0 copy-done.1
  33.9 0.0 copy-done.2
  33.9 0.0 copy-done.4
  33.9 0.0 copy-done.5
  33.9 0.0 copy-done.8
  33.9 15.5 %shard_map.113 = f32[2,1024,1024]{2,1,0:T(8,128)} custom-call(s32[2]{0:T(128)S(1)} %copy-done.8, f32[2,16,16]{2,1,0:T(8,128)S(1)} %copy-done.5, bf16[512,512]{1,0:T(8,128)(2,1)S(1)} %copy-done.2, bf16[512,512]{1,0:T(8,128)(2,1)S(1)} %copy-done.1, bf16[512,512]{1,0:T(8,128)(2,1)S(1)} %copy-done, bf16[128,512]{1,0:T(8,128)(2,1)S(1)} %copy-done.4, ...), custom_call_target="tpu_custom_call" | custom-call | tf_op jit(solution)/shard_map/pallas_call | solution.py:443
  (5 shorter events, 0.0 us)
Async XLA Ops:
  0.1 1.0 %copy-start.3 = (bf16[2,256,512]{2,1,0:T(8,128)(2,1)S(1)}, bf16[2,256,512]{2,1,0:T(8,128)(2,1)}, u32[]{:S(2)}) copy-start(bf16[2,256,512]{2,1,0:T(8,128)(2,1)} %raw_ref.1) | copy-start | bytes 1572868
  1.1 10.4 %copy-start.6 = (s32[2]{0:T(128)}, s32[2]{0:T(128)S(1)}, u32[]{:S(2)}) copy-start(s32[2]{0:T(128)S(1)} %pad_add_fusion.2.place_ref) | copy-start | bytes 28
  1.8 8.6 %collective-permute-start.5 = (bf16[2,256,128]{2,1,0:T(8,128)(2,1)S(1)}, bf16[2,256,128]{2,1,0:T(8,128)(2,1)S(1)}, u32[]{:S(2)}, u32[]{:S(2)}) collective-permute-start(bf16[2,256,128]{2,1,0:T(8,128)(2,1)S(1)} %get-tuple-element.19), channel_id=1, source_target_pairs={{0,4},{1,5},{2,6},{3,7},{4,0},{5,1},{6,2},{7,3},{8,12},{9,13},{10,... | collective-permute-start | bytes 393224 | tf_op jit(solution)/shard_map/ppermute | solution.py:477
  4.9 18.8 %collective-permute-start.3 = (bf16[2,256,128]{2,1,0:T(8,128)(2,1)S(1)}, bf16[2,256,128]{2,1,0:T(8,128)(2,1)S(1)}, u32[]{:S(2)}, u32[]{:S(2)}) collective-permute-start(bf16[2,256,128]{2,1,0:T(8,128)(2,1)S(1)} %get-tuple-element.18.rest_9_), channel_id=1, source_target_pairs={{0,2},{1,3},{2,0},{3,1},{4,6},{5,7},{6,4},{7,5},{8,10},{9,11},{10,... | collective-permute-start | bytes 393224 | tf_op jit(solution)/shard_map/ppermute | solution.py:477
  6.4 20.2 %collective-permute-start.2 = (bf16[2,256,128]{2,1,0:T(8,128)(2,1)S(1)}, bf16[2,256,128]{2,1,0:T(8,128)(2,1)S(1)}, u32[]{:S(2)}, u32[]{:S(2)}) collective-permute-start(bf16[2,256,128]{2,1,0:T(8,128)(2,1)S(1)} %get-tuple-element.18.rest_9_), channel_id=1, source_target_pairs={{0,1},{1,0},{2,3},{3,2},{4,5},{5,4},{6,7},{7,6},{8,9},{9,8},{10,11... | collective-permute-start | bytes 393224 | tf_op jit(solution)/shard_map/ppermute | solution.py:477
  6.4 3.1 %collective-permute-start = (s32[32]{0:T(128)}, s32[32]{0:T(128)S(1)}, u32[]{:S(2)}, u32[]{:S(2)}) collective-permute-start(s32[32]{0:T(128)} %param.13), channel_id=1, source_target_pairs={{0,1},{1,0},{2,3},{3,2},{4,5},{5,4},{6,7},{7,6},{8,9},{9,8},{10,11... | collective-permute-start | bytes 392 | tf_op jit(solution)/shard_map/ppermute | solution.py:477
  6.9 13.1 %collective-permute-start.9 = (bf16[2,256,128]{2,1,0:T(8,128)(2,1)S(1)}, bf16[2,256,128]{2,1,0:T(8,128)(2,1)S(1)}, u32[]{:S(2)}, u32[]{:S(2)}) collective-permute-start(bf16[2,256,128]{2,1,0:T(8,128)(2,1)S(1)} %get-tuple-element.20), channel_id=1, source_target_pairs={{0,8},{1,9},{2,10},{3,11},{4,12},{5,13},{6,14},{7,15},{8,0},{9,1},... | collective-permute-start | bytes 393224 | tf_op jit(solution)/shard_map/ppermute | solution.py:477
  9.5 1.4 %copy-start.11 = (s32[32]{0:T(128)}, s32[32]{0:T(128)S(1)}, u32[]{:S(2)}) copy-start(s32[32]{0:T(128)S(1)} %collective-permute-done) | copy-start | bytes 388
  9.5 12.1 %collective-permute-start.13 = (bf16[2,256,128]{2,1,0:T(8,128)(2,1)S(1)}, bf16[2,256,128]{2,1,0:T(8,128)(2,1)S(1)}, u32[]{:S(2)}, u32[]{:S(2)}) collective-permute-start(bf16[2,256,128]{2,1,0:T(8,128)(2,1)S(1)} %get-tuple-element.22), channel_id=1, source_target_pairs={{0,12},{1,13},{2,14},{3,15},{4,8},{5,9},{6,10},{7,11},{8,4},{9,5},... | collective-permute-start | bytes 393224 | tf_op jit(solution)/shard_map/ppermute | solution.py:477
  10.3 11.3 %collective-permute-start.7 = (bf16[2,256,128]{2,1,0:T(8,128)(2,1)S(1)}, bf16[2,256,128]{2,1,0:T(8,128)(2,1)S(1)}, u32[]{:S(2)}, u32[]{:S(2)}) collective-permute-start(bf16[2,256,128]{2,1,0:T(8,128)(2,1)S(1)} %collective-permute-done.5.rest_13_), channel_id=1, source_target_pairs={{0,2},{1,3},{2,0},{3,1},{4,6},{5,7},{6,4},{7,5},{8,10},{9,11},{10,... | collective-permute-start | bytes 393224 | tf_op jit(solution)/shard_map/ppermute | solution.py:477
  11.5 1.0 %copy-start.9 = (bf16[2,2,2,256,128]{4,3,2,1,0:T(8,128)(2,1)S(1)}, bf16[2,2,2,256,128]{4,3,2,1,0:T(8,128)(2,1)}, u32[]{:S(2)}) copy-start(bf16[2,2,2,256,128]{4,3,2,1,0:T(8,128)(2,1)} %refs_0_.1) | copy-start | bytes 1572868
  12.5 0.7 %copy-start.10 = (f32[2]{0:T(128)S(1)}, f32[2]{0:T(128)}, u32[]{:S(2)}) copy-start(f32[2]{0:T(128)} %rate_ref.1) | copy-start | bytes 28
  19.9 13.9 %copy-start = (bf16[512,512]{1,0:T(8,128)(2,1)S(1)}, bf16[512,512]{1,0:T(8,128)(2,1)}, u32[]{:S(2)}) copy-start(bf16[512,512]{1,0:T(8,128)(2,1)} %constant.45.clone.rest_2_) | copy-start | bytes 1572868
  19.9 13.9 %copy-start.1 = (bf16[512,512]{1,0:T(8,128)(2,1)S(1)}, bf16[512,512]{1,0:T(8,128)(2,1)}, u32[]{:S(2)}) copy-start(bf16[512,512]{1,0:T(8,128)(2,1)} %constant.44.clone.rest_1_) | copy-start | bytes 1572868
  19.9 13.9 %copy-start.2 = (bf16[512,512]{1,0:T(8,128)(2,1)S(1)}, bf16[512,512]{1,0:T(8,128)(2,1)}, u32[]{:S(2)}) copy-start(bf16[512,512]{1,0:T(8,128)(2,1)} %constant.43.clone.rest_0_) | copy-start | bytes 1572868
  19.9 13.9 %copy-start.4 = (bf16[128,512]{1,0:T(8,128)(2,1)S(1)}, bf16[128,512]{1,0:T(8,128)(2,1)}, u32[]{:S(2)}) copy-start(bf16[128,512]{1,0:T(8,128)(2,1)} %constant.46.clone.rest_3_) | copy-start | bytes 393220
  20.0 13.9 %copy-start.5 = (f32[2,16,16]{2,1,0:T(8,128)S(1)}, f32[2,16,16]{2,1,0:T(8,128)}, u32[]{:S(2)}) copy-start(f32[2,16,16]{2,1,0:T(8,128)} %constant.47.clone.turn_ref) | copy-start | bytes 6148
  20.0 3.6 %collective-permute-start.1 = (s32[2,32]{1,0:T(2,128)S(1)}, s32[2,32]{1,0:T(2,128)S(1)}, u32[]{:S(2)}, u32[]{:S(2)}) collective-permute-start(s32[2,32]{1,0:T(2,128)S(1)} %pad_add_fusion.1.near_ref), channel_id=1, source_target_pairs={{0,2},{1,3},{2,0},{3,1},{4,6},{5,7},{6,4},{7,5},{8,10},{9,11},{10,... | collective-permute-start | bytes 776 | tf_op jit(solution)/shard_map/ppermute | solution.py:477
  21.6 5.1 %collective-permute-start.6 = (bf16[2,256,128]{2,1,0:T(8,128)(2,1)S(1)}, bf16[2,256,128]{2,1,0:T(8,128)(2,1)S(1)}, u32[]{:S(2)}, u32[]{:S(2)}) collective-permute-start(bf16[2,256,128]{2,1,0:T(8,128)(2,1)S(1)} %collective-permute-done.5.rest_13_), channel_id=1, source_target_pairs={{0,1},{1,0},{2,3},{3,2},{4,5},{5,4},{6,7},{7,6},{8,9},{9,8},{10,11... | collective-permute-start | bytes 393224 | tf_op jit(solution)/shard_map/ppermute | solution.py:477
  21.6 6.5 %collective-permute-start.15 = (bf16[2,256,128]{2,1,0:T(8,128)(2,1)S(1)}, bf16[2,256,128]{2,1,0:T(8,128)(2,1)}, u32[]{:S(2)}, u32[]{:S(2)}) collective-permute-start(bf16[2,256,128]{2,1,0:T(8,128)(2,1)S(1)} %collective-permute-done.13.rest_21_), channel_id=1, source_target_pairs={{0,2},{1,3},{2,0},{3,1},{4,6},{5,7},{6,4},{7,5},{8,10},{9,11},{10,... | collective-permute-start | bytes 393224 | tf_op jit(solution)/shard_map/ppermute | solution.py:477
  23.6 0.6 %copy-start.12 = (s32[2,32]{1,0:T(2,128)}, s32[2,32]{1,0:T(2,128)S(1)}, u32[]{:S(2)}) copy-start(s32[2,32]{1,0:T(2,128)S(1)} %collective-permute-done.1) | copy-start | bytes 772
  23.6 4.4 %collective-permute-start.14 = (bf16[2,256,128]{2,1,0:T(8,128)(2,1)S(1)}, bf16[2,256,128]{2,1,0:T(8,128)(2,1)}, u32[]{:S(2)}, u32[]{:S(2)}) collective-permute-start(bf16[2,256,128]{2,1,0:T(8,128)(2,1)S(1)} %collective-permute-done.13.rest_21_), channel_id=1, source_target_pairs={{0,1},{1,0},{2,3},{3,2},{4,5},{5,4},{6,7},{7,6},{8,9},{9,8},{10,11... | collective-permute-start | bytes 393224 | tf_op jit(solution)/shard_map/ppermute | solution.py:477
  24.2 6.2 %collective-permute-start.11 = (bf16[2,256,128]{2,1,0:T(8,128)(2,1)S(1)}, bf16[2,256,128]{2,1,0:T(8,128)(2,1)}, u32[]{:S(2)}, u32[]{:S(2)}) collective-permute-start(bf16[2,256,128]{2,1,0:T(8,128)(2,1)S(1)} %shard_map.112.rest_17_), channel_id=1, source_target_pairs={{0,2},{1,3},{2,0},{3,1},{4,6},{5,7},{6,4},{7,5},{8,10},{9,11},{10,... | collective-permute-start | bytes 393224 | tf_op jit(solution)/shard_map/ppermute | solution.py:477
  26.6 7.2 %collective-permute-start.4 = (bf16[2,256,128]{2,1,0:T(8,128)(2,1)S(1)}, bf16[2,256,128]{2,1,0:T(8,128)(2,1)S(1)}, u32[]{:S(2)}, u32[]{:S(2)}) collective-permute-start(bf16[2,256,128]{2,1,0:T(8,128)(2,1)S(1)} %collective-permute-done.3.rest_11_), channel_id=1, source_target_pairs={{0,1},{1,0},{2,3},{3,2},{4,5},{5,4},{6,7},{7,6},{8,9},{9,8},{10,11... | collective-permute-start | bytes 393224 | tf_op jit(solution)/shard_map/ppermute | solution.py:477
  26.7 7.1 %collective-permute-start.10 = (bf16[2,256,128]{2,1,0:T(8,128)(2,1)S(1)}, bf16[2,256,128]{2,1,0:T(8,128)(2,1)S(1)}, u32[]{:S(2)}, u32[]{:S(2)}) collective-permute-start(bf16[2,256,128]{2,1,0:T(8,128)(2,1)S(1)} %shard_map.112.rest_17_), channel_id=1, source_target_pairs={{0,1},{1,0},{2,3},{3,2},{4,5},{5,4},{6,7},{7,6},{8,9},{9,8},{10,11... | collective-permute-start | bytes 393224 | tf_op jit(solution)/shard_map/ppermute | solution.py:477
  28.1 5.7 %collective-permute-start.8 = (bf16[2,256,128]{2,1,0:T(8,128)(2,1)S(1)}, bf16[2,256,128]{2,1,0:T(8,128)(2,1)S(1)}, u32[]{:S(2)}, u32[]{:S(2)}) collective-permute-start(bf16[2,256,128]{2,1,0:T(8,128)(2,1)S(1)} %collective-permute-done.7.refs_2_.rest_15_), channel_id=1, source_target_pairs={{0,1},{1,0},{2,3},{3,2},{4,5},{5,4},{6,7},{7,6},{8,9},{9,8},{10,11... | collective-permute-start | bytes 393224 | tf_op jit(solution)/shard_map/ppermute | solution.py:477
  28.1 5.7 %collective-permute-start.16 = (bf16[2,256,128]{2,1,0:T(8,128)(2,1)}, bf16[2,256,128]{2,1,0:T(8,128)(2,1)S(1)}, u32[]{:S(2)}, u32[]{:S(2)}) collective-permute-start(bf16[2,256,128]{2,1,0:T(8,128)(2,1)} %collective-permute-done.15.rest_23_), channel_id=1, source_target_pairs={{0,1},{1,0},{2,3},{3,2},{4,5},{5,4},{6,7},{7,6},{8,9},{9,8},{10,11... | collective-permute-start | bytes 393224 | tf_op jit(solution)/shard_map/ppermute | solution.py:477
  30.4 3.4 %collective-permute-start.12 = (bf16[2,256,128]{2,1,0:T(8,128)(2,1)}, bf16[2,256,128]{2,1,0:T(8,128)(2,1)S(1)}, u32[]{:S(2)}, u32[]{:S(2)}) collective-permute-start(bf16[2,256,128]{2,1,0:T(8,128)(2,1)} %collective-permute-done.11.rest_19_), channel_id=1, source_target_pairs={{0,1},{1,0},{2,3},{3,2},{4,5},{5,4},{6,7},{7,6},{8,9},{9,8},{10,11... | collective-permute-start | bytes 393224 | tf_op jit(solution)/shard_map/ppermute | solution.py:477
  31.1 0.7 %copy-start.7 = (s32[2]{0:T(128)S(1)}, s32[2]{0:T(128)}, u32[]{:S(2)}) copy-start(s32[2]{0:T(128)} %copy-done.6) | copy-start | bytes 28
  31.8 2.1 %copy-start.8 = (s32[2]{0:T(128)S(1)}, s32[2]{0:T(128)}, u32[]{:S(2)}) copy-start(s32[2]{0:T(128)} %copy-done.6) | copy-start | bytes 28

commit v5 on v4

--- a/solution.py
+++ b/solution.py
@@ -175,43 +175,58 @@
             two_ref[child, row + TILE : row + 2 * TILE] = jnp.concatenate([imag, real], 1)
 
 
-def table_kernel(pulse_count, total, place_ref, rate_ref, near_ref, *refs):
-    sources, targets, done_ref = refs[:2], refs[2:6], refs[6]
-    inputs, held, sems = refs[7:9], refs[9:13], refs[13]
+def store_all(held, targets, sems):
+    return [
+        pltpu.make_async_copy(ref, target, sems.at[spot])
+        for spot, (ref, target) in enumerate(zip(held, targets))
+    ]
+
+
+def phase_kernel(total, place_ref, rate_ref, *refs):
+    targets, done_ref, held, sems = refs[:2], refs[2], refs[3:5], refs[5]
+    stores = store_all(held, targets, sems)
+    start = (place_ref[1] * (total // QUAD)).astype(jnp.float32)
+    for level in (1, 0):
+        phase_rows(held[level], rate_ref[level], start, total)
+        stores[level].start()
+    done_ref[0] = 1
+    for store in stores:
+        store.wait()
+
+
+def weight_kernel(pulse_count, total, place_ref, *refs):
+    offset_refs, filter_ref, sources = refs[:QUAD], refs[QUAD], refs[QUAD + 1 : QUAD + 3]
+    targets, done_ref = refs[QUAD + 4 : QUAD + 7], refs[QUAD + 7]
+    inputs, held, sems = refs[QUAD + 8 : QUAD + 10], refs[QUAD + 10 : QUAD + 13], refs[QUAD + 13]
+    stores = store_all(held, targets, sems)
     loads = [
-        pltpu.make_async_copy(source, ref, sems.at[spot])
+        pltpu.make_async_copy(source, ref, sems.at[spot + 3])
         for spot, (source, ref) in enumerate(zip(sources, inputs))
-    ]
-    stores = [
-        pltpu.make_async_copy(ref, target, sems.at[spot + 2])
-        for spot, (ref, target) in enumerate(zip(held, targets))
     ]
     for load in loads:
         load.start()
-    start = (place_ref[1] * (total // QUAD)).astype(jnp.float32)
-    phase_rows(held[3], rate_ref[1], start, total)
-    stores[3].start()
-    phase_rows(held[2], rate_ref[0], start, total)
-    stores[2].start()
+    gain_rows(total, place_ref, offset_refs, filter_ref, held[0])
+    stores[0].start()
     for load in loads:
         load.wait()
-    weight_rows(pulse_count, *inputs, *held[:2])
-    stores[0].start()
+    weight_rows(pulse_count, *inputs, *held[1:])
     stores[1].start()
+    stores[2].start()
     done_ref[0] = 1
     for store in stores:
         store.wait()
 
 
-def gain_kernel(total, place_ref, offset_ref, filter_ref, out_ref):
+def gain_rows(total, place_ref, offset_refs, filter_ref, out_ref):
     second = total // FIRST
-    offsets = jnp.concatenate(
-        [
-            offset_ref[pl.ds(place_ref[1] ^ member, 1), :]
-            for member in range(QUAD)
-        ],
-        1,
-    )
+    member = place_ref[1]
+    offsets = []
+    for owner in range(QUAD):
+        value = offset_refs[0][...]
+        for rel in range(1, QUAD):
+            value = jnp.where((member ^ rel) == owner, offset_refs[rel][...], value)
+        offsets.append(value)
+    offsets = jnp.concatenate(offsets, 1)
     shift = offsets - place_ref[1] * (total // QUAD)
     scale = -2.0 * math.pi / total
 
@@ -229,18 +244,15 @@
 
 
 def kernel(count, total, place_ref, turn_ref, *rest):
-    fone_ref, ftwo_ref, itwo_ref, ione_ref, gain_ref = rest[:5]
-    sources, pieces, out_ref, rest = rest[5:9], rest[9:-13], rest[-13], rest[-12:]
-    held, rest = rest[:4], rest[4:]
-    rows_one_ref, rows_two_ref, phase_one_ref, phase_two_ref = held
-    samples, partial_ref, folded, compressed, image, ready, load_sems, sems = rest
+    fone_ref, ftwo_ref, itwo_ref, ione_ref = rest[:4]
+    sources, pieces, out_ref, rest = rest[4:9], rest[9:-15], rest[-15], rest[-14:]
+    held, rest = rest[:5], rest[5:]
+    gain_ref, rows_one_ref, rows_two_ref, phase_one_ref, phase_two_ref = held
+    samples, partial_ref, folded, compressed, image, ready, load_sems, piece_sem, sems = rest
     loads = [
         pltpu.make_async_copy(source, ref, load_sems.at[spot])
         for spot, (source, ref) in enumerate(zip(sources, held))
     ]
-    for load in loads:
-        load.start()
-
     span = total // count
     second = total // FIRST
     chunks = second // TILE
@@ -259,19 +271,27 @@
         )
 
     index = place_ref[0] * QUAD + place_ref[1]
-    tiles = span // TILE
-    per_row = chunks // tiles
+    per_row = second // span
+    arrivals = []
     for number, piece in enumerate(pieces):
         source = index ^ number
-        first_tile = pl.multiple_of(source % per_row * tiles, tiles)
-        samples[:, source // per_row, pl.ds(first_tile, tiles)] = piece[...].reshape(
-            2, tiles, TILE, LANES
+        rows = pl.ds(pl.multiple_of(source % per_row * span, TILE), span)
+        arrivals.append(
+            pltpu.make_async_copy(piece, samples.at[:, source // per_row, rows], piece_sem)
         )
+    for copy in arrivals + loads:
+        copy.start()
+    for copy in arrivals:
+        copy.wait()
 
     @pl.loop(0, chunks // 2, unroll=True)
     def _(pair):
         right = jnp.concatenate(
-            [samples[:, :, 2 * pair + side].reshape(2 * half, LANES) for side in range(2)], 1
+            [
+                samples[:, :, pl.ds((2 * pair + side) * TILE, TILE)].reshape(2 * half, LANES)
+                for side in range(2)
+            ],
+            1,
         )
         result = dot(fone_ref[...], right)
         for side in range(2):
@@ -284,6 +304,8 @@
                 real, imag = turned(real, imag, chunk, k_one, -1.0)
                 partial_ref[k_one, 0, chunk] = real
                 partial_ref[k_one, 1, chunk] = imag
+
+    loads[0].wait()
 
     @pl.loop(0, FIRST // 2, unroll=True)
     def _(pair):
@@ -318,7 +340,7 @@
                 folded[chunk, 0, k_one] = real
                 folded[chunk, 1, k_one] = imag
 
-    for load in loads:
+    for load in loads[1:]:
         load.wait()
 
     @pl.loop(0, chunks // 2, unroll=True)
@@ -427,8 +449,8 @@
     )(value, flag, *others)
 
 
-def focus(place, turns, tables, gain, made, pieces):
-    rows_one, rows_two, phase_one, _ = made
+def focus(place, turns, tables, made, pieces):
+    _, rows_one, rows_two, phase_one, _ = made
     count = len(pieces)
     total = phase_one.shape[1] * phase_one.shape[3] * QUAD
     second = total // FIRST
@@ -443,21 +465,22 @@
     return pl.pallas_call(
         functools.partial(kernel, count, total),
         out_shape=jax.ShapeDtypeStruct((2, angle_blocks * parents, total // QUAD), f32),
-        in_specs=[smem, smem] + [vmem] * 5 + [far] * len(made) + [vmem] * len(pieces),
+        in_specs=[smem, smem] + [vmem] * 4 + [far] * (len(made) + count),
         out_specs=far,
         scratch_shapes=[pltpu.VMEM(array.shape, bf16) for array in made]
         + [
-            pltpu.VMEM((2, FIRST, chunks, TILE, LANES), bf16),
+            pltpu.VMEM((2, FIRST, second, LANES), bf16),
             pltpu.VMEM((FIRST, 2, chunks, TILE, LANES), bf16),
             pltpu.VMEM((chunks, 2, FIRST, TILE, LANES), bf16),
             pltpu.VMEM((FIRST // QUAD, chunks, TILE, 2 * LANES), bf16),
             pltpu.VMEM((2, angle_blocks, 2, children, step_width), bf16),
             pltpu.VMEM((2, 2, angle_blocks * parents, step_width), f32),
-            pltpu.SemaphoreType.DMA((4,)),
+            pltpu.SemaphoreType.DMA((5,)),
+            pltpu.SemaphoreType.DMA,
             pltpu.SemaphoreType.DMA((2,)),
         ],
         compiler_params=pltpu.CompilerParams(vmem_limit_bytes=46 * 1024 * 1024),
-    )(place, turns, *tables, gain, *made, *pieces)
+    )(place, turns, *tables, *made, *pieces)
 
 
 def body(raw_echo, range_filter, range_offsets, interp_weight, phase_rate):
@@ -480,6 +503,7 @@
         return jax.ShapeDtypeStruct(dims, kind)
 
     flag = shape((1,), jnp.int32)
+    large = pltpu.CompilerParams(vmem_limit_bytes=52 * 1024 * 1024)
     small = pltpu.CompilerParams(vmem_limit_bytes=2 * 1024 * 1024)
 
     def cost(flops, moved):
@@ -492,51 +516,63 @@
         out_specs=[vmem] * groups,
         compiler_params=small,
     )(place, raw_echo)
-    offset_near = jnp.stack([range_offsets, move(range_offsets, 1)])
-    offsets = jnp.concatenate([offset_near, move(offset_near, 2)])
-
-    far = pl.BlockSpec(memory_space=pltpu.HBM)
+    offsets = range_offsets.reshape(1, pulse_count)
+    offsets = [offsets] + [move(offsets, rel) for rel in range(1, QUAD)]
+
+    far = pl.BlockSpec(memory_space=pl.ANY)
     child_angles = interp_weight.shape[4]
     steer = jnp.asarray(steer_blocks(pulse_count, child_angles))
-    made_shapes = [
-        (2 * A0 // child_angles, 8 * child_angles, 2 * LANES),
-        (2, 2 * interp_weight.shape[3], 2 * child_angles),
+    phase_shapes = [
         (2, width // LANES, 2 * A0, LANES),
         (2, width // LANES, 4 * A0, LANES),
     ]
-    *made, made_flag = pl.pallas_call(
-        functools.partial(table_kernel, pulse_count, total),
-        out_shape=[shape(dims) for dims in made_shapes] + [flag],
-        in_specs=[smem, smem, vmem, far, far],
-        out_specs=[far] * 4 + [smem],
-        scratch_shapes=[
-            pltpu.VMEM(dims, bf16) for dims in [interp_weight.shape, steer.shape, *made_shapes]
-        ]
-        + [pltpu.SemaphoreType.DMA((6,))],
+    *phases, phase_flag = pl.pallas_call(
+        functools.partial(phase_kernel, total),
+        out_shape=[shape(dims) for dims in phase_shapes] + [flag],
+        in_specs=[smem, smem],
+        out_specs=[far] * 2 + [smem],
+        scratch_shapes=[pltpu.VMEM(dims, bf16) for dims in phase_shapes]
+        + [pltpu.SemaphoreType.DMA((2,))],
         cost_estimate=cost(2**30, 2**23),
-        compiler_params=pltpu.CompilerParams(vmem_limit_bytes=52 * 1024 * 1024),
-    )(place, phase_rate, offset_near, interp_weight, steer)
+        compiler_params=large,
+    )(place, phase_rate)
 
     own = [cut[0]] + [move(cut[step], QUAD * step) for step in range(1, groups)]
     across = [move(own[0], 2), move(own[1], 2)]
     if groups > 2:
-        own[2] = hold(own[2], made_flag, after=across[1])
-    else:
-        made[0] = hold(made[0], made_flag)
+        own[2] = hold(own[2], phase_flag, after=across[1])
+    weight_shapes = [
+        (2, FIRST, second, LANES),
+        (2 * A0 // child_angles, 8 * child_angles, 2 * LANES),
+        (2, 2 * interp_weight.shape[3], 2 * child_angles),
+    ]
+    *weights, weight_flag = pl.pallas_call(
+        functools.partial(weight_kernel, pulse_count, total),
+        out_shape=[shape(dims) for dims in weight_shapes] + [flag],
+        in_specs=[smem] + [vmem] * (QUAD + 1) + [far] * 3,
+        out_specs=[far] * 3 + [smem],
+        scratch_shapes=[
+            pltpu.VMEM(dims, bf16) for dims in [interp_weight.shape, steer.shape, *weight_shapes]
+        ]
+        + [pltpu.SemaphoreType.DMA((5,))],
+        cost_estimate=cost(2**30, 2**22),
+        compiler_params=large,
+    )(
+        place,
+        *offsets,
+        range_filter.reshape(2, second, FIRST),
+        interp_weight,
+        steer,
+        own[min(2, groups - 1)],
+    )
+    if groups > 3:
+        own[3] = hold(own[3], weight_flag)
     across += [move(piece, 2) for piece in own[2:]]
     beside = [move(piece, 1) for piece in own]
     diagonal = [move(piece, 1) for piece in across]
-    gain = pl.pallas_call(
-        functools.partial(gain_kernel, total),
-        out_shape=shape((2, FIRST, second, LANES)),
-        in_specs=[smem, vmem, vmem],
-        out_specs=vmem,
-        cost_estimate=cost(2**28, 2**22),
-        compiler_params=small,
-    )(place, offsets, range_filter.reshape(2, second, FIRST))
     pieces = [part for four in zip(own, beside, across, diagonal) for part in four]
     tables = [jnp.asarray(t) for t in dft_tables(total)]
-    return focus(place, jnp.asarray(turn_table(total)), tables, gain, made, pieces)
+    return focus(place, jnp.asarray(turn_table(total)), tables, [*weights, *phases], pieces)
 
 
 def solution(mesh):

time: 49.8 us -> 57.6 us (1.16)
  waiting for transfers between devices: 3.55 us -> 8.46 us
  starting transfers between devices: 13.8 us -> 17 us
  Pallas kernels: 25.5 us -> 28.2 us
  local copies, waits for them, and re-layouts: 4.88 us -> 3.46 us
  other arithmetic: 1.43 us -> 0.07 us
    ppermute x17 -> x18, waiting for transfers between devices: 3.55 us -> 8.46 us  [move(): return lax.ppermute(value, 'ap', [(i, i ^ bits) for i in range(count)])]
    pallas_call x2, Pallas kernels: 8.71 us -> 12.1 us  [the longest x1 6.15 us: body(): pl.pallas_call(functools.partial(weight_kernel, pulse_count, total), out_...]
    ppermute x17 -> x18, starting transfers between devices: 13.8 us -> 17 us  [move(): return lax.ppermute(value, 'ap', [(i, i ^ bits) for i in range(count)])]
    pallas_call x1, Pallas kernels: 15.5 us -> 14.1 us  [focus(): pl.pallas_call(functools.partial(kernel, count, total), out_shape=jax.Sha...]
    reshape x1, local copies, waits for them, and re-layouts: 0.89 us -> 0.13 us  [body(): range_filter.reshape(2, second, FIRST)]
    concatenate x1 -> x0, other arithmetic: 0.69 us -> none  [body(): offsets = jnp.concatenate([offset_near, move(offset_near, 2)])]
    unnamed x26 -> x22, local copies, waits for them, and re-layouts: 3.99 us -> 3.33 us
    another operation x1 -> x0, other arithmetic: 0.66 us -> none  [body(): offset_near = jnp.stack([range_offsets, move(range_offsets, 1)])]
  transfers between devices with their start and end apart: 17 -> 18, of which waited for: 3 -> 4; matrix products, arithmetic and copies ran while one was open for 5% -> 0% of each run, Pallas kernels for 19% -> 23%
where the time goes in v5:
time: 57.6 us; the launch traced here: 57.3 us
  Pallas kernels  28.2 us (49%)
  starting transfers between devices  17 us (30%)
  waiting for transfers between devices  8.46 us (15%)
  local copies, waits for them, and re-layouts  3.46 us (6%)
    ppermute x18, starting transfers between devices, move(): return lax.ppermute(value, 'ap', [(i, i ^ bits) for i in range(count)])  17 us
    pallas_call x1, Pallas kernels, focus(): pl.pallas_call(functools.partial(kernel, count, total), out_shape=jax.Sha...  14.1 us
    ppermute x18, waiting for transfers between devices, move(): return lax.ppermute(value, 'ap', [(i, i ^ bits) for i in range(count)])  8.46 us
    pallas_call x1, Pallas kernels, body(): pl.pallas_call(functools.partial(weight_kernel, pulse_count, total), out_...  6.15 us
    pallas_call x1, Pallas kernels, body(): pl.pallas_call(functools.partial(phase_kernel, total), out_shape=[shape(d...  5.97 us
    unnamed x22, local copies, waits for them, and re-layouts  3.33 us
    pallas_call x2, Pallas kernels, hold(): pl.pallas_call(hold_kernel, out_shape=jax.ShapeDtypeStruct(value.shape, v...  1.28 us
  transfers between devices with their start and end apart: 18, of which 4 were waited for; matrix products, arithmetic and copies ran while one was open for 0% of the time, Pallas kernels for 23%

profile of v5, /device:TPU:0, one launch (start us, length us, event | category | flops | bytes accessed | tf_op | source)
XLA Modules:
  0.0 57.3 jit_solution(2098940378702690497)
XLA Ops:
  0.0 0.1 pad_add_fusion.place_ref
  0.1 0.0 copy-start.4
  0.1 1.0 %copy-done.4 = bf16[2,256,512]{2,1,0:T(8,128)(2,1)S(1)} copy-done((bf16[2,256,512]{2,1,0:T(8,128)(2,1)S(1)}, bf16[2,256,512]{2,1,0:T(8,128)(2,1)}, u32[]{:S(2)}) %copy-start.4) | copy-done | bytes 524312
  1.1 0.0 copy-start.10
  1.1 0.6 %shard_map.109 = (bf16[2,256,128]{2,1,0:T(8,128)(2,1)S(1)}, bf16[2,256,128]{2,1,0:T(8,128)(2,1)S(1)}, bf16[2,256,128]{2,1,0:T(8,128)(2,1)S(1)}, bf16[2,256,128]{2,1,0:T(8,128)(2,1)S(1)}) custom-call(s32[2]{0:T(128)S(1)} %pad_add_fusion.place_ref, bf16[2,256,512]{2,1,0:T(8,128)(2,1)S(1)} %copy-done.4), custom_call_target="tpu_custom_call" | custom-call | tf_op jit(solution)/shard_map/pallas_call | solution.py:512
  1.8 3.1 %collective-permute-start.4 = (bf16[2,256,128]{2,1,0:T(8,128)(2,1)S(1)}, bf16[2,256,128]{2,1,0:T(8,128)(2,1)S(1)}, u32[]{:S(2)}, u32[]{:S(2)}) collective-permute-start(bf16[2,256,128]{2,1,0:T(8,128)(2,1)S(1)} %get-tuple-element.18), channel_id=1, source_target_pairs={{0,4},{1,5},{2,6},{3,7},{4,0},{5,1},{6,2},{7,3},{8,12},{9,13},{10,... | collective-permute-start | bytes 393224 | tf_op jit(solution)/shard_map/ppermute | solution.py:500
  4.9 2.6 %collective-permute-start.3 = (bf16[2,256,128]{2,1,0:T(8,128)(2,1)S(1)}, bf16[2,256,128]{2,1,0:T(8,128)(2,1)S(1)}, u32[]{:S(2)}, u32[]{:S(2)}) collective-permute-start(bf16[2,256,128]{2,1,0:T(8,128)(2,1)S(1)} %get-tuple-element.16), channel_id=1, source_target_pairs={{0,8},{1,9},{2,10},{3,11},{4,12},{5,13},{6,14},{7,15},{8,0},{9,1},... | collective-permute-start | bytes 393224 | tf_op jit(solution)/shard_map/ppermute | solution.py:500
  7.4 2.8 %collective-permute-done.4.rest_13_ = bf16[2,256,128]{2,1,0:T(8,128)(2,1)S(1)} collective-permute-done((bf16[2,256,128]{2,1,0:T(8,128)(2,1)S(1)}, bf16[2,256,128]{2,1,0:T(8,128)(2,1)S(1)}, u32[]{:S(2)}, u32[]{:S(2)}) %collective-permute-start.4) | collective-permute-done | bytes 131104 | tf_op jit(solution)/shard_map/ppermute | solution.py:500
  10.2 1.8 %collective-permute-start.5 = (bf16[2,256,128]{2,1,0:T(8,128)(2,1)S(1)}, bf16[2,256,128]{2,1,0:T(8,128)(2,1)S(1)}, u32[]{:S(2)}, u32[]{:S(2)}) collective-permute-start(bf16[2,256,128]{2,1,0:T(8,128)(2,1)S(1)} %collective-permute-done.4.rest_13_), channel_id=1, source_target_pairs={{0,2},{1,3},{2,0},{3,1},{4,6},{5,7},{6,4},{7,5},{8,10},{9,11},{10,... | collective-permute-start | bytes 393224 | tf_op jit(solution)/shard_map/ppermute | solution.py:500
  12.0 0.2 collective-permute-start.7
  12.2 0.0 collective-permute-start.2
  12.2 0.0 copy-start.7
  12.2 3.5 %collective-permute-start.14 = (bf16[2,256,128]{2,1,0:T(8,128)(2,1)S(1)}, bf16[2,256,128]{2,1,0:T(8,128)(2,1)S(1)}, u32[]{:S(2)}, u32[]{:S(2)}) collective-permute-start(bf16[2,256,128]{2,1,0:T(8,128)(2,1)S(1)} %get-tuple-element.25), channel_id=1, source_target_pairs={{0,12},{1,13},{2,14},{3,15},{4,8},{5,9},{6,10},{7,11},{8,4},{9,5},... | collective-permute-start | bytes 393224 | tf_op jit(solution)/shard_map/ppermute | solution.py:500
  15.7 0.7 %copy-done.8 = f32[2]{0:T(128)S(1)} copy-done((f32[2]{0:T(128)S(1)}, f32[2]{0:T(128)}, u32[]{:S(2)}) %copy-start.8) | copy-done | bytes 32
  16.4 6.0 %shard_map.110 = (bf16[2,8,512,128]{3,2,1,0:T(8,128)(2,1)}, bf16[2,8,1024,128]{3,2,1,0:T(8,128)(2,1)}, s32[1]{0:T(128)}) custom-call(s32[2]{0:T(128)S(1)} %pad_add_fusion.place_ref, f32[2]{0:T(128)S(1)} %copy-done.8), custom_call_target="tpu_custom_call" | custom-call | flops 1073741824 | bytes 8388608 | tf_op jit(solution)/shard_map/pallas_call | solution.py:529
  22.4 0.0 copy-done.10
  22.4 0.1 reshape.7.refs_4_
  22.5 0.0 collective-permute-done.3.refs_0_
  22.5 0.0 copy-done.9
  22.5 1.6 %collective-permute-start.1 = (s32[1,32]{1,0:T(1,128)S(1)}, s32[1,32]{1,0:T(1,128)S(1)}, u32[]{:S(2)}, u32[]{:S(2)}) collective-permute-start(s32[1,32]{1,0:T(1,128)S(1)} %bitcast.4), channel_id=1, source_target_pairs={{0,2},{1,3},{2,0},{3,1},{4,6},{5,7},{6,4},{7,5},{8,10},{9,11},{10,... | collective-permute-start | bytes 392 | tf_op jit(solution)/shard_map/ppermute | solution.py:500
  24.1 0.0 collective-permute-done.5.refs_2_.rest_15_
  24.1 0.1 collective-permute-start
  24.2 0.6 %shard_map.111.refs_7_.rest_17_ = bf16[2,256,128]{2,1,0:T(8,128)(2,1)S(1)} custom-call(bf16[2,256,128]{2,1,0:T(8,128)(2,1)S(1)} %collective-permute-done.3.refs_0_, s32[1]{0:T(128)} %get-tuple-element.17.refs_1_, bf16[2,256,128]{2,1,0:T(8,128)(2,1)S(1)} %collective-permute-done.5.refs_2_.rest_15_), custom_call_target="tpu_custom_call", output_to_operand_aliasing={{}: (0, {})} | custom-call | flops 1 | bytes 1 | tf_op jit(solution)/shard_map/pallas_call | solution.py:441
  24.8 0.0 copy-start.1
  24.8 0.0 copy-start.2
  24.9 0.0 copy-start.3
  24.9 0.0 copy-start.5
  24.9 0.0 copy-start.6
  24.9 0.0 collective-permute-done.2.refs_3_
  24.9 0.5 collective-permute-start.6
  25.4 0.7 %collective-permute-done.1.refs_2_ = s32[1,32]{1,0:T(1,128)S(1)} collective-permute-done((s32[1,32]{1,0:T(1,128)S(1)}, s32[1,32]{1,0:T(1,128)S(1)}, u32[]{:S(2)}, u32[]{:S(2)}) %collective-permute-start.1) | collective-permute-done | bytes 160 | tf_op jit(solution)/shard_map/ppermute | solution.py:500
  26.1 0.2 collective-permute-start.9
  26.3 0.0 collective-permute-done.7.rest_11_
  26.3 0.3 collective-permute-start.8
  26.6 0.0 collective-permute-done.refs_1_
  26.6 1.5 %collective-permute-start.12 = (bf16[2,256,128]{2,1,0:T(8,128)(2,1)S(1)}, bf16[2,256,128]{2,1,0:T(8,128)(2,1)S(1)}, u32[]{:S(2)}, u32[]{:S(2)}) collective-permute-start(bf16[2,256,128]{2,1,0:T(8,128)(2,1)S(1)} %shard_map.111.refs_7_.rest_17_), channel_id=1, source_target_pairs={{0,2},{1,3},{2,0},{3,1},{4,6},{5,7},{6,4},{7,5},{8,10},{9,11},{10,... | collective-permute-start | bytes 393224 | tf_op jit(solution)/shard_map/ppermute | solution.py:500
  28.2 0.0 copy-done.7
  28.2 6.1 %shard_map.112 = (bf16[2,16,256,128]{3,2,1,0:T(8,128)(2,1)}, bf16[4,1024,256]{2,1,0:T(8,128)(2,1)}, bf16[2,512,256]{2,1,0:T(8,128)(2,1)S(1)}, s32[1]{0:T(128)}) custom-call(s32[2]{0:T(128)S(1)} %pad_add_fusion.place_ref, s32[1,32]{1,0:T(1,128)S(1)} %bitcast.6, s32[1,32]{1,0:T(1,128)S(1)} %collective-permute-done.refs_1_, ...), custom_call_target="tpu_custom_call" | custom-call | flops 1073741824 | bytes 4194304 | tf_op jit(solution)/shard_map/pallas_call | solution.py:549
  34.3 0.0 collective-permute-done.14.refs_0_
  34.3 0.6 %shard_map.113.rest_21_ = bf16[2,256,128]{2,1,0:T(8,128)(2,1)S(1)} custom-call(bf16[2,256,128]{2,1,0:T(8,128)(2,1)S(1)} %collective-permute-done.14.refs_0_, s32[1]{0:T(128)} %get-tuple-element.26.refs_1_), custom_call_target="tpu_custom_call", output_to_operand_aliasing={{}: (0, {})} | custom-call | flops 1 | bytes 1 | tf_op jit(solution)/shard_map/pallas_call | solution.py:441
  35.0 0.6 %collective-permute-start.16 = (bf16[2,256,128]{2,1,0:T(8,128)(2,1)S(1)}, bf16[2,256,128]{2,1,0:T(8,128)(2,1)S(1)}, u32[]{:S(2)}, u32[]{:S(2)}) collective-permute-start(bf16[2,256,128]{2,1,0:T(8,128)(2,1)S(1)} %shard_map.113.rest_21_), channel_id=1, source_target_pairs={{0,2},{1,3},{2,0},{3,1},{4,6},{5,7},{6,4},{7,5},{8,10},{9,11},{10,... | collective-permute-start | bytes 393224 | tf_op jit(solution)/shard_map/ppermute | solution.py:500
  35.6 0.0 collective-permute-done.6.rest_10_
  35.6 0.0 collective-permute-start.11
  35.6 0.0 collective-permute-done.9.rest_14_
  35.6 0.5 collective-permute-start.15
  36.1 0.0 collective-permute-done.8.rest_12_
  36.1 0.1 collective-permute-start.10
  36.2 0.0 collective-permute-done.12.rest_19_
  36.2 0.4 collective-permute-start.13
  36.6 3.6 %collective-permute-done.16.rest_23_ = bf16[2,256,128]{2,1,0:T(8,128)(2,1)S(1)} collective-permute-done((bf16[2,256,128]{2,1,0:T(8,128)(2,1)S(1)}, bf16[2,256,128]{2,1,0:T(8,128)(2,1)S(1)}, u32[]{:S(2)}, u32[]{:S(2)}) %collective-permute-start.16) | collective-permute-done | bytes 131104 | tf_op jit(solution)/shard_map/ppermute | solution.py:500
  40.2 0.0 collective-permute-start.17
  40.2 0.0 collective-permute-done.10.rest_16_
  40.2 0.0 collective-permute-done.11.rest_18_
  40.3 0.0 collective-permute-done.15.rest_22_
  40.3 0.0 collective-permute-done.13.rest_20_
  40.3 1.3 %collective-permute-done.17.rest_24_ = bf16[2,256,128]{2,1,0:T(8,128)(2,1)S(1)} collective-permute-done((bf16[2,256,128]{2,1,0:T(8,128)(2,1)S(1)}, bf16[2,256,128]{2,1,0:T(8,128)(2,1)S(1)}, u32[]{:S(2)}, u32[]{:S(2)}) %collective-permute-start.17) | collective-permute-done | bytes 131104 | tf_op jit(solution)/shard_map/ppermute | solution.py:500
  41.6 0.0 copy-done.1
  41.6 0.0 copy-done.2
  41.6 0.0 copy-done.3
  41.6 0.0 copy-done.5
  41.6 0.0 copy-done.6
  41.6 0.0 copy-start
  41.6 1.6 %copy-done = bf16[2,16,256,128]{3,2,1,0:T(8,128)(2,1)S(1)} copy-done((bf16[2,16,256,128]{3,2,1,0:T(8,128)(2,1)S(1)}, bf16[2,16,256,128]{3,2,1,0:T(8,128)(2,1)}, u32[]{:S(2)}) %copy-start) | copy-done | bytes 2097176
  43.2 14.1 %shard_map.114 = f32[2,1024,1024]{2,1,0:T(8,128)} custom-call(s32[2]{0:T(128)S(1)} %pad_add_fusion.place_ref, f32[2,16,16]{2,1,0:T(8,128)S(1)} %copy-done.6, bf16[512,512]{1,0:T(8,128)(2,1)S(1)} %copy-done.3, bf16[512,512]{1,0:T(8,128)(2,1)S(1)} %copy-done.2, bf16[512,512]{1,0:T(8,128)(2,1)S(1)} %copy-done.1, bf16[128,512]{1,0:T(8,128)(2,1)S(1)} %copy-done.5, ...), custom_call_target="tpu_custom_call" | custom-call | tf_op jit(solution)/shard_map/pallas_call | solution.py:465
  (2 shorter events, 0.0 us)
Async XLA Ops:
  0.1 1.0 %copy-start.4 = (bf16[2,256,512]{2,1,0:T(8,128)(2,1)S(1)}, bf16[2,256,512]{2,1,0:T(8,128)(2,1)}, u32[]{:S(2)}) copy-start(bf16[2,256,512]{2,1,0:T(8,128)(2,1)} %raw_ref.1) | copy-start | bytes 1572868
  1.1 21.2 %copy-start.10 = (f32[2,4096]{1,0:T(2,128)S(1)}, f32[2,4096]{1,0:T(2,128)}, u32[]{:S(2)}) copy-start(f32[2,4096]{1,0:T(2,128)} %param.12) | copy-start | bytes 98308
  1.8 8.4 %collective-permute-start.4 = (bf16[2,256,128]{2,1,0:T(8,128)(2,1)S(1)}, bf16[2,256,128]{2,1,0:T(8,128)(2,1)S(1)}, u32[]{:S(2)}, u32[]{:S(2)}) collective-permute-start(bf16[2,256,128]{2,1,0:T(8,128)(2,1)S(1)} %get-tuple-element.18), channel_id=1, source_target_pairs={{0,4},{1,5},{2,6},{3,7},{4,0},{5,1},{6,2},{7,3},{8,12},{9,13},{10,... | collective-permute-start | bytes 393224 | tf_op jit(solution)/shard_map/ppermute | solution.py:500
  4.9 17.7 %collective-permute-start.3 = (bf16[2,256,128]{2,1,0:T(8,128)(2,1)S(1)}, bf16[2,256,128]{2,1,0:T(8,128)(2,1)S(1)}, u32[]{:S(2)}, u32[]{:S(2)}) collective-permute-start(bf16[2,256,128]{2,1,0:T(8,128)(2,1)S(1)} %get-tuple-element.16), channel_id=1, source_target_pairs={{0,8},{1,9},{2,10},{3,11},{4,12},{5,13},{6,14},{7,15},{8,0},{9,1},... | collective-permute-start | bytes 393224 | tf_op jit(solution)/shard_map/ppermute | solution.py:500
  10.2 13.9 %collective-permute-start.5 = (bf16[2,256,128]{2,1,0:T(8,128)(2,1)S(1)}, bf16[2,256,128]{2,1,0:T(8,128)(2,1)S(1)}, u32[]{:S(2)}, u32[]{:S(2)}) collective-permute-start(bf16[2,256,128]{2,1,0:T(8,128)(2,1)S(1)} %collective-permute-done.4.rest_13_), channel_id=1, source_target_pairs={{0,2},{1,3},{2,0},{3,1},{4,6},{5,7},{6,4},{7,5},{8,10},{9,11},{10,... | collective-permute-start | bytes 393224 | tf_op jit(solution)/shard_map/ppermute | solution.py:500
  12.0 14.3 %collective-permute-start.7 = (bf16[2,256,128]{2,1,0:T(8,128)(2,1)S(1)}, bf16[2,256,128]{2,1,0:T(8,128)(2,1)S(1)}, u32[]{:S(2)}, u32[]{:S(2)}) collective-permute-start(bf16[2,256,128]{2,1,0:T(8,128)(2,1)S(1)} %get-tuple-element.24.rest_9_), channel_id=1, source_target_pairs={{0,2},{1,3},{2,0},{3,1},{4,6},{5,7},{6,4},{7,5},{8,10},{9,11},{10,... | collective-permute-start | bytes 393224 | tf_op jit(solution)/shard_map/ppermute | solution.py:500
  12.2 12.7 %collective-permute-start.2 = (s32[1,32]{1,0:T(1,128)}, s32[1,32]{1,0:T(1,128)S(1)}, u32[]{:S(2)}, u32[]{:S(2)}) collective-permute-start(s32[1,32]{1,0:T(1,128)} %bitcast.3), channel_id=1, source_target_pairs={{0,3},{1,2},{2,1},{3,0},{4,7},{5,6},{6,5},{7,4},{8,11},{9,10},{10,... | collective-permute-start | bytes 392 | tf_op jit(solution)/shard_map/ppermute | solution.py:500
  12.2 15.9 %copy-start.7 = (bf16[2,2,2,256,128]{4,3,2,1,0:T(8,128)(2,1)S(1)}, bf16[2,2,2,256,128]{4,3,2,1,0:T(8,128)(2,1)}, u32[]{:S(2)}) copy-start(bf16[2,2,2,256,128]{4,3,2,1,0:T(8,128)(2,1)} %refs_5_.1) | copy-start | bytes 1572868
  12.2 22.1 %collective-permute-start.14 = (bf16[2,256,128]{2,1,0:T(8,128)(2,1)S(1)}, bf16[2,256,128]{2,1,0:T(8,128)(2,1)S(1)}, u32[]{:S(2)}, u32[]{:S(2)}) collective-permute-start(bf16[2,256,128]{2,1,0:T(8,128)(2,1)S(1)} %get-tuple-element.25), channel_id=1, source_target_pairs={{0,12},{1,13},{2,14},{3,15},{4,8},{5,9},{6,10},{7,11},{8,4},{9,5},... | collective-permute-start | bytes 393224 | tf_op jit(solution)/shard_map/ppermute | solution.py:500
  15.7 0.7 %copy-start.8 = (f32[2]{0:T(128)S(1)}, f32[2]{0:T(128)}, u32[]{:S(2)}) copy-start(f32[2]{0:T(128)} %rate_ref.1) | copy-start | bytes 28
  16.4 6.1 %copy-start.9 = (s32[32]{0:T(128)S(1)}, s32[32]{0:T(128)}, u32[]{:S(2)}) copy-start(s32[32]{0:T(128)} %param.13) | copy-start | bytes 388
  22.5 3.6 %collective-permute-start.1 = (s32[1,32]{1,0:T(1,128)S(1)}, s32[1,32]{1,0:T(1,128)S(1)}, u32[]{:S(2)}, u32[]{:S(2)}) collective-permute-start(s32[1,32]{1,0:T(1,128)S(1)} %bitcast.4), channel_id=1, source_target_pairs={{0,2},{1,3},{2,0},{3,1},{4,6},{5,7},{6,4},{7,5},{8,10},{9,11},{10,... | collective-permute-start | bytes 392 | tf_op jit(solution)/shard_map/ppermute | solution.py:500
  24.1 2.5 %collective-permute-start = (s32[1,32]{1,0:T(1,128)S(1)}, s32[1,32]{1,0:T(1,128)S(1)}, u32[]{:S(2)}, u32[]{:S(2)}) collective-permute-start(s32[1,32]{1,0:T(1,128)S(1)} %bitcast.5), channel_id=1, source_target_pairs={{0,1},{1,0},{2,3},{3,2},{4,5},{5,4},{6,7},{7,6},{8,9},{9,8},{10,11... | collective-permute-start | bytes 392 | tf_op jit(solution)/shard_map/ppermute | solution.py:500
  24.8 16.8 %copy-start.1 = (bf16[512,512]{1,0:T(8,128)(2,1)S(1)}, bf16[512,512]{1,0:T(8,128)(2,1)}, u32[]{:S(2)}) copy-start(bf16[512,512]{1,0:T(8,128)(2,1)} %constant.45.clone.rest_2_) | copy-start | bytes 1572868
  24.8 16.8 %copy-start.2 = (bf16[512,512]{1,0:T(8,128)(2,1)S(1)}, bf16[512,512]{1,0:T(8,128)(2,1)}, u32[]{:S(2)}) copy-start(bf16[512,512]{1,0:T(8,128)(2,1)} %constant.44.clone.rest_1_) | copy-start | bytes 1572868
  24.9 16.7 %copy-start.3 = (bf16[512,512]{1,0:T(8,128)(2,1)S(1)}, bf16[512,512]{1,0:T(8,128)(2,1)}, u32[]{:S(2)}) copy-start(bf16[512,512]{1,0:T(8,128)(2,1)} %constant.43.clone.rest_0_) | copy-start | bytes 1572868
  24.9 16.7 %copy-start.5 = (bf16[128,512]{1,0:T(8,128)(2,1)S(1)}, bf16[128,512]{1,0:T(8,128)(2,1)}, u32[]{:S(2)}) copy-start(bf16[128,512]{1,0:T(8,128)(2,1)} %constant.46.clone.rest_3_) | copy-start | bytes 393220
  24.9 16.7 %copy-start.6 = (f32[2,16,16]{2,1,0:T(8,128)S(1)}, f32[2,16,16]{2,1,0:T(8,128)}, u32[]{:S(2)}) copy-start(f32[2,16,16]{2,1,0:T(8,128)} %constant.47.clone.turn_ref) | copy-start | bytes 6148
  24.9 10.7 %collective-permute-start.6 = (bf16[2,256,128]{2,1,0:T(8,128)(2,1)S(1)}, bf16[2,256,128]{2,1,0:T(8,128)(2,1)S(1)}, u32[]{:S(2)}, u32[]{:S(2)}) collective-permute-start(bf16[2,256,128]{2,1,0:T(8,128)(2,1)S(1)} %get-tuple-element.24.rest_9_), channel_id=1, source_target_pairs={{0,1},{1,0},{2,3},{3,2},{4,5},{5,4},{6,7},{7,6},{8,9},{9,8},{10,11... | collective-permute-start | bytes 393224 | tf_op jit(solution)/shard_map/ppermute | solution.py:500
  26.1 9.4 %collective-permute-start.9 = (bf16[2,256,128]{2,1,0:T(8,128)(2,1)S(1)}, bf16[2,256,128]{2,1,0:T(8,128)(2,1)S(1)}, u32[]{:S(2)}, u32[]{:S(2)}) collective-permute-start(bf16[2,256,128]{2,1,0:T(8,128)(2,1)S(1)} %collective-permute-done.4.rest_13_), channel_id=1, source_target_pairs={{0,1},{1,0},{2,3},{3,2},{4,5},{5,4},{6,7},{7,6},{8,9},{9,8},{10,11... | collective-permute-start | bytes 393224 | tf_op jit(solution)/shard_map/ppermute | solution.py:500
  26.3 9.7 %collective-permute-start.8 = (bf16[2,256,128]{2,1,0:T(8,128)(2,1)S(1)}, bf16[2,256,128]{2,1,0:T(8,128)(2,1)S(1)}, u32[]{:S(2)}, u32[]{:S(2)}) collective-permute-start(bf16[2,256,128]{2,1,0:T(8,128)(2,1)S(1)} %collective-permute-done.7.rest_11_), channel_id=1, source_target_pairs={{0,1},{1,0},{2,3},{3,2},{4,5},{5,4},{6,7},{7,6},{8,9},{9,8},{10,11... | collective-permute-start | bytes 393224 | tf_op jit(solution)/shard_map/ppermute | solution.py:500
  26.6 9.5 %collective-permute-start.12 = (bf16[2,256,128]{2,1,0:T(8,128)(2,1)S(1)}, bf16[2,256,128]{2,1,0:T(8,128)(2,1)S(1)}, u32[]{:S(2)}, u32[]{:S(2)}) collective-permute-start(bf16[2,256,128]{2,1,0:T(8,128)(2,1)S(1)} %shard_map.111.refs_7_.rest_17_), channel_id=1, source_target_pairs={{0,2},{1,3},{2,0},{3,1},{4,6},{5,7},{6,4},{7,5},{8,10},{9,11},{10,... | collective-permute-start | bytes 393224 | tf_op jit(solution)/shard_map/ppermute | solution.py:500
  35.0 5.3 %collective-permute-start.16 = (bf16[2,256,128]{2,1,0:T(8,128)(2,1)S(1)}, bf16[2,256,128]{2,1,0:T(8,128)(2,1)S(1)}, u32[]{:S(2)}, u32[]{:S(2)}) collective-permute-start(bf16[2,256,128]{2,1,0:T(8,128)(2,1)S(1)} %shard_map.113.rest_21_), channel_id=1, source_target_pairs={{0,2},{1,3},{2,0},{3,1},{4,6},{5,7},{6,4},{7,5},{8,10},{9,11},{10,... | collective-permute-start | bytes 393224 | tf_op jit(solution)/shard_map/ppermute | solution.py:500
  35.6 4.7 %collective-permute-start.11 = (bf16[2,256,128]{2,1,0:T(8,128)(2,1)S(1)}, bf16[2,256,128]{2,1,0:T(8,128)(2,1)S(1)}, u32[]{:S(2)}, u32[]{:S(2)}) collective-permute-start(bf16[2,256,128]{2,1,0:T(8,128)(2,1)S(1)} %shard_map.111.refs_7_.rest_17_), channel_id=1, source_target_pairs={{0,1},{1,0},{2,3},{3,2},{4,5},{5,4},{6,7},{7,6},{8,9},{9,8},{10,11... | collective-permute-start | bytes 393224 | tf_op jit(solution)/shard_map/ppermute | solution.py:500
  35.6 4.7 %collective-permute-start.15 = (bf16[2,256,128]{2,1,0:T(8,128)(2,1)S(1)}, bf16[2,256,128]{2,1,0:T(8,128)(2,1)S(1)}, u32[]{:S(2)}, u32[]{:S(2)}) collective-permute-start(bf16[2,256,128]{2,1,0:T(8,128)(2,1)S(1)} %shard_map.113.rest_21_), channel_id=1, source_target_pairs={{0,1},{1,0},{2,3},{3,2},{4,5},{5,4},{6,7},{7,6},{8,9},{9,8},{10,11... | collective-permute-start | bytes 393224 | tf_op jit(solution)/shard_map/ppermute | solution.py:500
  36.1 4.2 %collective-permute-start.10 = (bf16[2,256,128]{2,1,0:T(8,128)(2,1)S(1)}, bf16[2,256,128]{2,1,0:T(8,128)(2,1)S(1)}, u32[]{:S(2)}, u32[]{:S(2)}) collective-permute-start(bf16[2,256,128]{2,1,0:T(8,128)(2,1)S(1)} %collective-permute-done.5.refs_2_.rest_15_), channel_id=1, source_target_pairs={{0,1},{1,0},{2,3},{3,2},{4,5},{5,4},{6,7},{7,6},{8,9},{9,8},{10,11... | collective-permute-start | bytes 393224 | tf_op jit(solution)/shard_map/ppermute | solution.py:500
  36.2 4.1 %collective-permute-start.13 = (bf16[2,256,128]{2,1,0:T(8,128)(2,1)S(1)}, bf16[2,256,128]{2,1,0:T(8,128)(2,1)S(1)}, u32[]{:S(2)}, u32[]{:S(2)}) collective-permute-start(bf16[2,256,128]{2,1,0:T(8,128)(2,1)S(1)} %collective-permute-done.12.rest_19_), channel_id=1, source_target_pairs={{0,1},{1,0},{2,3},{3,2},{4,5},{5,4},{6,7},{7,6},{8,9},{9,8},{10,11... | collective-permute-start | bytes 393224 | tf_op jit(solution)/shard_map/ppermute | solution.py:500
  40.2 1.3 %collective-permute-start.17 = (bf16[2,256,128]{2,1,0:T(8,128)(2,1)S(1)}, bf16[2,256,128]{2,1,0:T(8,128)(2,1)S(1)}, u32[]{:S(2)}, u32[]{:S(2)}) collective-permute-start(bf16[2,256,128]{2,1,0:T(8,128)(2,1)S(1)} %collective-permute-done.16.rest_23_), channel_id=1, source_target_pairs={{0,1},{1,0},{2,3},{3,2},{4,5},{5,4},{6,7},{7,6},{8,9},{9,8},{10,11... | collective-permute-start | bytes 393224 | tf_op jit(solution)/shard_map/ppermute | solution.py:500
  41.6 1.6 %copy-start = (bf16[2,16,256,128]{3,2,1,0:T(8,128)(2,1)S(1)}, bf16[2,16,256,128]{3,2,1,0:T(8,128)(2,1)}, u32[]{:S(2)}) copy-start(bf16[2,16,256,128]{3,2,1,0:T(8,128)(2,1)} %get-tuple-element.19.rest_4_) | copy-start | bytes 6291460

commit v6 on v5

--- a/solution.py
+++ b/solution.py
@@ -175,46 +175,15 @@
             two_ref[child, row + TILE : row + 2 * TILE] = jnp.concatenate([imag, real], 1)
 
 
-def store_all(held, targets, sems):
-    return [
-        pltpu.make_async_copy(ref, target, sems.at[spot])
-        for spot, (ref, target) in enumerate(zip(held, targets))
-    ]
-
-
-def phase_kernel(total, place_ref, rate_ref, *refs):
-    targets, done_ref, held, sems = refs[:2], refs[2], refs[3:5], refs[5]
-    stores = store_all(held, targets, sems)
+def table_kernel(pulse_count, total, place_ref, rate_ref, *refs):
+    offset_refs, filter_ref, weight_ref, steer_ref = refs[:QUAD], *refs[QUAD : QUAD + 3]
+    gain_ref, one_ref, two_ref, phase_one_ref, phase_two_ref, done_ref = refs[QUAD + 3 :]
     start = (place_ref[1] * (total // QUAD)).astype(jnp.float32)
-    for level in (1, 0):
-        phase_rows(held[level], rate_ref[level], start, total)
-        stores[level].start()
     done_ref[0] = 1
-    for store in stores:
-        store.wait()
-
-
-def weight_kernel(pulse_count, total, place_ref, *refs):
-    offset_refs, filter_ref, sources = refs[:QUAD], refs[QUAD], refs[QUAD + 1 : QUAD + 3]
-    targets, done_ref = refs[QUAD + 4 : QUAD + 7], refs[QUAD + 7]
-    inputs, held, sems = refs[QUAD + 8 : QUAD + 10], refs[QUAD + 10 : QUAD + 13], refs[QUAD + 13]
-    stores = store_all(held, targets, sems)
-    loads = [
-        pltpu.make_async_copy(source, ref, sems.at[spot + 3])
-        for spot, (source, ref) in enumerate(zip(sources, inputs))
-    ]
-    for load in loads:
-        load.start()
-    gain_rows(total, place_ref, offset_refs, filter_ref, held[0])
-    stores[0].start()
-    for load in loads:
-        load.wait()
-    weight_rows(pulse_count, *inputs, *held[1:])
-    stores[1].start()
-    stores[2].start()
-    done_ref[0] = 1
-    for store in stores:
-        store.wait()
+    phase_rows(phase_one_ref, rate_ref[0], start, total)
+    phase_rows(phase_two_ref, rate_ref[1], start, total)
+    gain_rows(total, place_ref, offset_refs, filter_ref, gain_ref)
+    weight_rows(pulse_count, weight_ref, steer_ref, one_ref, two_ref)
 
 
 def gain_rows(total, place_ref, offset_refs, filter_ref, out_ref):
@@ -245,14 +214,9 @@
 
 def kernel(count, total, place_ref, turn_ref, *rest):
     fone_ref, ftwo_ref, itwo_ref, ione_ref = rest[:4]
-    sources, pieces, out_ref, rest = rest[4:9], rest[9:-15], rest[-15], rest[-14:]
-    held, rest = rest[:5], rest[5:]
-    gain_ref, rows_one_ref, rows_two_ref, phase_one_ref, phase_two_ref = held
-    samples, partial_ref, folded, compressed, image, ready, load_sems, piece_sem, sems = rest
-    loads = [
-        pltpu.make_async_copy(source, ref, load_sems.at[spot])
-        for spot, (source, ref) in enumerate(zip(sources, held))
-    ]
+    gain_ref, rows_one_ref, rows_two_ref, phase_one_ref, phase_two_ref = rest[4:9]
+    pieces, out_ref, rest = rest[9:-8], rest[-8], rest[-7:]
+    samples, partial_ref, folded, compressed, image, ready, sems = rest
     span = total // count
     second = total // FIRST
     chunks = second // TILE
@@ -272,17 +236,10 @@
 
     index = place_ref[0] * QUAD + place_ref[1]
     per_row = second // span
-    arrivals = []
     for number, piece in enumerate(pieces):
         source = index ^ number
         rows = pl.ds(pl.multiple_of(source % per_row * span, TILE), span)
-        arrivals.append(
-            pltpu.make_async_copy(piece, samples.at[:, source // per_row, rows], piece_sem)
-        )
-    for copy in arrivals + loads:
-        copy.start()
-    for copy in arrivals:
-        copy.wait()
+        samples[:, source // per_row, rows] = piece[...]
 
     @pl.loop(0, chunks // 2, unroll=True)
     def _(pair):
@@ -304,8 +261,6 @@
                 real, imag = turned(real, imag, chunk, k_one, -1.0)
                 partial_ref[k_one, 0, chunk] = real
                 partial_ref[k_one, 1, chunk] = imag
-
-    loads[0].wait()
 
     @pl.loop(0, FIRST // 2, unroll=True)
     def _(pair):
@@ -340,9 +295,6 @@
                 folded[chunk, 0, k_one] = real
                 folded[chunk, 1, k_one] = imag
 
-    for load in loads[1:]:
-        load.wait()
-
     @pl.loop(0, chunks // 2, unroll=True)
     def _(pair):
         right = jnp.concatenate(
@@ -465,21 +417,18 @@
     return pl.pallas_call(
         functools.partial(kernel, count, total),
         out_shape=jax.ShapeDtypeStruct((2, angle_blocks * parents, total // QUAD), f32),
-        in_specs=[smem, smem] + [vmem] * 4 + [far] * (len(made) + count),
+        in_specs=[smem, smem] + [vmem] * (9 + count),
         out_specs=far,
-        scratch_shapes=[pltpu.VMEM(array.shape, bf16) for array in made]
-        + [
+        scratch_shapes=[
             pltpu.VMEM((2, FIRST, second, LANES), bf16),
             pltpu.VMEM((FIRST, 2, chunks, TILE, LANES), bf16),
             pltpu.VMEM((chunks, 2, FIRST, TILE, LANES), bf16),
             pltpu.VMEM((FIRST // QUAD, chunks, TILE, 2 * LANES), bf16),
             pltpu.VMEM((2, angle_blocks, 2, children, step_width), bf16),
             pltpu.VMEM((2, 2, angle_blocks * parents, step_width), f32),
-            pltpu.SemaphoreType.DMA((5,)),
-            pltpu.SemaphoreType.DMA,
             pltpu.SemaphoreType.DMA((2,)),
         ],
-        compiler_params=pltpu.CompilerParams(vmem_limit_bytes=46 * 1024 * 1024),
+        compiler_params=pltpu.CompilerParams(vmem_limit_bytes=24 * 1024 * 1024),
     )(place, turns, *tables, *made, *pieces)
 
 
@@ -503,7 +452,6 @@
         return jax.ShapeDtypeStruct(dims, kind)
 
     flag = shape((1,), jnp.int32)
-    large = pltpu.CompilerParams(vmem_limit_bytes=52 * 1024 * 1024)
     small = pltpu.CompilerParams(vmem_limit_bytes=2 * 1024 * 1024)
 
     def cost(flops, moved):
@@ -516,63 +464,44 @@
         out_specs=[vmem] * groups,
         compiler_params=small,
     )(place, raw_echo)
-    offsets = range_offsets.reshape(1, pulse_count)
-    offsets = [offsets] + [move(offsets, rel) for rel in range(1, QUAD)]
-
-    far = pl.BlockSpec(memory_space=pl.ANY)
+    near = jnp.stack([range_offsets, move(range_offsets, 1)])
+    joined = [near, move(near, 2)]
+    offsets = [joined[rel // 2][rel % 2 : rel % 2 + 1] for rel in range(QUAD)]
+
     child_angles = interp_weight.shape[4]
     steer = jnp.asarray(steer_blocks(pulse_count, child_angles))
-    phase_shapes = [
-        (2, width // LANES, 2 * A0, LANES),
-        (2, width // LANES, 4 * A0, LANES),
-    ]
-    *phases, phase_flag = pl.pallas_call(
-        functools.partial(phase_kernel, total),
-        out_shape=[shape(dims) for dims in phase_shapes] + [flag],
-        in_specs=[smem, smem],
-        out_specs=[far] * 2 + [smem],
-        scratch_shapes=[pltpu.VMEM(dims, bf16) for dims in phase_shapes]
-        + [pltpu.SemaphoreType.DMA((2,))],
+    *made, made_flag = pl.pallas_call(
+        functools.partial(table_kernel, pulse_count, total),
+        out_shape=[
+            shape((2, FIRST, second, LANES)),
+            shape((2 * A0 // child_angles, 8 * child_angles, 2 * LANES)),
+            shape((2, 2 * interp_weight.shape[3], 2 * child_angles)),
+            shape((2, width // LANES, 2 * A0, LANES)),
+            shape((2, width // LANES, 4 * A0, LANES)),
+            flag,
+        ],
+        in_specs=[smem, smem] + [vmem] * (QUAD + 3),
+        out_specs=[vmem] * 5 + [smem],
         cost_estimate=cost(2**30, 2**23),
-        compiler_params=large,
-    )(place, phase_rate)
-
-    own = [cut[0]] + [move(cut[step], QUAD * step) for step in range(1, groups)]
-    across = [move(own[0], 2), move(own[1], 2)]
-    if groups > 2:
-        own[2] = hold(own[2], phase_flag, after=across[1])
-    weight_shapes = [
-        (2, FIRST, second, LANES),
-        (2 * A0 // child_angles, 8 * child_angles, 2 * LANES),
-        (2, 2 * interp_weight.shape[3], 2 * child_angles),
-    ]
-    *weights, weight_flag = pl.pallas_call(
-        functools.partial(weight_kernel, pulse_count, total),
-        out_shape=[shape(dims) for dims in weight_shapes] + [flag],
-        in_specs=[smem] + [vmem] * (QUAD + 1) + [far] * 3,
-        out_specs=[far] * 3 + [smem],
-        scratch_shapes=[
-            pltpu.VMEM(dims, bf16) for dims in [interp_weight.shape, steer.shape, *weight_shapes]
-        ]
-        + [pltpu.SemaphoreType.DMA((5,))],
-        cost_estimate=cost(2**30, 2**22),
-        compiler_params=large,
+        compiler_params=small,
     )(
         place,
+        phase_rate,
         *offsets,
         range_filter.reshape(2, second, FIRST),
         interp_weight,
         steer,
-        own[min(2, groups - 1)],
     )
-    if groups > 3:
-        own[3] = hold(own[3], weight_flag)
-    across += [move(piece, 2) for piece in own[2:]]
+
+    own = [cut[0]] + [move(cut[step], QUAD * step) for step in range(1, groups)]
+    first = move(own[1], 2)
+    own[2 % groups] = hold(own[2 % groups], made_flag, after=first)
+    across = [move(own[0], 2), first] + [move(piece, 2) for piece in own[2:]]
     beside = [move(piece, 1) for piece in own]
     diagonal = [move(piece, 1) for piece in across]
     pieces = [part for four in zip(own, beside, across, diagonal) for part in four]
     tables = [jnp.asarray(t) for t in dft_tables(total)]
-    return focus(place, jnp.asarray(turn_table(total)), tables, [*weights, *phases], pieces)
+    return focus(place, jnp.asarray(turn_table(total)), tables, made, pieces)
 
 
 def solution(mesh):

time: 57.6 us -> 47.3 us (0.82)
  Pallas kernels: 28.2 us -> 19.6 us
  waiting for transfers between devices: 8.46 us -> 6.05 us
  starting transfers between devices: 17 us -> 14.9 us
  local copies, waits for them, and re-layouts: 3.46 us -> 5.53 us
  other arithmetic: 0.07 us -> 0.74 us
    pallas_call x2 -> x1, Pallas kernels: 12.1 us -> 5.79 us  [body(): pl.pallas_call(functools.partial(table_kernel, pulse_count, total), out_s...]
    ppermute x18 -> x17, waiting for transfers between devices: 8.46 us -> 6.05 us  [move(): return lax.ppermute(value, 'ap', [(i, i ^ bits) for i in range(count)])]
    ppermute x18 -> x17, starting transfers between devices: 17 us -> 14.9 us  [move(): return lax.ppermute(value, 'ap', [(i, i ^ bits) for i in range(count)])]
    pallas_call x1, Pallas kernels: 14.1 us -> 12.5 us  [focus(): pl.pallas_call(functools.partial(kernel, count, total), out_shape=jax.Sha...]
    unnamed x22 -> x20, local copies, waits for them, and re-layouts: 3.33 us -> 4.64 us
    reshape x1, local copies, waits for them, and re-layouts: 0.13 us -> 0.89 us  [body(): range_filter.reshape(2, second, FIRST)]
    another operation x0 -> x1, other arithmetic: none -> 0.66 us  [body(): near = jnp.stack([range_offsets, move(range_offsets, 1)])]
    pallas_call x2 -> x1, Pallas kernels: 1.28 us -> 0.64 us  [hold(): pl.pallas_call(hold_kernel, out_shape=jax.ShapeDtypeStruct(value.shape, v...]
  transfers between devices with their start and end apart: 18 -> 17, of which waited for: 4 -> 3; matrix products, arithmetic and copies ran while one was open for 0% -> 3% of each run, Pallas kernels for 23% -> 14%
where the time goes in v6:
time: 47.3 us; the launch traced here: 47 us
  Pallas kernels  19.6 us (41%)
  starting transfers between devices  14.9 us (32%)
  waiting for transfers between devices  6.05 us (13%)
  local copies, waits for them, and re-layouts  5.53 us (12%)
  other arithmetic  0.74 us (2%)
    ppermute x17, starting transfers between devices, move(): return lax.ppermute(value, 'ap', [(i, i ^ bits) for i in range(count)])  14.9 us
    pallas_call x1, Pallas kernels, focus(): pl.pallas_call(functools.partial(kernel, count, total), out_shape=jax.Sha...  12.5 us
    ppermute x17, waiting for transfers between devices, move(): return lax.ppermute(value, 'ap', [(i, i ^ bits) for i in range(count)])  6.05 us
    pallas_call x1, Pallas kernels, body(): pl.pallas_call(functools.partial(table_kernel, pulse_count, total), out_s...  5.79 us
    unnamed x20, local copies, waits for them, and re-layouts  4.64 us
  transfers between devices with their start and end apart: 17, of which 3 were waited for; matrix products, arithmetic and copies ran while one was open for 3% of the time, Pallas kernels for 14%

profile of v6, /device:TPU:0, one launch (start us, length us, event | category | flops | bytes accessed | tf_op | source)
XLA Modules:
  0.0 47.0 jit_solution(10735121805956860603)
XLA Ops:
  0.0 0.1 pad_add_fusion.1.place_ref
  0.1 0.0 copy-start.3
  0.1 1.0 %copy-done.3 = bf16[2,256,512]{2,1,0:T(8,128)(2,1)S(1)} copy-done((bf16[2,256,512]{2,1,0:T(8,128)(2,1)S(1)}, bf16[2,256,512]{2,1,0:T(8,128)(2,1)}, u32[]{:S(2)}) %copy-start.3) | copy-done | bytes 524312
  1.1 0.6 %shard_map.110 = (bf16[2,256,128]{2,1,0:T(8,128)(2,1)S(1)}, bf16[2,256,128]{2,1,0:T(8,128)(2,1)S(1)}, bf16[2,256,128]{2,1,0:T(8,128)(2,1)S(1)}, bf16[2,256,128]{2,1,0:T(8,128)(2,1)S(1)}) custom-call(s32[2]{0:T(128)S(1)} %pad_add_fusion.1.place_ref, bf16[2,256,512]{2,1,0:T(8,128)(2,1)S(1)} %copy-done.3), custom_call_target="tpu_custom_call" | custom-call | tf_op jit(solution)/shard_map/pallas_call | solution.py:460
  1.8 3.1 %collective-permute-start.5 = (bf16[2,256,128]{2,1,0:T(8,128)(2,1)S(1)}, bf16[2,256,128]{2,1,0:T(8,128)(2,1)S(1)}, u32[]{:S(2)}, u32[]{:S(2)}) collective-permute-start(bf16[2,256,128]{2,1,0:T(8,128)(2,1)S(1)} %get-tuple-element.21), channel_id=1, source_target_pairs={{0,4},{1,5},{2,6},{3,7},{4,0},{5,1},{6,2},{7,3},{8,12},{9,13},{10,... | collective-permute-start | bytes 393224 | tf_op jit(solution)/shard_map/ppermute | solution.py:449
  4.9 0.0 collective-permute-start
  4.9 1.5 %collective-permute-start.3 = (bf16[2,256,128]{2,1,0:T(8,128)(2,1)S(1)}, bf16[2,256,128]{2,1,0:T(8,128)(2,1)S(1)}, u32[]{:S(2)}, u32[]{:S(2)}) collective-permute-start(bf16[2,256,128]{2,1,0:T(8,128)(2,1)S(1)} %get-tuple-element.20.rest_9_), channel_id=1, source_target_pairs={{0,2},{1,3},{2,0},{3,1},{4,6},{5,7},{6,4},{7,5},{8,10},{9,11},{10,... | collective-permute-start | bytes 393224 | tf_op jit(solution)/shard_map/ppermute | solution.py:449
  6.4 0.0 collective-permute-done
  6.4 0.7 %pad_add_fusion = s32[2,32]{1,0:T(2,128)S(1)} fusion(s32[1,32]{1,0:T(1,128)S(1)} %bitcast.6, s32[1,32]{1,0:T(1,128)} %bitcast.4), kind=kLoop, calls=%fused_computation | loop fusion | flops 64 | bytes 512 | tf_op jit(solution)/shard_map/stack | solution.py:467
  7.0 1.2 %collective-permute-start.1 = (s32[2,32]{1,0:T(2,128)S(1)}, s32[2,32]{1,0:T(2,128)S(1)}, u32[]{:S(2)}, u32[]{:S(2)}) collective-permute-start(s32[2,32]{1,0:T(2,128)S(1)} %pad_add_fusion), channel_id=1, source_target_pairs={{0,2},{1,3},{2,0},{3,1},{4,6},{5,7},{6,4},{7,5},{8,10},{9,11},{10,... | collective-permute-start | bytes 776 | tf_op jit(solution)/shard_map/ppermute | solution.py:449
  8.3 0.0 collective-permute-start.2
  8.3 2.6 %collective-permute-start.9 = (bf16[2,256,128]{2,1,0:T(8,128)(2,1)S(1)}, bf16[2,256,128]{2,1,0:T(8,128)(2,1)S(1)}, u32[]{:S(2)}, u32[]{:S(2)}) collective-permute-start(bf16[2,256,128]{2,1,0:T(8,128)(2,1)S(1)} %get-tuple-element.22), channel_id=1, source_target_pairs={{0,8},{1,9},{2,10},{3,11},{4,12},{5,13},{6,14},{7,15},{8,0},{9,1},... | collective-permute-start | bytes 393224 | tf_op jit(solution)/shard_map/ppermute | solution.py:449
  10.9 0.9 %reshape.3.refs_4_ = f32[2,256,16]{2,1,0:T(8,128)S(1)} reshape(f32[2,4096]{1,0:T(2,128)} %param.12) | data formatting | bytes 65536 | tf_op jit(solution)/shard_map/reshape | solution.py:491
  11.8 0.0 collective-permute-done.1
  11.8 1.5 %collective-permute-start.13 = (bf16[2,256,128]{2,1,0:T(8,128)(2,1)S(1)}, bf16[2,256,128]{2,1,0:T(8,128)(2,1)S(1)}, u32[]{:S(2)}, u32[]{:S(2)}) collective-permute-start(bf16[2,256,128]{2,1,0:T(8,128)(2,1)S(1)} %get-tuple-element.24), channel_id=1, source_target_pairs={{0,12},{1,13},{2,14},{3,15},{4,8},{5,9},{6,10},{7,11},{8,4},{9,5},... | collective-permute-start | bytes 393224 | tf_op jit(solution)/shard_map/ppermute | solution.py:449
  13.3 0.0 collective-permute-done.5.rest_13_
  13.3 1.5 %collective-permute-start.7 = (bf16[2,256,128]{2,1,0:T(8,128)(2,1)S(1)}, bf16[2,256,128]{2,1,0:T(8,128)(2,1)S(1)}, u32[]{:S(2)}, u32[]{:S(2)}) collective-permute-start(bf16[2,256,128]{2,1,0:T(8,128)(2,1)S(1)} %collective-permute-done.5.rest_13_), channel_id=1, source_target_pairs={{0,2},{1,3},{2,0},{3,1},{4,6},{5,7},{6,4},{7,5},{8,10},{9,11},{10,... | collective-permute-start | bytes 393224 | tf_op jit(solution)/shard_map/ppermute | solution.py:449
  14.8 0.0 copy-start.6
  14.8 0.7 %copy-done.6 = s32[32]{0:T(128)S(1)} copy-done((s32[32]{0:T(128)S(1)}, s32[32]{0:T(128)}, u32[]{:S(2)}) %copy-start.6) | copy-done | bytes 152
  15.5 0.0 copy-start.7
  15.5 1.0 %copy-done.7 = bf16[2,2,2,256,128]{4,3,2,1,0:T(8,128)(2,1)S(1)} copy-done((bf16[2,2,2,256,128]{4,3,2,1,0:T(8,128)(2,1)S(1)}, bf16[2,2,2,256,128]{4,3,2,1,0:T(8,128)(2,1)}, u32[]{:S(2)}) %copy-start.7) | copy-done | bytes 524312
  16.5 0.0 copy-start.8
  16.5 0.7 %copy-done.8 = f32[2]{0:T(128)S(1)} copy-done((f32[2]{0:T(128)S(1)}, f32[2]{0:T(128)}, u32[]{:S(2)}) %copy-start.8) | copy-done | bytes 32
  17.2 0.0 copy-start.9
  17.2 1.2 %copy-done.9 = bf16[512,1024]{1,0:T(8,128)(2,1)S(1)} copy-done((bf16[512,1024]{1,0:T(8,128)(2,1)S(1)}, bf16[512,1024]{1,0:T(8,128)(2,1)}, u32[]{:S(2)}) %copy-start.9) | copy-done | bytes 1048600
  18.4 0.0 copy-start
  18.4 0.0 copy-start.1
  18.4 0.0 copy-start.2
  18.4 0.0 copy-start.4
  18.4 0.0 copy-start.5
  18.4 5.8 %shard_map.109 = (bf16[2,16,256,128]{3,2,1,0:T(8,128)(2,1)S(1)}, bf16[4,1024,256]{2,1,0:T(8,128)(2,1)S(1)}, bf16[2,512,256]{2,1,0:T(8,128)(2,1)S(1)}, bf16[2,8,5...) custom-call(s32[2]{0:T(128)S(1)} %pad_add_fusion.1.place_ref, f32[2]{0:T(128)S(1)} %copy-done.8, ...), custom_call_target="tpu_custom_call" | custom-call | flops 1073741824 | bytes 8388608 | tf_op jit(solution)/shard_map/pallas_call | solution.py:473
  24.2 0.0 collective-permute-done.9.refs_0_
  24.2 0.1 collective-permute-start.6
  24.3 0.0 collective-permute-done.13.rest_21_
  24.3 0.6 %collective-permute-start.15 = (bf16[2,256,128]{2,1,0:T(8,128)(2,1)S(1)}, bf16[2,256,128]{2,1,0:T(8,128)(2,1)S(1)}, u32[]{:S(2)}, u32[]{:S(2)}) collective-permute-start(bf16[2,256,128]{2,1,0:T(8,128)(2,1)S(1)} %collective-permute-done.13.rest_21_), channel_id=1, source_target_pairs={{0,2},{1,3},{2,0},{3,1},{4,6},{5,7},{6,4},{7,5},{8,10},{9,11},{10,... | collective-permute-start | bytes 393224 | tf_op jit(solution)/shard_map/ppermute | solution.py:449
  24.9 0.0 collective-permute-done.7.refs_2_.rest_15_
  24.9 0.2 collective-permute-start.14
  25.1 0.6 %shard_map.111.rest_17_ = bf16[2,256,128]{2,1,0:T(8,128)(2,1)S(1)} custom-call(bf16[2,256,128]{2,1,0:T(8,128)(2,1)S(1)} %collective-permute-done.9.refs_0_, s32[1]{0:T(128)} %get-tuple-element.23.refs_1_, bf16[2,256,128]{2,1,0:T(8,128)(2,1)S(1)} %collective-permute-done.7.refs_2_.rest_15_), custom_call_target="tpu_custom_call", output_to_operand_aliasing={{}: (0, {})} | custom-call | flops 1 | bytes 1 | tf_op jit(solution)/shard_map/pallas_call | solution.py:393
  25.7 0.0 collective-permute-done.3.rest_11_
  25.7 1.6 %collective-permute-start.11 = (bf16[2,256,128]{2,1,0:T(8,128)(2,1)S(1)}, bf16[2,256,128]{2,1,0:T(8,128)(2,1)S(1)}, u32[]{:S(2)}, u32[]{:S(2)}) collective-permute-start(bf16[2,256,128]{2,1,0:T(8,128)(2,1)S(1)} %shard_map.111.rest_17_), channel_id=1, source_target_pairs={{0,2},{1,3},{2,0},{3,1},{4,6},{5,7},{6,4},{7,5},{8,10},{9,11},{10,... | collective-permute-start | bytes 393224 | tf_op jit(solution)/shard_map/ppermute | solution.py:449
  27.3 0.0 collective-permute-done.2.rest_10_
  27.3 0.1 collective-permute-start.4
  27.4 0.0 collective-permute-done.6.rest_14_
  27.4 0.4 collective-permute-start.10
  27.8 2.9 %collective-permute-done.15.rest_23_ = bf16[2,256,128]{2,1,0:T(8,128)(2,1)S(1)} collective-permute-done((bf16[2,256,128]{2,1,0:T(8,128)(2,1)S(1)}, bf16[2,256,128]{2,1,0:T(8,128)(2,1)S(1)}, u32[]{:S(2)}, u32[]{:S(2)}) %collective-permute-start.15) | collective-permute-done | bytes 131104 | tf_op jit(solution)/shard_map/ppermute | solution.py:449
  30.7 0.0 collective-permute-start.8
  30.7 0.0 collective-permute-done.14.rest_22_
  30.7 0.5 %collective-permute-start.16 = (bf16[2,256,128]{2,1,0:T(8,128)(2,1)S(1)}, bf16[2,256,128]{2,1,0:T(8,128)(2,1)S(1)}, u32[]{:S(2)}, u32[]{:S(2)}) collective-permute-start(bf16[2,256,128]{2,1,0:T(8,128)(2,1)S(1)} %collective-permute-done.15.rest_23_), channel_id=1, source_target_pairs={{0,1},{1,0},{2,3},{3,2},{4,5},{5,4},{6,7},{7,6},{8,9},{9,8},{10,11... | collective-permute-start | bytes 393224 | tf_op jit(solution)/shard_map/ppermute | solution.py:449
  31.2 1.8 %collective-permute-done.11.rest_19_ = bf16[2,256,128]{2,1,0:T(8,128)(2,1)S(1)} collective-permute-done((bf16[2,256,128]{2,1,0:T(8,128)(2,1)S(1)}, bf16[2,256,128]{2,1,0:T(8,128)(2,1)S(1)}, u32[]{:S(2)}, u32[]{:S(2)}) %collective-permute-start.11) | collective-permute-done | bytes 131104 | tf_op jit(solution)/shard_map/ppermute | solution.py:449
  33.0 0.0 collective-permute-start.12
  33.0 0.0 collective-permute-done.4.rest_12_
  33.0 0.0 collective-permute-done.8.rest_16_
  33.1 0.0 collective-permute-done.16.rest_24_
  33.1 0.0 collective-permute-done.10.rest_18_
  33.1 1.3 %collective-permute-done.12.rest_20_ = bf16[2,256,128]{2,1,0:T(8,128)(2,1)S(1)} collective-permute-done((bf16[2,256,128]{2,1,0:T(8,128)(2,1)S(1)}, bf16[2,256,128]{2,1,0:T(8,128)(2,1)S(1)}, u32[]{:S(2)}, u32[]{:S(2)}) %collective-permute-start.12) | collective-permute-done | bytes 131104 | tf_op jit(solution)/shard_map/ppermute | solution.py:449
  34.4 0.0 copy-done
  34.4 0.0 copy-done.1
  34.4 0.0 copy-done.2
  34.4 0.0 copy-done.4
  34.4 0.0 copy-done.5
  34.4 12.5 %shard_map.112 = f32[2,1024,1024]{2,1,0:T(8,128)} custom-call(s32[2]{0:T(128)S(1)} %pad_add_fusion.1.place_ref, f32[2,16,16]{2,1,0:T(8,128)S(1)} %copy-done.5, bf16[512,512]{1,0:T(8,128)(2,1)S(1)} %copy-done.2, bf16[512,512]{1,0:T(8,128)(2,1)S(1)} %copy-done.1, bf16[512,512]{1,0:T(8,128)(2,1)S(1)} %copy-done, bf16[128,512]{1,0:T(8,128)(2,1)S(1)} %copy-done.4, ...), custom_call_target="tpu_custom_call" | custom-call | tf_op jit(solution)/shard_map/pallas_call | solution.py:417
  (1 shorter events, 0.0 us)
Async XLA Ops:
  0.1 1.0 %copy-start.3 = (bf16[2,256,512]{2,1,0:T(8,128)(2,1)S(1)}, bf16[2,256,512]{2,1,0:T(8,128)(2,1)}, u32[]{:S(2)}) copy-start(bf16[2,256,512]{2,1,0:T(8,128)(2,1)} %raw_ref.1) | copy-start | bytes 1572868
  1.8 11.5 %collective-permute-start.5 = (bf16[2,256,128]{2,1,0:T(8,128)(2,1)S(1)}, bf16[2,256,128]{2,1,0:T(8,128)(2,1)S(1)}, u32[]{:S(2)}, u32[]{:S(2)}) collective-permute-start(bf16[2,256,128]{2,1,0:T(8,128)(2,1)S(1)} %get-tuple-element.21), channel_id=1, source_target_pairs={{0,4},{1,5},{2,6},{3,7},{4,0},{5,1},{6,2},{7,3},{8,12},{9,13},{10,... | collective-permute-start | bytes 393224 | tf_op jit(solution)/shard_map/ppermute | solution.py:449
  4.9 1.5 %collective-permute-start = (s32[32]{0:T(128)}, s32[32]{0:T(128)S(1)}, u32[]{:S(2)}, u32[]{:S(2)}) collective-permute-start(s32[32]{0:T(128)} %param.13), channel_id=1, source_target_pairs={{0,1},{1,0},{2,3},{3,2},{4,5},{5,4},{6,7},{7,6},{8,9},{9,8},{10,11... | collective-permute-start | bytes 392 | tf_op jit(solution)/shard_map/ppermute | solution.py:449
  4.9 20.9 %collective-permute-start.3 = (bf16[2,256,128]{2,1,0:T(8,128)(2,1)S(1)}, bf16[2,256,128]{2,1,0:T(8,128)(2,1)S(1)}, u32[]{:S(2)}, u32[]{:S(2)}) collective-permute-start(bf16[2,256,128]{2,1,0:T(8,128)(2,1)S(1)} %get-tuple-element.20.rest_9_), channel_id=1, source_target_pairs={{0,2},{1,3},{2,0},{3,1},{4,6},{5,7},{6,4},{7,5},{8,10},{9,11},{10,... | collective-permute-start | bytes 393224 | tf_op jit(solution)/shard_map/ppermute | solution.py:449
  7.0 4.7 %collective-permute-start.1 = (s32[2,32]{1,0:T(2,128)S(1)}, s32[2,32]{1,0:T(2,128)S(1)}, u32[]{:S(2)}, u32[]{:S(2)}) collective-permute-start(s32[2,32]{1,0:T(2,128)S(1)} %pad_add_fusion), channel_id=1, source_target_pairs={{0,2},{1,3},{2,0},{3,1},{4,6},{5,7},{6,4},{7,5},{8,10},{9,11},{10,... | collective-permute-start | bytes 776 | tf_op jit(solution)/shard_map/ppermute | solution.py:449
  8.3 19.0 %collective-permute-start.2 = (bf16[2,256,128]{2,1,0:T(8,128)(2,1)S(1)}, bf16[2,256,128]{2,1,0:T(8,128)(2,1)S(1)}, u32[]{:S(2)}, u32[]{:S(2)}) collective-permute-start(bf16[2,256,128]{2,1,0:T(8,128)(2,1)S(1)} %get-tuple-element.20.rest_9_), channel_id=1, source_target_pairs={{0,1},{1,0},{2,3},{3,2},{4,5},{5,4},{6,7},{7,6},{8,9},{9,8},{10,11... | collective-permute-start | bytes 393224 | tf_op jit(solution)/shard_map/ppermute | solution.py:449
  8.3 15.9 %collective-permute-start.9 = (bf16[2,256,128]{2,1,0:T(8,128)(2,1)S(1)}, bf16[2,256,128]{2,1,0:T(8,128)(2,1)S(1)}, u32[]{:S(2)}, u32[]{:S(2)}) collective-permute-start(bf16[2,256,128]{2,1,0:T(8,128)(2,1)S(1)} %get-tuple-element.22), channel_id=1, source_target_pairs={{0,8},{1,9},{2,10},{3,11},{4,12},{5,13},{6,14},{7,15},{8,0},{9,1},... | collective-permute-start | bytes 393224 | tf_op jit(solution)/shard_map/ppermute | solution.py:449
  11.8 12.5 %collective-permute-start.13 = (bf16[2,256,128]{2,1,0:T(8,128)(2,1)S(1)}, bf16[2,256,128]{2,1,0:T(8,128)(2,1)S(1)}, u32[]{:S(2)}, u32[]{:S(2)}) collective-permute-start(bf16[2,256,128]{2,1,0:T(8,128)(2,1)S(1)} %get-tuple-element.24), channel_id=1, source_target_pairs={{0,12},{1,13},{2,14},{3,15},{4,8},{5,9},{6,10},{7,11},{8,4},{9,5},... | collective-permute-start | bytes 393224 | tf_op jit(solution)/shard_map/ppermute | solution.py:449
  13.3 11.6 %collective-permute-start.7 = (bf16[2,256,128]{2,1,0:T(8,128)(2,1)S(1)}, bf16[2,256,128]{2,1,0:T(8,128)(2,1)S(1)}, u32[]{:S(2)}, u32[]{:S(2)}) collective-permute-start(bf16[2,256,128]{2,1,0:T(8,128)(2,1)S(1)} %collective-permute-done.5.rest_13_), channel_id=1, source_target_pairs={{0,2},{1,3},{2,0},{3,1},{4,6},{5,7},{6,4},{7,5},{8,10},{9,11},{10,... | collective-permute-start | bytes 393224 | tf_op jit(solution)/shard_map/ppermute | solution.py:449
  14.8 0.7 %copy-start.6 = (s32[32]{0:T(128)S(1)}, s32[32]{0:T(128)}, u32[]{:S(2)}) copy-start(s32[32]{0:T(128)} %param.13) | copy-start | bytes 388
  15.5 1.0 %copy-start.7 = (bf16[2,2,2,256,128]{4,3,2,1,0:T(8,128)(2,1)S(1)}, bf16[2,2,2,256,128]{4,3,2,1,0:T(8,128)(2,1)}, u32[]{:S(2)}) copy-start(bf16[2,2,2,256,128]{4,3,2,1,0:T(8,128)(2,1)} %refs_5_.1) | copy-start | bytes 1572868
  16.5 0.7 %copy-start.8 = (f32[2]{0:T(128)S(1)}, f32[2]{0:T(128)}, u32[]{:S(2)}) copy-start(f32[2]{0:T(128)} %rate_ref.1) | copy-start | bytes 28
  17.2 1.2 %copy-start.9 = (bf16[512,1024]{1,0:T(8,128)(2,1)S(1)}, bf16[512,1024]{1,0:T(8,128)(2,1)}, u32[]{:S(2)}) copy-start(bf16[512,1024]{1,0:T(8,128)(2,1)} %constant.42.clone.refs_6_) | copy-start | bytes 3145732
  18.4 16.0 %copy-start = (bf16[512,512]{1,0:T(8,128)(2,1)S(1)}, bf16[512,512]{1,0:T(8,128)(2,1)}, u32[]{:S(2)}) copy-start(bf16[512,512]{1,0:T(8,128)(2,1)} %constant.45.clone.rest_2_) | copy-start | bytes 1572868
  18.4 16.0 %copy-start.1 = (bf16[512,512]{1,0:T(8,128)(2,1)S(1)}, bf16[512,512]{1,0:T(8,128)(2,1)}, u32[]{:S(2)}) copy-start(bf16[512,512]{1,0:T(8,128)(2,1)} %constant.44.clone.rest_1_) | copy-start | bytes 1572868
  18.4 16.0 %copy-start.2 = (bf16[512,512]{1,0:T(8,128)(2,1)S(1)}, bf16[512,512]{1,0:T(8,128)(2,1)}, u32[]{:S(2)}) copy-start(bf16[512,512]{1,0:T(8,128)(2,1)} %constant.43.clone.rest_0_) | copy-start | bytes 1572868
  18.4 16.0 %copy-start.4 = (bf16[128,512]{1,0:T(8,128)(2,1)S(1)}, bf16[128,512]{1,0:T(8,128)(2,1)}, u32[]{:S(2)}) copy-start(bf16[128,512]{1,0:T(8,128)(2,1)} %constant.46.clone.rest_3_) | copy-start | bytes 393220
  18.4 16.0 %copy-start.5 = (f32[2,16,16]{2,1,0:T(8,128)S(1)}, f32[2,16,16]{2,1,0:T(8,128)}, u32[]{:S(2)}) copy-start(f32[2,16,16]{2,1,0:T(8,128)} %constant.47.clone.turn_ref) | copy-start | bytes 6148
  24.2 3.2 %collective-permute-start.6 = (bf16[2,256,128]{2,1,0:T(8,128)(2,1)S(1)}, bf16[2,256,128]{2,1,0:T(8,128)(2,1)S(1)}, u32[]{:S(2)}, u32[]{:S(2)}) collective-permute-start(bf16[2,256,128]{2,1,0:T(8,128)(2,1)S(1)} %collective-permute-done.5.rest_13_), channel_id=1, source_target_pairs={{0,1},{1,0},{2,3},{3,2},{4,5},{5,4},{6,7},{7,6},{8,9},{9,8},{10,11... | collective-permute-start | bytes 393224 | tf_op jit(solution)/shard_map/ppermute | solution.py:449
  24.3 6.4 %collective-permute-start.15 = (bf16[2,256,128]{2,1,0:T(8,128)(2,1)S(1)}, bf16[2,256,128]{2,1,0:T(8,128)(2,1)S(1)}, u32[]{:S(2)}, u32[]{:S(2)}) collective-permute-start(bf16[2,256,128]{2,1,0:T(8,128)(2,1)S(1)} %collective-permute-done.13.rest_21_), channel_id=1, source_target_pairs={{0,2},{1,3},{2,0},{3,1},{4,6},{5,7},{6,4},{7,5},{8,10},{9,11},{10,... | collective-permute-start | bytes 393224 | tf_op jit(solution)/shard_map/ppermute | solution.py:449
  24.9 5.8 %collective-permute-start.14 = (bf16[2,256,128]{2,1,0:T(8,128)(2,1)S(1)}, bf16[2,256,128]{2,1,0:T(8,128)(2,1)S(1)}, u32[]{:S(2)}, u32[]{:S(2)}) collective-permute-start(bf16[2,256,128]{2,1,0:T(8,128)(2,1)S(1)} %collective-permute-done.13.rest_21_), channel_id=1, source_target_pairs={{0,1},{1,0},{2,3},{3,2},{4,5},{5,4},{6,7},{7,6},{8,9},{9,8},{10,11... | collective-permute-start | bytes 393224 | tf_op jit(solution)/shard_map/ppermute | solution.py:449
  25.7 7.3 %collective-permute-start.11 = (bf16[2,256,128]{2,1,0:T(8,128)(2,1)S(1)}, bf16[2,256,128]{2,1,0:T(8,128)(2,1)S(1)}, u32[]{:S(2)}, u32[]{:S(2)}) collective-permute-start(bf16[2,256,128]{2,1,0:T(8,128)(2,1)S(1)} %shard_map.111.rest_17_), channel_id=1, source_target_pairs={{0,2},{1,3},{2,0},{3,1},{4,6},{5,7},{6,4},{7,5},{8,10},{9,11},{10,... | collective-permute-start | bytes 393224 | tf_op jit(solution)/shard_map/ppermute | solution.py:449
  27.3 5.7 %collective-permute-start.4 = (bf16[2,256,128]{2,1,0:T(8,128)(2,1)S(1)}, bf16[2,256,128]{2,1,0:T(8,128)(2,1)S(1)}, u32[]{:S(2)}, u32[]{:S(2)}) collective-permute-start(bf16[2,256,128]{2,1,0:T(8,128)(2,1)S(1)} %collective-permute-done.3.rest_11_), channel_id=1, source_target_pairs={{0,1},{1,0},{2,3},{3,2},{4,5},{5,4},{6,7},{7,6},{8,9},{9,8},{10,11... | collective-permute-start | bytes 393224 | tf_op jit(solution)/shard_map/ppermute | solution.py:449
  27.4 5.7 %collective-permute-start.10 = (bf16[2,256,128]{2,1,0:T(8,128)(2,1)S(1)}, bf16[2,256,128]{2,1,0:T(8,128)(2,1)S(1)}, u32[]{:S(2)}, u32[]{:S(2)}) collective-permute-start(bf16[2,256,128]{2,1,0:T(8,128)(2,1)S(1)} %shard_map.111.rest_17_), channel_id=1, source_target_pairs={{0,1},{1,0},{2,3},{3,2},{4,5},{5,4},{6,7},{7,6},{8,9},{9,8},{10,11... | collective-permute-start | bytes 393224 | tf_op jit(solution)/shard_map/ppermute | solution.py:449
  30.7 2.4 %collective-permute-start.8 = (bf16[2,256,128]{2,1,0:T(8,128)(2,1)S(1)}, bf16[2,256,128]{2,1,0:T(8,128)(2,1)S(1)}, u32[]{:S(2)}, u32[]{:S(2)}) collective-permute-start(bf16[2,256,128]{2,1,0:T(8,128)(2,1)S(1)} %collective-permute-done.7.refs_2_.rest_15_), channel_id=1, source_target_pairs={{0,1},{1,0},{2,3},{3,2},{4,5},{5,4},{6,7},{7,6},{8,9},{9,8},{10,11... | collective-permute-start | bytes 393224 | tf_op jit(solution)/shard_map/ppermute | solution.py:449
  30.7 2.4 %collective-permute-start.16 = (bf16[2,256,128]{2,1,0:T(8,128)(2,1)S(1)}, bf16[2,256,128]{2,1,0:T(8,128)(2,1)S(1)}, u32[]{:S(2)}, u32[]{:S(2)}) collective-permute-start(bf16[2,256,128]{2,1,0:T(8,128)(2,1)S(1)} %collective-permute-done.15.rest_23_), channel_id=1, source_target_pairs={{0,1},{1,0},{2,3},{3,2},{4,5},{5,4},{6,7},{7,6},{8,9},{9,8},{10,11... | collective-permute-start | bytes 393224 | tf_op jit(solution)/shard_map/ppermute | solution.py:449
  33.0 1.3 %collective-permute-start.12 = (bf16[2,256,128]{2,1,0:T(8,128)(2,1)S(1)}, bf16[2,256,128]{2,1,0:T(8,128)(2,1)S(1)}, u32[]{:S(2)}, u32[]{:S(2)}) collective-permute-start(bf16[2,256,128]{2,1,0:T(8,128)(2,1)S(1)} %collective-permute-done.11.rest_19_), channel_id=1, source_target_pairs={{0,1},{1,0},{2,3},{3,2},{4,5},{5,4},{6,7},{7,6},{8,9},{9,8},{10,11... | collective-permute-start | bytes 393224 | tf_op jit(solution)/shard_map/ppermute | solution.py:449

commit v7 on v6

--- a/solution.py
+++ b/solution.py
@@ -176,8 +176,8 @@
 
 
 def table_kernel(pulse_count, total, place_ref, rate_ref, *refs):
-    offset_refs, filter_ref, weight_ref, steer_ref = refs[:QUAD], *refs[QUAD : QUAD + 3]
-    gain_ref, one_ref, two_ref, phase_one_ref, phase_two_ref, done_ref = refs[QUAD + 3 :]
+    offset_refs, filter_ref, weight_ref, steer_ref = refs[:2], *refs[2:5]
+    gain_ref, one_ref, two_ref, phase_one_ref, phase_two_ref, done_ref = refs[5:]
     start = (place_ref[1] * (total // QUAD)).astype(jnp.float32)
     done_ref[0] = 1
     phase_rows(phase_one_ref, rate_ref[0], start, total)
@@ -190,10 +190,11 @@
     second = total // FIRST
     member = place_ref[1]
     offsets = []
+    known = [offset_refs[rel // 2][rel % 2 : rel % 2 + 1, :] for rel in range(QUAD)]
     for owner in range(QUAD):
-        value = offset_refs[0][...]
+        value = known[0]
         for rel in range(1, QUAD):
-            value = jnp.where((member ^ rel) == owner, offset_refs[rel][...], value)
+            value = jnp.where((member ^ rel) == owner, known[rel], value)
         offsets.append(value)
     offsets = jnp.concatenate(offsets, 1)
     shift = offsets - place_ref[1] * (total // QUAD)
@@ -236,10 +237,15 @@
 
     index = place_ref[0] * QUAD + place_ref[1]
     per_row = second // span
-    for number, piece in enumerate(pieces):
-        source = index ^ number
+    order = ((step, rel) for step in (0, 1) for rel in range(QUAD))
+    order = sorted(order, key=lambda spot: spot[1])
+    order += [(step, rel) for step in range(2, count // QUAD) for rel in range(QUAD)]
+    loaded = [piece[spot] for piece in pieces[:QUAD] for spot in range(2)]
+    loaded += [piece[...] for piece in pieces[QUAD:]]
+    for (step, rel), piece in zip(order, loaded):
+        source = index ^ (QUAD * step + rel)
         rows = pl.ds(pl.multiple_of(source % per_row * span, TILE), span)
-        samples[:, source // per_row, rows] = piece[...]
+        samples[:, source // per_row, rows] = piece
 
     @pl.loop(0, chunks // 2, unroll=True)
     def _(pair):
@@ -383,6 +389,23 @@
         out_copy(step, step % 2).wait()
 
 
+def pack_kernel(*refs):
+    for spot in range(refs[-1].shape[0]):
+        refs[-1][spot] = refs[spot][...]
+
+
+def pack(pieces):
+    vmem = pl.BlockSpec(memory_space=pltpu.VMEM)
+    return pl.pallas_call(
+        pack_kernel,
+        out_shape=jax.ShapeDtypeStruct((len(pieces), *pieces[0].shape), pieces[0].dtype),
+        in_specs=[vmem] * len(pieces),
+        out_specs=vmem,
+        cost_estimate=pl.CostEstimate(flops=1, bytes_accessed=1, transcendentals=0),
+        compiler_params=pltpu.CompilerParams(vmem_limit_bytes=1024 * 1024),
+    )(*pieces)
+
+
 def hold_kernel(*refs):
     pass
 
@@ -403,7 +426,7 @@
 
 def focus(place, turns, tables, made, pieces):
     _, rows_one, rows_two, phase_one, _ = made
-    count = len(pieces)
+    count = len(pieces) + QUAD
     total = phase_one.shape[1] * phase_one.shape[3] * QUAD
     second = total // FIRST
     chunks = second // TILE
@@ -417,7 +440,7 @@
     return pl.pallas_call(
         functools.partial(kernel, count, total),
         out_shape=jax.ShapeDtypeStruct((2, angle_blocks * parents, total // QUAD), f32),
-        in_specs=[smem, smem] + [vmem] * (9 + count),
+        in_specs=[smem, smem] + [vmem] * (9 + len(pieces)),
         out_specs=far,
         scratch_shapes=[
             pltpu.VMEM((2, FIRST, second, LANES), bf16),
@@ -465,8 +488,7 @@
         compiler_params=small,
     )(place, raw_echo)
     near = jnp.stack([range_offsets, move(range_offsets, 1)])
-    joined = [near, move(near, 2)]
-    offsets = [joined[rel // 2][rel % 2 : rel % 2 + 1] for rel in range(QUAD)]
+    offsets = [near, move(near, 2)]
 
     child_angles = interp_weight.shape[4]
     steer = jnp.asarray(steer_blocks(pulse_count, child_angles))
@@ -480,7 +502,7 @@
             shape((2, width // LANES, 4 * A0, LANES)),
             flag,
         ],
-        in_specs=[smem, smem] + [vmem] * (QUAD + 3),
+        in_specs=[smem, smem] + [vmem] * 5,
         out_specs=[vmem] * 5 + [smem],
         cost_estimate=cost(2**30, 2**23),
         compiler_params=small,
@@ -494,12 +516,15 @@
     )
 
     own = [cut[0]] + [move(cut[step], QUAD * step) for step in range(1, groups)]
-    first = move(own[1], 2)
-    own[2 % groups] = hold(own[2 % groups], made_flag, after=first)
-    across = [move(own[0], 2), first] + [move(piece, 2) for piece in own[2:]]
-    beside = [move(piece, 1) for piece in own]
+    sent = [pack(own[:2])]
+    across = [move(sent[0], 2)]
+    if groups > 2:
+        own[2] = hold(own[2], made_flag, after=across[0])
+    sent += own[2:]
+    across += [move(piece, 2) for piece in own[2:]]
+    beside = [move(piece, 1) for piece in sent]
     diagonal = [move(piece, 1) for piece in across]
-    pieces = [part for four in zip(own, beside, across, diagonal) for part in four]
+    pieces = [part for four in zip(sent, beside, across, diagonal) for part in four]
     tables = [jnp.asarray(t) for t in dft_tables(total)]
     return focus(place, jnp.asarray(turn_table(total)), tables, made, pieces)
 

time: 47.3 us -> 50 us (1.057)
  waiting for transfers between devices: 6.05 us -> 12.1 us
  starting transfers between devices: 14.9 us -> 12.3 us
  local copies, waits for them, and re-layouts: 5.53 us -> 4.89 us
    ppermute x17 -> x14, waiting for transfers between devices: 6.05 us -> 12.1 us  [move(): return lax.ppermute(value, 'ap', [(i, i ^ bits) for i in range(count)])]
    ppermute x17 -> x14, starting transfers between devices: 14.9 us -> 12.3 us  [move(): return lax.ppermute(value, 'ap', [(i, i ^ bits) for i in range(count)])]
    unnamed x20 -> x18, local copies, waits for them, and re-layouts: 4.64 us -> 4 us
  transfers between devices with their start and end apart: 17 -> 14, of which waited for: 3 -> 5; matrix products, arithmetic and copies ran while one was open for 3% -> 3% of each run, Pallas kernels for 14% -> 13%
where the time goes in v7:
time: 50 us; the launch traced here: 49.7 us
  Pallas kernels  19.6 us (39%)
  starting transfers between devices  12.3 us (25%)
  waiting for transfers between devices  12.1 us (24%)
  local copies, waits for them, and re-layouts  4.89 us (10%)
  other arithmetic  0.74 us (1%)
    pallas_call x1, Pallas kernels, focus(): pl.pallas_call(functools.partial(kernel, count, total), out_shape=jax.Sha...  12.5 us
    ppermute x14, starting transfers between devices, move(): return lax.ppermute(value, 'ap', [(i, i ^ bits) for i in range(count)])  12.3 us
    ppermute x14, waiting for transfers between devices, move(): return lax.ppermute(value, 'ap', [(i, i ^ bits) for i in range(count)])  12.1 us
    pallas_call x1, Pallas kernels, body(): pl.pallas_call(functools.partial(table_kernel, pulse_count, total), out_s...  5.73 us
    unnamed x18, local copies, waits for them, and re-layouts  4 us
  transfers between devices with their start and end apart: 14, of which 5 were waited for; matrix products, arithmetic and copies ran while one was open for 3% of the time, Pallas kernels for 13%

profile of v7, /device:TPU:0, one launch (start us, length us, event | category | flops | bytes accessed | tf_op | source)
XLA Modules:
  0.0 49.7 jit_solution(5862011239299250416)
XLA Ops:
  0.0 0.1 pad_add_fusion.1.place_ref
  0.1 0.0 copy-start.3
  0.1 1.0 %copy-done.3 = bf16[2,256,512]{2,1,0:T(8,128)(2,1)S(1)} copy-done((bf16[2,256,512]{2,1,0:T(8,128)(2,1)S(1)}, bf16[2,256,512]{2,1,0:T(8,128)(2,1)}, u32[]{:S(2)}) %copy-start.3) | copy-done | bytes 524312
  1.1 0.6 %shard_map.110 = (bf16[2,256,128]{2,1,0:T(8,128)(2,1)S(1)}, bf16[2,256,128]{2,1,0:T(8,128)(2,1)S(1)}, bf16[2,256,128]{2,1,0:T(8,128)(2,1)S(1)}, bf16[2,256,128]{2,1,0:T(8,128)(2,1)S(1)}) custom-call(s32[2]{0:T(128)S(1)} %pad_add_fusion.1.place_ref, bf16[2,256,512]{2,1,0:T(8,128)(2,1)S(1)} %copy-done.3), custom_call_target="tpu_custom_call" | custom-call | tf_op jit(solution)/shard_map/pallas_call | solution.py:483
  1.8 3.1 %collective-permute-start.2 = (bf16[2,256,128]{2,1,0:T(8,128)(2,1)S(1)}, bf16[2,256,128]{2,1,0:T(8,128)(2,1)S(1)}, u32[]{:S(2)}, u32[]{:S(2)}) collective-permute-start(bf16[2,256,128]{2,1,0:T(8,128)(2,1)S(1)} %get-tuple-element.21), channel_id=1, source_target_pairs={{0,4},{1,5},{2,6},{3,7},{4,0},{5,1},{6,2},{7,3},{8,12},{9,13},{10,... | collective-permute-start | bytes 393224 | tf_op jit(solution)/shard_map/ppermute | solution.py:472
  4.9 3.5 %collective-permute-done.2.refs_1_ = bf16[2,256,128]{2,1,0:T(8,128)(2,1)S(1)} collective-permute-done((bf16[2,256,128]{2,1,0:T(8,128)(2,1)S(1)}, bf16[2,256,128]{2,1,0:T(8,128)(2,1)S(1)}, u32[]{:S(2)}, u32[]{:S(2)}) %collective-permute-start.2) | collective-permute-done | bytes 131104 | tf_op jit(solution)/shard_map/ppermute | solution.py:472
  8.4 1.7 %collective-permute-start.4 = (bf16[2,2,256,128]{3,2,1,0:T(8,128)(2,1)S(1)}, bf16[2,2,256,128]{3,2,1,0:T(8,128)(2,1)S(1)}, u32[]{:S(2)}, u32[]{:S(2)}) collective-permute-start(bf16[2,2,256,128]{3,2,1,0:T(8,128)(2,1)S(1)} %shard_map.111.rest_9_), channel_id=1, source_target_pairs={{0,2},{1,3},{2,0},{3,1},{4,6},{5,7},{6,4},{7,5},{8,10},{9,11},{10,... | collective-permute-start | bytes 786440 | tf_op jit(solution)/shard_map/ppermute | solution.py:472
  10.1 0.0 collective-permute-start
  10.1 2.6 %collective-permute-start.6 = (bf16[2,256,128]{2,1,0:T(8,128)(2,1)S(1)}, bf16[2,256,128]{2,1,0:T(8,128)(2,1)S(1)}, u32[]{:S(2)}, u32[]{:S(2)}) collective-permute-start(bf16[2,256,128]{2,1,0:T(8,128)(2,1)S(1)} %get-tuple-element.22), channel_id=1, source_target_pairs={{0,8},{1,9},{2,10},{3,11},{4,12},{5,13},{6,14},{7,15},{8,0},{9,1},... | collective-permute-start | bytes 393224 | tf_op jit(solution)/shard_map/ppermute | solution.py:472
  12.7 1.3 %collective-permute-start.10 = (bf16[2,256,128]{2,1,0:T(8,128)(2,1)S(1)}, bf16[2,256,128]{2,1,0:T(8,128)(2,1)S(1)}, u32[]{:S(2)}, u32[]{:S(2)}) collective-permute-start(bf16[2,256,128]{2,1,0:T(8,128)(2,1)S(1)} %get-tuple-element.24), channel_id=1, source_target_pairs={{0,12},{1,13},{2,14},{3,15},{4,8},{5,9},{6,10},{7,11},{8,4},{9,5},... | collective-permute-start | bytes 393224 | tf_op jit(solution)/shard_map/ppermute | solution.py:472
  14.1 0.0 collective-permute-done
  14.1 0.7 %pad_add_fusion.refs_0_ = s32[2,32]{1,0:T(2,128)S(1)} fusion(s32[1,32]{1,0:T(1,128)S(1)} %bitcast.5, s32[1,32]{1,0:T(1,128)} %bitcast.4), kind=kLoop, calls=%fused_computation | loop fusion | flops 64 | bytes 512 | tf_op jit(solution)/shard_map/stack | solution.py:490
  14.7 0.5 %collective-permute-start.1 = (s32[2,32]{1,0:T(2,128)S(1)}, s32[2,32]{1,0:T(2,128)S(1)}, u32[]{:S(2)}, u32[]{:S(2)}) collective-permute-start(s32[2,32]{1,0:T(2,128)S(1)} %pad_add_fusion.refs_0_), channel_id=1, source_target_pairs={{0,2},{1,3},{2,0},{3,1},{4,6},{5,7},{6,4},{7,5},{8,10},{9,11},{10,... | collective-permute-start | bytes 776 | tf_op jit(solution)/shard_map/ppermute | solution.py:472
  15.2 0.9 %reshape.3.refs_2_ = f32[2,256,16]{2,1,0:T(8,128)S(1)} reshape(f32[2,4096]{1,0:T(2,128)} %param.12) | data formatting | bytes 65536 | tf_op jit(solution)/shard_map/reshape | solution.py:513
  16.1 0.0 copy-start
  16.1 0.0 copy-start.1
  16.2 0.0 copy-start.2
  16.2 0.0 copy-start.4
  16.2 0.0 copy-start.5
  16.2 2.1 %collective-permute-done.1.refs_1_ = s32[2,32]{1,0:T(2,128)S(1)} collective-permute-done((s32[2,32]{1,0:T(2,128)S(1)}, s32[2,32]{1,0:T(2,128)S(1)}, u32[]{:S(2)}, u32[]{:S(2)}) %collective-permute-start.1) | collective-permute-done | bytes 288 | tf_op jit(solution)/shard_map/ppermute | solution.py:472
  18.3 0.0 copy-start.6
  18.3 1.0 %copy-done.6 = bf16[2,2,2,256,128]{4,3,2,1,0:T(8,128)(2,1)S(1)} copy-done((bf16[2,2,2,256,128]{4,3,2,1,0:T(8,128)(2,1)S(1)}, bf16[2,2,2,256,128]{4,3,2,1,0:T(8,128)(2,1)}, u32[]{:S(2)}) %copy-start.6) | copy-done | bytes 524312
  19.3 0.0 copy-start.7
  19.3 0.7 %copy-done.7 = f32[2]{0:T(128)S(1)} copy-done((f32[2]{0:T(128)S(1)}, f32[2]{0:T(128)}, u32[]{:S(2)}) %copy-start.7) | copy-done | bytes 32
  20.0 0.0 copy-start.8
  20.0 1.2 %copy-done.8 = bf16[512,1024]{1,0:T(8,128)(2,1)S(1)} copy-done((bf16[512,1024]{1,0:T(8,128)(2,1)S(1)}, bf16[512,1024]{1,0:T(8,128)(2,1)}, u32[]{:S(2)}) %copy-start.8) | copy-done | bytes 1048600
  21.2 5.7 %shard_map.109 = (bf16[2,16,256,128]{3,2,1,0:T(8,128)(2,1)S(1)}, bf16[4,1024,256]{2,1,0:T(8,128)(2,1)S(1)}, bf16[2,512,256]{2,1,0:T(8,128)(2,1)S(1)}, bf16[2,8,5...) custom-call(s32[2]{0:T(128)S(1)} %pad_add_fusion.1.place_ref, f32[2]{0:T(128)S(1)} %copy-done.7, ...), custom_call_target="tpu_custom_call" | custom-call | flops 1073741824 | bytes 8388608 | tf_op jit(solution)/shard_map/pallas_call | solution.py:495
  27.0 0.1 collective-permute-start.3
  27.0 0.0 collective-permute-done.10.rest_17_
  27.1 0.6 %collective-permute-start.12 = (bf16[2,256,128]{2,1,0:T(8,128)(2,1)S(1)}, bf16[2,256,128]{2,1,0:T(8,128)(2,1)S(1)}, u32[]{:S(2)}, u32[]{:S(2)}) collective-permute-start(bf16[2,256,128]{2,1,0:T(8,128)(2,1)S(1)} %collective-permute-done.10.rest_17_), channel_id=1, source_target_pairs={{0,2},{1,3},{2,0},{3,1},{4,6},{5,7},{6,4},{7,5},{8,10},{9,11},{10,... | collective-permute-start | bytes 393224 | tf_op jit(solution)/shard_map/ppermute | solution.py:472
  27.6 0.2 collective-permute-start.11
  27.8 0.0 collective-permute-done.6.refs_0_
  27.8 0.0 collective-permute-done.4.refs_2_.rest_11_
  27.8 0.6 %shard_map.112.rest_13_ = bf16[2,256,128]{2,1,0:T(8,128)(2,1)S(1)} custom-call(bf16[2,256,128]{2,1,0:T(8,128)(2,1)S(1)} %collective-permute-done.6.refs_0_, s32[1]{0:T(128)} %get-tuple-element.23.refs_1_, bf16[2,2,256,128]{3,2,1,0:T(8,128)(2,1)S(1)} %collective-permute-done.4.refs_2_.rest_11_), custom_call_target="tpu_custom_call", output_to_operand_aliasing={{}: (0, {})} | custom-call | flops 1 | bytes 1 | tf_op jit(solution)/shard_map/pallas_call | solution.py:416
  28.4 1.6 %collective-permute-start.8 = (bf16[2,256,128]{2,1,0:T(8,128)(2,1)S(1)}, bf16[2,256,128]{2,1,0:T(8,128)(2,1)S(1)}, u32[]{:S(2)}, u32[]{:S(2)}) collective-permute-start(bf16[2,256,128]{2,1,0:T(8,128)(2,1)S(1)} %shard_map.112.rest_13_), channel_id=1, source_target_pairs={{0,2},{1,3},{2,0},{3,1},{4,6},{5,7},{6,4},{7,5},{8,10},{9,11},{10,... | collective-permute-start | bytes 393224 | tf_op jit(solution)/shard_map/ppermute | solution.py:472
  30.0 0.1 collective-permute-start.5
  30.1 3.3 %collective-permute-done.12.rest_19_ = bf16[2,256,128]{2,1,0:T(8,128)(2,1)S(1)} collective-permute-done((bf16[2,256,128]{2,1,0:T(8,128)(2,1)S(1)}, bf16[2,256,128]{2,1,0:T(8,128)(2,1)S(1)}, u32[]{:S(2)}, u32[]{:S(2)}) %collective-permute-start.12) | collective-permute-done | bytes 131104 | tf_op jit(solution)/shard_map/ppermute | solution.py:472
  33.4 0.0 collective-permute-start.13
  33.4 0.0 collective-permute-done.11.rest_18_
  33.4 0.5 %collective-permute-start.7 = (bf16[2,256,128]{2,1,0:T(8,128)(2,1)S(1)}, bf16[2,256,128]{2,1,0:T(8,128)(2,1)S(1)}, u32[]{:S(2)}, u32[]{:S(2)}) collective-permute-start(bf16[2,256,128]{2,1,0:T(8,128)(2,1)S(1)} %shard_map.112.rest_13_), channel_id=1, source_target_pairs={{0,1},{1,0},{2,3},{3,2},{4,5},{5,4},{6,7},{7,6},{8,9},{9,8},{10,11... | collective-permute-start | bytes 393224 | tf_op jit(solution)/shard_map/ppermute | solution.py:472
  33.9 1.8 %collective-permute-done.8.rest_15_ = bf16[2,256,128]{2,1,0:T(8,128)(2,1)S(1)} collective-permute-done((bf16[2,256,128]{2,1,0:T(8,128)(2,1)S(1)}, bf16[2,256,128]{2,1,0:T(8,128)(2,1)S(1)}, u32[]{:S(2)}, u32[]{:S(2)}) %collective-permute-start.8) | collective-permute-done | bytes 131104 | tf_op jit(solution)/shard_map/ppermute | solution.py:472
  35.8 0.0 collective-permute-start.9
  35.8 0.0 collective-permute-done.13.rest_20_
  35.8 0.0 collective-permute-done.3.rest_10_
  35.8 0.0 collective-permute-done.7.rest_14_
  35.8 0.0 collective-permute-done.5.rest_12_
  35.8 1.3 %collective-permute-done.9.rest_16_ = bf16[2,256,128]{2,1,0:T(8,128)(2,1)S(1)} collective-permute-done((bf16[2,256,128]{2,1,0:T(8,128)(2,1)S(1)}, bf16[2,256,128]{2,1,0:T(8,128)(2,1)S(1)}, u32[]{:S(2)}, u32[]{:S(2)}) %collective-permute-start.9) | collective-permute-done | bytes 131104 | tf_op jit(solution)/shard_map/ppermute | solution.py:472
  37.1 0.0 copy-done
  37.1 0.0 copy-done.1
  37.1 0.0 copy-done.2
  37.1 0.0 copy-done.4
  37.1 0.0 copy-done.5
  37.1 12.5 %shard_map.113 = f32[2,1024,1024]{2,1,0:T(8,128)} custom-call(s32[2]{0:T(128)S(1)} %pad_add_fusion.1.place_ref, f32[2,16,16]{2,1,0:T(8,128)S(1)} %copy-done.5, bf16[512,512]{1,0:T(8,128)(2,1)S(1)} %copy-done.2, bf16[512,512]{1,0:T(8,128)(2,1)S(1)} %copy-done.1, bf16[512,512]{1,0:T(8,128)(2,1)S(1)} %copy-done, bf16[128,512]{1,0:T(8,128)(2,1)S(1)} %copy-done.4, ...), custom_call_target="tpu_custom_call" | custom-call | tf_op jit(solution)/shard_map/pallas_call | solution.py:440
  (1 shorter events, 0.0 us)
Async XLA Ops:
  0.1 1.0 %copy-start.3 = (bf16[2,256,512]{2,1,0:T(8,128)(2,1)S(1)}, bf16[2,256,512]{2,1,0:T(8,128)(2,1)}, u32[]{:S(2)}) copy-start(bf16[2,256,512]{2,1,0:T(8,128)(2,1)} %raw_ref.1) | copy-start | bytes 1572868
  1.8 6.6 %collective-permute-start.2 = (bf16[2,256,128]{2,1,0:T(8,128)(2,1)S(1)}, bf16[2,256,128]{2,1,0:T(8,128)(2,1)S(1)}, u32[]{:S(2)}, u32[]{:S(2)}) collective-permute-start(bf16[2,256,128]{2,1,0:T(8,128)(2,1)S(1)} %get-tuple-element.21), channel_id=1, source_target_pairs={{0,4},{1,5},{2,6},{3,7},{4,0},{5,1},{6,2},{7,3},{8,12},{9,13},{10,... | collective-permute-start | bytes 393224 | tf_op jit(solution)/shard_map/ppermute | solution.py:472
  8.4 19.4 %collective-permute-start.4 = (bf16[2,2,256,128]{3,2,1,0:T(8,128)(2,1)S(1)}, bf16[2,2,256,128]{3,2,1,0:T(8,128)(2,1)S(1)}, u32[]{:S(2)}, u32[]{:S(2)}) collective-permute-start(bf16[2,2,256,128]{3,2,1,0:T(8,128)(2,1)S(1)} %shard_map.111.rest_9_), channel_id=1, source_target_pairs={{0,2},{1,3},{2,0},{3,1},{4,6},{5,7},{6,4},{7,5},{8,10},{9,11},{10,... | collective-permute-start | bytes 786440 | tf_op jit(solution)/shard_map/ppermute | solution.py:472
  10.1 3.9 %collective-permute-start = (s32[32]{0:T(128)}, s32[32]{0:T(128)S(1)}, u32[]{:S(2)}, u32[]{:S(2)}) collective-permute-start(s32[32]{0:T(128)} %param.13), channel_id=1, source_target_pairs={{0,1},{1,0},{2,3},{3,2},{4,5},{5,4},{6,7},{7,6},{8,9},{9,8},{10,11... | collective-permute-start | bytes 392 | tf_op jit(solution)/shard_map/ppermute | solution.py:472
  10.1 17.7 %collective-permute-start.6 = (bf16[2,256,128]{2,1,0:T(8,128)(2,1)S(1)}, bf16[2,256,128]{2,1,0:T(8,128)(2,1)S(1)}, u32[]{:S(2)}, u32[]{:S(2)}) collective-permute-start(bf16[2,256,128]{2,1,0:T(8,128)(2,1)S(1)} %get-tuple-element.22), channel_id=1, source_target_pairs={{0,8},{1,9},{2,10},{3,11},{4,12},{5,13},{6,14},{7,15},{8,0},{9,1},... | collective-permute-start | bytes 393224 | tf_op jit(solution)/shard_map/ppermute | solution.py:472
  12.7 14.3 %collective-permute-start.10 = (bf16[2,256,128]{2,1,0:T(8,128)(2,1)S(1)}, bf16[2,256,128]{2,1,0:T(8,128)(2,1)S(1)}, u32[]{:S(2)}, u32[]{:S(2)}) collective-permute-start(bf16[2,256,128]{2,1,0:T(8,128)(2,1)S(1)} %get-tuple-element.24), channel_id=1, source_target_pairs={{0,12},{1,13},{2,14},{3,15},{4,8},{5,9},{6,10},{7,11},{8,4},{9,5},... | collective-permute-start | bytes 393224 | tf_op jit(solution)/shard_map/ppermute | solution.py:472
  14.7 3.6 %collective-permute-start.1 = (s32[2,32]{1,0:T(2,128)S(1)}, s32[2,32]{1,0:T(2,128)S(1)}, u32[]{:S(2)}, u32[]{:S(2)}) collective-permute-start(s32[2,32]{1,0:T(2,128)S(1)} %pad_add_fusion.refs_0_), channel_id=1, source_target_pairs={{0,2},{1,3},{2,0},{3,1},{4,6},{5,7},{6,4},{7,5},{8,10},{9,11},{10,... | collective-permute-start | bytes 776 | tf_op jit(solution)/shard_map/ppermute | solution.py:472
  16.1 21.0 %copy-start = (bf16[512,512]{1,0:T(8,128)(2,1)S(1)}, bf16[512,512]{1,0:T(8,128)(2,1)}, u32[]{:S(2)}) copy-start(bf16[512,512]{1,0:T(8,128)(2,1)} %constant.45.clone.rest_2_) | copy-start | bytes 1572868
  16.1 21.0 %copy-start.1 = (bf16[512,512]{1,0:T(8,128)(2,1)S(1)}, bf16[512,512]{1,0:T(8,128)(2,1)}, u32[]{:S(2)}) copy-start(bf16[512,512]{1,0:T(8,128)(2,1)} %constant.44.clone.rest_1_) | copy-start | bytes 1572868
  16.2 21.0 %copy-start.2 = (bf16[512,512]{1,0:T(8,128)(2,1)S(1)}, bf16[512,512]{1,0:T(8,128)(2,1)}, u32[]{:S(2)}) copy-start(bf16[512,512]{1,0:T(8,128)(2,1)} %constant.43.clone.rest_0_) | copy-start | bytes 1572868
  16.2 21.0 %copy-start.4 = (bf16[128,512]{1,0:T(8,128)(2,1)S(1)}, bf16[128,512]{1,0:T(8,128)(2,1)}, u32[]{:S(2)}) copy-start(bf16[128,512]{1,0:T(8,128)(2,1)} %constant.46.clone.rest_3_) | copy-start | bytes 393220
  16.2 21.0 %copy-start.5 = (f32[2,16,16]{2,1,0:T(8,128)S(1)}, f32[2,16,16]{2,1,0:T(8,128)}, u32[]{:S(2)}) copy-start(f32[2,16,16]{2,1,0:T(8,128)} %constant.47.clone.turn_ref) | copy-start | bytes 6148
  18.3 1.0 %copy-start.6 = (bf16[2,2,2,256,128]{4,3,2,1,0:T(8,128)(2,1)S(1)}, bf16[2,2,2,256,128]{4,3,2,1,0:T(8,128)(2,1)}, u32[]{:S(2)}) copy-start(bf16[2,2,2,256,128]{4,3,2,1,0:T(8,128)(2,1)} %refs_3_.1) | copy-start | bytes 1572868
  19.3 0.7 %copy-start.7 = (f32[2]{0:T(128)S(1)}, f32[2]{0:T(128)}, u32[]{:S(2)}) copy-start(f32[2]{0:T(128)} %rate_ref.1) | copy-start | bytes 28
  20.0 1.2 %copy-start.8 = (bf16[512,1024]{1,0:T(8,128)(2,1)S(1)}, bf16[512,1024]{1,0:T(8,128)(2,1)}, u32[]{:S(2)}) copy-start(bf16[512,1024]{1,0:T(8,128)(2,1)} %constant.42.clone.refs_4_) | copy-start | bytes 3145732
  27.0 8.8 %collective-permute-start.3 = (bf16[2,2,256,128]{3,2,1,0:T(8,128)(2,1)S(1)}, bf16[2,2,256,128]{3,2,1,0:T(8,128)(2,1)S(1)}, u32[]{:S(2)}, u32[]{:S(2)}) collective-permute-start(bf16[2,2,256,128]{3,2,1,0:T(8,128)(2,1)S(1)} %shard_map.111.rest_9_), channel_id=1, source_target_pairs={{0,1},{1,0},{2,3},{3,2},{4,5},{5,4},{6,7},{7,6},{8,9},{9,8},{10,11... | collective-permute-start | bytes 786440 | tf_op jit(solution)/shard_map/ppermute | solution.py:472
  27.1 6.4 %collective-permute-start.12 = (bf16[2,256,128]{2,1,0:T(8,128)(2,1)S(1)}, bf16[2,256,128]{2,1,0:T(8,128)(2,1)S(1)}, u32[]{:S(2)}, u32[]{:S(2)}) collective-permute-start(bf16[2,256,128]{2,1,0:T(8,128)(2,1)S(1)} %collective-permute-done.10.rest_17_), channel_id=1, source_target_pairs={{0,2},{1,3},{2,0},{3,1},{4,6},{5,7},{6,4},{7,5},{8,10},{9,11},{10,... | collective-permute-start | bytes 393224 | tf_op jit(solution)/shard_map/ppermute | solution.py:472
  27.6 5.8 %collective-permute-start.11 = (bf16[2,256,128]{2,1,0:T(8,128)(2,1)S(1)}, bf16[2,256,128]{2,1,0:T(8,128)(2,1)S(1)}, u32[]{:S(2)}, u32[]{:S(2)}) collective-permute-start(bf16[2,256,128]{2,1,0:T(8,128)(2,1)S(1)} %collective-permute-done.10.rest_17_), channel_id=1, source_target_pairs={{0,1},{1,0},{2,3},{3,2},{4,5},{5,4},{6,7},{7,6},{8,9},{9,8},{10,11... | collective-permute-start | bytes 393224 | tf_op jit(solution)/shard_map/ppermute | solution.py:472
  28.4 7.3 %collective-permute-start.8 = (bf16[2,256,128]{2,1,0:T(8,128)(2,1)S(1)}, bf16[2,256,128]{2,1,0:T(8,128)(2,1)S(1)}, u32[]{:S(2)}, u32[]{:S(2)}) collective-permute-start(bf16[2,256,128]{2,1,0:T(8,128)(2,1)S(1)} %shard_map.112.rest_13_), channel_id=1, source_target_pairs={{0,2},{1,3},{2,0},{3,1},{4,6},{5,7},{6,4},{7,5},{8,10},{9,11},{10,... | collective-permute-start | bytes 393224 | tf_op jit(solution)/shard_map/ppermute | solution.py:472
  30.0 5.8 %collective-permute-start.5 = (bf16[2,2,256,128]{3,2,1,0:T(8,128)(2,1)S(1)}, bf16[2,2,256,128]{3,2,1,0:T(8,128)(2,1)S(1)}, u32[]{:S(2)}, u32[]{:S(2)}) collective-permute-start(bf16[2,2,256,128]{3,2,1,0:T(8,128)(2,1)S(1)} %collective-permute-done.4.refs_2_.rest_11_), channel_id=1, source_target_pairs={{0,1},{1,0},{2,3},{3,2},{4,5},{5,4},{6,7},{7,6},{8,9},{9,8},{10,11... | collective-permute-start | bytes 786440 | tf_op jit(solution)/shard_map/ppermute | solution.py:472
  33.4 2.4 %collective-permute-start.13 = (bf16[2,256,128]{2,1,0:T(8,128)(2,1)S(1)}, bf16[2,256,128]{2,1,0:T(8,128)(2,1)S(1)}, u32[]{:S(2)}, u32[]{:S(2)}) collective-permute-start(bf16[2,256,128]{2,1,0:T(8,128)(2,1)S(1)} %collective-permute-done.12.rest_19_), channel_id=1, source_target_pairs={{0,1},{1,0},{2,3},{3,2},{4,5},{5,4},{6,7},{7,6},{8,9},{9,8},{10,11... | collective-permute-start | bytes 393224 | tf_op jit(solution)/shard_map/ppermute | solution.py:472
  33.4 2.4 %collective-permute-start.7 = (bf16[2,256,128]{2,1,0:T(8,128)(2,1)S(1)}, bf16[2,256,128]{2,1,0:T(8,128)(2,1)S(1)}, u32[]{:S(2)}, u32[]{:S(2)}) collective-permute-start(bf16[2,256,128]{2,1,0:T(8,128)(2,1)S(1)} %shard_map.112.rest_13_), channel_id=1, source_target_pairs={{0,1},{1,0},{2,3},{3,2},{4,5},{5,4},{6,7},{7,6},{8,9},{9,8},{10,11... | collective-permute-start | bytes 393224 | tf_op jit(solution)/shard_map/ppermute | solution.py:472
  35.8 1.3 %collective-permute-start.9 = (bf16[2,256,128]{2,1,0:T(8,128)(2,1)S(1)}, bf16[2,256,128]{2,1,0:T(8,128)(2,1)S(1)}, u32[]{:S(2)}, u32[]{:S(2)}) collective-permute-start(bf16[2,256,128]{2,1,0:T(8,128)(2,1)S(1)} %collective-permute-done.8.rest_15_), channel_id=1, source_target_pairs={{0,1},{1,0},{2,3},{3,2},{4,5},{5,4},{6,7},{7,6},{8,9},{9,8},{10,11... | collective-permute-start | bytes 393224 | tf_op jit(solution)/shard_map/ppermute | solution.py:472

commit v8 on v6

--- a/solution.py
+++ b/solution.py
@@ -61,30 +61,27 @@
     return np.stack([value.real, value.imag]).astype(np.float32)
 
 
-def steer_table(angle_count, pulse_count):
-    angle_index = np.arange(angle_count)[:, None]
-    pulse_index = np.arange(pulse_count)[None, :]
-    value = root(angle_count, (angle_index + angle_count // 2) * pulse_index)
-    value = (value / math.sqrt(pulse_count)).astype(np.complex64)
-    return value.real.astype(ml_dtypes.bfloat16), value.imag.astype(ml_dtypes.bfloat16)
-
-
-def steer_blocks(pulse_count, child_angles):
-    real, imag = steer_table(A0, pulse_count)
-    real, imag = real[:child_angles], imag[:child_angles]
-    table = np.zeros((2, 2, child_angles, 2, 2, 2, 2, 2, pulse_count), ml_dtypes.bfloat16)
-    for pair in range(2):
+def steer_tiles(pulse_count, child_angles):
+    size = (child_angles, LANES)
+    lane = lax.broadcasted_iota(jnp.int32, size, 1)
+    angle = lax.broadcasted_iota(jnp.int32, size, 0) + A0 // 2
+    turn = (angle * (lane % pulse_count)) & (A0 - 1)
+    real, imag = unit(turn.astype(jnp.float32) * (-2.0 * math.pi / A0))
+    real, imag = real / math.sqrt(pulse_count), imag / math.sqrt(pulse_count)
+    owner = lane // pulse_count
+    rows = (((real, -imag), (-imag, -real)), ((imag, real), (real, -imag)))
+
+    def tiles(pair, part):
+        blocks = []
         for child in range(2):
-            spot = (pair, child)
-            table[child, 0, :, pair, 0, 0, *spot] = real
-            table[child, 0, :, pair, 0, 1, *spot] = -imag
-            table[child, 1, :, pair, 0, 0, *spot] = -imag
-            table[child, 1, :, pair, 0, 1, *spot] = -real
-            table[child, 0, :, pair, 1, 0, *spot] = imag
-            table[child, 0, :, pair, 1, 1, *spot] = real
-            table[child, 1, :, pair, 1, 0, *spot] = real
-            table[child, 1, :, pair, 1, 1, *spot] = -imag
-    return table.reshape(4 * child_angles, 32 * pulse_count)
+            mine = owner == 2 * pair + child
+            for piece in rows[part]:
+                blocks.append(
+                    jnp.concatenate([jnp.where(mine, side, 0.0) for side in piece], 1)
+                )
+        return jnp.concatenate(blocks, 0).astype(jnp.bfloat16)
+
+    return tiles
 
 
 def small_unit(angle):
@@ -141,7 +138,8 @@
                 value = times(value, step)
 
 
-def weight_rows(pulse_count, weight_ref, steer_ref, one_ref, two_ref):
+def weight_rows(pulse_count, weight_ref, one_ref, two_ref):
+    steer = steer_tiles(pulse_count, weight_ref.shape[4])
     joined = jnp.concatenate([weight_ref[0, c, part] for c in range(2) for part in range(2)], 1)
     parents = joined.shape[0]
     width = one_ref.shape[2]
@@ -151,9 +149,8 @@
     children = one_ref.shape[1] // 8
     for pair in range(2):
         for part in range(2):
-            at = (pair * 2 + part) * width
             value = jnp.dot(
-                joined, steer_ref[:, at : at + width], preferred_element_type=jnp.float32
+                joined, steer(pair, part), preferred_element_type=jnp.float32
             )
             for turn in range(2):
                 turned = jnp.where(odd_pulse, -value, value) if turn else value
@@ -176,24 +173,25 @@
 
 
 def table_kernel(pulse_count, total, place_ref, rate_ref, *refs):
-    offset_refs, filter_ref, weight_ref, steer_ref = refs[:QUAD], *refs[QUAD : QUAD + 3]
-    gain_ref, one_ref, two_ref, phase_one_ref, phase_two_ref, done_ref = refs[QUAD + 3 :]
+    offset_refs, filter_ref, weight_ref = refs[:2], *refs[2:4]
+    gain_ref, one_ref, two_ref, phase_one_ref, phase_two_ref, done_ref = refs[4:]
     start = (place_ref[1] * (total // QUAD)).astype(jnp.float32)
     done_ref[0] = 1
     phase_rows(phase_one_ref, rate_ref[0], start, total)
     phase_rows(phase_two_ref, rate_ref[1], start, total)
     gain_rows(total, place_ref, offset_refs, filter_ref, gain_ref)
-    weight_rows(pulse_count, weight_ref, steer_ref, one_ref, two_ref)
+    weight_rows(pulse_count, weight_ref, one_ref, two_ref)
 
 
 def gain_rows(total, place_ref, offset_refs, filter_ref, out_ref):
     second = total // FIRST
     member = place_ref[1]
     offsets = []
+    known = [ref[row : row + 1, :] for ref in offset_refs for row in range(2)]
     for owner in range(QUAD):
-        value = offset_refs[0][...]
+        value = known[0]
         for rel in range(1, QUAD):
-            value = jnp.where((member ^ rel) == owner, offset_refs[rel][...], value)
+            value = jnp.where((member ^ rel) == owner, known[rel], value)
         offsets.append(value)
     offsets = jnp.concatenate(offsets, 1)
     shift = offsets - place_ref[1] * (total // QUAD)
@@ -465,11 +463,9 @@
         compiler_params=small,
     )(place, raw_echo)
     near = jnp.stack([range_offsets, move(range_offsets, 1)])
-    joined = [near, move(near, 2)]
-    offsets = [joined[rel // 2][rel % 2 : rel % 2 + 1] for rel in range(QUAD)]
+    offsets = [near, move(near, 2)]
 
     child_angles = interp_weight.shape[4]
-    steer = jnp.asarray(steer_blocks(pulse_count, child_angles))
     *made, made_flag = pl.pallas_call(
         functools.partial(table_kernel, pulse_count, total),
         out_shape=[
@@ -480,7 +476,7 @@
             shape((2, width // LANES, 4 * A0, LANES)),
             flag,
         ],
-        in_specs=[smem, smem] + [vmem] * (QUAD + 3),
+        in_specs=[smem, smem] + [vmem] * 4,
         out_specs=[vmem] * 5 + [smem],
         cost_estimate=cost(2**30, 2**23),
         compiler_params=small,
@@ -490,7 +486,6 @@
         *offsets,
         range_filter.reshape(2, second, FIRST),
         interp_weight,
-        steer,
     )
 
     own = [cut[0]] + [move(cut[step], QUAD * step) for step in range(1, groups)]

time: 47.3 us -> 46.5 us (0.983)
  waiting for transfers between devices: 6.05 us -> 8.95 us
  local copies, waits for them, and re-layouts: 5.53 us -> 3.66 us
  starting transfers between devices: 14.9 us -> 13.1 us
    ppermute x17, waiting for transfers between devices: 6.05 us -> 8.95 us  [move(): return lax.ppermute(value, 'ap', [(i, i ^ bits) for i in range(count)])]
    unnamed x20 -> x16, local copies, waits for them, and re-layouts: 4.64 us -> 2.77 us
    ppermute x17, starting transfers between devices: 14.9 us -> 13.1 us  [move(): return lax.ppermute(value, 'ap', [(i, i ^ bits) for i in range(count)])]
  transfers between devices with their start and end apart: 17 -> 17, of which waited for: 3 -> 4; matrix products, arithmetic and copies ran while one was open for 3% -> 3% of each run, Pallas kernels for 14% -> 14%
where the time goes in v8:
time: 46.5 us; the launch traced here: 46.2 us
  Pallas kernels  19.6 us (42%)
  starting transfers between devices  13.1 us (28%)
  waiting for transfers between devices  8.95 us (19%)
  local copies, waits for them, and re-layouts  3.66 us (8%)
  other arithmetic  0.74 us (2%)
    ppermute x17, starting transfers between devices, move(): return lax.ppermute(value, 'ap', [(i, i ^ bits) for i in range(count)])  13.1 us
    pallas_call x1, Pallas kernels, focus(): pl.pallas_call(functools.partial(kernel, count, total), out_shape=jax.Sha...  12.6 us
    ppermute x17, waiting for transfers between devices, move(): return lax.ppermute(value, 'ap', [(i, i ^ bits) for i in range(count)])  8.95 us
    pallas_call x1, Pallas kernels, body(): pl.pallas_call(functools.partial(table_kernel, pulse_count, total), out_s...  5.73 us
    unnamed x16, local copies, waits for them, and re-layouts  2.77 us
  transfers between devices with their start and end apart: 17, of which 4 were waited for; matrix products, arithmetic and copies ran while one was open for 3% of the time, Pallas kernels for 14%

profile of v8, /device:TPU:0, one launch (start us, length us, event | category | flops | bytes accessed | tf_op | source)
XLA Modules:
  0.0 46.2 jit_solution(1673541250687391820)
XLA Ops:
  0.0 0.1 pad_add_fusion.1.place_ref
  0.1 0.0 copy-start.3
  0.1 1.0 %copy-done.3 = bf16[2,256,512]{2,1,0:T(8,128)(2,1)S(1)} copy-done((bf16[2,256,512]{2,1,0:T(8,128)(2,1)S(1)}, bf16[2,256,512]{2,1,0:T(8,128)(2,1)}, u32[]{:S(2)}) %copy-start.3) | copy-done | bytes 524312
  1.1 0.6 %shard_map.101 = (bf16[2,256,128]{2,1,0:T(8,128)(2,1)S(1)}, bf16[2,256,128]{2,1,0:T(8,128)(2,1)S(1)}, bf16[2,256,128]{2,1,0:T(8,128)(2,1)S(1)}, bf16[2,256,128]{2,1,0:T(8,128)(2,1)S(1)}) custom-call(s32[2]{0:T(128)S(1)} %pad_add_fusion.1.place_ref, bf16[2,256,512]{2,1,0:T(8,128)(2,1)S(1)} %copy-done.3), custom_call_target="tpu_custom_call" | custom-call | tf_op jit(solution)/shard_map/pallas_call | solution.py:458
  1.8 3.1 %collective-permute-start.5 = (bf16[2,256,128]{2,1,0:T(8,128)(2,1)S(1)}, bf16[2,256,128]{2,1,0:T(8,128)(2,1)S(1)}, u32[]{:S(2)}, u32[]{:S(2)}) collective-permute-start(bf16[2,256,128]{2,1,0:T(8,128)(2,1)S(1)} %get-tuple-element.21), channel_id=1, source_target_pairs={{0,4},{1,5},{2,6},{3,7},{4,0},{5,1},{6,2},{7,3},{8,12},{9,13},{10,... | collective-permute-start | bytes 393224 | tf_op jit(solution)/shard_map/ppermute | solution.py:447
  4.9 0.0 collective-permute-start
  4.9 2.6 %collective-permute-start.9 = (bf16[2,256,128]{2,1,0:T(8,128)(2,1)S(1)}, bf16[2,256,128]{2,1,0:T(8,128)(2,1)S(1)}, u32[]{:S(2)}, u32[]{:S(2)}) collective-permute-start(bf16[2,256,128]{2,1,0:T(8,128)(2,1)S(1)} %get-tuple-element.22), channel_id=1, source_target_pairs={{0,8},{1,9},{2,10},{3,11},{4,12},{5,13},{6,14},{7,15},{8,0},{9,1},... | collective-permute-start | bytes 393224 | tf_op jit(solution)/shard_map/ppermute | solution.py:447
  7.4 0.0 collective-permute-start.13
  7.4 1.7 %collective-permute-start.3 = (bf16[2,256,128]{2,1,0:T(8,128)(2,1)S(1)}, bf16[2,256,128]{2,1,0:T(8,128)(2,1)S(1)}, u32[]{:S(2)}, u32[]{:S(2)}) collective-permute-start(bf16[2,256,128]{2,1,0:T(8,128)(2,1)S(1)} %get-tuple-element.20.rest_9_), channel_id=1, source_target_pairs={{0,2},{1,3},{2,0},{3,1},{4,6},{5,7},{6,4},{7,5},{8,10},{9,11},{10,... | collective-permute-start | bytes 393224 | tf_op jit(solution)/shard_map/ppermute | solution.py:447
  9.2 0.0 collective-permute-done.5.rest_13_
  9.2 0.8 %collective-permute-start.7 = (bf16[2,256,128]{2,1,0:T(8,128)(2,1)S(1)}, bf16[2,256,128]{2,1,0:T(8,128)(2,1)S(1)}, u32[]{:S(2)}, u32[]{:S(2)}) collective-permute-start(bf16[2,256,128]{2,1,0:T(8,128)(2,1)S(1)} %collective-permute-done.5.rest_13_), channel_id=1, source_target_pairs={{0,2},{1,3},{2,0},{3,1},{4,6},{5,7},{6,4},{7,5},{8,10},{9,11},{10,... | collective-permute-start | bytes 393224 | tf_op jit(solution)/shard_map/ppermute | solution.py:447
  10.0 0.0 collective-permute-done
  10.0 0.7 %pad_add_fusion.refs_0_ = s32[2,32]{1,0:T(2,128)S(1)} fusion(s32[1,32]{1,0:T(1,128)S(1)} %bitcast.5, s32[1,32]{1,0:T(1,128)} %bitcast.4), kind=kLoop, calls=%fused_computation | loop fusion | flops 64 | bytes 512 | tf_op jit(solution)/shard_map/stack | solution.py:465
  10.7 1.2 %collective-permute-start.1 = (s32[2,32]{1,0:T(2,128)S(1)}, s32[2,32]{1,0:T(2,128)S(1)}, u32[]{:S(2)}, u32[]{:S(2)}) collective-permute-start(s32[2,32]{1,0:T(2,128)S(1)} %pad_add_fusion.refs_0_), channel_id=1, source_target_pairs={{0,2},{1,3},{2,0},{3,1},{4,6},{5,7},{6,4},{7,5},{8,10},{9,11},{10,... | collective-permute-start | bytes 776 | tf_op jit(solution)/shard_map/ppermute | solution.py:447
  11.9 0.9 %reshape.3.refs_2_ = f32[2,256,16]{2,1,0:T(8,128)S(1)} reshape(f32[2,4096]{1,0:T(2,128)} %param.11) | data formatting | bytes 65536 | tf_op jit(solution)/shard_map/reshape | solution.py:487
  12.8 0.0 copy-start
  12.8 0.0 copy-start.1
  12.8 0.0 copy-start.2
  12.8 0.0 copy-start.4
  12.8 0.0 copy-start.5
  12.8 3.1 %collective-permute-done.1.refs_1_ = s32[2,32]{1,0:T(2,128)S(1)} collective-permute-done((s32[2,32]{1,0:T(2,128)S(1)}, s32[2,32]{1,0:T(2,128)S(1)}, u32[]{:S(2)}, u32[]{:S(2)}) %collective-permute-start.1) | collective-permute-done | bytes 288 | tf_op jit(solution)/shard_map/ppermute | solution.py:447
  15.9 0.0 collective-permute-start.2
  15.9 0.0 copy-start.6
  16.0 1.0 %copy-done.6 = bf16[2,2,2,256,128]{4,3,2,1,0:T(8,128)(2,1)S(1)} copy-done((bf16[2,2,2,256,128]{4,3,2,1,0:T(8,128)(2,1)S(1)}, bf16[2,2,2,256,128]{4,3,2,1,0:T(8,128)(2,1)}, u32[]{:S(2)}) %copy-start.6) | copy-done | bytes 524312
  17.0 0.0 copy-start.7
  17.0 0.7 %copy-done.7 = f32[2]{0:T(128)S(1)} copy-done((f32[2]{0:T(128)S(1)}, f32[2]{0:T(128)}, u32[]{:S(2)}) %copy-start.7) | copy-done | bytes 32
  17.6 5.7 %shard_map.100 = (bf16[2,16,256,128]{3,2,1,0:T(8,128)(2,1)S(1)}, bf16[4,1024,256]{2,1,0:T(8,128)(2,1)S(1)}, bf16[2,512,256]{2,1,0:T(8,128)(2,1)S(1)}, bf16[2,8,5...) custom-call(s32[2]{0:T(128)S(1)} %pad_add_fusion.1.place_ref, f32[2]{0:T(128)S(1)} %copy-done.7, ...), custom_call_target="tpu_custom_call" | custom-call | flops 1073741824 | bytes 8388608 | tf_op jit(solution)/shard_map/pallas_call | solution.py:469
  23.4 0.0 collective-permute-done.9.refs_0_
  23.4 0.6 %collective-permute-start.6 = (bf16[2,256,128]{2,1,0:T(8,128)(2,1)S(1)}, bf16[2,256,128]{2,1,0:T(8,128)(2,1)S(1)}, u32[]{:S(2)}, u32[]{:S(2)}) collective-permute-start(bf16[2,256,128]{2,1,0:T(8,128)(2,1)S(1)} %collective-permute-done.5.rest_13_), channel_id=1, source_target_pairs={{0,1},{1,0},{2,3},{3,2},{4,5},{5,4},{6,7},{7,6},{8,9},{9,8},{10,11... | collective-permute-start | bytes 393224 | tf_op jit(solution)/shard_map/ppermute | solution.py:447
  24.0 0.0 collective-permute-done.13.rest_21_
  24.0 1.5 %collective-permute-start.15 = (bf16[2,256,128]{2,1,0:T(8,128)(2,1)S(1)}, bf16[2,256,128]{2,1,0:T(8,128)(2,1)S(1)}, u32[]{:S(2)}, u32[]{:S(2)}) collective-permute-start(bf16[2,256,128]{2,1,0:T(8,128)(2,1)S(1)} %collective-permute-done.13.rest_21_), channel_id=1, source_target_pairs={{0,2},{1,3},{2,0},{3,1},{4,6},{5,7},{6,4},{7,5},{8,10},{9,11},{10,... | collective-permute-start | bytes 393224 | tf_op jit(solution)/shard_map/ppermute | solution.py:447
  25.5 0.0 collective-permute-done.7.refs_2_.rest_15_
  25.5 0.0 collective-permute-start.14
  25.5 0.6 %shard_map.102.rest_17_ = bf16[2,256,128]{2,1,0:T(8,128)(2,1)S(1)} custom-call(bf16[2,256,128]{2,1,0:T(8,128)(2,1)S(1)} %collective-permute-done.9.refs_0_, s32[1]{0:T(128)} %get-tuple-element.23.refs_1_, bf16[2,256,128]{2,1,0:T(8,128)(2,1)S(1)} %collective-permute-done.7.refs_2_.rest_15_), custom_call_target="tpu_custom_call", output_to_operand_aliasing={{}: (0, {})} | custom-call | flops 1 | bytes 1 | tf_op jit(solution)/shard_map/pallas_call | solution.py:391
  26.2 0.0 collective-permute-done.3.rest_11_
  26.2 0.6 %collective-permute-start.11 = (bf16[2,256,128]{2,1,0:T(8,128)(2,1)S(1)}, bf16[2,256,128]{2,1,0:T(8,128)(2,1)S(1)}, u32[]{:S(2)}, u32[]{:S(2)}) collective-permute-start(bf16[2,256,128]{2,1,0:T(8,128)(2,1)S(1)} %shard_map.102.rest_17_), channel_id=1, source_target_pairs={{0,2},{1,3},{2,0},{3,1},{4,6},{5,7},{6,4},{7,5},{8,10},{9,11},{10,... | collective-permute-start | bytes 393224 | tf_op jit(solution)/shard_map/ppermute | solution.py:447
  26.7 0.0 collective-permute-done.2.rest_10_
  26.7 0.2 collective-permute-start.4
  27.0 0.0 collective-permute-done.6.rest_14_
  27.0 0.3 collective-permute-start.10
  27.3 2.3 %collective-permute-done.15.rest_23_ = bf16[2,256,128]{2,1,0:T(8,128)(2,1)S(1)} collective-permute-done((bf16[2,256,128]{2,1,0:T(8,128)(2,1)S(1)}, bf16[2,256,128]{2,1,0:T(8,128)(2,1)S(1)}, u32[]{:S(2)}, u32[]{:S(2)}) %collective-permute-start.15) | collective-permute-done | bytes 131104 | tf_op jit(solution)/shard_map/ppermute | solution.py:447
  29.5 0.0 collective-permute-start.8
  29.5 0.0 collective-permute-done.14.rest_22_
  29.5 0.5 %collective-permute-start.16 = (bf16[2,256,128]{2,1,0:T(8,128)(2,1)S(1)}, bf16[2,256,128]{2,1,0:T(8,128)(2,1)S(1)}, u32[]{:S(2)}, u32[]{:S(2)}) collective-permute-start(bf16[2,256,128]{2,1,0:T(8,128)(2,1)S(1)} %collective-permute-done.15.rest_23_), channel_id=1, source_target_pairs={{0,1},{1,0},{2,3},{3,2},{4,5},{5,4},{6,7},{7,6},{8,9},{9,8},{10,11... | collective-permute-start | bytes 393224 | tf_op jit(solution)/shard_map/ppermute | solution.py:447
  30.0 2.2 %collective-permute-done.11.rest_19_ = bf16[2,256,128]{2,1,0:T(8,128)(2,1)S(1)} collective-permute-done((bf16[2,256,128]{2,1,0:T(8,128)(2,1)S(1)}, bf16[2,256,128]{2,1,0:T(8,128)(2,1)S(1)}, u32[]{:S(2)}, u32[]{:S(2)}) %collective-permute-start.11) | collective-permute-done | bytes 131104 | tf_op jit(solution)/shard_map/ppermute | solution.py:447
  32.3 0.0 collective-permute-start.12
  32.3 0.0 collective-permute-done.4.rest_12_
  32.3 0.0 collective-permute-done.8.rest_16_
  32.3 0.0 collective-permute-done.16.rest_24_
  32.3 0.0 collective-permute-done.10.rest_18_
  32.3 1.3 %collective-permute-done.12.rest_20_ = bf16[2,256,128]{2,1,0:T(8,128)(2,1)S(1)} collective-permute-done((bf16[2,256,128]{2,1,0:T(8,128)(2,1)S(1)}, bf16[2,256,128]{2,1,0:T(8,128)(2,1)S(1)}, u32[]{:S(2)}, u32[]{:S(2)}) %collective-permute-start.12) | collective-permute-done | bytes 131104 | tf_op jit(solution)/shard_map/ppermute | solution.py:447
  33.6 0.0 copy-done
  33.6 0.0 copy-done.1
  33.6 0.0 copy-done.2
  33.6 0.0 copy-done.4
  33.6 0.0 copy-done.5
  33.7 12.6 %shard_map.103 = f32[2,1024,1024]{2,1,0:T(8,128)} custom-call(s32[2]{0:T(128)S(1)} %pad_add_fusion.1.place_ref, f32[2,16,16]{2,1,0:T(8,128)S(1)} %copy-done.5, bf16[512,512]{1,0:T(8,128)(2,1)S(1)} %copy-done.2, bf16[512,512]{1,0:T(8,128)(2,1)S(1)} %copy-done.1, bf16[512,512]{1,0:T(8,128)(2,1)S(1)} %copy-done, bf16[128,512]{1,0:T(8,128)(2,1)S(1)} %copy-done.4, ...), custom_call_target="tpu_custom_call" | custom-call | tf_op jit(solution)/shard_map/pallas_call | solution.py:415
Async XLA Ops:
  0.1 1.0 %copy-start.3 = (bf16[2,256,512]{2,1,0:T(8,128)(2,1)S(1)}, bf16[2,256,512]{2,1,0:T(8,128)(2,1)}, u32[]{:S(2)}) copy-start(bf16[2,256,512]{2,1,0:T(8,128)(2,1)} %raw_ref.1) | copy-start | bytes 1572868
  1.8 7.4 %collective-permute-start.5 = (bf16[2,256,128]{2,1,0:T(8,128)(2,1)S(1)}, bf16[2,256,128]{2,1,0:T(8,128)(2,1)S(1)}, u32[]{:S(2)}, u32[]{:S(2)}) collective-permute-start(bf16[2,256,128]{2,1,0:T(8,128)(2,1)S(1)} %get-tuple-element.21), channel_id=1, source_target_pairs={{0,4},{1,5},{2,6},{3,7},{4,0},{5,1},{6,2},{7,3},{8,12},{9,13},{10,... | collective-permute-start | bytes 393224 | tf_op jit(solution)/shard_map/ppermute | solution.py:447
  4.9 5.2 %collective-permute-start = (s32[32]{0:T(128)}, s32[32]{0:T(128)S(1)}, u32[]{:S(2)}, u32[]{:S(2)}) collective-permute-start(s32[32]{0:T(128)} %param.12), channel_id=1, source_target_pairs={{0,1},{1,0},{2,3},{3,2},{4,5},{5,4},{6,7},{7,6},{8,9},{9,8},{10,11... | collective-permute-start | bytes 392 | tf_op jit(solution)/shard_map/ppermute | solution.py:447
  4.9 18.5 %collective-permute-start.9 = (bf16[2,256,128]{2,1,0:T(8,128)(2,1)S(1)}, bf16[2,256,128]{2,1,0:T(8,128)(2,1)S(1)}, u32[]{:S(2)}, u32[]{:S(2)}) collective-permute-start(bf16[2,256,128]{2,1,0:T(8,128)(2,1)S(1)} %get-tuple-element.22), channel_id=1, source_target_pairs={{0,8},{1,9},{2,10},{3,11},{4,12},{5,13},{6,14},{7,15},{8,0},{9,1},... | collective-permute-start | bytes 393224 | tf_op jit(solution)/shard_map/ppermute | solution.py:447
  7.4 16.5 %collective-permute-start.13 = (bf16[2,256,128]{2,1,0:T(8,128)(2,1)S(1)}, bf16[2,256,128]{2,1,0:T(8,128)(2,1)S(1)}, u32[]{:S(2)}, u32[]{:S(2)}) collective-permute-start(bf16[2,256,128]{2,1,0:T(8,128)(2,1)S(1)} %get-tuple-element.24), channel_id=1, source_target_pairs={{0,12},{1,13},{2,14},{3,15},{4,8},{5,9},{6,10},{7,11},{8,4},{9,5},... | collective-permute-start | bytes 393224 | tf_op jit(solution)/shard_map/ppermute | solution.py:447
  7.4 18.7 %collective-permute-start.3 = (bf16[2,256,128]{2,1,0:T(8,128)(2,1)S(1)}, bf16[2,256,128]{2,1,0:T(8,128)(2,1)S(1)}, u32[]{:S(2)}, u32[]{:S(2)}) collective-permute-start(bf16[2,256,128]{2,1,0:T(8,128)(2,1)S(1)} %get-tuple-element.20.rest_9_), channel_id=1, source_target_pairs={{0,2},{1,3},{2,0},{3,1},{4,6},{5,7},{6,4},{7,5},{8,10},{9,11},{10,... | collective-permute-start | bytes 393224 | tf_op jit(solution)/shard_map/ppermute | solution.py:447
  9.2 16.3 %collective-permute-start.7 = (bf16[2,256,128]{2,1,0:T(8,128)(2,1)S(1)}, bf16[2,256,128]{2,1,0:T(8,128)(2,1)S(1)}, u32[]{:S(2)}, u32[]{:S(2)}) collective-permute-start(bf16[2,256,128]{2,1,0:T(8,128)(2,1)S(1)} %collective-permute-done.5.rest_13_), channel_id=1, source_target_pairs={{0,2},{1,3},{2,0},{3,1},{4,6},{5,7},{6,4},{7,5},{8,10},{9,11},{10,... | collective-permute-start | bytes 393224 | tf_op jit(solution)/shard_map/ppermute | solution.py:447
  10.7 5.2 %collective-permute-start.1 = (s32[2,32]{1,0:T(2,128)S(1)}, s32[2,32]{1,0:T(2,128)S(1)}, u32[]{:S(2)}, u32[]{:S(2)}) collective-permute-start(s32[2,32]{1,0:T(2,128)S(1)} %pad_add_fusion.refs_0_), channel_id=1, source_target_pairs={{0,2},{1,3},{2,0},{3,1},{4,6},{5,7},{6,4},{7,5},{8,10},{9,11},{10,... | collective-permute-start | bytes 776 | tf_op jit(solution)/shard_map/ppermute | solution.py:447
  12.8 20.8 %copy-start = (bf16[512,512]{1,0:T(8,128)(2,1)S(1)}, bf16[512,512]{1,0:T(8,128)(2,1)}, u32[]{:S(2)}) copy-start(bf16[512,512]{1,0:T(8,128)(2,1)} %constant.42.clone.rest_2_) | copy-start | bytes 1572868
  12.8 20.8 %copy-start.1 = (bf16[512,512]{1,0:T(8,128)(2,1)S(1)}, bf16[512,512]{1,0:T(8,128)(2,1)}, u32[]{:S(2)}) copy-start(bf16[512,512]{1,0:T(8,128)(2,1)} %constant.41.clone.rest_1_) | copy-start | bytes 1572868
  12.8 20.8 %copy-start.2 = (bf16[512,512]{1,0:T(8,128)(2,1)S(1)}, bf16[512,512]{1,0:T(8,128)(2,1)}, u32[]{:S(2)}) copy-start(bf16[512,512]{1,0:T(8,128)(2,1)} %constant.40.clone.rest_0_) | copy-start | bytes 1572868
  12.8 20.8 %copy-start.4 = (bf16[128,512]{1,0:T(8,128)(2,1)S(1)}, bf16[128,512]{1,0:T(8,128)(2,1)}, u32[]{:S(2)}) copy-start(bf16[128,512]{1,0:T(8,128)(2,1)} %constant.43.clone.rest_3_) | copy-start | bytes 393220
  12.8 20.8 %copy-start.5 = (f32[2,16,16]{2,1,0:T(8,128)S(1)}, f32[2,16,16]{2,1,0:T(8,128)}, u32[]{:S(2)}) copy-start(f32[2,16,16]{2,1,0:T(8,128)} %constant.44.clone.turn_ref) | copy-start | bytes 6148
  15.9 10.8 %collective-permute-start.2 = (bf16[2,256,128]{2,1,0:T(8,128)(2,1)S(1)}, bf16[2,256,128]{2,1,0:T(8,128)(2,1)S(1)}, u32[]{:S(2)}, u32[]{:S(2)}) collective-permute-start(bf16[2,256,128]{2,1,0:T(8,128)(2,1)S(1)} %get-tuple-element.20.rest_9_), channel_id=1, source_target_pairs={{0,1},{1,0},{2,3},{3,2},{4,5},{5,4},{6,7},{7,6},{8,9},{9,8},{10,11... | collective-permute-start | bytes 393224 | tf_op jit(solution)/shard_map/ppermute | solution.py:447
  15.9 1.0 %copy-start.6 = (bf16[2,2,2,256,128]{4,3,2,1,0:T(8,128)(2,1)S(1)}, bf16[2,2,2,256,128]{4,3,2,1,0:T(8,128)(2,1)}, u32[]{:S(2)}) copy-start(bf16[2,2,2,256,128]{4,3,2,1,0:T(8,128)(2,1)} %refs_3_.1) | copy-start | bytes 1572868
  17.0 0.7 %copy-start.7 = (f32[2]{0:T(128)S(1)}, f32[2]{0:T(128)}, u32[]{:S(2)}) copy-start(f32[2]{0:T(128)} %rate_ref.1) | copy-start | bytes 28
  23.4 3.6 %collective-permute-start.6 = (bf16[2,256,128]{2,1,0:T(8,128)(2,1)S(1)}, bf16[2,256,128]{2,1,0:T(8,128)(2,1)S(1)}, u32[]{:S(2)}, u32[]{:S(2)}) collective-permute-start(bf16[2,256,128]{2,1,0:T(8,128)(2,1)S(1)} %collective-permute-done.5.rest_13_), channel_id=1, source_target_pairs={{0,1},{1,0},{2,3},{3,2},{4,5},{5,4},{6,7},{7,6},{8,9},{9,8},{10,11... | collective-permute-start | bytes 393224 | tf_op jit(solution)/shard_map/ppermute | solution.py:447
  24.0 5.5 %collective-permute-start.15 = (bf16[2,256,128]{2,1,0:T(8,128)(2,1)S(1)}, bf16[2,256,128]{2,1,0:T(8,128)(2,1)S(1)}, u32[]{:S(2)}, u32[]{:S(2)}) collective-permute-start(bf16[2,256,128]{2,1,0:T(8,128)(2,1)S(1)} %collective-permute-done.13.rest_21_), channel_id=1, source_target_pairs={{0,2},{1,3},{2,0},{3,1},{4,6},{5,7},{6,4},{7,5},{8,10},{9,11},{10,... | collective-permute-start | bytes 393224 | tf_op jit(solution)/shard_map/ppermute | solution.py:447
  25.5 4.0 %collective-permute-start.14 = (bf16[2,256,128]{2,1,0:T(8,128)(2,1)S(1)}, bf16[2,256,128]{2,1,0:T(8,128)(2,1)S(1)}, u32[]{:S(2)}, u32[]{:S(2)}) collective-permute-start(bf16[2,256,128]{2,1,0:T(8,128)(2,1)S(1)} %collective-permute-done.13.rest_21_), channel_id=1, source_target_pairs={{0,1},{1,0},{2,3},{3,2},{4,5},{5,4},{6,7},{7,6},{8,9},{9,8},{10,11... | collective-permute-start | bytes 393224 | tf_op jit(solution)/shard_map/ppermute | solution.py:447
  26.2 6.1 %collective-permute-start.11 = (bf16[2,256,128]{2,1,0:T(8,128)(2,1)S(1)}, bf16[2,256,128]{2,1,0:T(8,128)(2,1)S(1)}, u32[]{:S(2)}, u32[]{:S(2)}) collective-permute-start(bf16[2,256,128]{2,1,0:T(8,128)(2,1)S(1)} %shard_map.102.rest_17_), channel_id=1, source_target_pairs={{0,2},{1,3},{2,0},{3,1},{4,6},{5,7},{6,4},{7,5},{8,10},{9,11},{10,... | collective-permute-start | bytes 393224 | tf_op jit(solution)/shard_map/ppermute | solution.py:447
  26.7 5.5 %collective-permute-start.4 = (bf16[2,256,128]{2,1,0:T(8,128)(2,1)S(1)}, bf16[2,256,128]{2,1,0:T(8,128)(2,1)S(1)}, u32[]{:S(2)}, u32[]{:S(2)}) collective-permute-start(bf16[2,256,128]{2,1,0:T(8,128)(2,1)S(1)} %collective-permute-done.3.rest_11_), channel_id=1, source_target_pairs={{0,1},{1,0},{2,3},{3,2},{4,5},{5,4},{6,7},{7,6},{8,9},{9,8},{10,11... | collective-permute-start | bytes 393224 | tf_op jit(solution)/shard_map/ppermute | solution.py:447
  27.0 5.3 %collective-permute-start.10 = (bf16[2,256,128]{2,1,0:T(8,128)(2,1)S(1)}, bf16[2,256,128]{2,1,0:T(8,128)(2,1)S(1)}, u32[]{:S(2)}, u32[]{:S(2)}) collective-permute-start(bf16[2,256,128]{2,1,0:T(8,128)(2,1)S(1)} %shard_map.102.rest_17_), channel_id=1, source_target_pairs={{0,1},{1,0},{2,3},{3,2},{4,5},{5,4},{6,7},{7,6},{8,9},{9,8},{10,11... | collective-permute-start | bytes 393224 | tf_op jit(solution)/shard_map/ppermute | solution.py:447
  29.5 2.8 %collective-permute-start.8 = (bf16[2,256,128]{2,1,0:T(8,128)(2,1)S(1)}, bf16[2,256,128]{2,1,0:T(8,128)(2,1)S(1)}, u32[]{:S(2)}, u32[]{:S(2)}) collective-permute-start(bf16[2,256,128]{2,1,0:T(8,128)(2,1)S(1)} %collective-permute-done.7.refs_2_.rest_15_), channel_id=1, source_target_pairs={{0,1},{1,0},{2,3},{3,2},{4,5},{5,4},{6,7},{7,6},{8,9},{9,8},{10,11... | collective-permute-start | bytes 393224 | tf_op jit(solution)/shard_map/ppermute | solution.py:447
  29.5 2.8 %collective-permute-start.16 = (bf16[2,256,128]{2,1,0:T(8,128)(2,1)S(1)}, bf16[2,256,128]{2,1,0:T(8,128)(2,1)S(1)}, u32[]{:S(2)}, u32[]{:S(2)}) collective-permute-start(bf16[2,256,128]{2,1,0:T(8,128)(2,1)S(1)} %collective-permute-done.15.rest_23_), channel_id=1, source_target_pairs={{0,1},{1,0},{2,3},{3,2},{4,5},{5,4},{6,7},{7,6},{8,9},{9,8},{10,11... | collective-permute-start | bytes 393224 | tf_op jit(solution)/shard_map/ppermute | solution.py:447
  32.3 1.3 %collective-permute-start.12 = (bf16[2,256,128]{2,1,0:T(8,128)(2,1)S(1)}, bf16[2,256,128]{2,1,0:T(8,128)(2,1)S(1)}, u32[]{:S(2)}, u32[]{:S(2)}) collective-permute-start(bf16[2,256,128]{2,1,0:T(8,128)(2,1)S(1)} %collective-permute-done.11.rest_19_), channel_id=1, source_target_pairs={{0,1},{1,0},{2,3},{3,2},{4,5},{5,4},{6,7},{7,6},{8,9},{9,8},{10,11... | collective-permute-start | bytes 393224 | tf_op jit(solution)/shard_map/ppermute | solution.py:447

commit v9 on v8

--- a/solution.py
+++ b/solution.py
@@ -187,7 +187,7 @@
     second = total // FIRST
     member = place_ref[1]
     offsets = []
-    known = [ref[row : row + 1, :] for ref in offset_refs for row in range(2)]
+    known = [ref[row : row + 1, :] for row in range(2) for ref in offset_refs]
     for owner in range(QUAD):
         value = known[0]
         for rel in range(1, QUAD):
@@ -462,8 +462,8 @@
         out_specs=[vmem] * groups,
         compiler_params=small,
     )(place, raw_echo)
-    near = jnp.stack([range_offsets, move(range_offsets, 1)])
-    offsets = [near, move(near, 2)]
+    column = jnp.stack([range_offsets, move(range_offsets, 2)])
+    offsets = [column, move(column, 1)]
 
     child_angles = interp_weight.shape[4]
     *made, made_flag = pl.pallas_call(

time: 46.5 us -> 44.1 us (0.948)
  waiting for transfers between devices: 8.95 us -> 6.22 us
    ppermute x17, waiting for transfers between devices: 8.95 us -> 6.22 us  [move(): return lax.ppermute(value, 'ap', [(i, i ^ bits) for i in range(count)])]
  transfers between devices with their start and end apart: 17 -> 17, of which waited for: 4 -> 4; matrix products, arithmetic and copies ran while one was open for 3% -> 4% of each run, Pallas kernels for 14% -> 15%
where the time goes in v9:
time: 44.1 us; the launch traced here: 43.8 us
  Pallas kernels  19.6 us (44%)
  starting transfers between devices  13.5 us (31%)
  waiting for transfers between devices  6.22 us (14%)
  local copies, waits for them, and re-layouts  3.66 us (8%)
  other arithmetic  0.74 us (2%)
    ppermute x17, starting transfers between devices, move(): return lax.ppermute(value, 'ap', [(i, i ^ bits) for i in range(count)])  13.5 us
    pallas_call x1, Pallas kernels, focus(): pl.pallas_call(functools.partial(kernel, count, total), out_shape=jax.Sha...  12.5 us
    ppermute x17, waiting for transfers between devices, move(): return lax.ppermute(value, 'ap', [(i, i ^ bits) for i in range(count)])  6.22 us
    pallas_call x1, Pallas kernels, body(): pl.pallas_call(functools.partial(table_kernel, pulse_count, total), out_s...  5.73 us
    unnamed x16, local copies, waits for them, and re-layouts  2.77 us
    reshape x1, local copies, waits for them, and re-layouts, body(): range_filter.reshape(2, second, FIRST)  0.89 us
  transfers between devices with their start and end apart: 17, of which 4 were waited for; matrix products, arithmetic and copies ran while one was open for 4% of the time, Pallas kernels for 15%

profile of v9, /device:TPU:0, one launch (start us, length us, event | category | flops | bytes accessed | tf_op | source)
XLA Modules:
  0.0 43.8 jit_solution(8893304416829764156)
XLA Ops:
  0.0 0.1 pad_add_fusion.1.place_ref
  0.1 0.0 copy-start.3
  0.1 1.0 %copy-done.3 = bf16[2,256,512]{2,1,0:T(8,128)(2,1)S(1)} copy-done((bf16[2,256,512]{2,1,0:T(8,128)(2,1)S(1)}, bf16[2,256,512]{2,1,0:T(8,128)(2,1)}, u32[]{:S(2)}) %copy-start.3) | copy-done | bytes 524312
  1.1 0.6 %shard_map.101 = (bf16[2,256,128]{2,1,0:T(8,128)(2,1)S(1)}, bf16[2,256,128]{2,1,0:T(8,128)(2,1)S(1)}, bf16[2,256,128]{2,1,0:T(8,128)(2,1)S(1)}, bf16[2,256,128]{2,1,0:T(8,128)(2,1)S(1)}) custom-call(s32[2]{0:T(128)S(1)} %pad_add_fusion.1.place_ref, bf16[2,256,512]{2,1,0:T(8,128)(2,1)S(1)} %copy-done.3), custom_call_target="tpu_custom_call" | custom-call | tf_op jit(solution)/shard_map/pallas_call | solution.py:458
  1.8 3.1 %collective-permute-start.5 = (bf16[2,256,128]{2,1,0:T(8,128)(2,1)S(1)}, bf16[2,256,128]{2,1,0:T(8,128)(2,1)S(1)}, u32[]{:S(2)}, u32[]{:S(2)}) collective-permute-start(bf16[2,256,128]{2,1,0:T(8,128)(2,1)S(1)} %get-tuple-element.21), channel_id=1, source_target_pairs={{0,4},{1,5},{2,6},{3,7},{4,0},{5,1},{6,2},{7,3},{8,12},{9,13},{10,... | collective-permute-start | bytes 393224 | tf_op jit(solution)/shard_map/ppermute | solution.py:447
  4.9 1.5 %collective-permute-start = (s32[32]{0:T(128)}, s32[32]{0:T(128)S(1)}, u32[]{:S(2)}, u32[]{:S(2)}) collective-permute-start(s32[32]{0:T(128)} %param.12), channel_id=1, source_target_pairs={{0,2},{1,3},{2,0},{3,1},{4,6},{5,7},{6,4},{7,5},{8,10},{9,11},{10,... | collective-permute-start | bytes 392 | tf_op jit(solution)/shard_map/ppermute | solution.py:447
  6.4 2.6 %collective-permute-start.9 = (bf16[2,256,128]{2,1,0:T(8,128)(2,1)S(1)}, bf16[2,256,128]{2,1,0:T(8,128)(2,1)S(1)}, u32[]{:S(2)}, u32[]{:S(2)}) collective-permute-start(bf16[2,256,128]{2,1,0:T(8,128)(2,1)S(1)} %get-tuple-element.22), channel_id=1, source_target_pairs={{0,8},{1,9},{2,10},{3,11},{4,12},{5,13},{6,14},{7,15},{8,0},{9,1},... | collective-permute-start | bytes 393224 | tf_op jit(solution)/shard_map/ppermute | solution.py:447
  9.0 0.2 collective-permute-start.13
  9.2 0.3 collective-permute-start.3
  9.5 0.0 collective-permute-done.5.rest_13_
  9.5 2.0 %collective-permute-start.7 = (bf16[2,256,128]{2,1,0:T(8,128)(2,1)S(1)}, bf16[2,256,128]{2,1,0:T(8,128)(2,1)S(1)}, u32[]{:S(2)}, u32[]{:S(2)}) collective-permute-start(bf16[2,256,128]{2,1,0:T(8,128)(2,1)S(1)} %collective-permute-done.5.rest_13_), channel_id=1, source_target_pairs={{0,2},{1,3},{2,0},{3,1},{4,6},{5,7},{6,4},{7,5},{8,10},{9,11},{10,... | collective-permute-start | bytes 393224 | tf_op jit(solution)/shard_map/ppermute | solution.py:447
  11.4 0.0 collective-permute-done
  11.4 0.7 %pad_add_fusion.refs_0_ = s32[2,32]{1,0:T(2,128)S(1)} fusion(s32[1,32]{1,0:T(1,128)S(1)} %bitcast.5, s32[1,32]{1,0:T(1,128)} %bitcast.4), kind=kLoop, calls=%fused_computation | loop fusion | flops 64 | bytes 512 | tf_op jit(solution)/shard_map/stack | solution.py:465
  12.1 0.0 collective-permute-start.1
  12.1 0.9 %reshape.3.refs_2_ = f32[2,256,16]{2,1,0:T(8,128)S(1)} reshape(f32[2,4096]{1,0:T(2,128)} %param.11) | data formatting | bytes 65536 | tf_op jit(solution)/shard_map/reshape | solution.py:487
  13.0 0.0 copy-start
  13.0 0.0 copy-start.1
  13.0 0.0 copy-start.2
  13.0 0.0 copy-start.4
  13.1 0.0 copy-start.5
  13.1 0.2 collective-permute-done.1.refs_1_
  13.2 0.4 collective-permute-start.2
  13.7 0.0 copy-start.6
  13.7 1.0 %copy-done.6 = bf16[2,2,2,256,128]{4,3,2,1,0:T(8,128)(2,1)S(1)} copy-done((bf16[2,2,2,256,128]{4,3,2,1,0:T(8,128)(2,1)S(1)}, bf16[2,2,2,256,128]{4,3,2,1,0:T(8,128)(2,1)}, u32[]{:S(2)}) %copy-start.6) | copy-done | bytes 524312
  14.7 0.0 copy-start.7
  14.7 0.7 %copy-done.7 = f32[2]{0:T(128)S(1)} copy-done((f32[2]{0:T(128)S(1)}, f32[2]{0:T(128)}, u32[]{:S(2)}) %copy-start.7) | copy-done | bytes 32
  15.3 5.7 %shard_map.100 = (bf16[2,16,256,128]{3,2,1,0:T(8,128)(2,1)S(1)}, bf16[4,1024,256]{2,1,0:T(8,128)(2,1)S(1)}, bf16[2,512,256]{2,1,0:T(8,128)(2,1)S(1)}, bf16[2,8,5...) custom-call(s32[2]{0:T(128)S(1)} %pad_add_fusion.1.place_ref, f32[2]{0:T(128)S(1)} %copy-done.7, ...), custom_call_target="tpu_custom_call" | custom-call | flops 1073741824 | bytes 8388608 | tf_op jit(solution)/shard_map/pallas_call | solution.py:469
  21.1 0.0 collective-permute-done.9.refs_0_
  21.1 0.3 collective-permute-start.6
  21.4 0.0 collective-permute-done.13.rest_21_
  21.4 0.1 collective-permute-start.15
  21.5 0.0 collective-permute-done.7.refs_2_.rest_15_
  21.5 0.3 collective-permute-start.14
  21.8 0.6 %shard_map.102.rest_17_ = bf16[2,256,128]{2,1,0:T(8,128)(2,1)S(1)} custom-call(bf16[2,256,128]{2,1,0:T(8,128)(2,1)S(1)} %collective-permute-done.9.refs_0_, s32[1]{0:T(128)} %get-tuple-element.23.refs_1_, bf16[2,256,128]{2,1,0:T(8,128)(2,1)S(1)} %collective-permute-done.7.refs_2_.rest_15_), custom_call_target="tpu_custom_call", output_to_operand_aliasing={{}: (0, {})} | custom-call | flops 1 | bytes 1 | tf_op jit(solution)/shard_map/pallas_call | solution.py:391
  22.4 0.0 collective-permute-done.3.rest_11_
  22.4 1.7 %collective-permute-start.11 = (bf16[2,256,128]{2,1,0:T(8,128)(2,1)S(1)}, bf16[2,256,128]{2,1,0:T(8,128)(2,1)S(1)}, u32[]{:S(2)}, u32[]{:S(2)}) collective-permute-start(bf16[2,256,128]{2,1,0:T(8,128)(2,1)S(1)} %shard_map.102.rest_17_), channel_id=1, source_target_pairs={{0,2},{1,3},{2,0},{3,1},{4,6},{5,7},{6,4},{7,5},{8,10},{9,11},{10,... | collective-permute-start | bytes 393224 | tf_op jit(solution)/shard_map/ppermute | solution.py:447
  24.2 0.0 collective-permute-done.2.rest_10_
  24.2 0.2 collective-permute-start.4
  24.4 0.0 collective-permute-done.6.rest_14_
  24.4 0.3 collective-permute-start.10
  24.7 3.0 %collective-permute-done.15.rest_23_ = bf16[2,256,128]{2,1,0:T(8,128)(2,1)S(1)} collective-permute-done((bf16[2,256,128]{2,1,0:T(8,128)(2,1)S(1)}, bf16[2,256,128]{2,1,0:T(8,128)(2,1)S(1)}, u32[]{:S(2)}, u32[]{:S(2)}) %collective-permute-start.15) | collective-permute-done | bytes 131104 | tf_op jit(solution)/shard_map/ppermute | solution.py:447
  27.7 0.0 collective-permute-start.8
  27.7 0.0 collective-permute-done.14.rest_22_
  27.7 0.5 %collective-permute-start.16 = (bf16[2,256,128]{2,1,0:T(8,128)(2,1)S(1)}, bf16[2,256,128]{2,1,0:T(8,128)(2,1)S(1)}, u32[]{:S(2)}, u32[]{:S(2)}) collective-permute-start(bf16[2,256,128]{2,1,0:T(8,128)(2,1)S(1)} %collective-permute-done.15.rest_23_), channel_id=1, source_target_pairs={{0,1},{1,0},{2,3},{3,2},{4,5},{5,4},{6,7},{7,6},{8,9},{9,8},{10,11... | collective-permute-start | bytes 393224 | tf_op jit(solution)/shard_map/ppermute | solution.py:447
  28.2 1.7 %collective-permute-done.11.rest_19_ = bf16[2,256,128]{2,1,0:T(8,128)(2,1)S(1)} collective-permute-done((bf16[2,256,128]{2,1,0:T(8,128)(2,1)S(1)}, bf16[2,256,128]{2,1,0:T(8,128)(2,1)S(1)}, u32[]{:S(2)}, u32[]{:S(2)}) %collective-permute-start.11) | collective-permute-done | bytes 131104 | tf_op jit(solution)/shard_map/ppermute | solution.py:447
  29.9 0.0 collective-permute-start.12
  29.9 0.0 collective-permute-done.4.rest_12_
  29.9 0.0 collective-permute-done.8.rest_16_
  29.9 0.0 collective-permute-done.16.rest_24_
  29.9 0.0 collective-permute-done.10.rest_18_
  29.9 1.3 %collective-permute-done.12.rest_20_ = bf16[2,256,128]{2,1,0:T(8,128)(2,1)S(1)} collective-permute-done((bf16[2,256,128]{2,1,0:T(8,128)(2,1)S(1)}, bf16[2,256,128]{2,1,0:T(8,128)(2,1)S(1)}, u32[]{:S(2)}, u32[]{:S(2)}) %collective-permute-start.12) | collective-permute-done | bytes 131104 | tf_op jit(solution)/shard_map/ppermute | solution.py:447
  31.2 0.0 copy-done
  31.2 0.0 copy-done.1
  31.2 0.0 copy-done.2
  31.2 0.0 copy-done.4
  31.3 0.0 copy-done.5
  31.3 12.5 %shard_map.103 = f32[2,1024,1024]{2,1,0:T(8,128)} custom-call(s32[2]{0:T(128)S(1)} %pad_add_fusion.1.place_ref, f32[2,16,16]{2,1,0:T(8,128)S(1)} %copy-done.5, bf16[512,512]{1,0:T(8,128)(2,1)S(1)} %copy-done.2, bf16[512,512]{1,0:T(8,128)(2,1)S(1)} %copy-done.1, bf16[512,512]{1,0:T(8,128)(2,1)S(1)} %copy-done, bf16[128,512]{1,0:T(8,128)(2,1)S(1)} %copy-done.4, ...), custom_call_target="tpu_custom_call" | custom-call | tf_op jit(solution)/shard_map/pallas_call | solution.py:415
Async XLA Ops:
  0.1 1.0 %copy-start.3 = (bf16[2,256,512]{2,1,0:T(8,128)(2,1)S(1)}, bf16[2,256,512]{2,1,0:T(8,128)(2,1)}, u32[]{:S(2)}) copy-start(bf16[2,256,512]{2,1,0:T(8,128)(2,1)} %raw_ref.1) | copy-start | bytes 1572868
  1.8 7.7 %collective-permute-start.5 = (bf16[2,256,128]{2,1,0:T(8,128)(2,1)S(1)}, bf16[2,256,128]{2,1,0:T(8,128)(2,1)S(1)}, u32[]{:S(2)}, u32[]{:S(2)}) collective-permute-start(bf16[2,256,128]{2,1,0:T(8,128)(2,1)S(1)} %get-tuple-element.21), channel_id=1, source_target_pairs={{0,4},{1,5},{2,6},{3,7},{4,0},{5,1},{6,2},{7,3},{8,12},{9,13},{10,... | collective-permute-start | bytes 393224 | tf_op jit(solution)/shard_map/ppermute | solution.py:447
  4.9 6.6 %collective-permute-start = (s32[32]{0:T(128)}, s32[32]{0:T(128)S(1)}, u32[]{:S(2)}, u32[]{:S(2)}) collective-permute-start(s32[32]{0:T(128)} %param.12), channel_id=1, source_target_pairs={{0,2},{1,3},{2,0},{3,1},{4,6},{5,7},{6,4},{7,5},{8,10},{9,11},{10,... | collective-permute-start | bytes 392 | tf_op jit(solution)/shard_map/ppermute | solution.py:447
  6.4 14.7 %collective-permute-start.9 = (bf16[2,256,128]{2,1,0:T(8,128)(2,1)S(1)}, bf16[2,256,128]{2,1,0:T(8,128)(2,1)S(1)}, u32[]{:S(2)}, u32[]{:S(2)}) collective-permute-start(bf16[2,256,128]{2,1,0:T(8,128)(2,1)S(1)} %get-tuple-element.22), channel_id=1, source_target_pairs={{0,8},{1,9},{2,10},{3,11},{4,12},{5,13},{6,14},{7,15},{8,0},{9,1},... | collective-permute-start | bytes 393224 | tf_op jit(solution)/shard_map/ppermute | solution.py:447
  9.0 12.4 %collective-permute-start.13 = (bf16[2,256,128]{2,1,0:T(8,128)(2,1)S(1)}, bf16[2,256,128]{2,1,0:T(8,128)(2,1)S(1)}, u32[]{:S(2)}, u32[]{:S(2)}) collective-permute-start(bf16[2,256,128]{2,1,0:T(8,128)(2,1)S(1)} %get-tuple-element.24), channel_id=1, source_target_pairs={{0,12},{1,13},{2,14},{3,15},{4,8},{5,9},{6,10},{7,11},{8,4},{9,5},... | collective-permute-start | bytes 393224 | tf_op jit(solution)/shard_map/ppermute | solution.py:447
  9.2 13.2 %collective-permute-start.3 = (bf16[2,256,128]{2,1,0:T(8,128)(2,1)S(1)}, bf16[2,256,128]{2,1,0:T(8,128)(2,1)S(1)}, u32[]{:S(2)}, u32[]{:S(2)}) collective-permute-start(bf16[2,256,128]{2,1,0:T(8,128)(2,1)S(1)} %get-tuple-element.20.rest_9_), channel_id=1, source_target_pairs={{0,2},{1,3},{2,0},{3,1},{4,6},{5,7},{6,4},{7,5},{8,10},{9,11},{10,... | collective-permute-start | bytes 393224 | tf_op jit(solution)/shard_map/ppermute | solution.py:447
  9.5 12.0 %collective-permute-start.7 = (bf16[2,256,128]{2,1,0:T(8,128)(2,1)S(1)}, bf16[2,256,128]{2,1,0:T(8,128)(2,1)S(1)}, u32[]{:S(2)}, u32[]{:S(2)}) collective-permute-start(bf16[2,256,128]{2,1,0:T(8,128)(2,1)S(1)} %collective-permute-done.5.rest_13_), channel_id=1, source_target_pairs={{0,2},{1,3},{2,0},{3,1},{4,6},{5,7},{6,4},{7,5},{8,10},{9,11},{10,... | collective-permute-start | bytes 393224 | tf_op jit(solution)/shard_map/ppermute | solution.py:447
  12.1 1.1 %collective-permute-start.1 = (s32[2,32]{1,0:T(2,128)S(1)}, s32[2,32]{1,0:T(2,128)S(1)}, u32[]{:S(2)}, u32[]{:S(2)}) collective-permute-start(s32[2,32]{1,0:T(2,128)S(1)} %pad_add_fusion.refs_0_), channel_id=1, source_target_pairs={{0,1},{1,0},{2,3},{3,2},{4,5},{5,4},{6,7},{7,6},{8,9},{9,8},{10,11... | collective-permute-start | bytes 776 | tf_op jit(solution)/shard_map/ppermute | solution.py:447
  13.0 18.2 %copy-start = (bf16[512,512]{1,0:T(8,128)(2,1)S(1)}, bf16[512,512]{1,0:T(8,128)(2,1)}, u32[]{:S(2)}) copy-start(bf16[512,512]{1,0:T(8,128)(2,1)} %constant.42.clone.rest_2_) | copy-start | bytes 1572868
  13.0 18.2 %copy-start.1 = (bf16[512,512]{1,0:T(8,128)(2,1)S(1)}, bf16[512,512]{1,0:T(8,128)(2,1)}, u32[]{:S(2)}) copy-start(bf16[512,512]{1,0:T(8,128)(2,1)} %constant.41.clone.rest_1_) | copy-start | bytes 1572868
  13.0 18.2 %copy-start.2 = (bf16[512,512]{1,0:T(8,128)(2,1)S(1)}, bf16[512,512]{1,0:T(8,128)(2,1)}, u32[]{:S(2)}) copy-start(bf16[512,512]{1,0:T(8,128)(2,1)} %constant.40.clone.rest_0_) | copy-start | bytes 1572868
  13.0 18.2 %copy-start.4 = (bf16[128,512]{1,0:T(8,128)(2,1)S(1)}, bf16[128,512]{1,0:T(8,128)(2,1)}, u32[]{:S(2)}) copy-start(bf16[128,512]{1,0:T(8,128)(2,1)} %constant.43.clone.rest_3_) | copy-start | bytes 393220
  13.1 18.2 %copy-start.5 = (f32[2,16,16]{2,1,0:T(8,128)S(1)}, f32[2,16,16]{2,1,0:T(8,128)}, u32[]{:S(2)}) copy-start(f32[2,16,16]{2,1,0:T(8,128)} %constant.44.clone.turn_ref) | copy-start | bytes 6148
  13.2 10.9 %collective-permute-start.2 = (bf16[2,256,128]{2,1,0:T(8,128)(2,1)S(1)}, bf16[2,256,128]{2,1,0:T(8,128)(2,1)S(1)}, u32[]{:S(2)}, u32[]{:S(2)}) collective-permute-start(bf16[2,256,128]{2,1,0:T(8,128)(2,1)S(1)} %get-tuple-element.20.rest_9_), channel_id=1, source_target_pairs={{0,1},{1,0},{2,3},{3,2},{4,5},{5,4},{6,7},{7,6},{8,9},{9,8},{10,11... | collective-permute-start | bytes 393224 | tf_op jit(solution)/shard_map/ppermute | solution.py:447
  13.7 1.0 %copy-start.6 = (bf16[2,2,2,256,128]{4,3,2,1,0:T(8,128)(2,1)S(1)}, bf16[2,2,2,256,128]{4,3,2,1,0:T(8,128)(2,1)}, u32[]{:S(2)}) copy-start(bf16[2,2,2,256,128]{4,3,2,1,0:T(8,128)(2,1)} %refs_3_.1) | copy-start | bytes 1572868
  14.7 0.7 %copy-start.7 = (f32[2]{0:T(128)S(1)}, f32[2]{0:T(128)}, u32[]{:S(2)}) copy-start(f32[2]{0:T(128)} %rate_ref.1) | copy-start | bytes 28
  21.1 3.3 %collective-permute-start.6 = (bf16[2,256,128]{2,1,0:T(8,128)(2,1)S(1)}, bf16[2,256,128]{2,1,0:T(8,128)(2,1)S(1)}, u32[]{:S(2)}, u32[]{:S(2)}) collective-permute-start(bf16[2,256,128]{2,1,0:T(8,128)(2,1)S(1)} %collective-permute-done.5.rest_13_), channel_id=1, source_target_pairs={{0,1},{1,0},{2,3},{3,2},{4,5},{5,4},{6,7},{7,6},{8,9},{9,8},{10,11... | collective-permute-start | bytes 393224 | tf_op jit(solution)/shard_map/ppermute | solution.py:447
  21.4 6.3 %collective-permute-start.15 = (bf16[2,256,128]{2,1,0:T(8,128)(2,1)S(1)}, bf16[2,256,128]{2,1,0:T(8,128)(2,1)S(1)}, u32[]{:S(2)}, u32[]{:S(2)}) collective-permute-start(bf16[2,256,128]{2,1,0:T(8,128)(2,1)S(1)} %collective-permute-done.13.rest_21_), channel_id=1, source_target_pairs={{0,2},{1,3},{2,0},{3,1},{4,6},{5,7},{6,4},{7,5},{8,10},{9,11},{10,... | collective-permute-start | bytes 393224 | tf_op jit(solution)/shard_map/ppermute | solution.py:447
  21.5 6.3 %collective-permute-start.14 = (bf16[2,256,128]{2,1,0:T(8,128)(2,1)S(1)}, bf16[2,256,128]{2,1,0:T(8,128)(2,1)S(1)}, u32[]{:S(2)}, u32[]{:S(2)}) collective-permute-start(bf16[2,256,128]{2,1,0:T(8,128)(2,1)S(1)} %collective-permute-done.13.rest_21_), channel_id=1, source_target_pairs={{0,1},{1,0},{2,3},{3,2},{4,5},{5,4},{6,7},{7,6},{8,9},{9,8},{10,11... | collective-permute-start | bytes 393224 | tf_op jit(solution)/shard_map/ppermute | solution.py:447
  22.4 7.5 %collective-permute-start.11 = (bf16[2,256,128]{2,1,0:T(8,128)(2,1)S(1)}, bf16[2,256,128]{2,1,0:T(8,128)(2,1)S(1)}, u32[]{:S(2)}, u32[]{:S(2)}) collective-permute-start(bf16[2,256,128]{2,1,0:T(8,128)(2,1)S(1)} %shard_map.102.rest_17_), channel_id=1, source_target_pairs={{0,2},{1,3},{2,0},{3,1},{4,6},{5,7},{6,4},{7,5},{8,10},{9,11},{10,... | collective-permute-start | bytes 393224 | tf_op jit(solution)/shard_map/ppermute | solution.py:447
  24.2 5.7 %collective-permute-start.4 = (bf16[2,256,128]{2,1,0:T(8,128)(2,1)S(1)}, bf16[2,256,128]{2,1,0:T(8,128)(2,1)S(1)}, u32[]{:S(2)}, u32[]{:S(2)}) collective-permute-start(bf16[2,256,128]{2,1,0:T(8,128)(2,1)S(1)} %collective-permute-done.3.rest_11_), channel_id=1, source_target_pairs={{0,1},{1,0},{2,3},{3,2},{4,5},{5,4},{6,7},{7,6},{8,9},{9,8},{10,11... | collective-permute-start | bytes 393224 | tf_op jit(solution)/shard_map/ppermute | solution.py:447
  24.4 5.5 %collective-permute-start.10 = (bf16[2,256,128]{2,1,0:T(8,128)(2,1)S(1)}, bf16[2,256,128]{2,1,0:T(8,128)(2,1)S(1)}, u32[]{:S(2)}, u32[]{:S(2)}) collective-permute-start(bf16[2,256,128]{2,1,0:T(8,128)(2,1)S(1)} %shard_map.102.rest_17_), channel_id=1, source_target_pairs={{0,1},{1,0},{2,3},{3,2},{4,5},{5,4},{6,7},{7,6},{8,9},{9,8},{10,11... | collective-permute-start | bytes 393224 | tf_op jit(solution)/shard_map/ppermute | solution.py:447
  27.7 2.2 %collective-permute-start.8 = (bf16[2,256,128]{2,1,0:T(8,128)(2,1)S(1)}, bf16[2,256,128]{2,1,0:T(8,128)(2,1)S(1)}, u32[]{:S(2)}, u32[]{:S(2)}) collective-permute-start(bf16[2,256,128]{2,1,0:T(8,128)(2,1)S(1)} %collective-permute-done.7.refs_2_.rest_15_), channel_id=1, source_target_pairs={{0,1},{1,0},{2,3},{3,2},{4,5},{5,4},{6,7},{7,6},{8,9},{9,8},{10,11... | collective-permute-start | bytes 393224 | tf_op jit(solution)/shard_map/ppermute | solution.py:447
  27.7 2.2 %collective-permute-start.16 = (bf16[2,256,128]{2,1,0:T(8,128)(2,1)S(1)}, bf16[2,256,128]{2,1,0:T(8,128)(2,1)S(1)}, u32[]{:S(2)}, u32[]{:S(2)}) collective-permute-start(bf16[2,256,128]{2,1,0:T(8,128)(2,1)S(1)} %collective-permute-done.15.rest_23_), channel_id=1, source_target_pairs={{0,1},{1,0},{2,3},{3,2},{4,5},{5,4},{6,7},{7,6},{8,9},{9,8},{10,11... | collective-permute-start | bytes 393224 | tf_op jit(solution)/shard_map/ppermute | solution.py:447
  29.9 1.3 %collective-permute-start.12 = (bf16[2,256,128]{2,1,0:T(8,128)(2,1)S(1)}, bf16[2,256,128]{2,1,0:T(8,128)(2,1)S(1)}, u32[]{:S(2)}, u32[]{:S(2)}) collective-permute-start(bf16[2,256,128]{2,1,0:T(8,128)(2,1)S(1)} %collective-permute-done.11.rest_19_), channel_id=1, source_target_pairs={{0,1},{1,0},{2,3},{3,2},{4,5},{5,4},{6,7},{7,6},{8,9},{9,8},{10,11... | collective-permute-start | bytes 393224 | tf_op jit(solution)/shard_map/ppermute | solution.py:447
